TPU v7x, 256 devices: a whole 4x4x8 slice. The times are simulated.
256 devices in a mesh: ctx: 16 (over z, core), vocab: 16 (over x, y).
Axes of the slice: x: 4, y: 4, z: 8, core: 2. Of those that a mesh axis runs over, the one named last changes fastest.
Arguments:
- hidden_states: bfloat16 [2048, 3584], P('ctx'), may hold values from -40 to 40, as said below
- head_weight: bfloat16 [3584, 81920], P(None, ('ctx', 'vocab')), may hold values from -3 to 3, as said below
- token_ids: int32 [2048], P('ctx'), may hold values from 0 to 81919
- response_mask: int32 [2048], P('ctx'), may hold values 0 or 1
- teacher_logprob: float32 [2048], P('ctx'), may hold values from -18 to -8
Outputs:
- hidden_grad: bfloat16 [2048, 3584], P('ctx', 'vocab')
- head_grad: bfloat16 [3584, 81920], P(None, ('ctx', 'vocab'))
Inputs may be any that keep to these rules, and one draw needn't show every extreme that they name: `hidden_states`: rows of scale about 1 to 4; a few rows may be strongly aligned with head columns. `head_weight`: head entries of order 3 / sqrt(3584).
All inputs are finite; a program needn't handle non-finite values. No bound on the sum of `response_mask` on one device may be relied on, other than what follows from the above.
Results may differ from a plain program's by a relative error of at most 0.02.
Values may be sent and summed in bfloat16 or wider, within the bound.
No kernel may reach another device: no remote copies, remote signals or barrier semaphores. Data moves between devices by JAX's collectives and lax.ppermute only.
A program may use at most 128 MiB of HBM per device.

v0:
```python
import jax
import jax.numpy as jnp
from jax import lax
from jax.sharding import PartitionSpec as P


def combined_all(part, axis, combine):
    gathered = jax.tree.map(lambda a: lax.all_gather(a, axis), part)

    def take(source):
        return jax.tree.map(lambda a: lax.dynamic_index_in_dim(a, source, 0, False), gathered)

    return lax.fori_loop(
        1, lax.axis_size(axis), lambda source, state: combine(state, take(source)), take(0)
    )


def entering(part, axis, combine, identity):
    count = lax.axis_size(axis)
    place = lax.axis_index(axis)
    ahead = count - 1 - place
    gathered = lax.all_gather(part, axis)
    state = jnp.zeros_like(part) + jnp.asarray(identity, part.dtype)

    def one(turn, state):
        source = count - 1 - turn
        return combine(state, lax.dynamic_index_in_dim(gathered, source, 0, False))

    return lax.fori_loop(0, ahead, one, state)


def combine_stats(left, right):
    left_max, left_sum, left_pick = left
    right_max, right_sum, right_pick = right
    merged = jnp.maximum(left_max, right_max)
    joined = left_sum * jnp.exp(left_max - merged) + right_sum * jnp.exp(right_max - merged)
    return (merged, joined, left_pick + right_pick)


def add_values(earlier, later_value):
    return earlier + later_value


def reverse_cumsum(values):
    return jnp.flip(jnp.cumsum(jnp.flip(values)))


def on_device(hidden_states, head_weight, token_ids, response_mask, teacher_logprob):
    own_rows = hidden_states.shape[0]
    ctx_count = lax.axis_size("ctx")
    vocab_count = lax.axis_size("vocab")
    gathered, all_ids = (
        lax.all_gather(hidden_states, "ctx", axis=0, tiled=True),
        lax.all_gather(token_ids, "ctx", axis=0, tiled=True),
    )
    all_rows = gathered.shape[0]
    columns_here = head_weight.shape[1]
    logits = jnp.dot(gathered, head_weight, preferred_element_type=jnp.float32)
    column_start = (lax.axis_index("ctx") * vocab_count + lax.axis_index("vocab")) * columns_here
    columns = column_start + jnp.arange(columns_here, dtype=jnp.int32)
    matches = all_ids[:, None] == columns[None, :]
    row_max = jnp.max(logits, axis=1)
    exp_sum = jnp.sum(jnp.exp(logits - row_max[:, None]), axis=1)
    picked = jnp.sum(jnp.where(matches, logits, jnp.float32(0.0)), axis=1)
    group_max, group_sum, group_pick = combined_all(
        (row_max, exp_sum, picked), "vocab", combine_stats
    )
    shaped = (
        group_max.reshape(ctx_count, own_rows),
        group_sum.reshape(ctx_count, own_rows),
        group_pick.reshape(ctx_count, own_rows),
    )
    peer_max, peer_sum, peer_pick = (
        lax.all_to_all(shaped[0], "ctx", split_axis=0, concat_axis=0, tiled=True),
        lax.all_to_all(shaped[1], "ctx", split_axis=0, concat_axis=0, tiled=True),
        lax.all_to_all(shaped[2], "ctx", split_axis=0, concat_axis=0, tiled=True),
    )
    merged_max = jnp.max(peer_max, axis=0)
    merged_sum = jnp.sum(peer_sum * jnp.exp(peer_max - merged_max[None, :]), axis=0)
    own_norm = merged_max + jnp.log(merged_sum)
    own_pick = jnp.sum(peer_pick, axis=0)
    own_mask = response_mask.astype(jnp.float32)
    ratio = own_mask * (own_pick - own_norm - teacher_logprob)
    beyond = entering(jnp.sum(ratio), "ctx", add_values, jnp.float32(0.0))
    own_weight = own_mask * (reverse_cumsum(ratio) + beyond) / float(all_rows)
    token_weight, log_norm = (
        lax.all_gather(own_weight, "ctx", axis=0, tiled=True),
        lax.all_gather(own_norm, "ctx", axis=0, tiled=True),
    )
    softmax_part = jnp.exp(logits - log_norm[:, None])
    logit_grad = (token_weight[:, None] * (matches.astype(jnp.float32) - softmax_part)).astype(
        jnp.bfloat16
    )
    head_grad = lax.dot_general(
        gathered, logit_grad, (((0,), (0,)), ((), ())), preferred_element_type=jnp.float32
    ).astype(jnp.bfloat16)
    token_part = lax.psum_scatter(
        lax.dot_general(
            logit_grad, head_weight, (((1,), (1,)), ((), ())), preferred_element_type=jnp.float32
        ).astype(jnp.bfloat16),
        "ctx",
        scatter_dimension=0,
        tiled=True,
    )
    hidden_grad = lax.psum_scatter(token_part, "vocab", scatter_dimension=1, tiled=True)
    return (hidden_grad, head_grad)


def solution(mesh):
    placed = (P("ctx", None), P(None, ("ctx", "vocab")), P("ctx"), P("ctx"), P("ctx"))
    return jax.shard_map(
        on_device,
        mesh=mesh,
        in_specs=placed,
        out_specs=(P("ctx", "vocab"), P(None, ("ctx", "vocab"))),
        check_vma=False,
    )
```

profile of v0, /device:TPU:8, one launch (start us, length us, event | category | flops | bytes accessed | tf_op | source)
XLA Modules:
  0.0 492.5 jit_solution(3465607424955050714)
XLA Ops:
  7.2 0.7 all-gather.8.cloned.1.call-update
  7.9 20.0 %all-gather.3 = s32[16,1,128]{2,1,0:T(1,128)S(1)} all-gather(s32[1,1,128]{2,1,0:T(1,128)} %bitcast.54), channel_id=1, replica_groups=mesh['ctx'=16,'vocab'=16] {'ctx'}, dimensions={0}, use_global_device_ids=true | all-gather | bytes 8704 | tf_op jit(solution)/shard_map/all_gather | solution.py:54
  28.0 70.3 %all-gather.8.cloned.1.call-done = bf16[2048,3584]{1,0:T(8,128)(2,1)} async-done(((bf16[128,3584]{1,0:T(8,128)(2,1)}), bf16[2048,3584]{1,0:T(8,128)(2,1)}) %all-gather.8.cloned.1.call-update) | async-done | bytes 14680080 | tf_op jit(solution)/shard_map/all_gather | solution.py:53
  98.3 8.2 %fusion.9 = (f32[2048]{0:T(1024)S(1)}, f32[2048,320]{0,1:T(8,128)S(1)}) fusion(bf16[2048,3584]{1,0:T(8,128)(2,1)} %all-gather.8.cloned.1.call-done, bf16[3584,320]{0,1:T(8,128)(2,1)S(1)} %copy-done), kind=kOutput, calls=%fused_computation.21 | convolution fusion | flops 4698273792 | bytes 19603456 | tf_op jit(solution)/shard_map/dot_general | solution.py:58
  106.6 1.4 copy-done.1
  108.0 0.6 fusion.1
  108.7 23.3 %all-gather.2 = f32[32768]{0:T(1024)S(1)} all-gather(f32[2048]{0:T(1024)S(1)} %get-tuple-element.252), channel_id=4, replica_groups=mesh['ctx'=16,'vocab'=16] {'vocab'}, dimensions={0}, use_global_device_ids=true | all-gather | bytes 139264 | tf_op jit(solution)/shard_map/all_gather | solution.py:8
  132.0 22.0 %all-gather = f32[32768]{0:T(1024)S(1)} all-gather(f32[2048]{0:T(1024)S(1)} %get-tuple-element.283), channel_id=2, replica_groups=mesh['ctx'=16,'vocab'=16] {'vocab'}, dimensions={0}, use_global_device_ids=true | all-gather | bytes 139264 | tf_op jit(solution)/shard_map/all_gather | solution.py:8
  154.1 22.4 %all-gather.1 = f32[32768]{0:T(1024)S(1)} all-gather(f32[2048]{0:T(1024)S(1)} %get-tuple-element.253), channel_id=3, replica_groups=mesh['ctx'=16,'vocab'=16] {'vocab'}, dimensions={0}, use_global_device_ids=true | all-gather | bytes 139264 | tf_op jit(solution)/shard_map/all_gather | solution.py:8
  176.5 0.6 slice.7
  177.1 20.6 %while.31 = (s32[]{:T(128)}, f32[2048]{0:T(1024)S(1)}, f32[2048]{0:T(1024)}, f32[2048]{0:T(1024)S(1)}, f32[16,2048]{1,0:T(8,128)S(1)}, /*index=5*/f32[16,2048]{1...) while((s32[]{:T(128)}, f32[2048]{0:T(1024)S(1)}, f32[2048]{0:T(1024)}, ...), condition=%wide.region_4.5_spmd, body=%wide.region_3.4_spmd.sunk | while | flops 14341 | bytes 123023 | solution.py:13
  177.2 1.3 multiply_add_fusion.2
  178.6 1.3 multiply_add_fusion.2
  179.9 1.3 multiply_add_fusion.2
  181.3 1.3 multiply_add_fusion.2
  182.7 1.3 multiply_add_fusion.2
  184.0 1.3 multiply_add_fusion.2
  185.4 1.3 multiply_add_fusion.2
  186.8 1.3 multiply_add_fusion.2
  188.1 1.3 multiply_add_fusion.2
  189.5 1.3 multiply_add_fusion.2
  190.9 1.3 multiply_add_fusion.2
  192.2 1.3 multiply_add_fusion.2
  193.6 1.3 multiply_add_fusion.2
  195.0 1.3 multiply_add_fusion.2
  196.3 1.3 multiply_add_fusion.2
  197.7 11.7 %all_to_all.33 = f32[16,1,128]{2,1,0:T(1,128)S(1)} all-to-all(f32[16,1,128]{2,1,0:T(1,128)S(1)} %bitcast.42), channel_id=1, replica_groups=mesh['ctx'=16,'vocab'=16] {'ctx'}, dimensions={0} | all-to-all | bytes 16384 | tf_op jit(solution)/shard_map/all_to_all | solution.py:74
  209.4 10.1 %all_to_all.34 = f32[16,1,128]{2,1,0:T(1,128)S(1)} all-to-all(f32[16,1,128]{2,1,0:T(1,128)S(1)} %bitcast.41), channel_id=1, replica_groups=mesh['ctx'=16,'vocab'=16] {'ctx'}, dimensions={0} | all-to-all | bytes 16384 | tf_op jit(solution)/shard_map/all_to_all | solution.py:76
  219.5 3.5 all-to-all-start.2
  223.0 0.6 dynamic-slice
  223.7 6.7 %all-to-all-done.2 = f32[16,1,128]{2,1,0:T(1,128)S(1)} async-done(((f32[16,1,128]{2,1,0:T(1,128)}), f32[16,1,128]{2,1,0:T(1,128)S(1)}, u32[]{:S(2)}, u32[]{:S(2)}) %all-to-all-start.2) | async-done | bytes 8224 | tf_op jit(solution)/shard_map/all_to_all | solution.py:75
  230.4 0.6 fusion.8
  231.1 1.4 dynamic-update-slice
  232.4 23.5 %all-reduce = f32[16]{0:T(128)S(1)} all-reduce(f32[16]{0:T(128)S(1)} %dynamic-update-slice), channel_id=1, replica_groups=mesh['ctx'=16,'vocab'=16] {'ctx'}, use_global_device_ids=true, to_apply=%add | all-reduce | flops 16 | bytes 128
  256.0 18.9 %while.32 = (s32[]{:T(128)}, f32[]{:T(128)}, s32[]{:T(128)}, f32[16]{0:T(128)S(1)}, s32[]{:T(128)}, /*index=5*/s32[]{:T(128)}, s32[]{:T(128)}, s32[]{:T(128)}) while((s32[]{:T(128)}, f32[]{:T(128)}, s32[]{:T(128)}, f32[16]{0:T(128)S(1)}, s32[]{:T(128)}, /*index=5*/s32[]{:T(128)}, s32[]{:T(128)}, s32[]{:T(128)}) %tuple.80), condition=%wide.region_11.12_spmd, body=%wide.region_10.11_spmd.sunk | while | flops 7 | bytes 163 | solution.py:29
  257.3 0.6 dynamic_slice.58
  258.6 0.6 dynamic_slice.58
  259.8 0.6 dynamic_slice.58
  261.1 0.6 dynamic_slice.58
  262.3 0.6 dynamic_slice.58
  263.6 0.6 dynamic_slice.58
  274.9 14.1 %all-gather.5 = f32[16,1,128]{2,1,0:T(1,128)S(1)} all-gather(f32[1,1,128]{2,1,0:T(1,128)S(1)} %get-tuple-element.282), channel_id=1, replica_groups=mesh['ctx'=16,'vocab'=16] {'ctx'}, dimensions={0}, use_global_device_ids=true | all-gather | bytes 8704 | tf_op jit(solution)/shard_map/all_gather | solution.py:88
  289.5 16.0 %all-gather.4 = f32[16,1,128]{2,1,0:T(1,128)S(1)} all-gather(f32[1,1,128]{2,1,0:T(1,128)S(1)} %multiply_bitcast_fusion), channel_id=1, replica_groups=mesh['ctx'=16,'vocab'=16] {'ctx'}, dimensions={0}, use_global_device_ids=true | all-gather | bytes 8704 | tf_op jit(solution)/shard_map/all_gather | solution.py:87
  305.5 13.3 %convolution_convert_fusion = bf16[2048,3584]{1,0:T(8,128)(2,1)} fusion(bf16[3584,320]{0,1:T(8,128)(2,1)S(1)} %copy-done, f32[2048,320]{0,1:T(8,128)} %copy-done.1, f32[2048]{0:T(1024)S(1)} %bitcast.49, f32[2048]{0:T(1024)S(1)} %bitcast.51, s32[2048]{0:T(1024)S(1)} %bitcast.45, s32[320]{0:T(512)S(1)} %iota_add_fusion), kind=kOutput, calls=%fused_computation.4 | convolution fusion | flops 4708892672 | bytes 19621120 | tf_op jit(solution)/shard_map/dot_general | solution.py:98
  319.0 86.2 %reduce-scatter.5.cloned.1.call-done = bf16[128,3584]{1,0:T(8,128)(2,1)} async-done(((bf16[2048,3584]{1,0:T(8,128)(2,1)}), bf16[128,3584]{1,0:T(8,128)(2,1)}) %reduce-scatter.5.cloned.1.call-update) | async-done | bytes 917520 | tf_op jit(solution)/shard_map/reduce_scatter | solution.py:97
  405.2 2.2 copy.20
  407.5 12.6 %fusion = bf16[3584,320]{0,1:T(8,128)(2,1)} fusion(bf16[2048,3584]{1,0:T(8,128)(2,1)} %all-gather.8.cloned.1.call-done, f32[2048,320]{0,1:T(8,128)} %copy-done.1, f32[2048]{0:T(1024)S(1)} %bitcast.50, f32[2048]{0:T(1024)S(1)} %bitcast.52, s32[2048]{0:T(1024)S(1)} %bitcast.46, s32[320]{0:T(512)S(1)} %iota_add_fusion), kind=kOutput, calls=%fused_computation.6 | convolution fusion | flops 4702699520 | bytes 19621120 | tf_op jit(solution)/shard_map/dot_general | solution.py:94
  420.1 65.9 %reduce-scatter.7.cloned.1.call-done = bf16[224,128]{1,0:T(8,128)(2,1)} async-done(((bf16[3584,128]{1,0:T(8,128)(2,1)}), bf16[224,128]{1,0:T(8,128)(2,1)}) %reduce-scatter.7.cloned.1.call-update) | async-done | bytes 57360
  (84 shorter events, 7.0 us)
Async XLA Ops:
  7.2 91.1 %copy-start = (bf16[3584,320]{0,1:T(8,128)(2,1)S(1)}, bf16[3584,320]{0,1:T(8,128)(2,1)}, u32[]{:S(2)}) copy-start(bf16[3584,320]{0,1:T(8,128)(2,1)} %param.10) | copy-start | bytes 6881284
  7.2 91.1 %all-gather.8.cloned.1.call-start = ((), (), s32[]{:S(2)}) async-start(), calls=%async_computation.5 | async-start | bytes 15597568 | tf_op jit(solution)/shard_map/all_gather | solution.py:53
  106.6 1.5 copy-start.1
  106.6 116.5 %copy-start.4 = (u32[256]{0:T(256)S(1)}, u32[256]{0:T(256)}, u32[]{:S(2)}) copy-start(u32[256]{0:T(256)} %constant.101) | copy-start | bytes 3076
  106.6 123.9 %copy-start.2 = (s32[128]{0:T(128)S(1)}, s32[128]{0:T(128)}, u32[]{:S(2)}) copy-start(s32[128]{0:T(128)} %param.12) | copy-start | bytes 1540
  106.6 123.8 %copy-start.3 = (f32[128]{0:T(128)S(1)}, f32[128]{0:T(128)}, u32[]{:S(2)}) copy-start(f32[128]{0:T(128)} %param.13) | copy-start | bytes 1540
  219.5 10.9 %all-to-all-start.2 = ((f32[16,1,128]{2,1,0:T(1,128)}), f32[16,1,128]{2,1,0:T(1,128)S(1)}, u32[]{:S(2)}, u32[]{:S(2)}) async-start(f32[16,1,128]{2,1,0:T(1,128)} %bitcast.9), calls=%async_computation.2 | async-start | bytes 16384 | tf_op jit(solution)/shard_map/all_to_all | solution.py:75
  223.0 182.3 %reduce-scatter.5.cloned.1.call-start = ((), (), s32[]{:S(2)}) async-start(), calls=%async_computation.6 | async-start | bytes 15597568 | tf_op jit(solution)/shard_map/reduce_scatter | solution.py:97
  318.8 167.1 %reduce-scatter.7.cloned.1.call-start = ((), (), s32[]{:S(2)}) async-start(), calls=%async_computation.7 | async-start | bytes 974848
Sparse Core Ops, SparseCore 0:
  9.8 88.4 all-gather.7
  318.9 86.2 reduce-scatter.4
  409.3 76.5 reduce-scatter.6
where the time goes:
time: 494 us; the launch traced here: 492 us
  waiting for transfers between devices  230 us (47%)
  blocking collectives  163 us (33%)
  matrix products  34.1 us (7%)
  other arithmetic  21.4 us (4%)
  local copies, waits for them, and re-layouts  15.9 us (3%)
  between operations  13.9 us (3%)
  loops' own time  10.4 us (2%)
    reduce_scatter x1, waiting for transfers between devices, on_device(): lax.psum_scatter(lax.dot_general(logit_grad, head_weight, (((1,), (1,)),...  86.2 us
    all_gather x1, waiting for transfers between devices, on_device(): lax.all_gather(hidden_states, 'ctx', axis=0, tiled=True)  70.3 us
    all_gather x3, blocking collectives, combined_all(): gathered = jax.tree.map(lambda a: lax.all_gather(a, axis), part)  67.7 us
    unnamed x4, waiting for transfers between devices  66.6 us
    unnamed x1, blocking collectives  23.5 us
    all_gather x1, blocking collectives, on_device(): lax.all_gather(token_ids, 'ctx', axis=0, tiled=True)  20 us
    add x15, other arithmetic, combine_stats(): left_sum * jnp.exp(left_max - merged)  19.7 us
    all_gather x1, blocking collectives, on_device(): lax.all_gather(own_weight, 'ctx', axis=0, tiled=True)  16 us
  transfers between devices with their start and end apart: 4, of which 4 were waited for; matrix products, arithmetic and copies ran while one was open for 3% of the time, Pallas kernels for 0%

commit v1 on v0

v1 whole, which is shorter than its diff:
```python
import jax
import jax.numpy as jnp
from jax import lax
from jax.sharding import Mesh, PartitionSpec as P

F32 = jnp.float32
BF16 = jnp.bfloat16
Z, CORES, X, Y = 8, 2, 4, 4
PLANE = X * Y
SWAP = [(0, 1), (1, 0)]


def broadcast_gather(part, axes, count):
    copies = jnp.broadcast_to(part[None], (count,) + part.shape)
    return lax.all_to_all(copies, axes, 0, 0, tiled=True)


def merge_stats(parts):
    top = jnp.max(parts[:, 0], axis=0)
    total = jnp.sum(parts[:, 1] * jnp.exp(parts[:, 0] - top[None]), axis=0)
    return jnp.stack([top, total, jnp.sum(parts[:, 2], axis=0)])


def on_device(hidden, weight, token_ids, response_mask, teacher_logprob):
    own_rows, features = hidden.shape
    columns_here = weight.shape[1]
    core, z = lax.axis_index("core"), lax.axis_index("z")
    rows = Z * own_rows
    tokens = rows * CORES

    other_weight = lax.ppermute(weight, "core", SWAP)
    both = jnp.concatenate([weight, other_weight], axis=1)
    gathered = lax.all_gather(hidden, "z", axis=0, tiled=True)
    facts = jnp.stack(
        [token_ids.astype(F32), response_mask.astype(F32), teacher_logprob]
    )
    facts = lax.all_gather(facts, ("z", "core"), axis=0).reshape(Z, CORES, 3, own_rows)
    mine = lax.dynamic_index_in_dim(facts, core, 1, False)
    ids = mine[:, 0].astype(jnp.int32).reshape(rows)

    place = lax.axis_index("x") * Y + lax.axis_index("y")
    first = ((z * CORES + core) * PLANE + place) * columns_here
    second = ((z * CORES + 1 - core) * PLANE + place) * columns_here
    span = jnp.arange(columns_here, dtype=jnp.int32)
    columns = jnp.concatenate([first + span, second + span])

    logits = jnp.dot(gathered, both, preferred_element_type=F32)
    matches = ids[:, None] == columns[None, :]
    top = jnp.max(logits, axis=1)
    total = jnp.sum(jnp.exp(logits - top[:, None]), axis=1)
    picked = jnp.sum(jnp.where(matches, logits, F32(0.0)), axis=1)
    stats = jnp.stack([top, total, picked])

    share = rows // PLANE
    stats = stats.reshape(3, PLANE, share).transpose(1, 0, 2)
    stats = merge_stats(lax.all_to_all(stats, ("x", "y"), 0, 0, tiled=True))
    stats = merge_stats(broadcast_gather(stats, "z", Z))
    final = jnp.stack([stats[0] + jnp.log(stats[1]), stats[2]])
    final = broadcast_gather(final, ("core", "x", "y"), CORES * PLANE)
    final = final.reshape(CORES, PLANE, 2, share).transpose(0, 2, 1, 3)
    final = final.reshape(CORES, 2, Z, own_rows)

    mask = facts[:, :, 1]
    norms, picks = final[:, 0].transpose(1, 0, 2), final[:, 1].transpose(1, 0, 2)
    ratio = (mask * (picks - norms - facts[:, :, 2])).reshape(Z * CORES, own_rows)
    place_in = jnp.arange(own_rows, dtype=jnp.int32)
    later = (place_in[None, :] >= place_in[:, None]).astype(F32)
    within = jnp.sum(ratio[:, None, :] * later[None], axis=2)
    shard = jnp.arange(Z * CORES, dtype=jnp.int32)
    after = (shard[None, :] > shard[:, None]).astype(F32)
    beyond = jnp.sum(jnp.sum(ratio, axis=1)[None, :] * after, axis=1)
    weights = mask * (within + beyond[:, None]).reshape(Z, CORES, own_rows) / float(tokens)
    weights = lax.dynamic_index_in_dim(weights, core, 1, False).reshape(rows)
    norm = lax.dynamic_index_in_dim(norms, core, 1, False).reshape(rows)

    grad = weights[:, None] * (matches.astype(F32) - jnp.exp(logits - norm[:, None]))
    grad = grad.astype(BF16)

    partial = lax.dot_general(
        grad, both, (((1,), (1,)), ((), ())), preferred_element_type=F32
    ).astype(BF16)
    mine = lax.psum_scatter(partial, "z", scatter_dimension=0, tiled=True)
    cut = features // PLANE
    blocks = mine.reshape(own_rows, PLANE, cut).transpose(1, 0, 2)
    blocks = lax.all_to_all(blocks, ("x", "y"), 0, 0, tiled=True)
    hidden_grad = jnp.sum(blocks.astype(F32), axis=0).astype(BF16)

    far = lax.dot_general(
        gathered, grad[:, columns_here:], (((0,), (0,)), ((), ())), preferred_element_type=F32
    ).astype(BF16)
    far = lax.ppermute(far, "core", SWAP)
    near = lax.dot_general(
        gathered, grad[:, :columns_here], (((0,), (0,)), ((), ())), preferred_element_type=F32
    )
    head_grad = (near + far.astype(F32)).astype(BF16)
    return hidden_grad, head_grad


def solution(mesh):
    fine = Mesh(mesh.devices.reshape(Z, CORES, X, Y), ("z", "core", "x", "y"))
    by_token = ("z", "core")
    by_column = P(None, ("z", "core", "x", "y"))
    return jax.shard_map(
        on_device,
        mesh=fine,
        in_specs=(P(by_token, None), by_column, P(by_token), P(by_token), P(by_token)),
        out_specs=(P(by_token, ("x", "y")), by_column),
        check_vma=False,
    )
```

time: 494 us -> 271 us (0.55)
  blocking collectives: 163 us -> 33.3 us
  waiting for transfers between devices: 230 us -> 155 us
  other arithmetic: 21.4 us -> 6.35 us
  starting transfers between devices: 3.77 us -> 16.7 us
  loops' own time: 10.4 us -> 0 us
    all_gather x6 -> x1, blocking collectives: 118 us -> 20 us  [on_device(): lax.all_gather(facts, ('z', 'core'), axis=0).reshape(Z, CORES, 3, own_rows)]
    unnamed x4 -> x2, waiting for transfers between devices: 66.6 us -> 0.7 us
    unnamed x1 -> x0, blocking collectives: 23.5 us -> none
    add x31 -> x2, other arithmetic: 19.8 us -> 0.01 us  [the longest x1 0.01 us: on_device(): final = jnp.stack([stats[0] + jnp.log(stats[1]), stats[2]])]
    reduce_scatter x1, waiting for transfers between devices: 86.2 us -> 70.3 us  [on_device(): mine = lax.psum_scatter(partial, 'z', scatter_dimension=0, tiled=True)]
    all_to_all x1 -> x3, waiting for transfers between devices: 6.71 us -> 20.8 us  [the longest x2 13.8 us: broadcast_gather(): return lax.all_to_all(copies, axes, 0, 0, tiled=True)]
    all_to_all x1 -> x3, starting transfers between devices: 3.47 us -> 16.5 us  [the longest x2 9.24 us: broadcast_gather(): return lax.all_to_all(copies, axes, 0, 0, tiled=True)]
    another operation x2 -> x0, loops' own time: 10.4 us -> none  [the longest x1 10.1 us: entering(): return lax.fori_loop(0, ahead, one, state)]
  transfers between devices with their start and end apart: 4 -> 7, of which waited for: 4 -> 5; matrix products, arithmetic and copies ran while one was open for 3% -> 8% of each run, Pallas kernels for 0% -> 0%
where the time goes in v1:
time: 271 us
  waiting for transfers between devices  155 us (57%)
  matrix products  33.6 us (12%)
  blocking collectives  33.3 us (12%)
  starting transfers between devices  16.7 us (6%)
  between operations  14.2 us (5%)
  local copies, waits for them, and re-layouts  12.1 us (4%)
  other arithmetic  6.35 us (2%)
    reduce_scatter x1, waiting for transfers between devices, on_device(): mine = lax.psum_scatter(partial, 'z', scatter_dimension=0, tiled=True)  70.3 us
    all_gather x1, waiting for transfers between devices, on_device(): gathered = lax.all_gather(hidden, 'z', axis=0, tiled=True)  62.8 us
    all_gather x1, blocking collectives, on_device(): lax.all_gather(facts, ('z', 'core'), axis=0).reshape(Z, CORES, 3, own_rows)  20 us
    all_to_all x2, waiting for transfers between devices, broadcast_gather(): return lax.all_to_all(copies, axes, 0, 0, tiled=True)  13.8 us
    all_to_all x1, blocking collectives, on_device(): stats = merge_stats(lax.all_to_all(stats, ('x', 'y'), 0, 0, tiled=True))  13.3 us
    dot_general x1, matrix products, on_device(): lax.dot_general(grad, both, (((1,), (1,)), ((), ())), preferred_element_t...  10.3 us
    all_to_all x2, starting transfers between devices, broadcast_gather(): return lax.all_to_all(copies, axes, 0, 0, tiled=True)  9.24 us
    dot_general x1, matrix products, on_device(): logits = jnp.dot(gathered, both, preferred_element_type=F32)  8.59 us
  transfers between devices with their start and end apart: 7, of which 5 were waited for; matrix products, arithmetic and copies ran while one was open for 8% of the time, Pallas kernels for 0%

profile of v1, /device:TPU:8, one launch (start us, length us, event | category | flops | bytes accessed | tf_op | source)
XLA Modules:
  0.0 270.9 jit_solution(4189119046911549072)
XLA Ops:
  7.2 0.7 all-gather.4.cloned.1.call-update
  7.9 0.1 collective-permute-start
  8.0 0.7 convert_bitcast_fusion
  8.7 0.7 maximum_bitcast_fusion.1
  9.4 20.0 %all-gather.1 = f32[16,3,128]{2,1,0:T(4,128)S(1)} all-gather(f32[1,3,128]{2,1,0:T(4,128)S(1)} %maximum_bitcast_fusion.1), channel_id=2, replica_groups=mesh['z'=8,'core'=2,'x'=4,'y'=4] {'z','core'}, dimensions={0}, use_global_device_ids=true | all-gather | bytes 26112 | tf_op jit(solution)/shard_map/all_gather | solution.py:37
  29.4 0.1 pad_add_fusion
  29.5 3.2 %constant_dynamic-update-slice_fusion.1 = bf16[3584,640]{0,1:T(8,128)(2,1)} fusion(bf16[3584,320]{0,1:T(8,128)(2,1)} %param.6), kind=kLoop, calls=%fused_computation.33 | loop fusion | bytes 4587520
  32.7 1.5 constant_dynamic-update-slice_fusion
  34.2 62.8 %all-gather.4.cloned.1.call-done = bf16[1024,3584]{1,0:T(8,128)(2,1)} async-done(((bf16[128,3584]{1,0:T(8,128)(2,1)}), bf16[1024,3584]{1,0:T(8,128)(2,1)}) %all-gather.4.cloned.1.call-update) | async-done | bytes 7340048 | tf_op jit(solution)/shard_map/all_gather | solution.py:33
  97.0 8.6 %fusion.23 = (f32[1024]{0:T(1024)S(1)}, f32[640,1024]{1,0:T(8,128)S(1)}) fusion(bf16[3584,640]{0,1:T(8,128)(2,1)} %constant_dynamic-update-slice_fusion, bf16[1024,3584]{1,0:T(8,128)(2,1)} %all-gather.4.cloned.1.call-done), kind=kOutput, calls=%fused_computation.56 | convolution fusion | flops 4698274816 | bytes 14553088 | tf_op jit(solution)/shard_map/dot_general | solution.py:47
  105.6 0.1 stack.47
  105.7 0.6 fusion.6
  106.3 0.1 stack.48
  106.4 0.1 stack.49
  106.5 0.1 reshape.96
  106.6 13.3 %all_to_all.20 = f32[16,1,192]{2,1,0:T(1,128)S(1)} all-to-all(f32[16,1,192]{2,1,0:T(1,128)S(1)} %reshape.96), channel_id=1, replica_groups=mesh['z'=8,'core'=2,'x'=4,'y'=4] {'x','y'}, dimensions={0} | all-to-all | bytes 24576 | tf_op jit(solution)/shard_map/all_to_all | solution.py:56
  119.9 0.5 broadcast.19
  120.4 0.7 reduce.7
  121.1 0.1 reshape.97
  121.3 0.7 reshape.98
  122.0 4.3 %all-to-all-start.1 = ((f32[8,1,192]{2,1,0:T(1,128)}), f32[8,1,192]{2,1,0:T(1,128)S(1)}, u32[]{:S(2)}, u32[]{:S(2)}) async-start(f32[8,1,192]{2,1,0:T(1,128)} %reshape.98), calls=%async_computation.1 | async-start | bytes 16384 | tf_op jit(solution)/shard_map/all_to_all | solution.py:15
  126.3 7.7 %all-to-all-done.1 = f32[8,1,192]{2,1,0:T(1,128)S(1)} async-done(((f32[8,1,192]{2,1,0:T(1,128)}), f32[8,1,192]{2,1,0:T(1,128)S(1)}, u32[]{:S(2)}, u32[]{:S(2)}) %all-to-all-start.1) | async-done | bytes 6176 | tf_op jit(solution)/shard_map/all_to_all | solution.py:15
  134.0 0.7 reduce.8
  134.7 0.1 reshape.99
  134.9 0.7 reshape.100
  135.6 4.9 %all-to-all-start.2 = ((f32[32,1,128]{2,1,0:T(1,128)}), f32[32,1,128]{2,1,0:T(1,128)S(1)}, u32[]{:S(2)}, u32[]{:S(2)}) async-start(f32[32,1,128]{2,1,0:T(1,128)} %reshape.100), calls=%async_computation.2 | async-start | bytes 32768 | tf_op jit(solution)/shard_map/all_to_all | solution.py:15
  140.6 6.0 %all-to-all-done.2 = f32[32,1,128]{2,1,0:T(1,128)S(1)} async-done(((f32[32,1,128]{2,1,0:T(1,128)}), f32[32,1,128]{2,1,0:T(1,128)S(1)}, u32[]{:S(2)}, u32[]{:S(2)}) %all-to-all-start.2) | async-done | bytes 16416 | tf_op jit(solution)/shard_map/all_to_all | solution.py:15
  146.6 0.7 reduce.9
  147.3 0.1 reshape.101
  147.4 0.1 reshape.95
  147.5 0.1 fusion.18
  147.6 0.1 mul.79
  147.7 0.1 select_reduce_fusion
  147.8 0.1 add.75
  147.9 0.1 constant_dynamic-slice_fusion
  148.0 0.3 multiply_reduce_fusion
  148.3 0.1 fusion.16
  148.4 0.7 fusion.4
  149.1 1.0 copy-done
  150.1 10.3 %convolution_convert_fusion = bf16[1024,3584]{1,0:T(8,128)(2,1)} fusion(bf16[1024,640]{0,1:T(8,128)(2,1)S(1)} %fusion.4, bf16[3584,640]{0,1:T(8,128)(2,1)} %constant_dynamic-update-slice_fusion), kind=kOutput, calls=%fused_computation | convolution fusion | flops 4701290496 | bytes 13238272 | tf_op jit(solution)/shard_map/dot_general | solution.py:79
  160.5 1.3 copy-done.1
  161.8 7.0 %fusion = bf16[3584,320]{0,1:T(8,128)(2,1)} fusion(bf16[1024,3584]{1,0:T(8,128)(2,1)} %all-gather.4.cloned.1.call-done, bf16[1024,640]{0,1:T(8,128)(2,1)S(1)} %copy-done.1), kind=kOutput, calls=%fused_computation.3 | convolution fusion | flops 2349957120 | bytes 10289152 | tf_op jit(solution)/shard_map/dot_general | solution.py:88
  168.8 70.3 %reduce-scatter.2.cloned.1.call-done = bf16[128,3584]{1,0:T(8,128)(2,1)} async-done(((bf16[1024,3584]{1,0:T(8,128)(2,1)}), bf16[128,3584]{1,0:T(8,128)(2,1)}) %reduce-scatter.2.cloned.1.call-update) | async-done | bytes 917520 | tf_op jit(solution)/shard_map/reduce_scatter | solution.py:82
  239.1 2.2 copy.60
  241.3 7.3 %all-to-all-start.3 = ((bf16[16,128,224]{1,2,0:T(8,128)(2,1)}), bf16[16,128,224]{1,2,0:T(8,128)(2,1)S(1)}, u32[]{:S(2)}, u32[]{:S(2)}) async-start(bf16[16,128,224]{1,2,0:T(8,128)(2,1)} %bitcast.31), calls=%async_computation.4 | async-start | bytes 1835008 | tf_op jit(solution)/shard_map/all_to_all | solution.py:85
  248.6 7.7 %add_convert_fusion = bf16[3584,320]{0,1:T(8,128)(2,1)} fusion(bf16[3584,320]{0,1:T(8,128)(2,1)} %collective-permute-done.1, bf16[1024,3584]{1,0:T(8,128)(2,1)} %all-gather.4.cloned.1.call-done, bf16[1024,640]{0,1:T(8,128)(2,1)S(1)} %copy-done.1), kind=kOutput, calls=%fused_computation.4 | convolution fusion | flops 2352250880 | bytes 12582912 | tf_op jit(solution)/shard_map/dot_general | solution.py:92
  256.2 7.1 %all-to-all-done.3 = bf16[16,128,224]{1,2,0:T(8,128)(2,1)S(1)} async-done(((bf16[16,128,224]{1,2,0:T(8,128)(2,1)}), bf16[16,128,224]{1,2,0:T(8,128)(2,1)S(1)}, u32[]{:S(2)}, u32[]{:S(2)}) %all-to-all-start.3) | async-done | bytes 917536 | tf_op jit(solution)/shard_map/all_to_all | solution.py:85
  263.3 0.7 reduce_sum.105
  (31 shorter events, 0.4 us)
Async XLA Ops:
  7.2 89.9 %all-gather.4.cloned.1.call-start = ((), (), s32[]{:S(2)}) async-start(), calls=%async_computation.5 | async-start | bytes 8257536 | tf_op jit(solution)/shard_map/all_gather | solution.py:33
  7.9 24.8 %collective-permute-start = (bf16[3584,320]{0,1:T(8,128)(2,1)}, bf16[3584,320]{0,1:T(8,128)(2,1)S(1)}, u32[]{:S(2)}, u32[]{:S(2)}) collective-permute-start(bf16[3584,320]{0,1:T(8,128)(2,1)} %param.6), channel_id=1, source_target_pairs={{0,16},{16,0},{1,17},{17,1},{2,18},{18,2},{3,19},{19,3},{4,20},{20... | collective-permute-start | bytes 6881288 | tf_op jit(solution)/shard_map/ppermute | solution.py:31
  122.0 12.0 %all-to-all-start.1 = ((f32[8,1,192]{2,1,0:T(1,128)}), f32[8,1,192]{2,1,0:T(1,128)S(1)}, u32[]{:S(2)}, u32[]{:S(2)}) async-start(f32[8,1,192]{2,1,0:T(1,128)} %reshape.98), calls=%async_computation.1 | async-start | bytes 16384 | tf_op jit(solution)/shard_map/all_to_all | solution.py:15
  135.6 11.0 %all-to-all-start.2 = ((f32[32,1,128]{2,1,0:T(1,128)}), f32[32,1,128]{2,1,0:T(1,128)S(1)}, u32[]{:S(2)}, u32[]{:S(2)}) async-start(f32[32,1,128]{2,1,0:T(1,128)} %reshape.100), calls=%async_computation.2 | async-start | bytes 32768 | tf_op jit(solution)/shard_map/all_to_all | solution.py:15
  140.5 98.6 %reduce-scatter.2.cloned.1.call-start = ((), (), s32[]{:S(2)}) async-start(), calls=%async_computation.6 | async-start | bytes 8257536 | tf_op jit(solution)/shard_map/reduce_scatter | solution.py:82
  149.1 1.1 copy-start
  160.5 1.3 copy-start.1
  168.8 79.8 %collective-permute-start.1 = (bf16[3584,320]{0,1:T(8,128)(2,1)}, bf16[3584,320]{0,1:T(8,128)(2,1)}, u32[]{:S(2)}, u32[]{:S(2)}) collective-permute-start(bf16[3584,320]{0,1:T(8,128)(2,1)} %fusion), channel_id=1, source_target_pairs={{0,16},{16,0},{1,17},{17,1},{2,18},{18,2},{3,19},{19,3},{4,20},{20... | collective-permute-start | bytes 6881288 | tf_op jit(solution)/shard_map/ppermute | solution.py:91
  241.3 22.0 %all-to-all-start.3 = ((bf16[16,128,224]{1,2,0:T(8,128)(2,1)}), bf16[16,128,224]{1,2,0:T(8,128)(2,1)S(1)}, u32[]{:S(2)}, u32[]{:S(2)}) async-start(bf16[16,128,224]{1,2,0:T(8,128)(2,1)} %bitcast.31), calls=%async_computation.4 | async-start | bytes 1835008 | tf_op jit(solution)/shard_map/all_to_all | solution.py:85
Sparse Core Ops, SparseCore 0:
  9.8 87.2 all-gather.3
  160.6 78.4 reduce-scatter.1

commit v2 on v1

v2 whole, which is shorter than its diff:
```python
import jax
import jax.numpy as jnp
from jax import lax
from jax.sharding import Mesh, PartitionSpec as P

F32 = jnp.float32
BF16 = jnp.bfloat16
Z, CORES, X, Y = 8, 2, 4, 4
PLANE = X * Y
SWAP = [(0, 1), (1, 0)]
HALVES, GROUPS = 2, 8


def broadcast_gather(part, axes, count):
    copies = jnp.broadcast_to(part[None], (count,) + part.shape)
    return lax.all_to_all(copies, axes, 0, 0, tiled=True)


def merge_stats(parts):
    top = jnp.max(parts[:, 0], axis=0)
    total = jnp.sum(parts[:, 1] * jnp.exp(parts[:, 0] - top[None]), axis=0)
    return jnp.stack([top, total, jnp.sum(parts[:, 2], axis=0)])


def block_stats(logits, matches):
    top = jnp.max(logits, axis=1)
    total = jnp.sum(jnp.exp(logits - top[:, None]), axis=1)
    picked = jnp.sum(jnp.where(matches, logits, F32(0.0)), axis=1)
    return jnp.stack([top, total, picked])


def dot(left, right, contract):
    return lax.dot_general(left, right, (contract, ((), ())), preferred_element_type=F32)


def on_device(hidden, weight, token_ids, response_mask, teacher_logprob):
    own_rows, features = hidden.shape
    columns_here = weight.shape[1]
    core, z = lax.axis_index("core"), lax.axis_index("z")
    place = lax.axis_index("x") * Y + lax.axis_index("y")
    split = own_rows // 2
    group = split // GROUPS
    wide = features // HALVES
    half = Z * split
    tokens = own_rows * Z * CORES

    other_weight = lax.ppermute(weight, "core", SWAP)
    both = jnp.concatenate([weight, other_weight], axis=1)

    late = lax.all_gather(hidden[split:], "z", axis=0, tiled=True)
    piece = lax.dynamic_slice(
        hidden, (place % GROUPS * group, place // GROUPS * wide), (group, wide)
    )
    pieces = broadcast_gather(piece, "z", Z).reshape(Z * group, wide)
    early = broadcast_gather(pieces, ("x", "y"), PLANE).reshape(HALVES, half, wide)

    facts = jnp.stack([token_ids.astype(F32), response_mask.astype(F32), teacher_logprob])
    facts = broadcast_gather(facts, ("z", "core"), Z * CORES)

    def local_order(values):
        first = values[:, :split].reshape(Z, GROUPS, group).transpose(1, 0, 2)
        return first.reshape(half), values[:, split:].reshape(half)

    def whole_order(first, second):
        first = first.reshape(GROUPS, Z, group).transpose(1, 0, 2).reshape(Z, split)
        return jnp.concatenate([first, second.reshape(Z, split)], axis=1)

    own_facts = lax.dynamic_index_in_dim(facts.reshape(Z, CORES, 3, own_rows), core, 1, False)
    ids = [part.astype(jnp.int32) for part in local_order(own_facts[:, 0])]

    first = ((z * CORES + core) * PLANE + place) * columns_here
    second = ((z * CORES + 1 - core) * PLANE + place) * columns_here
    span = jnp.arange(columns_here, dtype=jnp.int32)
    columns = jnp.concatenate([first + span, second + span])
    matches = [part[:, None] == columns[None, :] for part in ids]

    logits = [
        dot(early[0], both[:wide], ((1,), (0,))) + dot(early[1], both[wide:], ((1,), (0,))),
        dot(late, both, ((1,), (0,))),
    ]
    stats = jnp.concatenate([block_stats(l, m) for l, m in zip(logits, matches)], axis=1)
    stats = merge_stats(broadcast_gather(stats, "z", Z))
    stats = merge_stats(broadcast_gather(stats, ("x", "y"), PLANE))
    norm = stats[0] + jnp.log(stats[1])
    norms = [norm[:half], norm[half:]]

    change = [
        m.astype(F32) - jnp.exp(l - n[:, None]) for l, m, n in zip(logits, matches, norms)
    ]
    change_low = [part.astype(BF16) for part in change]

    partial = dot(change_low[1], both, ((1,), (1,))).astype(BF16)
    late_sum = lax.psum_scatter(partial, "z", scatter_dimension=0, tiled=True)
    cut = features // PLANE
    partial = dot(both, change_low[0], ((1,), (1,))).astype(BF16)
    shared = lax.all_to_all(partial.reshape(PLANE, cut, half), ("x", "y"), 0, 0, tiled=True)
    early_sum = jnp.sum(shared.astype(F32), axis=0).astype(BF16).T
    early_sum = early_sum.reshape(GROUPS, Z, group, cut).transpose(1, 0, 2, 3)
    early_sum = lax.all_to_all(early_sum.reshape(Z, split, cut), "z", 0, 0, tiled=True)
    early_sum = jnp.sum(early_sum.astype(F32), axis=0)
    late_sum = late_sum.reshape(split, PLANE, cut).transpose(1, 0, 2)
    late_sum = lax.all_to_all(late_sum, ("x", "y"), 0, 0, tiled=True)
    late_sum = jnp.sum(late_sum.astype(F32), axis=0)

    picks = whole_order(stats[2, :half], stats[2, half:])
    known = whole_order(norms[0], norms[1])
    ratio = own_facts[:, 1] * (picks - known - own_facts[:, 2])
    other = lax.ppermute(jnp.sum(ratio, axis=1), "core", SWAP)
    steps = jnp.arange(own_rows, dtype=jnp.int32)
    later = (steps[None, :] >= steps[:, None]).astype(F32)
    within = jnp.sum(ratio[:, None, :] * later[None], axis=2)
    shard = jnp.arange(Z, dtype=jnp.int32)
    after = (shard[None, :] > shard[:, None]).astype(F32)
    at_or_after = jnp.where(core == 0, (shard[None, :] >= shard[:, None]).astype(F32), after)
    beyond = jnp.sum(jnp.sum(ratio, axis=1)[None, :] * after + other[None, :] * at_or_after, axis=1)
    weights = own_facts[:, 1] * (within + beyond[:, None]) / float(tokens)

    own_weight = lax.dynamic_index_in_dim(weights, z, 0, False)
    hidden_grad = jnp.concatenate([early_sum, late_sum]) * own_weight[:, None]

    grads = [(w[:, None] * part).astype(BF16) for w, part in zip(local_order(weights), change)]

    def head_part(low, high):
        first = dot(early, grads[0][:, low:high], ((1,), (0,))).reshape(features, high - low)
        return first + dot(late, grads[1][:, low:high], ((0,), (0,)))

    far = lax.ppermute(head_part(columns_here, 2 * columns_here).astype(BF16), "core", SWAP)
    head_grad = head_part(0, columns_here) + far.astype(F32)
    return hidden_grad.astype(BF16), head_grad.astype(BF16)


def solution(mesh):
    fine = Mesh(mesh.devices.reshape(Z, CORES, X, Y), ("z", "core", "x", "y"))
    by_token = ("z", "core")
    by_column = P(None, ("z", "core", "x", "y"))
    return jax.shard_map(
        on_device,
        mesh=fine,
        in_specs=(P(by_token, None), by_column, P(by_token), P(by_token), P(by_token)),
        out_specs=(P(by_token, ("x", "y")), by_column),
        check_vma=False,
    )
```

time: 271 us -> 260 us (0.959)
  waiting for transfers between devices: 155 us -> 86 us
  local copies, waits for them, and re-layouts: 12.1 us -> 29.1 us
  starting transfers between devices: 16.7 us -> 33.6 us
  blocking collectives: 33.3 us -> 46.6 us
  matrix products: 33.6 us -> 41.5 us
    reduce_scatter x1, waiting for transfers between devices: 70.3 us -> 0.01 us  [on_device(): late_sum = lax.psum_scatter(partial, 'z', scatter_dimension=0, tiled=True)]
    all_gather x1, waiting for transfers between devices: 62.8 us -> 0.02 us  [on_device(): late = lax.all_gather(hidden[split:], 'z', axis=0, tiled=True)]
    all_to_all x1 -> x3, blocking collectives: 13.3 us -> 46.6 us  [broadcast_gather(): return lax.all_to_all(copies, axes, 0, 0, tiled=True)]
    all_to_all x2, waiting for transfers between devices: 13.8 us -> 46.3 us  [broadcast_gather(): return lax.all_to_all(copies, axes, 0, 0, tiled=True)]
    all_to_all x1 -> x3, waiting for transfers between devices: 7.08 us -> 36.3 us  [the longest x1 32.4 us: on_device(): lax.all_to_all(partial.reshape(PLANE, cut, half), ('x', 'y'), 0, 0, tiled...]
    all_gather x1 -> x0, blocking collectives: 20 us -> none  [on_device(): lax.all_gather(facts, ('z', 'core'), axis=0).reshape(Z, CORES, 3, own_rows)]
    all_to_all x1 -> x3, starting transfers between devices: 7.26 us -> 16.9 us  [the longest x1 7.63 us: on_device(): late_sum = lax.all_to_all(late_sum, ('x', 'y'), 0, 0, tiled=True)]
    dot_general x4 -> x9, matrix products: 33.6 us -> 41.5 us  [dot(): lax.dot_general(left, right, (contract, ((), ())), preferred_element_type...]
  transfers between devices with their start and end apart: 7 -> 10, of which waited for: 5 -> 7; matrix products, arithmetic and copies ran while one was open for 8% -> 21% of each run, Pallas kernels for 0% -> 0%
where the time goes in v2:
time: 260 us; the launch traced here: 259 us
  waiting for transfers between devices  86 us (33%)
  blocking collectives  46.6 us (18%)
  matrix products  41.5 us (16%)
  starting transfers between devices  33.6 us (13%)
  local copies, waits for them, and re-layouts  29.1 us (11%)
  between operations  14.4 us (6%)
  other arithmetic  7.28 us (3%)
    all_to_all x3, blocking collectives, broadcast_gather(): return lax.all_to_all(copies, axes, 0, 0, tiled=True)  46.6 us
    all_to_all x2, waiting for transfers between devices, broadcast_gather(): return lax.all_to_all(copies, axes, 0, 0, tiled=True)  46.3 us
    dot_general x9, matrix products, dot(): lax.dot_general(left, right, (contract, ((), ())), preferred_element_type...  41.5 us
    all_to_all x1, waiting for transfers between devices, on_device(): lax.all_to_all(partial.reshape(PLANE, cut, half), ('x', 'y'), 0, 0, tiled...  32.4 us
    all_to_all x2, starting transfers between devices, broadcast_gather(): return lax.all_to_all(copies, axes, 0, 0, tiled=True)  16.1 us
    dot_general x2, local copies, waits for them, and re-layouts, dot(): lax.dot_general(left, right, (contract, ((), ())), preferred_element_type...  7.71 us
    all_to_all x1, starting transfers between devices, on_device(): late_sum = lax.all_to_all(late_sum, ('x', 'y'), 0, 0, tiled=True)  7.63 us
    all_to_all x1, starting transfers between devices, on_device(): lax.all_to_all(partial.reshape(PLANE, cut, half), ('x', 'y'), 0, 0, tiled...  5.85 us
  transfers between devices with their start and end apart: 10, of which 7 were waited for; matrix products, arithmetic and copies ran while one was open for 21% of the time, Pallas kernels for 0%

profile of v2, /device:TPU:8, one launch (start us, length us, event | category | flops | bytes accessed | tf_op | source)
XLA Modules:
  0.0 258.5 jit_solution(3274841496227295213)
XLA Ops:
  7.2 1.8 slice.97
  9.1 0.7 convert_bitcast_fusion
  9.7 0.7 pad_maximum_fusion.1
  10.4 0.6 broadcast_in_dim.16
  11.0 8.6 %all-to-all-start = ((f32[16,3,128]{2,1,0:T(4,128)}), f32[16,3,128]{2,1,0:T(4,128)S(1)}, u32[]{:S(2)}, u32[]{:S(2)}) async-start(f32[16,3,128]{2,1,0:T(4,128)} %broadcast_in_dim.16), calls=%async_computation | async-start | bytes 65536 | tf_op jit(solution)/shard_map/all_to_all | solution.py:16
  19.6 0.8 dynamic_slice.12
  20.4 6.9 %all-to-all-done = f32[16,3,128]{2,1,0:T(4,128)S(1)} async-done(((f32[16,3,128]{2,1,0:T(4,128)}), f32[16,3,128]{2,1,0:T(4,128)S(1)}, u32[]{:S(2)}, u32[]{:S(2)}) %all-to-all-start) | async-done | bytes 24608 | tf_op jit(solution)/shard_map/all_to_all | solution.py:16
  27.3 16.9 %all_to_all.40 = bf16[8,8,1792]{2,1,0:T(8,128)(2,1)S(1)} all-to-all(bf16[8,8,1792]{2,1,0:T(8,128)(2,1)S(1)} %broadcast_in_dim.18), channel_id=1, replica_groups=mesh['z'=8,'core'=2,'x'=4,'y'=4] {'z'}, dimensions={0} | all-to-all | bytes 458752 | tf_op jit(solution)/shard_map/all_to_all | solution.py:16
  44.2 2.3 broadcast_in_dim.20
  46.5 7.5 %all-to-all-start.2 = ((bf16[16,64,1792]{2,1,0:T(8,128)(2,1)}), bf16[16,64,1792]{2,1,0:T(8,128)(2,1)}, u32[]{:S(2)}, u32[]{:S(2)}) async-start(bf16[16,64,1792]{2,1,0:T(8,128)(2,1)} %broadcast_in_dim.20), calls=%async_computation.2 | async-start | bytes 7340032 | tf_op jit(solution)/shard_map/all_to_all | solution.py:16
  54.3 1.5 constant_dynamic-update-slice_fusion.1
  56.2 2.6 collective-permute-done
  58.7 3.2 %constant_dynamic-update-slice_fusion = bf16[3584,640]{0,1:T(8,128)(2,1)} fusion(bf16[3584,640]{0,1:T(8,128)(2,1)} %constant_dynamic-update-slice_fusion.1, bf16[3584,320]{0,1:T(8,128)(2,1)} %collective-permute-done), kind=kLoop, calls=%fused_computation.66 | loop fusion | bytes 4587520 | tf_op jit(solution)/shard_map/concatenate | solution.py:48
  61.9 39.4 %all-to-all-done.2 = bf16[16,64,1792]{2,1,0:T(8,128)(2,1)} async-done(((bf16[16,64,1792]{2,1,0:T(8,128)(2,1)}), bf16[16,64,1792]{2,1,0:T(8,128)(2,1)}, u32[]{:S(2)}, u32[]{:S(2)}) %all-to-all-start.2) | async-done | bytes 3670048 | tf_op jit(solution)/shard_map/all_to_all | solution.py:16
  101.3 2.5 fusion.48
  103.8 0.8 copy-done.5
  104.7 1.6 fusion.1
  106.3 1.7 fusion.51
  108.1 7.1 %fusion.52 = (f32[512]{0:T(512)S(1)}, f32[640,512]{1,0:T(8,128)}) fusion(bf16[3584,640]{0,1:T(8,128)(2,1)} %constant_dynamic-update-slice_fusion, bf16[512,3584]{1,0:T(8,128)(2,1)} %all-gather.2.cloned.1.call-done), kind=kOutput, calls=%fused_computation.101 | convolution fusion | flops 2349137408 | bytes 9570304 | tf_op jit(solution)/shard_map/dot_general | solution.py:33
  115.1 1.7 copy.57
  116.8 1.0 exponential_reduce_fusion
  117.9 11.5 %all_to_all.41 = f32[8,3,1024]{2,1,0:T(4,128)S(1)} all-to-all(f32[8,3,1024]{2,1,0:T(4,128)S(1)} %broadcast_in_dim.22), channel_id=1, replica_groups=mesh['z'=8,'core'=2,'x'=4,'y'=4] {'z'}, dimensions={0} | all-to-all | bytes 196608 | tf_op jit(solution)/shard_map/all_to_all | solution.py:16
  129.6 18.2 %all_to_all.42 = f32[16,3,1024]{2,1,0:T(4,128)S(1)} all-to-all(f32[16,3,1024]{2,1,0:T(4,128)S(1)} %broadcast_in_dim.23), channel_id=1, replica_groups=mesh['z'=8,'core'=2,'x'=4,'y'=4] {'x','y'}, dimensions={0} | all-to-all | bytes 393216 | tf_op jit(solution)/shard_map/all_to_all | solution.py:16
  148.0 7.0 %convolution_convert_fusion = bf16[512,3584]{1,0:T(8,128)(2,1)} fusion(bf16[3584,640]{0,1:T(8,128)(2,1)} %constant_dynamic-update-slice_fusion, f32[640,512]{0,1:T(8,128)S(1)} %copy.57, f32[512]{0:T(512)S(1)} %get-tuple-element.30, s32[640]{0:T(1024)S(1)} %pad_add_fusion, s32[512]{0:T(512)S(1)} %convert_element_type.97), kind=kOutput, calls=%fused_computation | convolution fusion | flops 2352283648 | bytes 9574912 | tf_op jit(solution)/shard_map/dot_general | solution.py:33
  155.1 6.0 %copy.69 = bf16[2,1792,512]{2,1,0:T(8,128)(2,1)} copy(bf16[2,1792,512]{1,2,0:T(8,128)(2,1)} %bitcast.36) | data formatting | bytes 7340032 | tf_op jit(solution)/shard_map/dot_general | solution.py:33
  161.8 7.3 %convolution_convert_fusion.1 = bf16[3584,512]{1,0:T(8,128)(2,1)} fusion(bf16[3584,640]{0,1:T(8,128)(2,1)} %constant_dynamic-update-slice_fusion, f32[512,640]{1,0:T(8,128)S(1)} %get-tuple-element.36, f32[512]{0:T(512)S(1)} %get-tuple-element.29, s32[640]{0:T(1024)S(1)} %pad_add_fusion, s32[512]{0:T(512)S(1)} %convert_element_type.94), kind=kOutput, calls=%fused_computation.1 | convolution fusion | flops 2352283648 | bytes 9574912 | tf_op jit(solution)/shard_map/dot_general | solution.py:33
  169.1 5.8 %all-to-all-start.5 = ((bf16[16,224,512]{2,1,0:T(8,128)(2,1)}), bf16[16,224,512]{2,1,0:T(8,128)(2,1)}, u32[]{:S(2)}, u32[]{:S(2)}) async-start(bf16[16,224,512]{2,1,0:T(8,128)(2,1)} %bitcast.114), calls=%async_computation.5 | async-start | bytes 7340032 | tf_op jit(solution)/shard_map/all_to_all | solution.py:96
  175.3 0.3 collective-permute-start.1
  175.6 0.2 multiply_reduce_fusion
  175.8 0.8 collective-permute-done.1
  177.2 0.9 multiply_convert_fusion.1
  178.1 1.4 copy-done
  179.5 1.5 convolution_bitcast_fusion
  181.0 0.6 copy-done.1
  181.6 3.0 %fusion = bf16[3584,320]{0,1:T(8,128)(2,1)} fusion(f32[3584,320]{0,1:T(8,128)S(1)} %convolution_bitcast_fusion, bf16[3584,512]{1,0:T(8,128)(2,1)S(1)} %bitcast.113, bf16[512,640]{1,0:T(8,128)(2,1)S(1)} %get-tuple-element.24), kind=kOutput, calls=%fused_computation.6 | convolution fusion | flops 1176698880 | bytes 10944512 | tf_op jit(solution)/shard_map/dot_general | solution.py:33
  184.6 0.2 collective-permute-start.2
  184.8 32.4 %all-to-all-done.5 = bf16[16,224,512]{2,1,0:T(8,128)(2,1)} async-done(((bf16[16,224,512]{2,1,0:T(8,128)(2,1)}), bf16[16,224,512]{2,1,0:T(8,128)(2,1)}, u32[]{:S(2)}, u32[]{:S(2)}) %all-to-all-start.5) | async-done | bytes 3670048 | tf_op jit(solution)/shard_map/all_to_all | solution.py:96
  217.2 2.6 %reduce_sum.140 = bf16[224,512]{1,0:T(8,128)(2,1)S(1)} reduce(bf16[16,224,512]{2,1,0:T(8,128)(2,1)} %all-to-all-done.5, bf16[]{:T(256)} %constant.77.clone.1), dimensions={0}, to_apply=%region_11.12 | reduce | flops 1720320 | bytes 3899394 | tf_op jit(solution)/shard_map/reduce_sum | solution.py:97
  219.9 0.7 copy.106
  220.6 3.4 %all-to-all-start.6 = ((bf16[8,64,224]{2,1,0:T(8,128)(2,1)}), bf16[8,64,224]{2,1,0:T(8,128)(2,1)S(1)}, u32[]{:S(2)}, u32[]{:S(2)}) async-start(bf16[8,64,224]{2,1,0:T(8,128)(2,1)} %bitcast.109), calls=%async_computation.6 | async-start | bytes 524288 | tf_op jit(solution)/shard_map/all_to_all | solution.py:99
  224.0 5.5 %convolution_bitcast_fusion.1 = f32[3584,320]{0,1:T(8,128)} fusion(bf16[512,3584]{1,0:T(8,128)(2,1)} %all-gather.2.cloned.1.call-done, bf16[512,640]{1,0:T(8,128)(2,1)S(1)} %get-tuple-element.25), kind=kOutput, calls=%fused_computation.5 | convolution fusion | flops 1174405120 | bytes 8650752 | tf_op jit(solution)/shard_map/dot_general | solution.py:33
  229.5 1.8 reshape.164
  231.3 1.0 copy.105
  232.3 2.1 all-to-all-done.6
  234.4 7.6 %all-to-all-start.7 = ((bf16[16,64,224]{2,1,0:T(8,128)(2,1)}), bf16[16,64,224]{2,1,0:T(8,128)(2,1)S(1)}, u32[]{:S(2)}, u32[]{:S(2)}) async-start(bf16[16,64,224]{2,1,0:T(8,128)(2,1)} %bitcast.108), calls=%async_computation.8 | async-start | bytes 1048576 | tf_op jit(solution)/shard_map/all_to_all | solution.py:102
  242.1 6.9 %add_convert_fusion = bf16[3584,320]{0,1:T(8,128)(2,1)} fusion(bf16[3584,320]{0,1:T(8,128)(2,1)} %collective-permute-done.2, f32[3584,320]{0,1:T(8,128)} %convolution_bitcast_fusion.1, bf16[3584,512]{1,0:T(8,128)(2,1)} %bitcast.112, bf16[512,640]{1,0:T(8,128)(2,1)S(1)} %copy-done.3), kind=kOutput, calls=%fused_computation.7 | convolution fusion | flops 1178992640 | bytes 13238272 | tf_op jit(solution)/shard_map/dot_general | solution.py:33
  249.0 1.8 all-to-all-done.7
  251.0 0.7 copy.71
  (66 shorter events, 3.1 us)
Async XLA Ops:
  7.2 100.9 %all-gather.2.cloned.1.call-start = ((), (), s32[]{:S(2)}) async-start(), calls=%async_computation.9 | async-start | bytes 4128768 | tf_op jit(solution)/shard_map/all_gather | solution.py:50
  11.0 16.3 %all-to-all-start = ((f32[16,3,128]{2,1,0:T(4,128)}), f32[16,3,128]{2,1,0:T(4,128)S(1)}, u32[]{:S(2)}, u32[]{:S(2)}) async-start(f32[16,3,128]{2,1,0:T(4,128)} %broadcast_in_dim.16), calls=%async_computation | async-start | bytes 65536 | tf_op jit(solution)/shard_map/all_to_all | solution.py:16
  46.5 7.6 %copy-start.4 = (bf16[3584,320]{0,1:T(8,128)(2,1)S(1)}, bf16[3584,320]{0,1:T(8,128)(2,1)}, u32[]{:S(2)}) copy-start(bf16[3584,320]{0,1:T(8,128)(2,1)} %param.6) | copy-start | bytes 6881284
  46.5 54.8 %all-to-all-start.2 = ((bf16[16,64,1792]{2,1,0:T(8,128)(2,1)}), bf16[16,64,1792]{2,1,0:T(8,128)(2,1)}, u32[]{:S(2)}, u32[]{:S(2)}) async-start(bf16[16,64,1792]{2,1,0:T(8,128)(2,1)} %broadcast_in_dim.20), calls=%async_computation.2 | async-start | bytes 7340032 | tf_op jit(solution)/shard_map/all_to_all | solution.py:16
  54.0 175.5 %reduce-scatter.2.cloned.1.call-start = ((), (), s32[]{:S(2)}) async-start(), calls=%async_computation.10 | async-start | bytes 4128768 | tf_op jit(solution)/shard_map/reduce_scatter | solution.py:93
  54.1 4.7 %collective-permute-start = (bf16[3584,320]{0,1:T(8,128)(2,1)S(1)}, bf16[3584,320]{0,1:T(8,128)(2,1)}, u32[]{:S(2)}, u32[]{:S(2)}) collective-permute-start(bf16[3584,320]{0,1:T(8,128)(2,1)S(1)} %copy-done.4), channel_id=1, source_target_pairs={{0,16},{16,0},{1,17},{17,1},{2,18},{18,2},{3,19},{19,3},{4,20},{20... | collective-permute-start | bytes 6881288 | tf_op jit(solution)/shard_map/ppermute | solution.py:47
  101.3 3.4 %copy-start.5 = (bf16[3584,640]{0,1:T(8,128)(2,1)S(1)}, bf16[3584,640]{0,1:T(8,128)(2,1)}, u32[]{:S(2)}) copy-start(bf16[3584,640]{0,1:T(8,128)(2,1)} %constant_dynamic-update-slice_fusion) | copy-start | bytes 13762564
  169.1 48.1 %all-to-all-start.5 = ((bf16[16,224,512]{2,1,0:T(8,128)(2,1)}), bf16[16,224,512]{2,1,0:T(8,128)(2,1)}, u32[]{:S(2)}, u32[]{:S(2)}) async-start(bf16[16,224,512]{2,1,0:T(8,128)(2,1)} %bitcast.114), calls=%async_computation.5 | async-start | bytes 7340032 | tf_op jit(solution)/shard_map/all_to_all | solution.py:96
  175.3 1.4 collective-permute-start.1
  177.2 2.3 copy-start
  178.1 2.9 %copy-start.2 = (bf16[512,640]{1,0:T(8,128)(2,1)}, bf16[512,640]{1,0:T(8,128)(2,1)S(1)}, u32[]{:S(2)}) copy-start(bf16[512,640]{1,0:T(8,128)(2,1)S(1)} %get-tuple-element.24) | copy-start | bytes 1966084
  179.5 2.1 copy-start.1
  184.6 57.5 %collective-permute-start.2 = (bf16[3584,320]{0,1:T(8,128)(2,1)}, bf16[3584,320]{0,1:T(8,128)(2,1)}, u32[]{:S(2)}, u32[]{:S(2)}) collective-permute-start(bf16[3584,320]{0,1:T(8,128)(2,1)} %fusion), channel_id=1, source_target_pairs={{0,16},{16,0},{1,17},{17,1},{2,18},{18,2},{3,19},{19,3},{4,20},{20... | collective-permute-start | bytes 6881288 | tf_op jit(solution)/shard_map/ppermute | solution.py:127
  220.6 13.8 %all-to-all-start.6 = ((bf16[8,64,224]{2,1,0:T(8,128)(2,1)}), bf16[8,64,224]{2,1,0:T(8,128)(2,1)S(1)}, u32[]{:S(2)}, u32[]{:S(2)}) async-start(bf16[8,64,224]{2,1,0:T(8,128)(2,1)} %bitcast.109), calls=%async_computation.6 | async-start | bytes 524288 | tf_op jit(solution)/shard_map/all_to_all | solution.py:99
  229.5 12.6 %copy-start.3 = (bf16[512,640]{1,0:T(8,128)(2,1)S(1)}, bf16[512,640]{1,0:T(8,128)(2,1)}, u32[]{:S(2)}) copy-start(bf16[512,640]{1,0:T(8,128)(2,1)} %copy-done.2) | copy-start | bytes 1966084
  234.4 16.4 %all-to-all-start.7 = ((bf16[16,64,224]{2,1,0:T(8,128)(2,1)}), bf16[16,64,224]{2,1,0:T(8,128)(2,1)S(1)}, u32[]{:S(2)}, u32[]{:S(2)}) async-start(bf16[16,64,224]{2,1,0:T(8,128)(2,1)} %bitcast.108), calls=%async_computation.8 | async-start | bytes 1048576 | tf_op jit(solution)/shard_map/all_to_all | solution.py:102
Sparse Core Ops, SparseCore 0:
  10.4 57.6 all-gather.1
  155.2 44.3 reduce-scatter.1

commit v3 on v2

v3 whole, which is shorter than its diff:
```python
import jax
import jax.numpy as jnp
from jax import lax
from jax.experimental import pallas as pl
from jax.experimental.pallas import tpu as pltpu
from jax.sharding import Mesh, PartitionSpec as P

F32 = jnp.float32
BF16 = jnp.bfloat16
Z, CORES, X, Y = 8, 2, 4, 4
PLANE = X * Y
SWAP = [(0, 1), (1, 0)]
WIDE, GROUPS = 4, 4
EARLY = 48
LANES = 128


def broadcast_gather(part, axes, count):
    copies = jnp.broadcast_to(part[None], (count,) + part.shape)
    return lax.all_to_all(copies, axes, 0, 0, tiled=True)


def merge_stats(parts):
    top = jnp.max(parts[:, 0], axis=0)
    total = jnp.sum(parts[:, 1] * jnp.exp(parts[:, 0] - top[None]), axis=0)
    return jnp.stack([top, total, jnp.sum(parts[:, 2], axis=0)])


def dot(left, right, contract):
    return lax.dot_general(left, right, (contract, ((), ())), preferred_element_type=F32)


def params(megabytes):
    return pltpu.CompilerParams(vmem_limit_bytes=megabytes << 20)


def cost(flops, nbytes):
    return pl.CostEstimate(flops=flops, bytes_accessed=nbytes, transcendentals=0)


SMEM = pl.BlockSpec(memory_space=pltpu.SMEM)


def whole(shape):
    return pl.BlockSpec(shape, lambda *_: (0,) * len(shape))


def column_of(starts_ref, shape, low, half):
    row = lax.broadcasted_iota(jnp.int32, shape, 0) + low
    return row + jnp.where(row < half, starts_ref[0], starts_ref[1] - half)


def logits_and_stats(starts, ids, hidden, weight_t):
    columns, features = weight_t.shape
    tokens = hidden.shape[-2]
    block = features // WIDE
    if hidden.ndim == 3:
        spec = pl.BlockSpec((None, tokens, block), lambda k: (k, 0, 0))
    else:
        spec = pl.BlockSpec((tokens, block), lambda k: (0, k))

    def body(starts_ref, ids_ref, h_ref, w_ref, logits_ref, stats_ref):
        step = pl.program_id(0)
        part = dot(w_ref[...], h_ref[...], ((1,), (1,)))

        @pl.when(step == 0)
        def _():
            logits_ref[...] = part

        @pl.when(step > 0)
        def _():
            logits_ref[...] += part

        @pl.when(step == WIDE - 1)
        def _():
            logits = logits_ref[...]
            match = column_of(starts_ref, logits.shape, 0, columns // 2) == ids_ref[...]
            top = jnp.max(logits, axis=0, keepdims=True)
            total = jnp.sum(jnp.exp(logits - top), axis=0, keepdims=True)
            picked = jnp.sum(jnp.where(match, logits, 0.0), axis=0, keepdims=True)
            stats_ref[...] = jnp.concatenate([top, total, picked] + [jnp.zeros_like(top)] * 5)

    return pl.pallas_call(
        body,
        grid=(WIDE,),
        in_specs=[SMEM, whole((1, tokens)), spec, pl.BlockSpec((columns, block), lambda k: (0, k))],
        out_specs=[whole((columns, tokens)), whole((8, tokens))],
        out_shape=[
            jax.ShapeDtypeStruct((columns, tokens), F32),
            jax.ShapeDtypeStruct((8, tokens), F32),
        ],
        compiler_params=params(20),
        cost_estimate=cost(
            2 * columns * tokens * features, 2 * features * (columns + tokens) + 4 * columns * tokens
        ),
    )(starts, ids, hidden, weight_t)


def change_of(starts_ref, logits, norm, ids, low, half):
    match = column_of(starts_ref, logits.shape, low, half) == ids
    return jnp.where(match, 1.0, 0.0) - jnp.exp(logits - norm)


def partial_product(starts, ids, logits_t, norm, weight, by_feature):
    columns, tokens = logits_t.shape
    features = weight.shape[0] if by_feature else weight.shape[1]
    block = features // 7

    def body(starts_ref, ids_ref, logits_ref, norm_ref, w_ref, out_ref, held):
        @pl.when(pl.program_id(0) == 0)
        def _():
            change = change_of(
                starts_ref, logits_ref[...], norm_ref[...], ids_ref[...], 0, columns // 2
            )
            held[...] = (change if by_feature else change.T).astype(BF16)

        if by_feature:
            out = dot(w_ref[...], held[...], ((1,), (0,)))
        else:
            out = dot(held[...], w_ref[...], ((1,), (0,)))
        out_ref[...] = out.astype(BF16)

    if by_feature:
        w_spec = pl.BlockSpec((block, columns), lambda k: (k, 0))
        out_spec, out_dims = pl.BlockSpec((block, tokens), lambda k: (k, 0)), (features, tokens)
        held = (columns, tokens)
    else:
        w_spec = pl.BlockSpec((columns, block), lambda k: (0, k))
        out_spec, out_dims = pl.BlockSpec((tokens, block), lambda k: (0, k)), (tokens, features)
        held = (tokens, columns)
    return pl.pallas_call(
        body,
        grid=(7,),
        in_specs=[SMEM, whole((1, tokens)), whole((columns, tokens)), whole((1, tokens)), w_spec],
        out_specs=out_spec,
        out_shape=jax.ShapeDtypeStruct(out_dims, BF16),
        scratch_shapes=[pltpu.VMEM(held, BF16)],
        compiler_params=params(20),
        cost_estimate=cost(
            2 * columns * tokens * features, 2 * features * (columns + tokens) + 4 * columns * tokens
        ),
    )(starts, ids, logits_t, norm, weight)


def head_half(starts, early, late, low, high, added):
    columns = early[1].shape[0]
    here = high - low
    sizes = [early[1].shape[1], late[1].shape[1]]
    features = late[4].shape[1]
    block = features // WIDE

    def body(starts_ref, *refs):
        sides = [refs[0:5], refs[5:10]]
        rest = refs[10:]
        held = rest[-2:]
        out_ref = rest[-3]

        @pl.when(pl.program_id(0) == 0)
        def _():
            for (ids, logits, norm, scale, _), into in zip(sides, held):
                change = change_of(
                    starts_ref, logits[low:high], norm[...], ids[...], low, columns // 2
                )
                into[...] = (change * scale[...]).astype(BF16)

        total = dot(held[0][...], sides[0][4][...], ((1,), (0,)))
        total += dot(held[1][...], sides[1][4][...], ((1,), (0,)))
        total = total.T
        if added is not None:
            total += rest[0][...].astype(F32)
        out_ref[...] = total.astype(BF16)

    specs = [SMEM]
    for size, spec in zip(
        sizes,
        (
            pl.BlockSpec((None, sizes[0], block), lambda k: (k, 0, 0)),
            pl.BlockSpec((sizes[1], block), lambda k: (0, k)),
        ),
    ):
        specs += [whole((1, size)), whole((columns, size)), whole((1, size)), whole((1, size)), spec]
    out_spec = pl.BlockSpec((block, here), lambda k: (k, 0))
    operands = list(early) + list(late)
    if added is not None:
        specs.append(out_spec)
        operands.append(added)
    return pl.pallas_call(
        body,
        grid=(WIDE,),
        in_specs=specs,
        out_specs=out_spec,
        out_shape=jax.ShapeDtypeStruct((features, here), BF16),
        scratch_shapes=[pltpu.VMEM((here, size), BF16) for size in sizes],
        compiler_params=params(28),
        cost_estimate=cost(
            2 * here * sum(sizes) * features, 2 * features * (here + sum(sizes)) + 4 * columns * sum(sizes)
        ),
    )(starts, *operands)


def pack_facts(token_ids, response_mask, teacher_logprob):
    high = lax.reduce_precision(teacher_logprob, 8, 7)
    rest = teacher_logprob - high
    middle = lax.reduce_precision(rest, 8, 7)
    rows = [
        token_ids // 16384,
        token_ids // 128 % 128,
        token_ids % 128,
        response_mask,
        high,
        middle,
        rest - middle,
        jnp.zeros_like(high),
    ]
    return jnp.stack([row.astype(F32) for row in rows]).astype(BF16)


def unpack_facts(rows):
    rows = rows.astype(F32)
    ids = (rows[:, 0] * 16384.0 + rows[:, 1] * 128.0 + rows[:, 2]).astype(jnp.int32)
    return ids, rows[:, 3], rows[:, 4] + rows[:, 5] + rows[:, 6]


def on_device(hidden, weight, token_ids, response_mask, teacher_logprob):
    own_rows, features = hidden.shape
    columns_here = weight.shape[1]
    core, z = lax.axis_index("core"), lax.axis_index("z")
    place = lax.axis_index("x") * Y + lax.axis_index("y")
    group = EARLY // GROUPS
    wide = features // WIDE
    first_half, second_half = Z * EARLY, Z * (own_rows - EARLY)
    all_rows = first_half + second_half
    tokens = all_rows * CORES

    other_weight = lax.ppermute(weight, "core", SWAP)
    both = jnp.concatenate([weight, other_weight], axis=1)
    both_t = both.T

    late = lax.all_gather(hidden[EARLY:], "z", axis=0, tiled=True)
    piece = lax.dynamic_slice(
        hidden, (place % GROUPS * group, place // GROUPS * wide), (group, wide)
    )
    facts = pack_facts(token_ids, response_mask, teacher_logprob)
    facts = jnp.pad(facts, ((0, group - facts.shape[0]), (0, 0)))
    pieces = broadcast_gather(jnp.concatenate([piece, facts], axis=1), "z", Z)
    ids, mask, teacher = unpack_facts(pieces[:, :8, wide:])
    pieces = pieces[:, :, :wide].reshape(Z * group, wide)
    early = broadcast_gather(pieces, ("x", "y"), PLANE).reshape(WIDE, first_half, wide)

    def local_order(values):
        first = values[:, :EARLY].reshape(Z, GROUPS, group).transpose(1, 0, 2)
        return first.reshape(1, first_half), values[:, EARLY:].reshape(1, second_half)

    def whole_order(values):
        first = values[:first_half].reshape(GROUPS, Z, group).transpose(1, 0, 2)
        second = values[first_half:].reshape(Z, own_rows - EARLY)
        return jnp.concatenate([first.reshape(Z, EARLY), second], axis=1)

    ids = local_order(ids)
    starts = jnp.stack(
        [((z * CORES + c) * PLANE + place) * columns_here for c in (core, 1 - core)]
    ).astype(jnp.int32)

    early_logits, early_stats = logits_and_stats(starts, ids[0], early, both_t)
    late_logits, late_stats = logits_and_stats(starts, ids[1], late, both_t)
    stats = jnp.concatenate([early_stats[:3], late_stats[:3]], axis=1)
    stats = stats.reshape(3 * all_rows // LANES, LANES)

    def merged(stats, axes, count):
        parts = broadcast_gather(stats, axes, count)
        merged = merge_stats(parts.reshape(count, 3, all_rows // LANES, LANES))
        return merged.reshape(3 * all_rows // LANES, LANES)

    stats = merged(stats, "z", Z)
    stats = merged(stats, ("x", "y"), PLANE).reshape(3, all_rows)
    norm = stats[0] + jnp.log(stats[1])
    norms = norm[None, :first_half], norm[None, first_half:]

    partial = partial_product(starts, ids[1], late_logits, norms[1], both_t, False)
    late_sum = lax.psum_scatter(partial, "z", scatter_dimension=0, tiled=True)
    cut = features // PLANE
    partial = partial_product(starts, ids[0], early_logits, norms[0], both, True)
    shared = lax.all_to_all(
        partial.reshape(PLANE, cut, first_half), ("x", "y"), 0, 0, tiled=True
    )
    early_sum = jnp.sum(shared.astype(F32), axis=0).astype(BF16).T
    early_sum = early_sum.reshape(GROUPS, Z, group, cut).transpose(1, 0, 2, 3)
    early_sum = lax.all_to_all(early_sum.reshape(Z, EARLY, cut), "z", 0, 0, tiled=True)
    early_sum = jnp.sum(early_sum.astype(F32), axis=0)
    late_sum = late_sum.reshape(own_rows - EARLY, PLANE, cut).transpose(1, 0, 2)
    late_sum = lax.all_to_all(late_sum, ("x", "y"), 0, 0, tiled=True)
    late_sum = jnp.sum(late_sum.astype(F32), axis=0)

    ratio = mask * (whole_order(stats[2]) - whole_order(norm) - teacher)
    shard_sums = jnp.sum(ratio, axis=1)
    other_sums = lax.ppermute(shard_sums, "core", SWAP)
    steps = jnp.arange(own_rows, dtype=jnp.int32)
    later = (steps[None, :] >= steps[:, None]).astype(F32)
    within = jnp.sum(ratio[:, None, :] * later[None], axis=2)
    shard = jnp.arange(Z, dtype=jnp.int32)
    after = (shard[None, :] > shard[:, None]).astype(F32)
    from_here = (shard[None, :] >= shard[:, None]).astype(F32)
    beyond = shard_sums[None, :] * after
    beyond += other_sums[None, :] * jnp.where(core == 0, from_here, after)
    weights = mask * (within + jnp.sum(beyond, axis=1)[:, None]) / float(tokens)

    own_weight = lax.dynamic_index_in_dim(weights, z, 0, False)
    hidden_grad = jnp.concatenate([early_sum, late_sum]) * own_weight[:, None]

    weights = local_order(weights)
    sides = (
        (ids[0], early_logits, norms[0], weights[0], early),
        (ids[1], late_logits, norms[1], weights[1], late),
    )
    far = head_half(starts, *sides, columns_here, 2 * columns_here, None)
    far = lax.ppermute(far, "core", SWAP)
    head_grad = head_half(starts, *sides, 0, columns_here, far)
    return hidden_grad.astype(BF16), head_grad


def solution(mesh):
    fine = Mesh(mesh.devices.reshape(Z, CORES, X, Y), ("z", "core", "x", "y"))
    by_token = ("z", "core")
    by_column = P(None, ("z", "core", "x", "y"))
    return jax.shard_map(
        on_device,
        mesh=fine,
        in_specs=(P(by_token, None), by_column, P(by_token), P(by_token), P(by_token)),
        out_specs=(P(by_token, ("x", "y")), by_column),
        check_vma=False,
    )
```

time: 260 us -> 245 us (0.942)
  local copies, waits for them, and re-layouts: 29.1 us -> 73.6 us
  matrix products: 41.5 us -> 0 us
  Pallas kernels: 0 us -> 34.4 us
  waiting for transfers between devices: 86 us -> 57.4 us
  blocking collectives: 46.6 us -> 24.8 us
    dot_general x9 -> x0, matrix products: 41.5 us -> none  [dot(): lax.dot_general(left, right, (contract, ((), ())), preferred_element_type...]
    unnamed x14 -> x45, local copies, waits for them, and re-layouts: 5.15 us -> 43 us
    pallas_call x0 -> x6, Pallas kernels: none -> 34.4 us  [the longest x2 11.9 us: logits_and_stats(): pl.pallas_call(body, grid=(WIDE,), in_specs=[SMEM, whole((1, tokens)), sp...]
    all_to_all x3 -> x2, blocking collectives: 46.6 us -> 24.8 us  [broadcast_gather(): return lax.all_to_all(copies, axes, 0, 0, tiled=True)]
    all_to_all x2, waiting for transfers between devices: 34.5 us -> 17.5 us  [the longest x1 10.9 us: on_device(): lax.all_to_all(partial.reshape(PLANE, cut, first_half), ('x', 'y'), 0, 0,...]
    dot_general x2 -> x0, local copies, waits for them, and re-layouts: 7.71 us -> none  [dot(): lax.dot_general(left, right, (contract, ((), ())), preferred_element_type...]
    concatenate x1 -> x2, local copies, waits for them, and re-layouts: 3.16 us -> 10.7 us  [on_device(): both = jnp.concatenate([weight, other_weight], axis=1)]
    all_to_all x2, waiting for transfers between devices: 46.3 us -> 39 us  [broadcast_gather(): return lax.all_to_all(copies, axes, 0, 0, tiled=True)]
  transfers between devices with their start and end apart: 10 -> 10, of which waited for: 7 -> 5; matrix products, arithmetic and copies ran while one was open for 21% -> 17% of each run, Pallas kernels for 0% -> 9%
where the time goes in v3:
time: 245 us; the launch traced here: 243 us
  local copies, waits for them, and re-layouts  73.6 us (30%)
  waiting for transfers between devices  57.4 us (23%)
  Pallas kernels  34.4 us (14%)
  starting transfers between devices  32.6 us (13%)
  blocking collectives  24.8 us (10%)
  between operations  14.5 us (6%)
  other arithmetic  5.62 us (2%)
    unnamed x45, local copies, waits for them, and re-layouts  43 us
    all_to_all x2, waiting for transfers between devices, broadcast_gather(): return lax.all_to_all(copies, axes, 0, 0, tiled=True)  39 us
    all_to_all x2, blocking collectives, broadcast_gather(): return lax.all_to_all(copies, axes, 0, 0, tiled=True)  24.8 us
    all_to_all x2, starting transfers between devices, broadcast_gather(): return lax.all_to_all(copies, axes, 0, 0, tiled=True)  16 us
    pallas_call x2, Pallas kernels, logits_and_stats(): pl.pallas_call(body, grid=(WIDE,), in_specs=[SMEM, whole((1, tokens)), sp...  11.9 us
    pallas_call x2, Pallas kernels, head_half(): pl.pallas_call(body, grid=(WIDE,), in_specs=specs, out_specs=out_spec, ou...  11.5 us
    pallas_call x2, Pallas kernels, partial_product(): pl.pallas_call(body, grid=(7,), in_specs=[SMEM, whole((1, tokens)), whole...  11 us
    all_to_all x1, waiting for transfers between devices, on_device(): lax.all_to_all(partial.reshape(PLANE, cut, first_half), ('x', 'y'), 0, 0,...  10.9 us
  transfers between devices with their start and end apart: 10, of which 5 were waited for; matrix products, arithmetic and copies ran while one was open for 17% of the time, Pallas kernels for 9%

profile of v3, /device:TPU:8, one launch (start us, length us, event | category | flops | bytes accessed | tf_op | source)
XLA Modules:
  0.0 242.8 jit_solution(2979191426587173391)
XLA Ops:
  7.2 1.9 slice.100
  12.2 8.5 %all-to-all-start = ((bf16[8,12,1024]{2,1,0:T(8,128)(2,1)}), bf16[8,12,1024]{2,1,0:T(8,128)(2,1)S(1)}, u32[]{:S(2)}, u32[]{:S(2)}) async-start(bf16[8,12,1024]{2,1,0:T(8,128)(2,1)} %broadcast_in_dim.18), calls=%async_computation | async-start | bytes 524288 | tf_op jit(solution)/shard_map/all_to_all | solution.py:20
  20.7 13.4 %all-to-all-done = bf16[8,12,1024]{2,1,0:T(8,128)(2,1)S(1)} async-done(((bf16[8,12,1024]{2,1,0:T(8,128)(2,1)}), bf16[8,12,1024]{2,1,0:T(8,128)(2,1)S(1)}, u32[]{:S(2)}, u32[]{:S(2)}) %all-to-all-start) | async-done | bytes 196640 | tf_op jit(solution)/shard_map/all_to_all | solution.py:20
  34.2 1.8 broadcast_in_dim.20
  36.0 7.5 %all-to-all-start.1 = ((bf16[16,96,896]{2,1,0:T(8,128)(2,1)}), bf16[16,96,896]{2,1,0:T(8,128)(2,1)S(1)}, u32[]{:S(2)}, u32[]{:S(2)}) async-start(bf16[16,96,896]{2,1,0:T(8,128)(2,1)} %broadcast_in_dim.20), calls=%async_computation.1 | async-start | bytes 5505024 | tf_op jit(solution)/shard_map/all_to_all | solution.py:20
  43.6 3.2 %constant_dynamic-update-slice_fusion.1 = bf16[3584,640]{0,1:T(8,128)(2,1)} fusion(bf16[3584,320]{0,1:T(8,128)(2,1)} %param.6), kind=kLoop, calls=%fused_computation.31 | loop fusion | bytes 4587520
  47.2 3.4 %constant_dynamic-update-slice_fusion = bf16[3584,640]{0,1:T(8,128)(2,1)} fusion(bf16[3584,640]{0,1:T(8,128)(2,1)} %constant_dynamic-update-slice_fusion.1, bf16[3584,320]{0,1:T(8,128)(2,1)} %collective-permute-done), kind=kLoop, calls=%fused_computation.30 | loop fusion | bytes 4587520 | tf_op jit(solution)/shard_map/concatenate | solution.py:236
  50.5 25.5 %all-to-all-done.1 = bf16[16,96,896]{2,1,0:T(8,128)(2,1)S(1)} async-done(((bf16[16,96,896]{2,1,0:T(8,128)(2,1)}), bf16[16,96,896]{2,1,0:T(8,128)(2,1)S(1)}, u32[]{:S(2)}, u32[]{:S(2)}) %all-to-all-start.1) | async-done | bytes 2752544 | tf_op jit(solution)/shard_map/all_to_all | solution.py:20
  76.1 2.3 copy-done
  78.4 4.8 %shard_map.68 = (f32[640,384]{1,0:T(8,128)S(1)}, f32[8,384]{1,0:T(8,128)S(1)}) custom-call(s32[2]{0:T(128)S(1)} %pad_add_fusion.starts_ref, s32[1,384]{1,0:T(1,128)S(1)} %reshape.176.ids_ref.refs_0_, bf16[4,384,896]{2,1,0:T(8,128)(2,1)S(1)} %bitcast.98, bf16[640,3584]{1,0:T(8,128)(2,1)S(1)} %bitcast.101), custom_call_target="tpu_custom_call" | custom-call | flops 1761607680 | bytes 8323072 | tf_op jit(solution)/shard_map/pallas_call | solution.py:83
  84.2 2.3 copy-done.1
  86.5 2.3 copy-done.4
  88.8 7.0 %shard_map.69 = (f32[640,640]{1,0:T(8,128)S(1)}, f32[8,640]{1,0:T(8,128)S(1)}) custom-call(s32[2]{0:T(128)S(1)} %pad_add_fusion.starts_ref, s32[1,640]{1,0:T(1,128)S(1)} %reshape.178.ids_ref.refs_5_, bf16[640,3584]{1,0:T(8,128)(2,1)S(1)} %copy-done.4, bf16[640,3584]{1,0:T(8,128)(2,1)S(1)} %bitcast.102), custom_call_target="tpu_custom_call" | custom-call | flops 2936012800 | bytes 10813440 | tf_op jit(solution)/shard_map/pallas_call | solution.py:83
  95.9 1.2 copy-done.15
  97.1 12.6 %all_to_all.35 = f32[8,24,128]{2,1,0:T(8,128)S(1)} all-to-all(f32[8,24,128]{2,1,0:T(8,128)S(1)} %broadcast_in_dim.22), channel_id=1, replica_groups=mesh['z'=8,'core'=2,'x'=4,'y'=4] {'z'}, dimensions={0} | all-to-all | bytes 196608 | tf_op jit(solution)/shard_map/all_to_all | solution.py:20
  109.7 12.2 %all_to_all.36 = f32[16,24,128]{2,1,0:T(8,128)S(1)} all-to-all(f32[16,24,128]{2,1,0:T(8,128)S(1)} %broadcast_in_dim.24), channel_id=1, replica_groups=mesh['z'=8,'core'=2,'x'=4,'y'=4] {'x','y'}, dimensions={0} | all-to-all | bytes 393216 | tf_op jit(solution)/shard_map/all_to_all | solution.py:20
  122.0 2.3 copy-done.2
  124.3 1.4 copy-done.16
  125.7 6.4 %shard_map.71 = bf16[640,3584]{1,0:T(8,128)(2,1)S(1)} custom-call(s32[2]{0:T(128)S(1)} %pad_add_fusion.starts_ref, s32[1,640]{1,0:T(1,128)S(1)} %reshape.178.ids_ref.refs_5_, f32[640,640]{1,0:T(8,128)S(1)} %copy-done.16, f32[1,640]{1,0:T(1,128)S(1)} %bitcast.108, bf16[640,3584]{1,0:T(8,128)(2,1)S(1)} %bitcast.103), custom_call_target="tpu_custom_call" | custom-call | flops 2936012800 | bytes 10813440 | tf_op jit(solution)/shard_map/pallas_call | solution.py:131
  132.2 2.1 copy-done.19
  134.3 7.3 %copy.59.w_ref = bf16[3584,640]{1,0:T(8,128)(2,1)} copy(bf16[3584,640]{0,1:T(8,128)(2,1)} %constant_dynamic-update-slice_fusion) | data formatting | bytes 9175040 | tf_op jit(solution)/shard_map/concatenate | solution.py:236
  142.6 2.3 copy-done.3
  144.9 1.2 copy-done.12
  146.1 4.6 %shard_map.70 = bf16[3584,384]{1,0:T(8,128)(2,1)S(1)} custom-call(s32[2]{0:T(128)S(1)} %pad_add_fusion.starts_ref, s32[1,384]{1,0:T(1,128)S(1)} %reshape.176.ids_ref.refs_0_, f32[640,384]{1,0:T(8,128)S(1)} %copy-done.12, f32[1,384]{1,0:T(1,128)S(1)} %bitcast.105, bf16[3584,640]{1,0:T(8,128)(2,1)S(1)} %copy-done.3), custom_call_target="tpu_custom_call" | custom-call | flops 1761607680 | bytes 8323072 | tf_op jit(solution)/shard_map/pallas_call | solution.py:131
  150.7 1.6 copy-done.9
  152.3 5.6 %all-to-all-start.4 = ((bf16[16,224,384]{2,1,0:T(8,128)(2,1)}), bf16[16,224,384]{2,1,0:T(8,128)(2,1)}, u32[]{:S(2)}, u32[]{:S(2)}) async-start(bf16[16,224,384]{2,1,0:T(8,128)(2,1)} %bitcast.104), calls=%async_computation.4 | async-start | bytes 5505024 | tf_op jit(solution)/shard_map/all_to_all | solution.py:283
  159.9 2.3 copy-done.5
  162.3 1.2 copy-done.13
  163.5 1.4 copy-done.17
  164.9 5.6 %shard_map.72 = bf16[3584,320]{1,0:T(8,128)(2,1)S(1)} custom-call(s32[2]{0:T(128)S(1)} %pad_add_fusion.starts_ref, s32[1,384]{1,0:T(1,128)S(1)} %reshape.176.ids_ref.refs_0_, f32[640,384]{1,0:T(8,128)S(1)} %copy-done.13, f32[1,384]{1,0:T(1,128)S(1)} %bitcast.106, f32[1,384]{1,0:T(1,128)S(1)} %reshape.192.refs_3_, bf16[4,384,896]{2,1,0:T(8,128)(2,1)S(1)} %bitcast.99, ...), custom_call_target="tpu_custom_call" | custom-call | flops 2348810240 | bytes 12255232 | tf_op jit(solution)/shard_map/pallas_call | solution.py:187
  170.5 1.5 copy-done.10
  172.0 4.4 %copy.71 = bf16[3584,320]{0,1:T(8,128)(2,1)} copy(bf16[3584,320]{1,0:T(8,128)(2,1)} %copy-done.10) | data formatting | bytes 4587520 | tf_op jit(solution)/shard_map/pallas_call | solution.py:187
  176.7 10.9 %all-to-all-done.4 = bf16[16,224,384]{2,1,0:T(8,128)(2,1)} async-done(((bf16[16,224,384]{2,1,0:T(8,128)(2,1)}), bf16[16,224,384]{2,1,0:T(8,128)(2,1)}, u32[]{:S(2)}, u32[]{:S(2)}) %all-to-all-start.4) | async-done | bytes 2752544 | tf_op jit(solution)/shard_map/all_to_all | solution.py:283
  187.6 2.2 reduce_sum.96
  190.8 4.0 %all-to-all-start.5 = ((bf16[8,48,224]{2,1,0:T(8,128)(2,1)}), bf16[8,48,224]{2,1,0:T(8,128)(2,1)}, u32[]{:S(2)}, u32[]{:S(2)}) async-start(bf16[8,48,224]{2,1,0:T(8,128)(2,1)} %copy.62), calls=%async_computation.5 | async-start | bytes 393216 | tf_op jit(solution)/shard_map/all_to_all | solution.py:288
  194.8 2.1 reshape.184
  196.9 1.0 copy.88
  198.0 6.6 %all-to-all-done.5 = bf16[8,48,224]{2,1,0:T(8,128)(2,1)} async-done(((bf16[8,48,224]{2,1,0:T(8,128)(2,1)}), bf16[8,48,224]{2,1,0:T(8,128)(2,1)}, u32[]{:S(2)}, u32[]{:S(2)}) %all-to-all-start.5) | async-done | bytes 172064 | tf_op jit(solution)/shard_map/all_to_all | solution.py:288
  204.6 6.6 %all-to-all-start.6 = ((bf16[16,80,224]{2,1,0:T(8,128)(2,1)}), bf16[16,80,224]{2,1,0:T(8,128)(2,1)S(1)}, u32[]{:S(2)}, u32[]{:S(2)}) async-start(bf16[16,80,224]{2,1,0:T(8,128)(2,1)} %bitcast.91), calls=%async_computation.7 | async-start | bytes 1310720 | tf_op jit(solution)/shard_map/all_to_all | solution.py:291
  211.2 4.4 %copy.72.refs_10_ = bf16[3584,320]{1,0:T(8,128)(2,1)} copy(bf16[3584,320]{0,1:T(8,128)(2,1)} %collective-permute-done.2) | data formatting | bytes 4587520 | tf_op jit(solution)/shard_map/ppermute | solution.py:316
  215.6 2.3 copy-done.6
  217.9 1.8 copy-done.7
  219.6 1.2 copy-done.14
  220.8 1.4 copy-done.18
  222.3 5.9 %shard_map.73 = bf16[3584,320]{1,0:T(8,128)(2,1)S(1)} custom-call(s32[2]{0:T(128)S(1)} %pad_add_fusion.starts_ref, s32[1,384]{1,0:T(1,128)S(1)} %reshape.176.ids_ref.refs_0_, f32[640,384]{1,0:T(8,128)S(1)} %copy-done.14, f32[1,384]{1,0:T(1,128)S(1)} %bitcast.107, f32[1,384]{1,0:T(1,128)S(1)} %reshape.192.refs_3_, bf16[4,384,896]{2,1,0:T(8,128)(2,1)S(1)} %bitcast.100, ...), custom_call_target="tpu_custom_call" | custom-call | flops 2348810240 | bytes 12255232 | tf_op jit(solution)/shard_map/pallas_call | solution.py:187
  228.2 1.5 copy-done.8
  229.7 4.4 %copy.74 = bf16[3584,320]{0,1:T(8,128)(2,1)} copy(bf16[3584,320]{1,0:T(8,128)(2,1)} %copy-done.8) | data formatting | bytes 4587520
  234.1 1.0 convert_reduce_fusion.1
  (103 shorter events, 9.8 us)
Async XLA Ops:
  7.2 77.1 %all-gather.2.cloned.1.call-start = ((), (), s32[]{:S(2)}) async-start(), calls=%async_computation.8 | async-start | bytes 5160960 | tf_op jit(solution)/shard_map/all_gather | solution.py:239
  12.2 21.9 %all-to-all-start = ((bf16[8,12,1024]{2,1,0:T(8,128)(2,1)}), bf16[8,12,1024]{2,1,0:T(8,128)(2,1)S(1)}, u32[]{:S(2)}, u32[]{:S(2)}) async-start(bf16[8,12,1024]{2,1,0:T(8,128)(2,1)} %broadcast_in_dim.18), calls=%async_computation | async-start | bytes 524288 | tf_op jit(solution)/shard_map/all_to_all | solution.py:20
  20.7 26.5 %collective-permute-start = (bf16[3584,320]{0,1:T(8,128)(2,1)}, bf16[3584,320]{0,1:T(8,128)(2,1)}, u32[]{:S(2)}, u32[]{:S(2)}) collective-permute-start(bf16[3584,320]{0,1:T(8,128)(2,1)} %param.6), channel_id=1, source_target_pairs={{0,16},{16,0},{1,17},{17,1},{2,18},{18,2},{3,19},{19,3},{4,20},{20... | collective-permute-start | bytes 6881288 | tf_op jit(solution)/shard_map/ppermute | solution.py:235
  36.0 40.1 %all-to-all-start.1 = ((bf16[16,96,896]{2,1,0:T(8,128)(2,1)}), bf16[16,96,896]{2,1,0:T(8,128)(2,1)S(1)}, u32[]{:S(2)}, u32[]{:S(2)}) async-start(bf16[16,96,896]{2,1,0:T(8,128)(2,1)} %broadcast_in_dim.20), calls=%async_computation.1 | async-start | bytes 5505024 | tf_op jit(solution)/shard_map/all_to_all | solution.py:20
  43.5 151.4 %reduce-scatter.2.cloned.1.call-start = ((), (), s32[]{:S(2)}) async-start(), calls=%async_computation.9 | async-start | bytes 5160960 | tf_op jit(solution)/shard_map/reduce_scatter | solution.py:280
  76.1 2.3 copy-start
  83.2 1.0 copy-start.11
  84.2 2.3 copy-start.1
  86.5 2.3 copy-start.4
  95.8 1.2 copy-start.15
  122.0 2.3 copy-start.2
  124.3 1.4 copy-start.16
  132.2 2.1 copy-start.19
  142.6 2.3 copy-start.3
  144.9 1.2 copy-start.12
  150.7 1.6 copy-start.9
  152.3 35.3 %all-to-all-start.4 = ((bf16[16,224,384]{2,1,0:T(8,128)(2,1)}), bf16[16,224,384]{2,1,0:T(8,128)(2,1)}, u32[]{:S(2)}, u32[]{:S(2)}) async-start(bf16[16,224,384]{2,1,0:T(8,128)(2,1)} %bitcast.104), calls=%async_computation.4 | async-start | bytes 5505024 | tf_op jit(solution)/shard_map/all_to_all | solution.py:283
  158.1 1.2 collective-permute-start.1
  159.9 2.4 copy-start.5
  162.3 1.2 copy-start.13
  163.5 1.4 copy-start.17
  170.5 1.5 copy-start.10
  176.4 34.7 %collective-permute-start.2 = (bf16[3584,320]{0,1:T(8,128)(2,1)}, bf16[3584,320]{0,1:T(8,128)(2,1)}, u32[]{:S(2)}, u32[]{:S(2)}) collective-permute-start(bf16[3584,320]{0,1:T(8,128)(2,1)} %copy.71), channel_id=1, source_target_pairs={{0,16},{16,0},{1,17},{17,1},{2,18},{18,2},{3,19},{19,3},{4,20},{20... | collective-permute-start | bytes 6881288 | tf_op jit(solution)/shard_map/ppermute | solution.py:316
  190.8 13.8 %all-to-all-start.5 = ((bf16[8,48,224]{2,1,0:T(8,128)(2,1)}), bf16[8,48,224]{2,1,0:T(8,128)(2,1)}, u32[]{:S(2)}, u32[]{:S(2)}) async-start(bf16[8,48,224]{2,1,0:T(8,128)(2,1)} %copy.62), calls=%async_computation.5 | async-start | bytes 393216 | tf_op jit(solution)/shard_map/all_to_all | solution.py:288
  204.6 30.5 %all-to-all-start.6 = ((bf16[16,80,224]{2,1,0:T(8,128)(2,1)}), bf16[16,80,224]{2,1,0:T(8,128)(2,1)S(1)}, u32[]{:S(2)}, u32[]{:S(2)}) async-start(bf16[16,80,224]{2,1,0:T(8,128)(2,1)} %bitcast.91), calls=%async_computation.7 | async-start | bytes 1310720 | tf_op jit(solution)/shard_map/all_to_all | solution.py:291
  215.6 2.3 copy-start.6
  217.9 1.8 copy-start.7
  219.6 1.2 copy-start.14
  220.8 1.4 copy-start.18
  228.2 1.5 copy-start.8
Sparse Core Ops, SparseCore 0:
  10.4 63.0 all-gather.1
  134.4 52.9 reduce-scatter.1

commit v4 on v3

--- a/solution.py
+++ b/solution.py
@@ -13,6 +13,7 @@
 WIDE, GROUPS = 4, 4
 EARLY = 48
 LANES = 128
+PARAMS = pltpu.CompilerParams(vmem_limit_bytes=56 << 20)
 
 
 def broadcast_gather(part, axes, count):
@@ -28,10 +29,6 @@
 
 def dot(left, right, contract):
     return lax.dot_general(left, right, (contract, ((), ())), preferred_element_type=F32)
-
-
-def params(megabytes):
-    return pltpu.CompilerParams(vmem_limit_bytes=megabytes << 20)
 
 
 def cost(flops, nbytes):
@@ -89,7 +86,7 @@
             jax.ShapeDtypeStruct((columns, tokens), F32),
             jax.ShapeDtypeStruct((8, tokens), F32),
         ],
-        compiler_params=params(20),
+        compiler_params=PARAMS,
         cost_estimate=cost(
             2 * columns * tokens * features, 2 * features * (columns + tokens) + 4 * columns * tokens
         ),
@@ -101,9 +98,9 @@
     return jnp.where(match, 1.0, 0.0) - jnp.exp(logits - norm)
 
 
-def partial_product(starts, ids, logits_t, norm, weight, by_feature):
+def partial_product(starts, ids, logits_t, norm, weight_t, by_feature):
     columns, tokens = logits_t.shape
-    features = weight.shape[0] if by_feature else weight.shape[1]
+    features = weight_t.shape[1]
     block = features // 7
 
     def body(starts_ref, ids_ref, logits_ref, norm_ref, w_ref, out_ref, held):
@@ -115,31 +112,35 @@
             held[...] = (change if by_feature else change.T).astype(BF16)
 
         if by_feature:
-            out = dot(w_ref[...], held[...], ((1,), (0,)))
+            out = dot(w_ref[...], held[...], ((0,), (0,)))
         else:
             out = dot(held[...], w_ref[...], ((1,), (0,)))
         out_ref[...] = out.astype(BF16)
 
     if by_feature:
-        w_spec = pl.BlockSpec((block, columns), lambda k: (k, 0))
         out_spec, out_dims = pl.BlockSpec((block, tokens), lambda k: (k, 0)), (features, tokens)
         held = (columns, tokens)
     else:
-        w_spec = pl.BlockSpec((columns, block), lambda k: (0, k))
         out_spec, out_dims = pl.BlockSpec((tokens, block), lambda k: (0, k)), (tokens, features)
         held = (tokens, columns)
     return pl.pallas_call(
         body,
         grid=(7,),
-        in_specs=[SMEM, whole((1, tokens)), whole((columns, tokens)), whole((1, tokens)), w_spec],
+        in_specs=[
+            SMEM,
+            whole((1, tokens)),
+            whole((columns, tokens)),
+            whole((1, tokens)),
+            pl.BlockSpec((columns, block), lambda k: (0, k)),
+        ],
         out_specs=out_spec,
         out_shape=jax.ShapeDtypeStruct(out_dims, BF16),
         scratch_shapes=[pltpu.VMEM(held, BF16)],
-        compiler_params=params(20),
+        compiler_params=PARAMS,
         cost_estimate=cost(
             2 * columns * tokens * features, 2 * features * (columns + tokens) + 4 * columns * tokens
         ),
-    )(starts, ids, logits_t, norm, weight)
+    )(starts, ids, logits_t, norm, weight_t)
 
 
 def head_half(starts, early, late, low, high, added):
@@ -165,7 +166,6 @@
 
         total = dot(held[0][...], sides[0][4][...], ((1,), (0,)))
         total += dot(held[1][...], sides[1][4][...], ((1,), (0,)))
-        total = total.T
         if added is not None:
             total += rest[0][...].astype(F32)
         out_ref[...] = total.astype(BF16)
@@ -179,7 +179,7 @@
         ),
     ):
         specs += [whole((1, size)), whole((columns, size)), whole((1, size)), whole((1, size)), spec]
-    out_spec = pl.BlockSpec((block, here), lambda k: (k, 0))
+    out_spec = pl.BlockSpec((here, block), lambda k: (0, k))
     operands = list(early) + list(late)
     if added is not None:
         specs.append(out_spec)
@@ -189,9 +189,9 @@
         grid=(WIDE,),
         in_specs=specs,
         out_specs=out_spec,
-        out_shape=jax.ShapeDtypeStruct((features, here), BF16),
+        out_shape=jax.ShapeDtypeStruct((here, features), BF16),
         scratch_shapes=[pltpu.VMEM((here, size), BF16) for size in sizes],
-        compiler_params=params(28),
+        compiler_params=PARAMS,
         cost_estimate=cost(
             2 * here * sum(sizes) * features, 2 * features * (here + sum(sizes)) + 4 * columns * sum(sizes)
         ),
@@ -232,9 +232,8 @@
     all_rows = first_half + second_half
     tokens = all_rows * CORES
 
-    other_weight = lax.ppermute(weight, "core", SWAP)
-    both = jnp.concatenate([weight, other_weight], axis=1)
-    both_t = both.T
+    weight_t = weight.T
+    both_t = jnp.concatenate([weight_t, lax.ppermute(weight_t, "core", SWAP)])
 
     late = lax.all_gather(hidden[EARLY:], "z", axis=0, tiled=True)
     piece = lax.dynamic_slice(
@@ -279,7 +278,7 @@
     partial = partial_product(starts, ids[1], late_logits, norms[1], both_t, False)
     late_sum = lax.psum_scatter(partial, "z", scatter_dimension=0, tiled=True)
     cut = features // PLANE
-    partial = partial_product(starts, ids[0], early_logits, norms[0], both, True)
+    partial = partial_product(starts, ids[0], early_logits, norms[0], both_t, True)
     shared = lax.all_to_all(
         partial.reshape(PLANE, cut, first_half), ("x", "y"), 0, 0, tiled=True
     )
@@ -315,7 +314,7 @@
     far = head_half(starts, *sides, columns_here, 2 * columns_here, None)
     far = lax.ppermute(far, "core", SWAP)
     head_grad = head_half(starts, *sides, 0, columns_here, far)
-    return hidden_grad.astype(BF16), head_grad
+    return hidden_grad.astype(BF16), head_grad.T
 
 
 def solution(mesh):

time: 245 us -> 228 us (0.931)
  local copies, waits for them, and re-layouts: 73.6 us -> 18.2 us
  Pallas kernels: 34.4 us -> 51.7 us
  waiting for transfers between devices: 57.4 us -> 73.6 us
  starting transfers between devices: 32.6 us -> 35.5 us
  other arithmetic: 5.62 us -> 8.28 us
    unnamed x45 -> x5, local copies, waits for them, and re-layouts: 43 us -> 3.42 us
    all_to_all x1, waiting for transfers between devices: 10.9 us -> 27 us  [on_device(): lax.all_to_all(partial.reshape(PLANE, cut, first_half), ('x', 'y'), 0, 0,...]
    concatenate x2 -> x0, local copies, waits for them, and re-layouts: 10.7 us -> none  [on_device(): both = jnp.concatenate([weight, other_weight], axis=1)]
    pallas_call x2, Pallas kernels: 11 us -> 18.5 us  [partial_product(): pl.pallas_call(body, grid=(7,), in_specs=[SMEM, whole((1, tokens)), whole...]
    pallas_call x2, Pallas kernels: 11.5 us -> 17.1 us  [head_half(): pl.pallas_call(body, grid=(WIDE,), in_specs=specs, out_specs=out_spec, ou...]
    concatenate x0 -> x1, other arithmetic: none -> 4.83 us  [on_device(): both_t = jnp.concatenate([weight_t, lax.ppermute(weight_t, 'core', SWAP)])]
    ppermute x1 -> x0, local copies, waits for them, and re-layouts: 4.41 us -> none  [on_device(): far = lax.ppermute(far, 'core', SWAP)]
    pallas_call x1 -> x0, local copies, waits for them, and re-layouts: 4.39 us -> none  [head_half(): pl.pallas_call(body, grid=(WIDE,), in_specs=specs, out_specs=out_spec, ou...]
  transfers between devices with their start and end apart: 10 -> 10, of which waited for: 5 -> 5; matrix products, arithmetic and copies ran while one was open for 17% -> 9% of each run, Pallas kernels for 9% -> 15%
where the time goes in v4:
time: 228 us; the launch traced here: 226 us
  waiting for transfers between devices  73.6 us (32%)
  Pallas kernels  51.7 us (23%)
  starting transfers between devices  35.5 us (16%)
  blocking collectives  24.8 us (11%)
  local copies, waits for them, and re-layouts  18.2 us (8%)
  between operations  14.3 us (6%)
  other arithmetic  8.28 us (4%)
    all_to_all x2, waiting for transfers between devices, broadcast_gather(): return lax.all_to_all(copies, axes, 0, 0, tiled=True)  39 us
    all_to_all x1, waiting for transfers between devices, on_device(): lax.all_to_all(partial.reshape(PLANE, cut, first_half), ('x', 'y'), 0, 0,...  27 us
    all_to_all x2, blocking collectives, broadcast_gather(): return lax.all_to_all(copies, axes, 0, 0, tiled=True)  24.8 us
    pallas_call x2, Pallas kernels, partial_product(): pl.pallas_call(body, grid=(7,), in_specs=[SMEM, whole((1, tokens)), whole...  18.5 us
    pallas_call x2, Pallas kernels, head_half(): pl.pallas_call(body, grid=(WIDE,), in_specs=specs, out_specs=out_spec, ou...  17.1 us
    pallas_call x2, Pallas kernels, logits_and_stats(): pl.pallas_call(body, grid=(WIDE,), in_specs=[SMEM, whole((1, tokens)), sp...  16.1 us
    all_to_all x2, starting transfers between devices, broadcast_gather(): return lax.all_to_all(copies, axes, 0, 0, tiled=True)  16 us
    all_to_all x1, starting transfers between devices, on_device(): late_sum = lax.all_to_all(late_sum, ('x', 'y'), 0, 0, tiled=True)  10.7 us
  transfers between devices with their start and end apart: 10, of which 5 were waited for; matrix products, arithmetic and copies ran while one was open for 9% of the time, Pallas kernels for 15%

profile of v4, /device:TPU:8, one launch (start us, length us, event | category | flops | bytes accessed | tf_op | source)
XLA Modules:
  0.0 226.5 jit_solution(17656057116679461358)
XLA Ops:
  7.2 1.9 slice.100
  9.2 0.9 dynamic_slice.7
  10.1 0.7 fusion.23
  10.7 0.7 fusion.29
  11.5 0.7 broadcast_in_dim.18
  12.2 8.5 %all-to-all-start = ((bf16[8,12,1024]{2,1,0:T(8,128)(2,1)}), bf16[8,12,1024]{2,1,0:T(8,128)(2,1)S(1)}, u32[]{:S(2)}, u32[]{:S(2)}) async-start(bf16[8,12,1024]{2,1,0:T(8,128)(2,1)} %broadcast_in_dim.18), calls=%async_computation | async-start | bytes 524288 | tf_op jit(solution)/shard_map/all_to_all | solution.py:21
  20.7 13.4 %all-to-all-done = bf16[8,12,1024]{2,1,0:T(8,128)(2,1)S(1)} async-done(((bf16[8,12,1024]{2,1,0:T(8,128)(2,1)}), bf16[8,12,1024]{2,1,0:T(8,128)(2,1)S(1)}, u32[]{:S(2)}, u32[]{:S(2)}) %all-to-all-start) | async-done | bytes 196640 | tf_op jit(solution)/shard_map/all_to_all | solution.py:21
  34.2 1.7 broadcast_in_dim.20
  35.9 7.5 %all-to-all-start.1 = ((bf16[16,96,896]{2,1,0:T(8,128)(2,1)}), bf16[16,96,896]{2,1,0:T(8,128)(2,1)S(1)}, u32[]{:S(2)}, u32[]{:S(2)}) async-start(bf16[16,96,896]{2,1,0:T(8,128)(2,1)} %broadcast_in_dim.20), calls=%async_computation.1 | async-start | bytes 5505024 | tf_op jit(solution)/shard_map/all_to_all | solution.py:21
  43.5 0.6 pad_add_fusion.starts_ref
  44.2 0.7 reshape.178.ids_ref.refs_5_
  45.0 0.7 reshape.176.ids_ref.refs_0_
  45.7 4.8 %pad_maximum_fusion.w_ref = bf16[640,3584]{1,0:T(8,128)(2,1)} fusion(bf16[320,3584]{1,0:T(8,128)(2,1)} %collective-permute-done, bf16[320,3584]{1,0:T(8,128)(2,1)} %bitcast.12), kind=kLoop, calls=%fused_computation | loop fusion | flops 9175040 | bytes 9175040 | tf_op jit(solution)/shard_map/concatenate | solution.py:236
  50.5 25.6 %all-to-all-done.1 = bf16[16,96,896]{2,1,0:T(8,128)(2,1)S(1)} async-done(((bf16[16,96,896]{2,1,0:T(8,128)(2,1)}), bf16[16,96,896]{2,1,0:T(8,128)(2,1)S(1)}, u32[]{:S(2)}, u32[]{:S(2)}) %all-to-all-start.1) | async-done | bytes 2752544 | tf_op jit(solution)/shard_map/all_to_all | solution.py:21
  76.0 1.5 copy-done
  77.6 7.1 %shard_map.68 = (f32[640,384]{1,0:T(8,128)}, f32[8,384]{1,0:T(8,128)}) custom-call(s32[2]{0:T(128)} %pad_add_fusion.starts_ref, s32[1,384]{1,0:T(1,128)} %reshape.176.ids_ref.refs_0_, bf16[4,384,896]{2,1,0:T(8,128)(2,1)} %bitcast.99, bf16[640,3584]{1,0:T(8,128)(2,1)} %pad_maximum_fusion.w_ref), custom_call_target="tpu_custom_call" | custom-call | flops 1761607680 | bytes 8323072 | tf_op jit(solution)/shard_map/pallas_call | solution.py:80
  84.7 0.7 slice.98
  85.4 9.0 %shard_map.69 = (f32[640,640]{1,0:T(8,128)}, f32[8,640]{1,0:T(8,128)}) custom-call(s32[2]{0:T(128)} %pad_add_fusion.starts_ref, s32[1,640]{1,0:T(1,128)} %reshape.178.ids_ref.refs_5_, bf16[640,3584]{1,0:T(8,128)(2,1)} %all-gather.2.cloned.1.call-done.h_ref.refs_9_, bf16[640,3584]{1,0:T(8,128)(2,1)} %pad_maximum_fusion.w_ref), custom_call_target="tpu_custom_call" | custom-call | flops 2936012800 | bytes 10813440 | tf_op jit(solution)/shard_map/pallas_call | solution.py:80
  94.4 0.7 slice.101
  95.1 12.6 %all_to_all.35 = f32[8,24,128]{2,1,0:T(8,128)S(1)} all-to-all(f32[8,24,128]{2,1,0:T(8,128)S(1)} %broadcast_in_dim.22), channel_id=1, replica_groups=mesh['z'=8,'core'=2,'x'=4,'y'=4] {'z'}, dimensions={0} | all-to-all | bytes 196608 | tf_op jit(solution)/shard_map/all_to_all | solution.py:21
  107.8 12.2 %all_to_all.36 = f32[16,24,128]{2,1,0:T(8,128)S(1)} all-to-all(f32[16,24,128]{2,1,0:T(8,128)S(1)} %broadcast_in_dim.24), channel_id=1, replica_groups=mesh['z'=8,'core'=2,'x'=4,'y'=4] {'x','y'}, dimensions={0} | all-to-all | bytes 393216 | tf_op jit(solution)/shard_map/all_to_all | solution.py:21
  120.1 0.6 copy.77
  120.6 9.9 %shard_map.71 = bf16[640,3584]{1,0:T(8,128)(2,1)} custom-call(s32[2]{0:T(128)} %pad_add_fusion.starts_ref, s32[1,640]{1,0:T(1,128)} %reshape.178.ids_ref.refs_5_, f32[640,640]{1,0:T(8,128)} %get-tuple-element.9.logits_ref.refs_6_, f32[1,640]{1,0:T(1,128)} %bitcast.124, bf16[640,3584]{1,0:T(8,128)(2,1)} %pad_maximum_fusion.w_ref), custom_call_target="tpu_custom_call" | custom-call | flops 2936012800 | bytes 10813440 | tf_op jit(solution)/shard_map/pallas_call | solution.py:126
  130.9 0.1 reshape.186
  131.2 0.1 reshape.185
  131.5 0.6 copy.78
  132.1 0.2 fusion.18
  132.2 0.1 collective-permute-start.1
  132.3 8.7 %shard_map.70 = bf16[3584,384]{1,0:T(8,128)(2,1)} custom-call(s32[2]{0:T(128)} %pad_add_fusion.starts_ref, s32[1,384]{1,0:T(1,128)} %reshape.176.ids_ref.refs_0_, f32[640,384]{1,0:T(8,128)} %get-tuple-element.6.logits_ref.refs_1_, f32[1,384]{1,0:T(1,128)} %bitcast.121, bf16[640,3584]{1,0:T(8,128)(2,1)} %pad_maximum_fusion.w_ref), custom_call_target="tpu_custom_call" | custom-call | flops 1761607680 | bytes 8323072 | tf_op jit(solution)/shard_map/pallas_call | solution.py:126
  141.0 5.1 %all-to-all-start.4 = ((bf16[16,224,384]{2,1,0:T(8,128)(2,1)}), bf16[16,224,384]{2,1,0:T(8,128)(2,1)S(1)}, u32[]{:S(2)}, u32[]{:S(2)}) async-start(bf16[16,224,384]{2,1,0:T(8,128)(2,1)} %bitcast.102), calls=%async_computation.4 | async-start | bytes 5505024 | tf_op jit(solution)/shard_map/all_to_all | solution.py:282
  146.2 0.2 multiply_reduce_fusion
  146.4 0.1 add_reduce_fusion
  146.7 0.7 reshape.193.refs_8_
  147.4 0.6 reshape.192.refs_3_
  148.1 8.3 %shard_map.72 = bf16[320,3584]{1,0:T(8,128)(2,1)} custom-call(s32[2]{0:T(128)} %pad_add_fusion.starts_ref, s32[1,384]{1,0:T(1,128)} %reshape.176.ids_ref.refs_0_, f32[640,384]{1,0:T(8,128)} %get-tuple-element.6.logits_ref.refs_1_, f32[1,384]{1,0:T(1,128)} %bitcast.122, f32[1,384]{1,0:T(1,128)} %reshape.192.refs_3_, bf16[4,384,896]{2,1,0:T(8,128)(2,1)} %bitcast.100, ...), custom_call_target="tpu_custom_call" | custom-call | flops 2348810240 | bytes 12255232 | tf_op jit(solution)/shard_map/pallas_call | solution.py:187
  156.5 27.0 %all-to-all-done.4 = bf16[16,224,384]{2,1,0:T(8,128)(2,1)S(1)} async-done(((bf16[16,224,384]{2,1,0:T(8,128)(2,1)}), bf16[16,224,384]{2,1,0:T(8,128)(2,1)S(1)}, u32[]{:S(2)}, u32[]{:S(2)}) %all-to-all-start.4) | async-done | bytes 2752544 | tf_op jit(solution)/shard_map/all_to_all | solution.py:282
  183.5 0.4 reduce_sum.96
  183.9 0.1 copy.49
  184.2 0.7 copy.51
  184.9 3.6 %all-to-all-start.5 = ((bf16[8,48,224]{2,1,0:T(8,128)(2,1)}), bf16[8,48,224]{2,1,0:T(8,128)(2,1)S(1)}, u32[]{:S(2)}, u32[]{:S(2)}) async-start(bf16[8,48,224]{2,1,0:T(8,128)(2,1)} %copy.51), calls=%async_computation.5 | async-start | bytes 393216 | tf_op jit(solution)/shard_map/all_to_all | solution.py:287
  188.5 2.1 reshape.184
  190.6 1.0 copy.74
  191.6 6.5 %all-to-all-done.5 = bf16[8,48,224]{2,1,0:T(8,128)(2,1)S(1)} async-done(((bf16[8,48,224]{2,1,0:T(8,128)(2,1)}), bf16[8,48,224]{2,1,0:T(8,128)(2,1)S(1)}, u32[]{:S(2)}, u32[]{:S(2)}) %all-to-all-start.5) | async-done | bytes 172064 | tf_op jit(solution)/shard_map/all_to_all | solution.py:287
  198.2 10.7 %all-to-all-start.6 = ((bf16[16,80,224]{2,1,0:T(8,128)(2,1)}), bf16[16,80,224]{2,1,0:T(8,128)(2,1)S(1)}, u32[]{:S(2)}, u32[]{:S(2)}) async-start(bf16[16,80,224]{2,1,0:T(8,128)(2,1)} %bitcast.92), calls=%async_computation.7 | async-start | bytes 1310720 | tf_op jit(solution)/shard_map/all_to_all | solution.py:290
  208.9 8.8 %shard_map.73 = bf16[320,3584]{1,0:T(8,128)(2,1)} custom-call(s32[2]{0:T(128)} %pad_add_fusion.starts_ref, s32[1,384]{1,0:T(1,128)} %reshape.176.ids_ref.refs_0_, f32[640,384]{1,0:T(8,128)} %get-tuple-element.6.logits_ref.refs_1_, f32[1,384]{1,0:T(1,128)} %bitcast.123, f32[1,384]{1,0:T(1,128)} %reshape.192.refs_3_, bf16[4,384,896]{2,1,0:T(8,128)(2,1)} %bitcast.101, ...), custom_call_target="tpu_custom_call" | custom-call | flops 2348810240 | bytes 12255232 | tf_op jit(solution)/shard_map/pallas_call | solution.py:187
  217.7 1.0 all-to-all-done.6
  218.7 0.1 convert_reduce_fusion
  218.9 0.7 copy.60
  (60 shorter events, 1.9 us)
Async XLA Ops:
  7.2 78.2 %all-gather.2.cloned.1.call-start = ((), (), s32[]{:S(2)}) async-start(), calls=%async_computation.8 | async-start | bytes 5160960 | tf_op jit(solution)/shard_map/all_gather | solution.py:238
  12.2 21.9 %all-to-all-start = ((bf16[8,12,1024]{2,1,0:T(8,128)(2,1)}), bf16[8,12,1024]{2,1,0:T(8,128)(2,1)S(1)}, u32[]{:S(2)}, u32[]{:S(2)}) async-start(bf16[8,12,1024]{2,1,0:T(8,128)(2,1)} %broadcast_in_dim.18), calls=%async_computation | async-start | bytes 524288 | tf_op jit(solution)/shard_map/all_to_all | solution.py:21
  20.7 25.0 %collective-permute-start = (bf16[320,3584]{1,0:T(8,128)(2,1)}, bf16[320,3584]{1,0:T(8,128)(2,1)}, u32[]{:S(2)}, u32[]{:S(2)}) collective-permute-start(bf16[320,3584]{1,0:T(8,128)(2,1)} %bitcast.12), channel_id=1, source_target_pairs={{0,16},{16,0},{1,17},{17,1},{2,18},{18,2},{3,19},{19,3},{4,20},{20... | collective-permute-start | bytes 6881288 | tf_op jit(solution)/shard_map/ppermute | solution.py:236
  35.9 40.1 %all-to-all-start.1 = ((bf16[16,96,896]{2,1,0:T(8,128)(2,1)}), bf16[16,96,896]{2,1,0:T(8,128)(2,1)S(1)}, u32[]{:S(2)}, u32[]{:S(2)}) async-start(bf16[16,96,896]{2,1,0:T(8,128)(2,1)} %broadcast_in_dim.20), calls=%async_computation.1 | async-start | bytes 5505024 | tf_op jit(solution)/shard_map/all_to_all | solution.py:21
  43.4 145.1 %reduce-scatter.2.cloned.1.call-start = ((), (), s32[]{:S(2)}) async-start(), calls=%async_computation.9 | async-start | bytes 5160960 | tf_op jit(solution)/shard_map/reduce_scatter | solution.py:279
  76.0 1.5 copy-start
  132.2 14.1 %collective-permute-start.1 = (f32[8]{0:T(128)S(1)}, f32[8]{0:T(128)S(1)}, u32[]{:S(2)}, u32[]{:S(2)}) collective-permute-start(f32[8]{0:T(128)S(1)} %fusion.18), channel_id=1, source_target_pairs={{0,16},{16,0},{1,17},{17,1},{2,18},{18,2},{3,19},{19,3},{4,20},{20... | collective-permute-start | bytes 104 | tf_op jit(solution)/shard_map/ppermute | solution.py:295
  141.0 42.5 %all-to-all-start.4 = ((bf16[16,224,384]{2,1,0:T(8,128)(2,1)}), bf16[16,224,384]{2,1,0:T(8,128)(2,1)S(1)}, u32[]{:S(2)}, u32[]{:S(2)}) async-start(bf16[16,224,384]{2,1,0:T(8,128)(2,1)} %bitcast.102), calls=%async_computation.4 | async-start | bytes 5505024 | tf_op jit(solution)/shard_map/all_to_all | solution.py:282
  156.4 52.5 %collective-permute-start.2 = (bf16[320,3584]{1,0:T(8,128)(2,1)}, bf16[320,3584]{1,0:T(8,128)(2,1)}, u32[]{:S(2)}, u32[]{:S(2)}) collective-permute-start(bf16[320,3584]{1,0:T(8,128)(2,1)} %shard_map.72), channel_id=1, source_target_pairs={{0,16},{16,0},{1,17},{17,1},{2,18},{18,2},{3,19},{19,3},{4,20},{20... | collective-permute-start | bytes 6881288 | tf_op jit(solution)/shard_map/ppermute | solution.py:315
  184.9 13.3 %all-to-all-start.5 = ((bf16[8,48,224]{2,1,0:T(8,128)(2,1)}), bf16[8,48,224]{2,1,0:T(8,128)(2,1)S(1)}, u32[]{:S(2)}, u32[]{:S(2)}) async-start(bf16[8,48,224]{2,1,0:T(8,128)(2,1)} %copy.51), calls=%async_computation.5 | async-start | bytes 393216 | tf_op jit(solution)/shard_map/all_to_all | solution.py:287
  198.2 20.6 %all-to-all-start.6 = ((bf16[16,80,224]{2,1,0:T(8,128)(2,1)}), bf16[16,80,224]{2,1,0:T(8,128)(2,1)S(1)}, u32[]{:S(2)}, u32[]{:S(2)}) async-start(bf16[16,80,224]{2,1,0:T(8,128)(2,1)} %bitcast.92), calls=%async_computation.7 | async-start | bytes 1310720 | tf_op jit(solution)/shard_map/all_to_all | solution.py:290
Sparse Core Ops, SparseCore 0:
  10.4 63.0 all-gather.1
  130.7 52.9 reduce-scatter.1

commit v5 on v4

--- a/solution.py
+++ b/solution.py
@@ -13,7 +13,8 @@
 WIDE, GROUPS = 4, 4
 EARLY = 48
 LANES = 128
-PARAMS = pltpu.CompilerParams(vmem_limit_bytes=56 << 20)
+LIMIT = 28
+PARAMS = pltpu.CompilerParams(vmem_limit_bytes=LIMIT << 20)
 
 
 def broadcast_gather(part, axes, count):
@@ -38,57 +39,60 @@
 SMEM = pl.BlockSpec(memory_space=pltpu.SMEM)
 
 
-def whole(shape):
-    return pl.BlockSpec(shape, lambda *_: (0,) * len(shape))
+VMEM = pl.BlockSpec(memory_space=pltpu.VMEM)
+ANY = pl.BlockSpec(memory_space=pl.ANY)
+HBM = pl.BlockSpec(memory_space=pltpu.HBM)
 
 
 def column_of(starts_ref, shape, low, half):
     row = lax.broadcasted_iota(jnp.int32, shape, 0) + low
     return row + jnp.where(row < half, starts_ref[0], starts_ref[1] - half)
+
+
+def feature_block(hidden_ref, k, block):
+    if len(hidden_ref.shape) == 3:
+        return hidden_ref.at[k]
+    return hidden_ref.at[:, pl.ds(k * block, block)]
 
 
 def logits_and_stats(starts, ids, hidden, weight_t):
     columns, features = weight_t.shape
     tokens = hidden.shape[-2]
     block = features // WIDE
-    if hidden.ndim == 3:
-        spec = pl.BlockSpec((None, tokens, block), lambda k: (k, 0, 0))
-    else:
-        spec = pl.BlockSpec((tokens, block), lambda k: (0, k))
-
-    def body(starts_ref, ids_ref, h_ref, w_ref, logits_ref, stats_ref):
-        step = pl.program_id(0)
-        part = dot(w_ref[...], h_ref[...], ((1,), (1,)))
-
-        @pl.when(step == 0)
-        def _():
-            logits_ref[...] = part
-
-        @pl.when(step > 0)
-        def _():
-            logits_ref[...] += part
-
-        @pl.when(step == WIDE - 1)
-        def _():
-            logits = logits_ref[...]
-            match = column_of(starts_ref, logits.shape, 0, columns // 2) == ids_ref[...]
-            top = jnp.max(logits, axis=0, keepdims=True)
-            total = jnp.sum(jnp.exp(logits - top), axis=0, keepdims=True)
-            picked = jnp.sum(jnp.where(match, logits, 0.0), axis=0, keepdims=True)
-            stats_ref[...] = jnp.concatenate([top, total, picked] + [jnp.zeros_like(top)] * 5)
+
+    def body(starts_ref, ids_ref, h_ref, w_ref, logits_ref, stats_ref, held, sems):
+        copies = [
+            pltpu.make_async_copy(feature_block(h_ref, k, block), held.at[k], sems.at[k])
+            for k in range(WIDE)
+        ]
+        for copy in copies:
+            copy.start()
+        for k in range(WIDE):
+            copies[k].wait()
+            part = dot(w_ref[:, k * block : (k + 1) * block], held[k], ((1,), (1,)))
+            logits_ref[...] = part if k == 0 else logits_ref[...] + part
+        logits = logits_ref[...]
+        match = column_of(starts_ref, logits.shape, 0, columns // 2) == ids_ref[...]
+        top = jnp.max(logits, axis=0, keepdims=True)
+        total = jnp.sum(jnp.exp(logits - top), axis=0, keepdims=True)
+        picked = jnp.sum(jnp.where(match, logits, 0.0), axis=0, keepdims=True)
+        stats_ref[...] = jnp.concatenate([top, total, picked] + [jnp.zeros_like(top)] * 5)
 
     return pl.pallas_call(
         body,
-        grid=(WIDE,),
-        in_specs=[SMEM, whole((1, tokens)), spec, pl.BlockSpec((columns, block), lambda k: (0, k))],
-        out_specs=[whole((columns, tokens)), whole((8, tokens))],
+        in_specs=[SMEM, VMEM, ANY if hidden.ndim == 3 else HBM, VMEM],
+        out_specs=[VMEM, VMEM],
         out_shape=[
             jax.ShapeDtypeStruct((columns, tokens), F32),
             jax.ShapeDtypeStruct((8, tokens), F32),
         ],
+        scratch_shapes=[
+            pltpu.VMEM((WIDE, tokens, block), BF16),
+            pltpu.SemaphoreType.DMA((WIDE,)),
+        ],
         compiler_params=PARAMS,
         cost_estimate=cost(
-            2 * columns * tokens * features, 2 * features * (columns + tokens) + 4 * columns * tokens
+            2 * columns * tokens * features, 2 * features * tokens
         ),
     )(starts, ids, hidden, weight_t)
 
@@ -101,101 +105,102 @@
 def partial_product(starts, ids, logits_t, norm, weight_t, by_feature):
     columns, tokens = logits_t.shape
     features = weight_t.shape[1]
-    block = features // 7
-
-    def body(starts_ref, ids_ref, logits_ref, norm_ref, w_ref, out_ref, held):
-        @pl.when(pl.program_id(0) == 0)
-        def _():
-            change = change_of(
-                starts_ref, logits_ref[...], norm_ref[...], ids_ref[...], 0, columns // 2
-            )
-            held[...] = (change if by_feature else change.T).astype(BF16)
-
-        if by_feature:
-            out = dot(w_ref[...], held[...], ((0,), (0,)))
-        else:
-            out = dot(held[...], w_ref[...], ((1,), (0,)))
-        out_ref[...] = out.astype(BF16)
+    steps = 7
+    block = features // steps
+
+    def body(starts_ref, ids_ref, logits_ref, norm_ref, w_ref, out_ref, held, ready, sems):
+        change = change_of(
+            starts_ref, logits_ref[...], norm_ref[...], ids_ref[...], 0, columns // 2
+        )
+        held[...] = (change if by_feature else change.T).astype(BF16)
+
+        def send(k):
+            span = pl.ds(k * block, block)
+            into = out_ref.at[span] if by_feature else out_ref.at[:, span]
+            return pltpu.make_async_copy(ready.at[k % 2], into, sems.at[k % 2])
+
+        for k in range(steps):
+            weights = w_ref[:, k * block : (k + 1) * block]
+            if by_feature:
+                out = dot(weights, held[...], ((0,), (0,)))
+            else:
+                out = dot(held[...], weights, ((1,), (0,)))
+            if k >= 2:
+                send(k - 2).wait()
+            ready[k % 2] = out.astype(BF16)
+            send(k).start()
+        send(steps - 2).wait()
+        send(steps - 1).wait()
 
     if by_feature:
-        out_spec, out_dims = pl.BlockSpec((block, tokens), lambda k: (k, 0)), (features, tokens)
-        held = (columns, tokens)
+        out_dims, out_block, held = (features, tokens), (block, tokens), (columns, tokens)
     else:
-        out_spec, out_dims = pl.BlockSpec((tokens, block), lambda k: (0, k)), (tokens, features)
-        held = (tokens, columns)
+        out_dims, out_block, held = (tokens, features), (tokens, block), (tokens, columns)
     return pl.pallas_call(
         body,
-        grid=(7,),
-        in_specs=[
-            SMEM,
-            whole((1, tokens)),
-            whole((columns, tokens)),
-            whole((1, tokens)),
-            pl.BlockSpec((columns, block), lambda k: (0, k)),
+        in_specs=[SMEM, VMEM, VMEM, VMEM, VMEM],
+        out_specs=ANY,
+        out_shape=jax.ShapeDtypeStruct(out_dims, BF16),
+        scratch_shapes=[
+            pltpu.VMEM(held, BF16),
+            pltpu.VMEM((2,) + out_block, BF16),
+            pltpu.SemaphoreType.DMA((2,)),
         ],
-        out_specs=out_spec,
-        out_shape=jax.ShapeDtypeStruct(out_dims, BF16),
-        scratch_shapes=[pltpu.VMEM(held, BF16)],
         compiler_params=PARAMS,
-        cost_estimate=cost(
-            2 * columns * tokens * features, 2 * features * (columns + tokens) + 4 * columns * tokens
-        ),
+        cost_estimate=cost(2 * columns * tokens * features, 2 * features * tokens),
     )(starts, ids, logits_t, norm, weight_t)
 
 
-def head_half(starts, early, late, low, high, added):
+def head_parts(starts, early, late):
     columns = early[1].shape[0]
-    here = high - low
+    half = columns // 2
     sizes = [early[1].shape[1], late[1].shape[1]]
     features = late[4].shape[1]
     block = features // WIDE
 
     def body(starts_ref, *refs):
         sides = [refs[0:5], refs[5:10]]
-        rest = refs[10:]
-        held = rest[-2:]
-        out_ref = rest[-3]
-
-        @pl.when(pl.program_id(0) == 0)
-        def _():
-            for (ids, logits, norm, scale, _), into in zip(sides, held):
-                change = change_of(
-                    starts_ref, logits[low:high], norm[...], ids[...], low, columns // 2
+        near_ref, far_ref = refs[10:12]
+        held, blocks = refs[12:14], refs[14:16]
+        sems = refs[16]
+        copies = [
+            [
+                pltpu.make_async_copy(
+                    feature_block(side[4], k, block), into.at[k], sems.at[number, k]
                 )
-                into[...] = (change * scale[...]).astype(BF16)
-
-        total = dot(held[0][...], sides[0][4][...], ((1,), (0,)))
-        total += dot(held[1][...], sides[1][4][...], ((1,), (0,)))
-        if added is not None:
-            total += rest[0][...].astype(F32)
-        out_ref[...] = total.astype(BF16)
-
-    specs = [SMEM]
-    for size, spec in zip(
-        sizes,
-        (
-            pl.BlockSpec((None, sizes[0], block), lambda k: (k, 0, 0)),
-            pl.BlockSpec((sizes[1], block), lambda k: (0, k)),
-        ),
-    ):
-        specs += [whole((1, size)), whole((columns, size)), whole((1, size)), whole((1, size)), spec]
-    out_spec = pl.BlockSpec((here, block), lambda k: (0, k))
-    operands = list(early) + list(late)
-    if added is not None:
-        specs.append(out_spec)
-        operands.append(added)
+                for number, (side, into) in enumerate(zip(sides, blocks))
+            ]
+            for k in range(WIDE)
+        ]
+        for pair in copies:
+            for copy in pair:
+                copy.start()
+        for (ids, logits, norm, scale, _), into in zip(sides, held):
+            change = change_of(starts_ref, logits[...], norm[...], ids[...], 0, half)
+            into[...] = (change * scale[...]).astype(BF16)
+        for k in range(WIDE):
+            total = None
+            for copy, grad, hidden in zip(copies[k], held, blocks):
+                copy.wait()
+                part = dot(grad[...], hidden[k], ((1,), (0,)))
+                total = part if total is None else total + part
+            near_ref[:, k * block : (k + 1) * block] = total[:half]
+            far_ref[:, k * block : (k + 1) * block] = total[half:].astype(BF16)
+
     return pl.pallas_call(
         body,
-        grid=(WIDE,),
-        in_specs=specs,
-        out_specs=out_spec,
-        out_shape=jax.ShapeDtypeStruct((here, features), BF16),
-        scratch_shapes=[pltpu.VMEM((here, size), BF16) for size in sizes],
+        in_specs=[SMEM, VMEM, VMEM, VMEM, VMEM, ANY, VMEM, VMEM, VMEM, VMEM, HBM],
+        out_specs=[VMEM, VMEM],
+        out_shape=[
+            jax.ShapeDtypeStruct((half, features), F32),
+            jax.ShapeDtypeStruct((half, features), BF16),
+        ],
+        scratch_shapes=[pltpu.VMEM((columns, size), BF16) for size in sizes]
+        + [pltpu.VMEM((WIDE, size, block), BF16) for size in sizes]
+        + [pltpu.SemaphoreType.DMA((2, WIDE))],
         compiler_params=PARAMS,
-        cost_estimate=cost(
-            2 * here * sum(sizes) * features, 2 * features * (here + sum(sizes)) + 4 * columns * sum(sizes)
-        ),
-    )(starts, *operands)
+        cost_estimate=cost(2 * columns * sum(sizes) * features, 2 * features * sum(sizes)),
+    )(starts, *early, *late)
 
 
 def pack_facts(token_ids, response_mask, teacher_logprob):
@@ -311,10 +316,9 @@
         (ids[0], early_logits, norms[0], weights[0], early),
         (ids[1], late_logits, norms[1], weights[1], late),
     )
-    far = head_half(starts, *sides, columns_here, 2 * columns_here, None)
-    far = lax.ppermute(far, "core", SWAP)
-    head_grad = head_half(starts, *sides, 0, columns_here, far)
-    return hidden_grad.astype(BF16), head_grad.T
+    near, far = head_parts(starts, *sides)
+    head_grad = near + lax.ppermute(far, "core", SWAP).astype(F32)
+    return hidden_grad.astype(BF16), head_grad.astype(BF16).T
 
 
 def solution(mesh):

time: 228 us -> 220 us (0.965)
  local copies, waits for them, and re-layouts: 18.2 us -> 37.3 us
  Pallas kernels: 51.7 us -> 35.1 us
  waiting for transfers between devices: 73.6 us -> 61.4 us
  other arithmetic: 8.28 us -> 13.9 us
  starting transfers between devices: 35.5 us -> 32.3 us
    unnamed x5 -> x31, local copies, waits for them, and re-layouts: 3.42 us -> 26.1 us
    all_to_all x1, waiting for transfers between devices: 27 us -> 8.23 us  [on_device(): lax.all_to_all(partial.reshape(PLANE, cut, first_half), ('x', 'y'), 0, 0,...]
    pallas_call x6 -> x5, Pallas kernels: 51.7 us -> 35.1 us  [the longest x1 11.9 us: head_parts(): pl.pallas_call(body, in_specs=[SMEM, VMEM, VMEM, VMEM, VMEM, ANY, VMEM, V...]
    transpose x0 -> x1, other arithmetic: none -> 4.25 us  [on_device(): return (hidden_grad.astype(BF16), head_grad.astype(BF16).T)]
    all_to_all x1, waiting for transfers between devices: 1.03 us -> 5.15 us  [on_device(): late_sum = lax.all_to_all(late_sum, ('x', 'y'), 0, 0, tiled=True)]
    all_to_all x1, starting transfers between devices: 10.7 us -> 6.61 us  [on_device(): late_sum = lax.all_to_all(late_sum, ('x', 'y'), 0, 0, tiled=True)]
    all_to_all x1, waiting for transfers between devices: 6.54 us -> 3.35 us  [on_device(): lax.all_to_all(early_sum.reshape(Z, EARLY, cut), 'z', 0, 0, tiled=True)]
    reduce_scatter x1, waiting for transfers between devices: 0.02 us -> 3.19 us  [on_device(): late_sum = lax.psum_scatter(partial, 'z', scatter_dimension=0, tiled=True)]
  transfers between devices with their start and end apart: 10 -> 10, of which waited for: 5 -> 7; matrix products, arithmetic and copies ran while one was open for 9% -> 10% of each run, Pallas kernels for 15% -> 10%
where the time goes in v5:
time: 220 us; the launch traced here: 219 us
  waiting for transfers between devices  61.4 us (28%)
  local copies, waits for them, and re-layouts  37.3 us (17%)
  Pallas kernels  35.1 us (16%)
  starting transfers between devices  32.3 us (15%)
  blocking collectives  24.8 us (11%)
  between operations  14.4 us (7%)
  other arithmetic  13.9 us (6%)
    all_to_all x2, waiting for transfers between devices, broadcast_gather(): return lax.all_to_all(copies, axes, 0, 0, tiled=True)  40.6 us
    unnamed x31, local copies, waits for them, and re-layouts  26.1 us
    all_to_all x2, blocking collectives, broadcast_gather(): return lax.all_to_all(copies, axes, 0, 0, tiled=True)  24.8 us
    all_to_all x2, starting transfers between devices, broadcast_gather(): return lax.all_to_all(copies, axes, 0, 0, tiled=True)  16 us
    pallas_call x1, Pallas kernels, head_parts(): pl.pallas_call(body, in_specs=[SMEM, VMEM, VMEM, VMEM, VMEM, ANY, VMEM, V...  11.9 us
    pallas_call x2, Pallas kernels, logits_and_stats(): pl.pallas_call(body, in_specs=[SMEM, VMEM, ANY if hidden.ndim == 3 else H...  11.8 us
    pallas_call x2, Pallas kernels, partial_product(): pl.pallas_call(body, in_specs=[SMEM, VMEM, VMEM, VMEM, VMEM], out_specs=A...  11.4 us
    all_to_all x1, waiting for transfers between devices, on_device(): lax.all_to_all(partial.reshape(PLANE, cut, first_half), ('x', 'y'), 0, 0,...  8.23 us
  transfers between devices with their start and end apart: 10, of which 7 were waited for; matrix products, arithmetic and copies ran while one was open for 10% of the time, Pallas kernels for 10%

profile of v5, /device:TPU:8, one launch (start us, length us, event | category | flops | bytes accessed | tf_op | source)
XLA Modules:
  0.0 219.2 jit_solution(15038896588583436864)
XLA Ops:
  7.2 1.9 slice.100
  9.2 0.9 dynamic_slice.7
  10.1 0.7 fusion.24
  10.7 0.7 fusion.30
  11.5 0.7 broadcast_in_dim.18
  12.2 8.5 %all-to-all-start = ((bf16[8,12,1024]{2,1,0:T(8,128)(2,1)}), bf16[8,12,1024]{2,1,0:T(8,128)(2,1)S(1)}, u32[]{:S(2)}, u32[]{:S(2)}) async-start(bf16[8,12,1024]{2,1,0:T(8,128)(2,1)} %broadcast_in_dim.18), calls=%async_computation | async-start | bytes 524288 | tf_op jit(solution)/shard_map/all_to_all | solution.py:22
  20.7 13.4 %all-to-all-done = bf16[8,12,1024]{2,1,0:T(8,128)(2,1)S(1)} async-done(((bf16[8,12,1024]{2,1,0:T(8,128)(2,1)}), bf16[8,12,1024]{2,1,0:T(8,128)(2,1)S(1)}, u32[]{:S(2)}, u32[]{:S(2)}) %all-to-all-start) | async-done | bytes 196640 | tf_op jit(solution)/shard_map/all_to_all | solution.py:22
  34.2 1.8 broadcast_in_dim.20
  36.0 7.5 %all-to-all-start.1 = ((bf16[16,96,896]{2,1,0:T(8,128)(2,1)}), bf16[16,96,896]{2,1,0:T(8,128)(2,1)S(1)}, u32[]{:S(2)}, u32[]{:S(2)}) async-start(bf16[16,96,896]{2,1,0:T(8,128)(2,1)} %broadcast_in_dim.20), calls=%async_computation.1 | async-start | bytes 5505024 | tf_op jit(solution)/shard_map/all_to_all | solution.py:22
  44.0 4.9 %pad_maximum_fusion.w_ref = bf16[640,3584]{1,0:T(8,128)(2,1)} fusion(bf16[320,3584]{1,0:T(8,128)(2,1)} %collective-permute-done, bf16[320,3584]{1,0:T(8,128)(2,1)} %bitcast.12), kind=kLoop, calls=%fused_computation | loop fusion | flops 9175040 | bytes 9175040 | tf_op jit(solution)/shard_map/concatenate | solution.py:241
  48.9 27.2 %all-to-all-done.1 = bf16[16,96,896]{2,1,0:T(8,128)(2,1)S(1)} async-done(((bf16[16,96,896]{2,1,0:T(8,128)(2,1)}), bf16[16,96,896]{2,1,0:T(8,128)(2,1)S(1)}, u32[]{:S(2)}, u32[]{:S(2)}) %all-to-all-start.1) | async-done | bytes 2752544 | tf_op jit(solution)/shard_map/all_to_all | solution.py:22
  76.1 2.3 %copy-done = bf16[640,3584]{1,0:T(8,128)(2,1)S(1)} copy-done((bf16[640,3584]{1,0:T(8,128)(2,1)S(1)}, bf16[640,3584]{1,0:T(8,128)(2,1)}, u32[]{:S(2)}) %copy-start) | copy-done | bytes 4587544
  78.4 5.1 %shard_map.68 = (f32[640,384]{1,0:T(8,128)S(1)}, f32[8,384]{1,0:T(8,128)S(1)}) custom-call(s32[2]{0:T(128)S(1)} %pad_add_fusion.starts_ref, s32[1,384]{1,0:T(1,128)S(1)} %reshape.176.ids_ref.refs_0_, bf16[4,384,896]{2,1,0:T(8,128)(2,1)S(1)} %bitcast.100, bf16[640,3584]{1,0:T(8,128)(2,1)S(1)} %copy-done), custom_call_target="tpu_custom_call" | custom-call | flops 1761607680 | bytes 2752512 | tf_op jit(solution)/shard_map/pallas_call | solution.py:81
  83.5 0.9 copy-done.6
  84.5 2.3 %copy-done.1 = bf16[640,3584]{1,0:T(8,128)(2,1)S(1)} copy-done((bf16[640,3584]{1,0:T(8,128)(2,1)S(1)}, bf16[640,3584]{1,0:T(8,128)(2,1)}, u32[]{:S(2)}) %copy-start.1) | copy-done | bytes 4587544
  86.8 2.3 %copy-done.9 = bf16[640,3584]{1,0:T(8,128)(2,1)S(1)} copy-done((bf16[640,3584]{1,0:T(8,128)(2,1)S(1)}, bf16[640,3584]{1,0:T(8,128)(2,1)}, u32[]{:S(2)}) %copy-start.9) | copy-done | bytes 4587544
  89.1 6.7 %shard_map.69 = (f32[640,640]{1,0:T(8,128)S(1)}, f32[8,640]{1,0:T(8,128)S(1)}) custom-call(s32[2]{0:T(128)S(1)} %pad_add_fusion.starts_ref, s32[1,640]{1,0:T(1,128)S(1)} %reshape.178.ids_ref.refs_5_, bf16[640,3584]{1,0:T(8,128)(2,1)S(1)} %copy-done.9, bf16[640,3584]{1,0:T(8,128)(2,1)S(1)} %copy-done.1), custom_call_target="tpu_custom_call" | custom-call | flops 2936012800 | bytes 4587520 | tf_op jit(solution)/shard_map/pallas_call | solution.py:81
  95.8 1.2 copy-done.11
  97.0 12.6 %all_to_all.35 = f32[8,24,128]{2,1,0:T(8,128)S(1)} all-to-all(f32[8,24,128]{2,1,0:T(8,128)S(1)} %broadcast_in_dim.22), channel_id=1, replica_groups=mesh['z'=8,'core'=2,'x'=4,'y'=4] {'z'}, dimensions={0} | all-to-all | bytes 196608 | tf_op jit(solution)/shard_map/all_to_all | solution.py:22
  109.7 12.2 %all_to_all.36 = f32[16,24,128]{2,1,0:T(8,128)S(1)} all-to-all(f32[16,24,128]{2,1,0:T(8,128)S(1)} %broadcast_in_dim.24), channel_id=1, replica_groups=mesh['z'=8,'core'=2,'x'=4,'y'=4] {'x','y'}, dimensions={0} | all-to-all | bytes 393216 | tf_op jit(solution)/shard_map/all_to_all | solution.py:22
  122.0 2.3 %copy-done.2 = bf16[640,3584]{1,0:T(8,128)(2,1)S(1)} copy-done((bf16[640,3584]{1,0:T(8,128)(2,1)S(1)}, bf16[640,3584]{1,0:T(8,128)(2,1)}, u32[]{:S(2)}) %copy-start.2) | copy-done | bytes 4587544
  124.2 1.4 copy-done.12
  125.7 6.0 %shard_map.71 = bf16[640,3584]{1,0:T(8,128)(2,1)S(1)} custom-call(s32[2]{0:T(128)S(1)} %pad_add_fusion.starts_ref, s32[1,640]{1,0:T(1,128)S(1)} %reshape.178.ids_ref.refs_5_, f32[640,640]{1,0:T(8,128)S(1)} %copy-done.12, f32[1,640]{1,0:T(1,128)S(1)} %bitcast.104, bf16[640,3584]{1,0:T(8,128)(2,1)S(1)} %copy-done.2), custom_call_target="tpu_custom_call" | custom-call | flops 2936012800 | bytes 4587520 | tf_op jit(solution)/shard_map/pallas_call | solution.py:139
  131.7 2.1 copy-done.4
  134.8 2.3 %copy-done.3 = bf16[640,3584]{1,0:T(8,128)(2,1)S(1)} copy-done((bf16[640,3584]{1,0:T(8,128)(2,1)S(1)}, bf16[640,3584]{1,0:T(8,128)(2,1)}, u32[]{:S(2)}) %copy-start.3) | copy-done | bytes 4587544
  137.1 1.2 copy-done.7
  138.3 5.4 %shard_map.70 = bf16[3584,384]{1,0:T(8,128)(2,1)} custom-call(s32[2]{0:T(128)S(1)} %pad_add_fusion.starts_ref, s32[1,384]{1,0:T(1,128)S(1)} %reshape.176.ids_ref.refs_0_, f32[640,384]{1,0:T(8,128)S(1)} %copy-done.7, f32[1,384]{1,0:T(1,128)S(1)} %bitcast.102, bf16[640,3584]{1,0:T(8,128)(2,1)S(1)} %copy-done.3), custom_call_target="tpu_custom_call" | custom-call | flops 1761607680 | bytes 2752512 | tf_op jit(solution)/shard_map/pallas_call | solution.py:139
  143.7 5.7 %all-to-all-start.4 = ((bf16[16,224,384]{2,1,0:T(8,128)(2,1)}), bf16[16,224,384]{2,1,0:T(8,128)(2,1)}, u32[]{:S(2)}, u32[]{:S(2)}) async-start(bf16[16,224,384]{2,1,0:T(8,128)(2,1)} %bitcast.23), calls=%async_computation.4 | async-start | bytes 5505024 | tf_op jit(solution)/shard_map/all_to_all | solution.py:287
  149.7 0.3 collective-permute-start.1
  150.3 0.8 collective-permute-done.1
  151.6 1.2 copy-done.8
  152.9 2.3 %copy-done.10 = bf16[640,3584]{1,0:T(8,128)(2,1)S(1)} copy-done((bf16[640,3584]{1,0:T(8,128)(2,1)S(1)}, bf16[640,3584]{1,0:T(8,128)(2,1)}, u32[]{:S(2)}) %copy-start.10) | copy-done | bytes 4587544
  155.2 1.4 copy-done.13
  156.6 11.9 %shard_map.72 = (f32[320,3584]{1,0:T(8,128)S(1)}, bf16[320,3584]{1,0:T(8,128)(2,1)}) custom-call(s32[2]{0:T(128)S(1)} %pad_add_fusion.starts_ref, s32[1,384]{1,0:T(1,128)S(1)} %reshape.176.ids_ref.refs_0_, f32[640,384]{1,0:T(8,128)S(1)} %copy-done.8, f32[1,384]{1,0:T(1,128)S(1)} %bitcast.103, f32[1,384]{1,0:T(1,128)S(1)} %reshape.192.refs_3_, ...), custom_call_target="tpu_custom_call" | custom-call | flops 4697620480 | bytes 7340032 | tf_op jit(solution)/shard_map/pallas_call | solution.py:190
  168.5 2.0 copy-done.5
  170.6 0.2 collective-permute-start.2
  170.8 8.2 %all-to-all-done.4 = bf16[16,224,384]{2,1,0:T(8,128)(2,1)} async-done(((bf16[16,224,384]{2,1,0:T(8,128)(2,1)}), bf16[16,224,384]{2,1,0:T(8,128)(2,1)}, u32[]{:S(2)}, u32[]{:S(2)}) %all-to-all-start.4) | async-done | bytes 2752544 | tf_op jit(solution)/shard_map/all_to_all | solution.py:287
  179.0 2.2 %reduce_sum.96 = bf16[224,384]{1,0:T(8,128)(2,1)S(1)} reduce(bf16[16,224,384]{2,1,0:T(8,128)(2,1)} %all-to-all-done.4, bf16[]{:T(256)} %constant.114.clone.1), dimensions={0}, to_apply=%region_5.6 | reduce | flops 1290240 | bytes 2924546 | tf_op jit(solution)/shard_map/reduce_sum | solution.py:290
  181.5 0.7 copy.51
  182.3 3.4 %all-to-all-start.5 = ((bf16[8,48,224]{2,1,0:T(8,128)(2,1)}), bf16[8,48,224]{2,1,0:T(8,128)(2,1)S(1)}, u32[]{:S(2)}, u32[]{:S(2)}) async-start(bf16[8,48,224]{2,1,0:T(8,128)(2,1)} %copy.51), calls=%async_computation.5 | async-start | bytes 393216 | tf_op jit(solution)/shard_map/all_to_all | solution.py:292
  185.7 3.2 %reduce-scatter.2.cloned.1.call-done = bf16[80,3584]{1,0:T(8,128)(2,1)} async-done(((bf16[640,3584]{1,0:T(8,128)(2,1)}), bf16[80,3584]{1,0:T(8,128)(2,1)}) %reduce-scatter.2.cloned.1.call-update) | async-done | bytes 573456 | tf_op jit(solution)/shard_map/reduce_scatter | solution.py:284
  188.9 2.1 reshape.184
  191.0 1.0 copy.74
  192.0 3.3 %all-to-all-done.5 = bf16[8,48,224]{2,1,0:T(8,128)(2,1)S(1)} async-done(((bf16[8,48,224]{2,1,0:T(8,128)(2,1)}), bf16[8,48,224]{2,1,0:T(8,128)(2,1)S(1)}, u32[]{:S(2)}, u32[]{:S(2)}) %all-to-all-start.5) | async-done | bytes 172064 | tf_op jit(solution)/shard_map/all_to_all | solution.py:292
  195.3 6.6 %all-to-all-start.6 = ((bf16[16,80,224]{2,1,0:T(8,128)(2,1)}), bf16[16,80,224]{2,1,0:T(8,128)(2,1)S(1)}, u32[]{:S(2)}, u32[]{:S(2)}) async-start(bf16[16,80,224]{2,1,0:T(8,128)(2,1)} %bitcast.93), calls=%async_computation.7 | async-start | bytes 1310720 | tf_op jit(solution)/shard_map/all_to_all | solution.py:295
  202.0 4.2 %fusion = bf16[3584,320]{0,1:T(8,128)(2,1)} fusion(f32[320,3584]{1,0:T(8,128)} %copy-done.5, bf16[320,3584]{1,0:T(8,128)(2,1)S(1)} %collective-permute-done.2), kind=kLoop, calls=%fused_computation.2 | loop fusion | flops 3440640 | bytes 9175040 | tf_op jit(solution)/shard_map/transpose | solution.py:321
  206.3 5.1 %all-to-all-done.6 = bf16[16,80,224]{2,1,0:T(8,128)(2,1)S(1)} async-done(((bf16[16,80,224]{2,1,0:T(8,128)(2,1)}), bf16[16,80,224]{2,1,0:T(8,128)(2,1)S(1)}, u32[]{:S(2)}, u32[]{:S(2)}) %all-to-all-start.6) | async-done | bytes 573472 | tf_op jit(solution)/shard_map/all_to_all | solution.py:295
  211.6 0.7 copy.60
  (86 shorter events, 3.3 us)
Async XLA Ops:
  7.2 77.3 %all-gather.2.cloned.1.call-start = ((), (), s32[]{:S(2)}) async-start(), calls=%async_computation.8 | async-start | bytes 5160960 | tf_op jit(solution)/shard_map/all_gather | solution.py:243
  12.2 21.9 %all-to-all-start = ((bf16[8,12,1024]{2,1,0:T(8,128)(2,1)}), bf16[8,12,1024]{2,1,0:T(8,128)(2,1)S(1)}, u32[]{:S(2)}, u32[]{:S(2)}) async-start(bf16[8,12,1024]{2,1,0:T(8,128)(2,1)} %broadcast_in_dim.18), calls=%async_computation | async-start | bytes 524288 | tf_op jit(solution)/shard_map/all_to_all | solution.py:22
  20.7 23.3 %collective-permute-start = (bf16[320,3584]{1,0:T(8,128)(2,1)}, bf16[320,3584]{1,0:T(8,128)(2,1)}, u32[]{:S(2)}, u32[]{:S(2)}) collective-permute-start(bf16[320,3584]{1,0:T(8,128)(2,1)} %bitcast.12), channel_id=1, source_target_pairs={{0,16},{16,0},{1,17},{17,1},{2,18},{18,2},{3,19},{19,3},{4,20},{20... | collective-permute-start | bytes 6881288 | tf_op jit(solution)/shard_map/ppermute | solution.py:241
  36.0 40.1 %all-to-all-start.1 = ((bf16[16,96,896]{2,1,0:T(8,128)(2,1)}), bf16[16,96,896]{2,1,0:T(8,128)(2,1)S(1)}, u32[]{:S(2)}, u32[]{:S(2)}) async-start(bf16[16,96,896]{2,1,0:T(8,128)(2,1)} %broadcast_in_dim.20), calls=%async_computation.1 | async-start | bytes 5505024 | tf_op jit(solution)/shard_map/all_to_all | solution.py:22
  43.5 145.4 %reduce-scatter.2.cloned.1.call-start = ((), (), s32[]{:S(2)}) async-start(), calls=%async_computation.9 | async-start | bytes 5160960 | tf_op jit(solution)/shard_map/reduce_scatter | solution.py:284
  76.1 2.3 %copy-start = (bf16[640,3584]{1,0:T(8,128)(2,1)S(1)}, bf16[640,3584]{1,0:T(8,128)(2,1)}, u32[]{:S(2)}) copy-start(bf16[640,3584]{1,0:T(8,128)(2,1)} %pad_maximum_fusion.w_ref) | copy-start | bytes 13762564
  83.5 1.0 copy-start.6
  84.5 2.3 %copy-start.1 = (bf16[640,3584]{1,0:T(8,128)(2,1)S(1)}, bf16[640,3584]{1,0:T(8,128)(2,1)}, u32[]{:S(2)}) copy-start(bf16[640,3584]{1,0:T(8,128)(2,1)} %pad_maximum_fusion.w_ref) | copy-start | bytes 13762564
  86.8 2.3 %copy-start.9 = (bf16[640,3584]{1,0:T(8,128)(2,1)S(1)}, bf16[640,3584]{1,0:T(8,128)(2,1)}, u32[]{:S(2)}) copy-start(bf16[640,3584]{1,0:T(8,128)(2,1)} %all-gather.2.cloned.1.call-done.h_ref.refs_9_) | copy-start | bytes 13762564
  95.8 1.2 copy-start.11
  121.9 2.3 %copy-start.2 = (bf16[640,3584]{1,0:T(8,128)(2,1)S(1)}, bf16[640,3584]{1,0:T(8,128)(2,1)}, u32[]{:S(2)}) copy-start(bf16[640,3584]{1,0:T(8,128)(2,1)} %pad_maximum_fusion.w_ref) | copy-start | bytes 13762564
  124.2 1.4 copy-start.12
  131.7 2.1 copy-start.4
  134.8 2.3 %copy-start.3 = (bf16[640,3584]{1,0:T(8,128)(2,1)S(1)}, bf16[640,3584]{1,0:T(8,128)(2,1)}, u32[]{:S(2)}) copy-start(bf16[640,3584]{1,0:T(8,128)(2,1)} %pad_maximum_fusion.w_ref) | copy-start | bytes 13762564
  137.1 1.2 copy-start.7
  143.7 35.3 %all-to-all-start.4 = ((bf16[16,224,384]{2,1,0:T(8,128)(2,1)}), bf16[16,224,384]{2,1,0:T(8,128)(2,1)}, u32[]{:S(2)}, u32[]{:S(2)}) async-start(bf16[16,224,384]{2,1,0:T(8,128)(2,1)} %bitcast.23), calls=%async_computation.4 | async-start | bytes 5505024 | tf_op jit(solution)/shard_map/all_to_all | solution.py:287
  149.7 1.4 collective-permute-start.1
  151.6 1.2 copy-start.8
  152.9 2.3 %copy-start.10 = (bf16[640,3584]{1,0:T(8,128)(2,1)S(1)}, bf16[640,3584]{1,0:T(8,128)(2,1)}, u32[]{:S(2)}) copy-start(bf16[640,3584]{1,0:T(8,128)(2,1)} %all-gather.2.cloned.1.call-done.h_ref.refs_9_) | copy-start | bytes 13762564
  155.2 1.4 copy-start.13
  168.5 2.1 copy-start.5
  170.6 31.4 %collective-permute-start.2 = (bf16[320,3584]{1,0:T(8,128)(2,1)}, bf16[320,3584]{1,0:T(8,128)(2,1)S(1)}, u32[]{:S(2)}, u32[]{:S(2)}) collective-permute-start(bf16[320,3584]{1,0:T(8,128)(2,1)} %get-tuple-element.13), channel_id=1, source_target_pairs={{0,16},{16,0},{1,17},{17,1},{2,18},{18,2},{3,19},{19,3},{4,20},{20... | collective-permute-start | bytes 6881288 | tf_op jit(solution)/shard_map/ppermute | solution.py:320
  182.3 13.1 %all-to-all-start.5 = ((bf16[8,48,224]{2,1,0:T(8,128)(2,1)}), bf16[8,48,224]{2,1,0:T(8,128)(2,1)S(1)}, u32[]{:S(2)}, u32[]{:S(2)}) async-start(bf16[8,48,224]{2,1,0:T(8,128)(2,1)} %copy.51), calls=%async_computation.5 | async-start | bytes 393216 | tf_op jit(solution)/shard_map/all_to_all | solution.py:292
  195.3 16.0 %all-to-all-start.6 = ((bf16[16,80,224]{2,1,0:T(8,128)(2,1)}), bf16[16,80,224]{2,1,0:T(8,128)(2,1)S(1)}, u32[]{:S(2)}, u32[]{:S(2)}) async-start(bf16[16,80,224]{2,1,0:T(8,128)(2,1)} %bitcast.93), calls=%async_computation.7 | async-start | bytes 1310720 | tf_op jit(solution)/shard_map/all_to_all | solution.py:295
Sparse Core Ops, SparseCore 0:
  10.4 63.0 all-gather.1
  134.0 54.8 reduce-scatter.1

commit v6 on v5

--- a/solution.py
+++ b/solution.py
@@ -13,7 +13,7 @@
 WIDE, GROUPS = 4, 4
 EARLY = 48
 LANES = 128
-LIMIT = 28
+LIMIT = 56
 PARAMS = pltpu.CompilerParams(vmem_limit_bytes=LIMIT << 20)
 
 
@@ -41,7 +41,6 @@
 
 VMEM = pl.BlockSpec(memory_space=pltpu.VMEM)
 ANY = pl.BlockSpec(memory_space=pl.ANY)
-HBM = pl.BlockSpec(memory_space=pltpu.HBM)
 
 
 def column_of(starts_ref, shape, low, half):
@@ -49,52 +48,78 @@
     return row + jnp.where(row < half, starts_ref[0], starts_ref[1] - half)
 
 
-def feature_block(hidden_ref, k, block):
-    if len(hidden_ref.shape) == 3:
-        return hidden_ref.at[k]
-    return hidden_ref.at[:, pl.ds(k * block, block)]
-
-
-def logits_and_stats(starts, ids, hidden, weight_t):
+def logits_and_stats(starts, ids, early, late, weight_t):
     columns, features = weight_t.shape
-    tokens = hidden.shape[-2]
+    sizes = early.shape[1], late.shape[0]
+    tokens = sum(sizes)
+    spans = (0, sizes[0]), (sizes[0], tokens)
     block = features // WIDE
 
-    def body(starts_ref, ids_ref, h_ref, w_ref, logits_ref, stats_ref, held, sems):
+    def body(starts_ref, ids_ref, e_ref, l_ref, w_ref, logits_ref, stats_ref, w, e, l, held, sems, out):
+        def span(k):
+            return pl.ds(k * block, block)
+
         copies = [
-            pltpu.make_async_copy(feature_block(h_ref, k, block), held.at[k], sems.at[k])
+            (
+                pltpu.make_async_copy(w_ref.at[:, span(k)], w.at[k], sems.at[k, 0]),
+                pltpu.make_async_copy(e_ref.at[k], e.at[k], sems.at[k, 1]),
+                pltpu.make_async_copy(l_ref.at[:, span(k)], l.at[k], sems.at[k, 2]),
+            )
             for k in range(WIDE)
         ]
-        for copy in copies:
+        for copy in copies[0] + copies[1]:
             copy.start()
+        sends = []
         for k in range(WIDE):
-            copies[k].wait()
-            part = dot(w_ref[:, k * block : (k + 1) * block], held[k], ((1,), (1,)))
-            logits_ref[...] = part if k == 0 else logits_ref[...] + part
-        logits = logits_ref[...]
-        match = column_of(starts_ref, logits.shape, 0, columns // 2) == ids_ref[...]
-        top = jnp.max(logits, axis=0, keepdims=True)
-        total = jnp.sum(jnp.exp(logits - top), axis=0, keepdims=True)
-        picked = jnp.sum(jnp.where(match, logits, 0.0), axis=0, keepdims=True)
-        stats_ref[...] = jnp.concatenate([top, total, picked] + [jnp.zeros_like(top)] * 5)
+            for copy in copies[k]:
+                copy.wait()
+            if k + 2 < WIDE:
+                for copy in copies[k + 2]:
+                    copy.start()
+            for side, (hidden, (low, high)) in enumerate(zip((e, l), spans)):
+                part = dot(w[k], hidden[k], ((1,), (1,)))
+                held[:, low:high] = part if k == 0 else held[:, low:high] + part
+                if k == WIDE - 1:
+                    send = pltpu.make_async_copy(
+                        held.at[:, pl.ds(low, high - low)],
+                        logits_ref.at[:, pl.ds(low, high - low)],
+                        out.at[side],
+                    )
+                    send.start()
+                    sends.append(send)
+        for low, high in spans:
+            logits = held[:, low:high]
+            match = column_of(starts_ref, logits.shape, 0, columns // 2) == ids_ref[:, low:high]
+            top = jnp.max(logits, axis=0, keepdims=True)
+            total = jnp.sum(jnp.exp(logits - top), axis=0, keepdims=True)
+            picked = jnp.sum(jnp.where(match, logits, 0.0), axis=0, keepdims=True)
+            stats_ref[:, low:high] = jnp.concatenate(
+                [top, total, picked] + [jnp.zeros_like(top)] * 5
+            )
+        for send in sends:
+            send.wait()
 
     return pl.pallas_call(
         body,
-        in_specs=[SMEM, VMEM, ANY if hidden.ndim == 3 else HBM, VMEM],
-        out_specs=[VMEM, VMEM],
+        in_specs=[SMEM, VMEM, ANY, ANY, ANY],
+        out_specs=[ANY, VMEM],
         out_shape=[
             jax.ShapeDtypeStruct((columns, tokens), F32),
             jax.ShapeDtypeStruct((8, tokens), F32),
         ],
         scratch_shapes=[
-            pltpu.VMEM((WIDE, tokens, block), BF16),
-            pltpu.SemaphoreType.DMA((WIDE,)),
+            pltpu.VMEM((WIDE, columns, block), BF16),
+            pltpu.VMEM((WIDE, sizes[0], block), BF16),
+            pltpu.VMEM((WIDE, sizes[1], block), BF16),
+            pltpu.VMEM((columns, tokens), F32),
+            pltpu.SemaphoreType.DMA((WIDE, 3)),
+            pltpu.SemaphoreType.DMA((2,)),
         ],
         compiler_params=PARAMS,
         cost_estimate=cost(
-            2 * columns * tokens * features, 2 * features * tokens
+            2 * columns * tokens * features, 2 * features * (columns + tokens) + 4 * columns * tokens
         ),
-    )(starts, ids, hidden, weight_t)
+    )(starts, ids, early, late, weight_t)
 
 
 def change_of(starts_ref, logits, norm, ids, low, half):
@@ -102,15 +127,27 @@
     return jnp.where(match, 1.0, 0.0) - jnp.exp(logits - norm)
 
 
-def partial_product(starts, ids, logits_t, norm, weight_t, by_feature):
-    columns, tokens = logits_t.shape
+def partial_product(starts, ids, logits_t, norm, weight_t, low, high, by_feature):
+    columns = logits_t.shape[0]
+    tokens = high - low
     features = weight_t.shape[1]
     steps = 7
     block = features // steps
 
-    def body(starts_ref, ids_ref, logits_ref, norm_ref, w_ref, out_ref, held, ready, sems):
+    def body(starts_ref, ids_ref, logits_ref, norm_ref, w_ref, out_ref, logits, w, held, ready, w_sems, sems):
+        fetch = pltpu.make_async_copy(
+            logits_ref.at[:, pl.ds(low, tokens)], logits, w_sems.at[steps]
+        )
+        fetch.start()
+        loads = [
+            pltpu.make_async_copy(w_ref.at[:, pl.ds(k * block, block)], w.at[k], w_sems.at[k])
+            for k in range(steps)
+        ]
+        for load in loads:
+            load.start()
+        fetch.wait()
         change = change_of(
-            starts_ref, logits_ref[...], norm_ref[...], ids_ref[...], 0, columns // 2
+            starts_ref, logits[...], norm_ref[:, low:high], ids_ref[:, low:high], 0, columns // 2
         )
         held[...] = (change if by_feature else change.T).astype(BF16)
 
@@ -120,11 +157,11 @@
             return pltpu.make_async_copy(ready.at[k % 2], into, sems.at[k % 2])
 
         for k in range(steps):
-            weights = w_ref[:, k * block : (k + 1) * block]
+            loads[k].wait()
             if by_feature:
-                out = dot(weights, held[...], ((0,), (0,)))
+                out = dot(w[k], held[...], ((0,), (0,)))
             else:
-                out = dot(held[...], weights, ((1,), (0,)))
+                out = dot(held[...], w[k], ((1,), (0,)))
             if k >= 2:
                 send(k - 2).wait()
             ready[k % 2] = out.astype(BF16)
@@ -138,69 +175,102 @@
         out_dims, out_block, held = (tokens, features), (tokens, block), (tokens, columns)
     return pl.pallas_call(
         body,
-        in_specs=[SMEM, VMEM, VMEM, VMEM, VMEM],
+        in_specs=[SMEM, VMEM, ANY, VMEM, ANY],
         out_specs=ANY,
         out_shape=jax.ShapeDtypeStruct(out_dims, BF16),
         scratch_shapes=[
+            pltpu.VMEM((columns, tokens), F32),
+            pltpu.VMEM((steps, columns, block), BF16),
             pltpu.VMEM(held, BF16),
             pltpu.VMEM((2,) + out_block, BF16),
+            pltpu.SemaphoreType.DMA((steps + 1,)),
             pltpu.SemaphoreType.DMA((2,)),
         ],
         compiler_params=PARAMS,
-        cost_estimate=cost(2 * columns * tokens * features, 2 * features * tokens),
+        cost_estimate=cost(
+            2 * columns * tokens * features, 2 * features * (columns + tokens) + 4 * columns * tokens
+        ),
     )(starts, ids, logits_t, norm, weight_t)
 
 
-def head_parts(starts, early, late):
-    columns = early[1].shape[0]
+def head_parts(starts, ids, logits_t, norm, scale, early, late):
+    columns, tokens = logits_t.shape
     half = columns // 2
-    sizes = [early[1].shape[1], late[1].shape[1]]
-    features = late[4].shape[1]
+    sizes = early.shape[1], late.shape[0]
+    spans = (0, sizes[0]), (sizes[0], tokens)
+    features = late.shape[1]
     block = features // WIDE
 
-    def body(starts_ref, *refs):
-        sides = [refs[0:5], refs[5:10]]
-        near_ref, far_ref = refs[10:12]
-        held, blocks = refs[12:14], refs[14:16]
-        sems = refs[16]
+    def body(starts_ref, ids_ref, logits_ref, norm_ref, scale_ref, e_ref, l_ref, near_ref, far_ref,
+             logits, e, l, held, near, far, sems, out):
+        fetch = pltpu.make_async_copy(logits_ref, logits, sems.at[WIDE, 0])
+        fetch.start()
         copies = [
-            [
+            (
+                pltpu.make_async_copy(e_ref.at[k], e.at[k], sems.at[k, 0]),
                 pltpu.make_async_copy(
-                    feature_block(side[4], k, block), into.at[k], sems.at[number, k]
-                )
-                for number, (side, into) in enumerate(zip(sides, blocks))
-            ]
+                    l_ref.at[:, pl.ds(k * block, block)], l.at[k], sems.at[k, 1]
+                ),
+            )
             for k in range(WIDE)
         ]
         for pair in copies:
             for copy in pair:
                 copy.start()
-        for (ids, logits, norm, scale, _), into in zip(sides, held):
-            change = change_of(starts_ref, logits[...], norm[...], ids[...], 0, half)
-            into[...] = (change * scale[...]).astype(BF16)
+        fetch.wait()
+        for low, high in spans:
+            change = change_of(
+                starts_ref, logits[:, low:high], norm_ref[:, low:high], ids_ref[:, low:high], 0, half
+            )
+            held[:, low:high] = (change * scale_ref[:, low:high]).astype(BF16)
+
+        def sends(k):
+            span = pl.ds(k * block, block)
+            return (
+                pltpu.make_async_copy(far.at[k % 2], far_ref.at[:, span], out.at[k % 2, 0]),
+                pltpu.make_async_copy(near.at[k % 2], near_ref.at[:, span], out.at[k % 2, 1]),
+            )
+
         for k in range(WIDE):
             total = None
-            for copy, grad, hidden in zip(copies[k], held, blocks):
+            for copy, (low, high), hidden in zip(copies[k], spans, (e, l)):
                 copy.wait()
-                part = dot(grad[...], hidden[k], ((1,), (0,)))
+                part = dot(held[:, low:high], hidden[k], ((1,), (0,)))
                 total = part if total is None else total + part
-            near_ref[:, k * block : (k + 1) * block] = total[:half]
-            far_ref[:, k * block : (k + 1) * block] = total[half:].astype(BF16)
+            if k >= 2:
+                for send in sends(k - 2):
+                    send.wait()
+            near[k % 2] = total[:half]
+            far[k % 2] = total[half:].astype(BF16)
+            for send in sends(k):
+                send.start()
+        for k in (WIDE - 2, WIDE - 1):
+            for send in sends(k):
+                send.wait()
 
     return pl.pallas_call(
         body,
-        in_specs=[SMEM, VMEM, VMEM, VMEM, VMEM, ANY, VMEM, VMEM, VMEM, VMEM, HBM],
-        out_specs=[VMEM, VMEM],
+        in_specs=[SMEM, VMEM, ANY, VMEM, VMEM, ANY, ANY],
+        out_specs=[ANY, ANY],
         out_shape=[
             jax.ShapeDtypeStruct((half, features), F32),
             jax.ShapeDtypeStruct((half, features), BF16),
         ],
-        scratch_shapes=[pltpu.VMEM((columns, size), BF16) for size in sizes]
-        + [pltpu.VMEM((WIDE, size, block), BF16) for size in sizes]
-        + [pltpu.SemaphoreType.DMA((2, WIDE))],
+        scratch_shapes=[
+            pltpu.VMEM((columns, tokens), F32),
+            pltpu.VMEM((WIDE, sizes[0], block), BF16),
+            pltpu.VMEM((WIDE, sizes[1], block), BF16),
+            pltpu.VMEM((columns, tokens), BF16),
+            pltpu.VMEM((2, half, block), F32),
+            pltpu.VMEM((2, half, block), BF16),
+            pltpu.SemaphoreType.DMA((WIDE + 1, 2)),
+            pltpu.SemaphoreType.DMA((2, 2)),
+        ],
         compiler_params=PARAMS,
-        cost_estimate=cost(2 * columns * sum(sizes) * features, 2 * features * sum(sizes)),
-    )(starts, *early, *late)
+        cost_estimate=cost(
+            2 * columns * tokens * features, 2 * features * (columns + tokens) + 4 * columns * tokens
+        ),
+    )(starts, ids, logits_t, norm, scale, early, late)
 
 
 def pack_facts(token_ids, response_mask, teacher_logprob):
@@ -253,7 +323,8 @@
 
     def local_order(values):
         first = values[:, :EARLY].reshape(Z, GROUPS, group).transpose(1, 0, 2)
-        return first.reshape(1, first_half), values[:, EARLY:].reshape(1, second_half)
+        second = values[:, EARLY:].reshape(second_half)
+        return jnp.concatenate([first.reshape(first_half), second])[None]
 
     def whole_order(values):
         first = values[:first_half].reshape(GROUPS, Z, group).transpose(1, 0, 2)
@@ -265,9 +336,8 @@
         [((z * CORES + c) * PLANE + place) * columns_here for c in (core, 1 - core)]
     ).astype(jnp.int32)
 
-    early_logits, early_stats = logits_and_stats(starts, ids[0], early, both_t)
-    late_logits, late_stats = logits_and_stats(starts, ids[1], late, both_t)
-    stats = jnp.concatenate([early_stats[:3], late_stats[:3]], axis=1)
+    logits, stats = logits_and_stats(starts, ids, early, late, both_t)
+    stats = stats[:3]
     stats = stats.reshape(3 * all_rows // LANES, LANES)
 
     def merged(stats, axes, count):
@@ -278,12 +348,14 @@
     stats = merged(stats, "z", Z)
     stats = merged(stats, ("x", "y"), PLANE).reshape(3, all_rows)
     norm = stats[0] + jnp.log(stats[1])
-    norms = norm[None, :first_half], norm[None, first_half:]
-
-    partial = partial_product(starts, ids[1], late_logits, norms[1], both_t, False)
+    norm_row = norm[None]
+
+    partial = partial_product(
+        starts, ids, logits, norm_row, both_t, first_half, all_rows, False
+    )
     late_sum = lax.psum_scatter(partial, "z", scatter_dimension=0, tiled=True)
     cut = features // PLANE
-    partial = partial_product(starts, ids[0], early_logits, norms[0], both_t, True)
+    partial = partial_product(starts, ids, logits, norm_row, both_t, 0, first_half, True)
     shared = lax.all_to_all(
         partial.reshape(PLANE, cut, first_half), ("x", "y"), 0, 0, tiled=True
     )
@@ -311,12 +383,7 @@
     own_weight = lax.dynamic_index_in_dim(weights, z, 0, False)
     hidden_grad = jnp.concatenate([early_sum, late_sum]) * own_weight[:, None]
 
-    weights = local_order(weights)
-    sides = (
-        (ids[0], early_logits, norms[0], weights[0], early),
-        (ids[1], late_logits, norms[1], weights[1], late),
-    )
-    near, far = head_parts(starts, *sides)
+    near, far = head_parts(starts, ids, logits, norm_row, local_order(weights), early, late)
     head_grad = near + lax.ppermute(far, "core", SWAP).astype(F32)
     return hidden_grad.astype(BF16), head_grad.astype(BF16).T
 

time: 220 us -> 211 us (0.959)
  local copies, waits for them, and re-layouts: 37.3 us -> 14.7 us
  Pallas kernels: 35.1 us -> 41.3 us
  waiting for transfers between devices: 61.4 us -> 67.3 us
    unnamed x31 -> x5, local copies, waits for them, and re-layouts: 26.1 us -> 2.87 us
    all_to_all x1, waiting for transfers between devices: 8.23 us -> 15.9 us  [on_device(): lax.all_to_all(partial.reshape(PLANE, cut, first_half), ('x', 'y'), 0, 0,...]
    pallas_call x5 -> x4, Pallas kernels: 35.1 us -> 41.3 us  [the longest x2 16 us: partial_product(): pl.pallas_call(body, in_specs=[SMEM, VMEM, ANY, VMEM, ANY], out_specs=ANY...]
  transfers between devices with their start and end apart: 10 -> 10, of which waited for: 7 -> 7; matrix products, arithmetic and copies ran while one was open for 10% -> 11% of each run, Pallas kernels for 10% -> 10%
where the time goes in v6:
time: 211 us; the launch traced here: 210 us
  waiting for transfers between devices  67.3 us (32%)
  Pallas kernels  41.3 us (20%)
  starting transfers between devices  32.6 us (15%)
  blocking collectives  24.8 us (12%)
  other arithmetic  15.1 us (7%)
  local copies, waits for them, and re-layouts  14.7 us (7%)
  between operations  14.3 us (7%)
    all_to_all x2, waiting for transfers between devices, broadcast_gather(): return lax.all_to_all(copies, axes, 0, 0, tiled=True)  39.6 us
    all_to_all x2, blocking collectives, broadcast_gather(): return lax.all_to_all(copies, axes, 0, 0, tiled=True)  24.8 us
    pallas_call x2, Pallas kernels, partial_product(): pl.pallas_call(body, in_specs=[SMEM, VMEM, ANY, VMEM, ANY], out_specs=ANY...  16 us
    all_to_all x2, starting transfers between devices, broadcast_gather(): return lax.all_to_all(copies, axes, 0, 0, tiled=True)  16 us
    all_to_all x1, waiting for transfers between devices, on_device(): lax.all_to_all(partial.reshape(PLANE, cut, first_half), ('x', 'y'), 0, 0,...  15.9 us
    pallas_call x1, Pallas kernels, head_parts(): pl.pallas_call(body, in_specs=[SMEM, VMEM, ANY, VMEM, VMEM, ANY, ANY], ou...  12.8 us
    pallas_call x1, Pallas kernels, logits_and_stats(): pl.pallas_call(body, in_specs=[SMEM, VMEM, ANY, ANY, ANY], out_specs=[ANY...  12.5 us
    all_to_all x1, starting transfers between devices, on_device(): late_sum = lax.all_to_all(late_sum, ('x', 'y'), 0, 0, tiled=True)  7.4 us
  transfers between devices with their start and end apart: 10, of which 7 were waited for; matrix products, arithmetic and copies ran while one was open for 11% of the time, Pallas kernels for 10%

profile of v6, /device:TPU:8, one launch (start us, length us, event | category | flops | bytes accessed | tf_op | source)
XLA Modules:
  0.0 210.1 jit_solution(353833205140603880)
XLA Ops:
  7.2 1.9 slice.94
  9.2 0.9 dynamic_slice.7
  10.1 0.7 fusion.24
  10.7 0.7 fusion.30
  11.5 0.7 broadcast_in_dim.18
  12.2 8.5 %all-to-all-start = ((bf16[8,12,1024]{2,1,0:T(8,128)(2,1)}), bf16[8,12,1024]{2,1,0:T(8,128)(2,1)S(1)}, u32[]{:S(2)}, u32[]{:S(2)}) async-start(bf16[8,12,1024]{2,1,0:T(8,128)(2,1)} %broadcast_in_dim.18), calls=%async_computation | async-start | bytes 524288 | tf_op jit(solution)/shard_map/all_to_all | solution.py:22
  20.7 13.4 %all-to-all-done = bf16[8,12,1024]{2,1,0:T(8,128)(2,1)S(1)} async-done(((bf16[8,12,1024]{2,1,0:T(8,128)(2,1)}), bf16[8,12,1024]{2,1,0:T(8,128)(2,1)S(1)}, u32[]{:S(2)}, u32[]{:S(2)}) %all-to-all-start) | async-done | bytes 196640 | tf_op jit(solution)/shard_map/all_to_all | solution.py:22
  34.2 1.8 broadcast_in_dim.21
  36.0 7.5 %all-to-all-start.1 = ((bf16[16,96,896]{2,1,0:T(8,128)(2,1)}), bf16[16,96,896]{2,1,0:T(8,128)(2,1)S(1)}, u32[]{:S(2)}, u32[]{:S(2)}) async-start(bf16[16,96,896]{2,1,0:T(8,128)(2,1)} %broadcast_in_dim.21), calls=%async_computation.1 | async-start | bytes 5505024 | tf_op jit(solution)/shard_map/all_to_all | solution.py:22
  43.5 0.6 pad_add_fusion.1.starts_ref
  44.4 0.1 reshape.198
  44.5 0.6 pad_add_fusion
  45.1 4.9 %pad_maximum_fusion.w_ref = bf16[640,3584]{1,0:T(8,128)(2,1)} fusion(bf16[320,3584]{1,0:T(8,128)(2,1)} %collective-permute-done, bf16[320,3584]{1,0:T(8,128)(2,1)} %bitcast.13), kind=kLoop, calls=%fused_computation | loop fusion | flops 9175040 | bytes 9175040 | tf_op jit(solution)/shard_map/concatenate | solution.py:311
  49.9 26.1 %all-to-all-done.1 = bf16[16,96,896]{2,1,0:T(8,128)(2,1)S(1)} async-done(((bf16[16,96,896]{2,1,0:T(8,128)(2,1)}), bf16[16,96,896]{2,1,0:T(8,128)(2,1)S(1)}, u32[]{:S(2)}, u32[]{:S(2)}) %all-to-all-start.1) | async-done | bytes 2752544 | tf_op jit(solution)/shard_map/all_to_all | solution.py:22
  76.1 1.5 copy-done
  77.6 12.5 %shard_map.68 = (f32[640,1024]{1,0:T(8,128)}, f32[8,1024]{1,0:T(8,128)}) custom-call(s32[2]{0:T(128)} %pad_add_fusion.1.starts_ref, s32[1,1024]{1,0:T(1,128)} %bitcast.108, bf16[4,384,896]{2,1,0:T(8,128)(2,1)} %bitcast.90, bf16[640,3584]{1,0:T(8,128)(2,1)} %all-gather.2.cloned.1.call-done.l_ref, bf16[640,3584]{1,0:T(8,128)(2,1)} %pad_maximum_fusion.w_ref), custom_call_target="tpu_custom_call" | custom-call | flops 4697620480 | bytes 14548992 | tf_op jit(solution)/shard_map/pallas_call | solution.py:102
  90.1 0.8 slice.95
  90.9 12.6 %all_to_all.35 = f32[8,24,128]{2,1,0:T(8,128)S(1)} all-to-all(f32[8,24,128]{2,1,0:T(8,128)S(1)} %broadcast_in_dim.23), channel_id=1, replica_groups=mesh['z'=8,'core'=2,'x'=4,'y'=4] {'z'}, dimensions={0} | all-to-all | bytes 196608 | tf_op jit(solution)/shard_map/all_to_all | solution.py:22
  103.5 12.2 %all_to_all.36 = f32[16,24,128]{2,1,0:T(8,128)S(1)} all-to-all(f32[16,24,128]{2,1,0:T(8,128)S(1)} %broadcast_in_dim.25), channel_id=1, replica_groups=mesh['z'=8,'core'=2,'x'=4,'y'=4] {'x','y'}, dimensions={0} | all-to-all | bytes 393216 | tf_op jit(solution)/shard_map/all_to_all | solution.py:22
  115.8 0.6 log_add_fusion
  116.4 8.6 %shard_map.70 = bf16[640,3584]{1,0:T(8,128)(2,1)} custom-call(s32[2]{0:T(128)} %pad_add_fusion.1.starts_ref, s32[1,1024]{1,0:T(1,128)} %bitcast.109, f32[640,1024]{1,0:T(8,128)} %get-tuple-element.6.logits_ref, f32[1,1024]{1,0:T(1,128)} %bitcast.101, bf16[640,3584]{1,0:T(8,128)(2,1)} %pad_maximum_fusion.w_ref), custom_call_target="tpu_custom_call" | custom-call | flops 2936012800 | bytes 10813440 | tf_op jit(solution)/shard_map/pallas_call | solution.py:176
  125.1 0.6 copy-done.1
  125.9 0.1 reshape.207
  126.6 7.4 %shard_map.69 = bf16[3584,384]{1,0:T(8,128)(2,1)} custom-call(s32[2]{0:T(128)} %pad_add_fusion.1.starts_ref, s32[1,1024]{1,0:T(1,128)} %bitcast.110, f32[640,1024]{1,0:T(8,128)} %get-tuple-element.6.logits_ref, f32[1,1024]{1,0:T(1,128)} %bitcast.102, bf16[640,3584]{1,0:T(8,128)(2,1)} %pad_maximum_fusion.w_ref), custom_call_target="tpu_custom_call" | custom-call | flops 1761607680 | bytes 8323072 | tf_op jit(solution)/shard_map/pallas_call | solution.py:176
  134.0 5.1 %all-to-all-start.4 = ((bf16[16,224,384]{2,1,0:T(8,128)(2,1)}), bf16[16,224,384]{2,1,0:T(8,128)(2,1)S(1)}, u32[]{:S(2)}, u32[]{:S(2)}) async-start(bf16[16,224,384]{2,1,0:T(8,128)(2,1)} %bitcast.89), calls=%async_computation.4 | async-start | bytes 5505024 | tf_op jit(solution)/shard_map/all_to_all | solution.py:359
  139.2 0.2 fusion.19
  139.3 0.3 collective-permute-start.1
  139.7 0.2 multiply_reduce_fusion
  140.0 0.8 collective-permute-done.1
  140.8 0.1 add_reduce_fusion
  141.2 0.1 reshape.214
  141.3 0.6 pad_maximum_fusion.1
  141.9 12.8 %shard_map.71 = (f32[320,3584]{1,0:T(8,128)}, bf16[320,3584]{1,0:T(8,128)(2,1)}) custom-call(s32[2]{0:T(128)} %pad_add_fusion.1.starts_ref, s32[1,1024]{1,0:T(1,128)} %bitcast.111, f32[640,1024]{1,0:T(8,128)} %get-tuple-element.6.logits_ref, f32[1,1024]{1,0:T(1,128)} %bitcast.103, f32[1,1024]{1,0:T(1,128)} %bitcast.118, bf16[4,384,896]{2,1,0:T(8,128)(2,1)} %bitcast.91, ...), custom_call_target="tpu_custom_call" | custom-call | flops 4697620480 | bytes 14548992 | tf_op jit(solution)/shard_map/pallas_call | solution.py:251
  154.7 0.3 collective-permute-start.2
  155.0 15.9 %all-to-all-done.4 = bf16[16,224,384]{2,1,0:T(8,128)(2,1)S(1)} async-done(((bf16[16,224,384]{2,1,0:T(8,128)(2,1)}), bf16[16,224,384]{2,1,0:T(8,128)(2,1)S(1)}, u32[]{:S(2)}, u32[]{:S(2)}) %all-to-all-start.4) | async-done | bytes 2752544 | tf_op jit(solution)/shard_map/all_to_all | solution.py:359
  170.9 0.4 reduce_sum.96
  171.4 0.1 copy.46
  171.7 0.7 copy.48
  172.4 3.4 %all-to-all-start.5 = ((bf16[8,48,224]{2,1,0:T(8,128)(2,1)}), bf16[8,48,224]{2,1,0:T(8,128)(2,1)S(1)}, u32[]{:S(2)}, u32[]{:S(2)}) async-start(bf16[8,48,224]{2,1,0:T(8,128)(2,1)} %copy.48), calls=%async_computation.5 | async-start | bytes 393216 | tf_op jit(solution)/shard_map/all_to_all | solution.py:364
  175.8 4.3 %reduce-scatter.2.cloned.1.call-done = bf16[80,3584]{1,0:T(8,128)(2,1)} async-done(((bf16[640,3584]{1,0:T(8,128)(2,1)}), bf16[80,3584]{1,0:T(8,128)(2,1)}) %reduce-scatter.2.cloned.1.call-update) | async-done | bytes 573456 | tf_op jit(solution)/shard_map/reduce_scatter | solution.py:356
  180.1 2.1 reshape.206
  182.2 1.0 copy.66
  183.2 2.3 %all-to-all-done.5 = bf16[8,48,224]{2,1,0:T(8,128)(2,1)S(1)} async-done(((bf16[8,48,224]{2,1,0:T(8,128)(2,1)}), bf16[8,48,224]{2,1,0:T(8,128)(2,1)S(1)}, u32[]{:S(2)}, u32[]{:S(2)}) %all-to-all-start.5) | async-done | bytes 172064 | tf_op jit(solution)/shard_map/all_to_all | solution.py:364
  185.4 7.4 %all-to-all-start.6 = ((bf16[16,80,224]{2,1,0:T(8,128)(2,1)}), bf16[16,80,224]{2,1,0:T(8,128)(2,1)S(1)}, u32[]{:S(2)}, u32[]{:S(2)}) async-start(bf16[16,80,224]{2,1,0:T(8,128)(2,1)} %bitcast.85), calls=%async_computation.7 | async-start | bytes 1310720 | tf_op jit(solution)/shard_map/all_to_all | solution.py:367
  192.9 5.0 %fusion = bf16[3584,320]{0,1:T(8,128)(2,1)} fusion(f32[320,3584]{1,0:T(8,128)} %get-tuple-element.8, bf16[320,3584]{1,0:T(8,128)(2,1)} %collective-permute-done.2), kind=kLoop, calls=%fused_computation.2 | loop fusion | flops 3440640 | bytes 9175040 | tf_op jit(solution)/shard_map/transpose | solution.py:388
  197.9 4.4 %all-to-all-done.6 = bf16[16,80,224]{2,1,0:T(8,128)(2,1)S(1)} async-done(((bf16[16,80,224]{2,1,0:T(8,128)(2,1)}), bf16[16,80,224]{2,1,0:T(8,128)(2,1)S(1)}, u32[]{:S(2)}, u32[]{:S(2)}) %all-to-all-start.6) | async-done | bytes 573472 | tf_op jit(solution)/shard_map/all_to_all | solution.py:367
  202.3 0.1 convert_reduce_fusion
  202.5 0.7 copy.57
  (59 shorter events, 2.0 us)
Async XLA Ops:
  7.2 68.9 %all-gather.2.cloned.1.call-start = ((), (), s32[]{:S(2)}) async-start(), calls=%async_computation.8 | async-start | bytes 5160960 | tf_op jit(solution)/shard_map/all_gather | solution.py:313
  12.2 21.9 %all-to-all-start = ((bf16[8,12,1024]{2,1,0:T(8,128)(2,1)}), bf16[8,12,1024]{2,1,0:T(8,128)(2,1)S(1)}, u32[]{:S(2)}, u32[]{:S(2)}) async-start(bf16[8,12,1024]{2,1,0:T(8,128)(2,1)} %broadcast_in_dim.18), calls=%async_computation | async-start | bytes 524288 | tf_op jit(solution)/shard_map/all_to_all | solution.py:22
  20.7 24.4 %collective-permute-start = (bf16[320,3584]{1,0:T(8,128)(2,1)}, bf16[320,3584]{1,0:T(8,128)(2,1)}, u32[]{:S(2)}, u32[]{:S(2)}) collective-permute-start(bf16[320,3584]{1,0:T(8,128)(2,1)} %bitcast.13), channel_id=1, source_target_pairs={{0,16},{16,0},{1,17},{17,1},{2,18},{18,2},{3,19},{19,3},{4,20},{20... | collective-permute-start | bytes 6881288 | tf_op jit(solution)/shard_map/ppermute | solution.py:311
  36.0 40.1 %all-to-all-start.1 = ((bf16[16,96,896]{2,1,0:T(8,128)(2,1)}), bf16[16,96,896]{2,1,0:T(8,128)(2,1)S(1)}, u32[]{:S(2)}, u32[]{:S(2)}) async-start(bf16[16,96,896]{2,1,0:T(8,128)(2,1)} %broadcast_in_dim.21), calls=%async_computation.1 | async-start | bytes 5505024 | tf_op jit(solution)/shard_map/all_to_all | solution.py:22
  43.5 136.6 %reduce-scatter.2.cloned.1.call-start = ((), (), s32[]{:S(2)}) async-start(), calls=%async_computation.9 | async-start | bytes 5160960 | tf_op jit(solution)/shard_map/reduce_scatter | solution.py:356
  76.1 1.5 copy-start
  125.0 0.7 copy-start.1
  134.0 36.9 %all-to-all-start.4 = ((bf16[16,224,384]{2,1,0:T(8,128)(2,1)}), bf16[16,224,384]{2,1,0:T(8,128)(2,1)S(1)}, u32[]{:S(2)}, u32[]{:S(2)}) async-start(bf16[16,224,384]{2,1,0:T(8,128)(2,1)} %bitcast.89), calls=%async_computation.4 | async-start | bytes 5505024 | tf_op jit(solution)/shard_map/all_to_all | solution.py:359
  139.3 1.4 collective-permute-start.1
  154.7 38.1 %collective-permute-start.2 = (bf16[320,3584]{1,0:T(8,128)(2,1)}, bf16[320,3584]{1,0:T(8,128)(2,1)}, u32[]{:S(2)}, u32[]{:S(2)}) collective-permute-start(bf16[320,3584]{1,0:T(8,128)(2,1)} %get-tuple-element.9), channel_id=1, source_target_pairs={{0,16},{16,0},{1,17},{17,1},{2,18},{18,2},{3,19},{19,3},{4,20},{20... | collective-permute-start | bytes 6881288 | tf_op jit(solution)/shard_map/ppermute | solution.py:387
  172.4 13.1 %all-to-all-start.5 = ((bf16[8,48,224]{2,1,0:T(8,128)(2,1)}), bf16[8,48,224]{2,1,0:T(8,128)(2,1)S(1)}, u32[]{:S(2)}, u32[]{:S(2)}) async-start(bf16[8,48,224]{2,1,0:T(8,128)(2,1)} %copy.48), calls=%async_computation.5 | async-start | bytes 393216 | tf_op jit(solution)/shard_map/all_to_all | solution.py:364
  185.4 16.8 %all-to-all-start.6 = ((bf16[16,80,224]{2,1,0:T(8,128)(2,1)}), bf16[16,80,224]{2,1,0:T(8,128)(2,1)S(1)}, u32[]{:S(2)}, u32[]{:S(2)}) async-start(bf16[16,80,224]{2,1,0:T(8,128)(2,1)} %bitcast.85), calls=%async_computation.7 | async-start | bytes 1310720 | tf_op jit(solution)/shard_map/all_to_all | solution.py:367
Sparse Core Ops, SparseCore 0:
  10.4 63.0 all-gather.1
  125.2 54.8 reduce-scatter.1

commit v7 on v1

v7 whole, which is shorter than its diff:
```python
import jax
import jax.numpy as jnp
from jax import lax
from jax.experimental import pallas as pl
from jax.experimental.pallas import tpu as pltpu
from jax.sharding import Mesh, PartitionSpec as P

F32 = jnp.float32
BF16 = jnp.bfloat16
Z, CORES, XH, XL, Y = 8, 2, 2, 2, 4
PLANE = XH * XL * Y
SWAP = [(0, 1), (1, 0)]
LANES = 128
STEPS = 7
PARAMS = pltpu.CompilerParams(vmem_limit_bytes=56 << 20)
SMEM = pl.BlockSpec(memory_space=pltpu.SMEM)
VMEM = pl.BlockSpec(memory_space=pltpu.VMEM)
ANY = pl.BlockSpec(memory_space=pl.ANY)


def broadcast_gather(part, axes, count):
    copies = jnp.broadcast_to(part[None], (count,) + part.shape)
    return lax.all_to_all(copies, axes, 0, 0, tiled=True)


def dot(left, right, contract):
    return lax.dot_general(left, right, (contract, ((), ())), preferred_element_type=F32)


def cost(flops, nbytes):
    return pl.CostEstimate(flops=flops, bytes_accessed=nbytes, transcendentals=0)


def matches_of(starts_ref, number, rows, ids):
    row = lax.broadcasted_iota(jnp.int32, (rows, ids.shape[1]), 0)
    return row + starts_ref[number] == ids


def logits_and_stats(starts, ids, hidden, weights):
    rows, features = weights[0].shape
    count = len(weights)
    columns, tokens = rows * count, hidden.shape[0]
    block = features // STEPS

    def body(starts_ref, ids_ref, h_ref, *refs):
        w_refs = refs[:count]
        logits_ref, stats_ref, w, h, held, sems, out = refs[count:]

        def loads(k):
            span = pl.ds(k * block, block)
            return [pltpu.make_async_copy(h_ref.at[:, span], h.at[k], sems.at[k, count])] + [
                pltpu.make_async_copy(
                    w_refs[i].at[:, span], w.at[k, pl.ds(i * rows, rows)], sems.at[k, i]
                )
                for i in range(count)
            ]

        copies = [loads(k) for k in range(STEPS)]
        for copy in copies[0] + copies[1]:
            copy.start()
        for k in range(STEPS):
            for copy in copies[k]:
                copy.wait()
            if k + 2 < STEPS:
                for copy in copies[k + 2]:
                    copy.start()
            part = dot(w[k], h[k], ((1,), (1,)))
            held[...] = part if k == 0 else held[...] + part
        send = pltpu.make_async_copy(held, logits_ref, out)
        send.start()
        ids = ids_ref[...]
        top = jnp.max(held[...], axis=0, keepdims=True)
        total, picked = jnp.zeros_like(top), jnp.zeros_like(top)
        for i in range(count):
            logits = held[i * rows : (i + 1) * rows]
            total += jnp.sum(jnp.exp(logits - top), axis=0, keepdims=True)
            match = matches_of(starts_ref, i, rows, ids)
            picked += jnp.sum(jnp.where(match, logits, 0.0), axis=0, keepdims=True)
        stats_ref[...] = jnp.concatenate([top, total, picked] + [jnp.zeros_like(top)] * 5)
        send.wait()

    return pl.pallas_call(
        body,
        in_specs=[SMEM, VMEM, ANY] + [ANY] * count,
        out_specs=[ANY, VMEM],
        out_shape=[
            jax.ShapeDtypeStruct((columns, tokens), F32),
            jax.ShapeDtypeStruct((8, tokens), F32),
        ],
        scratch_shapes=[
            pltpu.VMEM((STEPS, columns, block), BF16),
            pltpu.VMEM((STEPS, tokens, block), BF16),
            pltpu.VMEM((columns, tokens), F32),
            pltpu.SemaphoreType.DMA((STEPS, count + 1)),
            pltpu.SemaphoreType.DMA,
        ],
        compiler_params=PARAMS,
        cost_estimate=cost(
            2 * columns * tokens * features, 2 * features * (columns + tokens) + 4 * columns * tokens
        ),
    )(starts, ids, hidden, *weights)


def fetch_changes(starts_ref, ids_ref, norm_ref, logits_ref, logits, held, sems, numbers, rows, scale_ref):
    copies = [
        pltpu.make_async_copy(
            logits_ref.at[pl.ds(number * rows, rows)], logits.at[pl.ds(i * rows, rows)], sems.at[i]
        )
        for i, number in enumerate(numbers)
    ]

    def fill():
        ids, norm = ids_ref[...], norm_ref[...]
        for i, (copy, number) in enumerate(zip(copies, numbers)):
            copy.wait()
            span = slice(i * rows, (i + 1) * rows)
            match = matches_of(starts_ref, number, rows, ids)
            change = jnp.where(match, 1.0, 0.0) - jnp.exp(logits[span] - norm)
            if scale_ref is not None:
                change = change * scale_ref[...]
            held[span] = change.astype(BF16)

    return copies, fill


def partial_product(starts, ids, logits_t, norm, weights):
    columns, tokens = logits_t.shape
    rows, features = weights[0].shape
    count = len(weights)
    block = features // STEPS

    def body(starts_ref, ids_ref, logits_ref, norm_ref, *refs):
        w_refs = refs[:count]
        out_ref, logits, w, held, ready, l_sems, w_sems, sems = refs[count:]
        first, fill = fetch_changes(
            starts_ref, ids_ref, norm_ref, logits_ref, logits, held, l_sems, range(count), rows, None
        )
        loads = [
            [
                pltpu.make_async_copy(
                    w_refs[i].at[:, pl.ds(k * block, block)],
                    w.at[k, pl.ds(i * rows, rows)],
                    w_sems.at[k, i],
                )
                for i in range(count)
            ]
            for k in range(STEPS)
        ]
        for copy in first:
            copy.start()
        for load in loads:
            for copy in load:
                copy.start()
        fill()

        def send(k):
            return pltpu.make_async_copy(
                ready.at[k % 2], out_ref.at[:, pl.ds(k * block, block)], sems.at[k % 2]
            )

        for k in range(STEPS):
            for copy in loads[k]:
                copy.wait()
            out = dot(held[...], w[k], ((0,), (0,)))
            if k >= 2:
                send(k - 2).wait()
            ready[k % 2] = out.astype(BF16)
            send(k).start()
        send(STEPS - 2).wait()
        send(STEPS - 1).wait()

    return pl.pallas_call(
        body,
        in_specs=[SMEM, VMEM, ANY, VMEM] + [ANY] * count,
        out_specs=ANY,
        out_shape=jax.ShapeDtypeStruct((tokens, features), BF16),
        scratch_shapes=[
            pltpu.VMEM((columns, tokens), F32),
            pltpu.VMEM((STEPS, columns, block), BF16),
            pltpu.VMEM((columns, tokens), BF16),
            pltpu.VMEM((2, tokens, block), BF16),
            pltpu.SemaphoreType.DMA((count,)),
            pltpu.SemaphoreType.DMA((STEPS, count)),
            pltpu.SemaphoreType.DMA((2,)),
        ],
        compiler_params=PARAMS,
        cost_estimate=cost(
            2 * columns * tokens * features, 2 * features * (columns + tokens) + 4 * columns * tokens
        ),
    )(starts, ids, logits_t, norm, *weights)


def head_parts(starts, ids, logits_t, norm, scale, hidden, numbers, rows):
    tokens, features = hidden.shape
    block = features // STEPS
    columns = 2 * rows

    def body(starts_ref, ids_ref, logits_ref, norm_ref, scale_ref, h_ref, keep_ref, give_ref,
             logits, h, held, keep, give, l_sems, h_sems, sems):
        first, fill = fetch_changes(
            starts_ref, ids_ref, norm_ref, logits_ref, logits, held, l_sems, numbers, rows, scale_ref
        )
        loads = [
            pltpu.make_async_copy(h_ref.at[:, pl.ds(k * block, block)], h.at[k], h_sems.at[k])
            for k in range(STEPS)
        ]
        for copy in first + loads:
            copy.start()
        fill()

        def sends(k):
            span = pl.ds(k * block, block)
            return (
                pltpu.make_async_copy(keep.at[k % 2], keep_ref.at[:, span], sems.at[k % 2, 0]),
                pltpu.make_async_copy(give.at[k % 2], give_ref.at[:, span], sems.at[k % 2, 1]),
            )

        for k in range(STEPS):
            loads[k].wait()
            out = dot(held[...], h[k], ((1,), (0,)))
            if k >= 2:
                for send in sends(k - 2):
                    send.wait()
            keep[k % 2] = out[:rows]
            give[k % 2] = out[rows:].astype(BF16)
            for send in sends(k):
                send.start()
        for k in (STEPS - 2, STEPS - 1):
            for send in sends(k):
                send.wait()

    return pl.pallas_call(
        body,
        in_specs=[SMEM, VMEM, ANY, VMEM, VMEM, ANY],
        out_specs=[ANY, ANY],
        out_shape=[
            jax.ShapeDtypeStruct((rows, features), F32),
            jax.ShapeDtypeStruct((rows, features), BF16),
        ],
        scratch_shapes=[
            pltpu.VMEM((columns, tokens), F32),
            pltpu.VMEM((STEPS, tokens, block), BF16),
            pltpu.VMEM((columns, tokens), BF16),
            pltpu.VMEM((2, rows, block), F32),
            pltpu.VMEM((2, rows, block), BF16),
            pltpu.SemaphoreType.DMA((2,)),
            pltpu.SemaphoreType.DMA((STEPS,)),
            pltpu.SemaphoreType.DMA((2, 2)),
        ],
        compiler_params=PARAMS,
        cost_estimate=cost(
            2 * columns * tokens * features, 2 * features * (columns + tokens) + 4 * columns * tokens
        ),
    )(starts, ids, logits_t, norm, scale, hidden)


def pick_one(values, *places):
    for place in places:
        values = lax.dynamic_index_in_dim(values, place, 0, False)
    return values


def on_device(hidden, weight, token_ids, response_mask, teacher_logprob):
    own_rows, features = hidden.shape
    columns_here = weight.shape[1]
    core, z = lax.axis_index("core"), lax.axis_index("z")
    xh, side, y = lax.axis_index("xh"), lax.axis_index("xl"), lax.axis_index("y")
    rows = own_rows // 2
    here = Z * rows
    lines = here // LANES
    tokens = own_rows * Z * CORES

    own = weight.T
    across = lax.ppermute(own, "xl", SWAP)
    gathered = lax.all_gather(
        lax.dynamic_slice_in_dim(hidden, side * rows, rows, 0), "z", axis=0, tiled=True
    )
    weights = [own, lax.ppermute(own, "core", SWAP), across, lax.ppermute(across, "core", SWAP)]
    starts = jnp.stack(
        [
            (((z * CORES + c) * XH + xh) * XL + s) * Y * columns_here + y * columns_here
            for s in (side, 1 - side)
            for c in (core, 1 - core)
        ]
    ).astype(jnp.int32)

    facts = jnp.stack([token_ids.astype(F32), response_mask.astype(F32), teacher_logprob])
    facts = broadcast_gather(facts, ("z", "core"), Z * CORES)
    facts = facts.reshape(Z, CORES, 3, XL, rows).transpose(2, 1, 3, 0, 4)
    ids = pick_one(facts[0], core, side).astype(jnp.int32).reshape(1, here)

    logits, stats = logits_and_stats(starts, ids, gathered, weights)
    stats = broadcast_gather(stats[:3].reshape(3 * lines, LANES), "z", Z)
    stats = stats.reshape(Z, 3, lines, LANES)
    top = jnp.max(stats[:, 0], axis=0)
    total = jnp.sum(stats[:, 1] * jnp.exp(stats[:, 0] - top[None]), axis=0)
    stats = jnp.concatenate([top, total, jnp.sum(stats[:, 2], axis=0)])
    stats = broadcast_gather(stats, ("core", "xh", "xl", "y"), CORES * PLANE)
    stats = stats.reshape(CORES, XH, XL, Y, 3, lines, LANES)
    top = jnp.max(stats[:, :, :, :, 0], axis=(1, 3))
    shrink = jnp.exp(stats[:, :, :, :, 0] - top[:, None, :, None])
    total = jnp.sum(stats[:, :, :, :, 1] * shrink, axis=(1, 3))
    picked = jnp.sum(stats[:, :, :, :, 2], axis=(1, 3))
    norms = top + jnp.log(total)
    norm = pick_one(norms, core, side).reshape(1, here)

    partial = partial_product(starts, ids, logits, norm, weights)
    summed = lax.psum_scatter(partial, "z", scatter_dimension=0, tiled=True)
    cut = features // PLANE
    summed = summed.reshape(rows, PLANE, cut).transpose(1, 0, 2)
    summed = lax.all_to_all(summed, ("xh", "xl", "y"), 0, 0, tiled=True)
    summed = summed.reshape(XH, XL, Y, rows, cut).astype(F32)
    summed = jnp.sum(summed, axis=(0, 2)).reshape(own_rows, cut)

    by_shard = (CORES, XL, Z, rows)
    ratio = facts[1] * (picked.reshape(by_shard) - norms.reshape(by_shard) - facts[2])
    steps = jnp.arange(rows, dtype=jnp.int32)
    later = (steps[None, :] >= steps[:, None]).astype(F32)
    within = jnp.sum(ratio[..., None, :] * later, axis=-1)
    parts = jnp.sum(ratio, axis=-1).transpose(2, 0, 1).reshape(-1)
    order = jnp.arange(parts.shape[0], dtype=jnp.int32)
    after = (order[None, :] > order[:, None]).astype(F32)
    beyond = jnp.sum(parts[None, :] * after, axis=1).reshape(Z, CORES, XL).transpose(1, 2, 0)
    scales = facts[1] * (within + beyond[..., None]) / float(tokens)

    own_scale = lax.dynamic_index_in_dim(pick_one(scales, core), z, 1, False).reshape(own_rows)
    hidden_grad = summed * own_scale[:, None]

    scale = pick_one(scales, core, side).reshape(1, here)
    keep, give = head_parts(starts, ids, logits, norm, scale, gathered, (2, 3), columns_here)
    theirs = (keep + lax.ppermute(give, "core", SWAP).astype(F32)).astype(BF16)
    from_across = lax.ppermute(theirs, "xl", SWAP)
    keep, give = head_parts(starts, ids, logits, norm, scale, gathered, (0, 1), columns_here)
    head_grad = keep + lax.ppermute(give, "core", SWAP).astype(F32) + from_across.astype(F32)
    return hidden_grad.astype(BF16), head_grad.astype(BF16).T


def solution(mesh):
    names = ("z", "core", "xh", "xl", "y")
    fine = Mesh(mesh.devices.reshape(Z, CORES, XH, XL, Y), names)
    by_token, by_column = ("z", "core"), P(None, names)
    return jax.shard_map(
        on_device,
        mesh=fine,
        in_specs=(P(by_token, None), by_column, P(by_token), P(by_token), P(by_token)),
        out_specs=(P(by_token, names[2:]), by_column),
        check_vma=False,
    )
```

time: 271 us -> 224 us (0.83)
  waiting for transfers between devices: 155 us -> 98.3 us
  Pallas kernels: 0 us -> 40.7 us
  matrix products: 33.6 us -> 0 us
  blocking collectives: 33.3 us -> 25.7 us
  other arithmetic: 6.35 us -> 12.3 us
    ppermute x2 -> x6, waiting for transfers between devices: 0.01 us -> 70.2 us  [the longest x1 50.3 us: on_device(): across = lax.ppermute(own, 'xl', SWAP)]
    all_gather x1, waiting for transfers between devices: 62.8 us -> 0.01 us  [on_device(): lax.all_gather(lax.dynamic_slice_in_dim(hidden, side * rows, rows, 0), 'z...]
    reduce_scatter x1, waiting for transfers between devices: 70.3 us -> 20.5 us  [on_device(): summed = lax.psum_scatter(partial, 'z', scatter_dimension=0, tiled=True)]
    pallas_call x0 -> x4, Pallas kernels: none -> 40.7 us  [the longest x2 17 us: head_parts(): pl.pallas_call(body, in_specs=[SMEM, VMEM, ANY, VMEM, VMEM, ANY], out_spe...]
    dot_general x4 -> x0, matrix products: 33.6 us -> none  [the longest x1 10.3 us: on_device(): lax.dot_general(grad, both, (((1,), (1,)), ((), ())), preferred_element_t...]
    all_gather x1 -> x0, blocking collectives: 20 us -> none  [on_device(): lax.all_gather(facts, ('z', 'core'), axis=0).reshape(Z, CORES, 3, own_rows)]
    all_to_all x1 -> x2, blocking collectives: 13.3 us -> 25.7 us  [broadcast_gather(): return lax.all_to_all(copies, axes, 0, 0, tiled=True)]
    all_to_all x2 -> x1, waiting for transfers between devices: 13.8 us -> 6.99 us  [broadcast_gather(): return lax.all_to_all(copies, axes, 0, 0, tiled=True)]
  transfers between devices with their start and end apart: 7 -> 10, of which waited for: 5 -> 5; matrix products, arithmetic and copies ran while one was open for 8% -> 8% of each run, Pallas kernels for 0% -> 8%
where the time goes in v7:
time: 224 us; the launch traced here: 223 us
  waiting for transfers between devices  98.3 us (44%)
  Pallas kernels  40.7 us (18%)
  blocking collectives  25.7 us (11%)
  starting transfers between devices  18.8 us (8%)
  between operations  14.3 us (6%)
  local copies, waits for them, and re-layouts  12.6 us (6%)
  other arithmetic  12.3 us (5%)
    ppermute x1, waiting for transfers between devices, on_device(): across = lax.ppermute(own, 'xl', SWAP)  50.3 us
    all_to_all x2, blocking collectives, broadcast_gather(): return lax.all_to_all(copies, axes, 0, 0, tiled=True)  25.7 us
    reduce_scatter x1, waiting for transfers between devices, on_device(): summed = lax.psum_scatter(partial, 'z', scatter_dimension=0, tiled=True)  20.5 us
    ppermute x1, waiting for transfers between devices, on_device(): from_across = lax.ppermute(theirs, 'xl', SWAP)  19.9 us
    pallas_call x2, Pallas kernels, head_parts(): pl.pallas_call(body, in_specs=[SMEM, VMEM, ANY, VMEM, VMEM, ANY], out_spe...  17 us
    pallas_call x1, Pallas kernels, partial_product(): pl.pallas_call(body, in_specs=[SMEM, VMEM, ANY, VMEM] + [ANY] * count, ou...  12.8 us
    pallas_call x1, Pallas kernels, logits_and_stats(): pl.pallas_call(body, in_specs=[SMEM, VMEM, ANY] + [ANY] * count, out_spec...  10.9 us
    all_to_all x1, starting transfers between devices, broadcast_gather(): return lax.all_to_all(copies, axes, 0, 0, tiled=True)  8.62 us
  transfers between devices with their start and end apart: 10, of which 5 were waited for; matrix products, arithmetic and copies ran while one was open for 8% of the time, Pallas kernels for 8%

profile of v7, /device:TPU:8, one launch (start us, length us, event | category | flops | bytes accessed | tf_op | source)
XLA Modules:
  0.0 222.7 jit_solution(17220546905820266957)
XLA Ops:
  7.2 1.1 copy-done
  8.3 0.8 constant_dynamic-slice_fusion.2
  9.2 1.6 collective-permute-start.1
  10.8 50.3 %collective-permute-done.1.refs_2_ = bf16[320,3584]{1,0:T(8,128)(2,1)S(1)} collective-permute-done((bf16[320,3584]{1,0:T(8,128)(2,1)}, bf16[320,3584]{1,0:T(8,128)(2,1)S(1)}, u32[]{:S(2)}, u32[]{:S(2)}) %collective-permute-start.1) | collective-permute-done | bytes 2293792 | tf_op jit(solution)/shard_map/ppermute | solution.py:274
  61.1 0.7 convert_bitcast_fusion
  61.8 0.7 pad_maximum_fusion.1
  62.5 0.6 broadcast_in_dim.8
  63.1 8.6 %all-to-all-start = ((f32[16,3,128]{2,1,0:T(4,128)}), f32[16,3,128]{2,1,0:T(4,128)S(1)}, u32[]{:S(2)}, u32[]{:S(2)}) async-start(f32[16,3,128]{2,1,0:T(4,128)} %broadcast_in_dim.8), calls=%async_computation | async-start | bytes 65536 | tf_op jit(solution)/shard_map/all_to_all | solution.py:23
  71.8 0.6 pad_add_fusion.starts_ref
  72.4 7.0 %all-to-all-done = f32[16,3,128]{2,1,0:T(4,128)S(1)} async-done(((f32[16,3,128]{2,1,0:T(4,128)}), f32[16,3,128]{2,1,0:T(4,128)S(1)}, u32[]{:S(2)}, u32[]{:S(2)}) %all-to-all-start) | async-done | bytes 24608 | tf_op jit(solution)/shard_map/all_to_all | solution.py:23
  79.4 0.1 reshape.118
  79.6 0.7 convert_element_type.54.ids_ref
  80.2 10.9 %shard_map.68 = (f32[1280,512]{1,0:T(8,128)}, f32[8,512]{1,0:T(8,128)}) custom-call(s32[4]{0:T(128)} %pad_add_fusion.starts_ref, s32[1,512]{1,0:T(1,128)} %convert_element_type.54.ids_ref, bf16[512,3584]{1,0:T(8,128)(2,1)} %all-gather.2.cloned.1.call-done.h_ref, bf16[320,3584]{1,0:T(8,128)(2,1)} %bitcast.87, bf16[320,3584]{1,0:T(8,128)(2,1)} %collective-permute-done.refs_1_, ...), custom_call_target="tpu_custom_call" | custom-call | flops 4697620480 | bytes 15466496 | tf_op jit(solution)/shard_map/pallas_call | solution.py:82
  91.2 0.7 slice.34
  91.9 10.7 %all_to_all.20 = f32[8,12,128]{2,1,0:T(8,128)S(1)} all-to-all(f32[8,12,128]{2,1,0:T(8,128)S(1)} %broadcast_in_dim.10), channel_id=1, replica_groups=mesh['z'=8,'core'=2,'xh'=2,'xl'=2,'y'=4] {'z'}, dimensions={0} | all-to-all | bytes 98304 | tf_op jit(solution)/shard_map/all_to_all | solution.py:23
  102.8 14.9 %all_to_all.21 = f32[32,12,128]{2,1,0:T(8,128)S(1)} all-to-all(f32[32,12,128]{2,1,0:T(8,128)S(1)} %broadcast_in_dim.11), channel_id=1, replica_groups=mesh['z'=8,'core'=2,'xh'=2,'xl'=2,'y'=4] {'core','xh','xl','y'}, dimensions={0} | all-to-all | bytes 393216 | tf_op jit(solution)/shard_map/all_to_all | solution.py:23
  117.7 0.1 copy.38
  117.8 0.1 slice_reduce_fusion
  117.9 0.6 dynamic-slice_bitcast_fusion.norm_ref
  118.5 12.8 %shard_map.69 = bf16[512,3584]{1,0:T(8,128)(2,1)} custom-call(s32[4]{0:T(128)} %pad_add_fusion.starts_ref, s32[1,512]{1,0:T(1,128)} %convert_element_type.54.ids_ref, f32[1280,512]{1,0:T(8,128)} %get-tuple-element.8.logits_ref, f32[1,512]{1,0:T(1,128)} %dynamic-slice_bitcast_fusion.norm_ref, bf16[320,3584]{1,0:T(8,128)(2,1)} %bitcast.88, ...), custom_call_target="tpu_custom_call" | custom-call | flops 4697620480 | bytes 15466496 | tf_op jit(solution)/shard_map/pallas_call | solution.py:172
  131.4 0.1 sub.47
  131.4 0.1 fusion.12
  131.5 0.1 copy.43
  131.6 0.1 mul.113
  131.7 0.1 select_reduce_fusion
  131.8 0.1 reshape.115
  132.0 0.1 copy.44
  132.0 0.4 multiply_reduce_fusion
  132.4 0.1 multiply_multiply_fusion
  132.5 0.6 reshape.116.scale_ref
  133.1 8.2 %shard_map.71 = (f32[320,3584]{1,0:T(8,128)}, bf16[320,3584]{1,0:T(8,128)(2,1)}) custom-call(s32[4]{0:T(128)} %pad_add_fusion.starts_ref, s32[1,512]{1,0:T(1,128)} %convert_element_type.54.ids_ref, f32[1280,512]{1,0:T(8,128)} %get-tuple-element.8.logits_ref, f32[1,512]{1,0:T(1,128)} %dynamic-slice_bitcast_fusion.norm_ref, f32[1,512]{1,0:T(1,128)} %reshape.116.scale_ref, ...), custom_call_target="tpu_custom_call" | custom-call | flops 2348810240 | bytes 9568256 | tf_op jit(solution)/shard_map/pallas_call | solution.py:232
  141.3 0.1 collective-permute-start.4
  141.4 8.8 %shard_map.70 = (f32[320,3584]{1,0:T(8,128)}, bf16[320,3584]{1,0:T(8,128)(2,1)}) custom-call(s32[4]{0:T(128)} %pad_add_fusion.starts_ref, s32[1,512]{1,0:T(1,128)} %convert_element_type.54.ids_ref, f32[1280,512]{1,0:T(8,128)} %get-tuple-element.8.logits_ref, f32[1,512]{1,0:T(1,128)} %dynamic-slice_bitcast_fusion.norm_ref, f32[1,512]{1,0:T(1,128)} %reshape.116.scale_ref, ...), custom_call_target="tpu_custom_call" | custom-call | flops 2348810240 | bytes 9568256 | tf_op jit(solution)/shard_map/pallas_call | solution.py:232
  150.3 0.6 collective-permute-start.3
  150.8 1.4 copy-done.1
  152.2 2.2 %add_convert_fusion.1 = bf16[320,3584]{1,0:T(8,128)(2,1)S(1)} fusion(f32[320,3584]{1,0:T(8,128)S(1)} %bitcast.73, bf16[320,3584]{1,0:T(8,128)(2,1)} %copy-done.1), kind=kLoop, calls=%fused_computation.1 | loop fusion | flops 3440640 | bytes 9175040 | tf_op jit(solution)/shard_map/convert_element_type | solution.py:331
  154.5 0.6 collective-permute-start.5
  155.1 0.1 mul.117
  155.2 20.5 %reduce-scatter.2.cloned.1.call-done = bf16[64,3584]{1,0:T(8,128)(2,1)} async-done(((bf16[512,3584]{1,0:T(8,128)(2,1)}), bf16[64,3584]{1,0:T(8,128)(2,1)}) %reduce-scatter.2.cloned.1.call-update) | async-done | bytes 458768 | tf_op jit(solution)/shard_map/reduce_scatter | solution.py:308
  175.7 2.6 %reshape.113 = bf16[64,16,224]{2,1,0:T(8,128)(2,1)} reshape(bf16[64,3584]{1,0:T(8,128)(2,1)} %reduce-scatter.2.cloned.1.call-done) | data formatting | bytes 917504 | tf_op jit(solution)/shard_map/reshape | solution.py:310
  178.2 2.0 copy.51
  180.2 7.2 %all-to-all-start.3 = ((bf16[16,64,224]{2,1,0:T(8,128)(2,1)}), bf16[16,64,224]{2,1,0:T(8,128)(2,1)}, u32[]{:S(2)}, u32[]{:S(2)}) async-start(bf16[16,64,224]{2,1,0:T(8,128)(2,1)} %bitcast.74), calls=%async_computation.4 | async-start | bytes 1048576 | tf_op jit(solution)/shard_map/all_to_all | solution.py:311
  187.4 19.9 %collective-permute-done.5 = bf16[320,3584]{1,0:T(8,128)(2,1)} collective-permute-done((bf16[320,3584]{1,0:T(8,128)(2,1)S(1)}, bf16[320,3584]{1,0:T(8,128)(2,1)}, u32[]{:S(2)}, u32[]{:S(2)}) %collective-permute-start.5) | collective-permute-done | bytes 2293792 | tf_op jit(solution)/shard_map/ppermute | solution.py:332
  207.3 5.9 %fusion = bf16[3584,320]{0,1:T(8,128)(2,1)} fusion(bf16[320,3584]{1,0:T(8,128)(2,1)} %collective-permute-done.5, f32[320,3584]{1,0:T(8,128)} %get-tuple-element.10, bf16[320,3584]{1,0:T(8,128)(2,1)} %collective-permute-done.3), kind=kLoop, calls=%fused_computation.2 | loop fusion | flops 5734400 | bytes 11468800 | tf_op jit(solution)/shard_map/transpose | solution.py:335
  213.2 0.6 all-to-all-done.3
  213.9 1.1 convert_reduce_fusion
  215.0 0.1 fusion.1
  215.1 0.7 copy.45
  (36 shorter events, 0.4 us)
Async XLA Ops:
  7.2 1.2 copy-start
  7.2 73.0 %all-gather.2.cloned.1.call-start = ((), (), s32[]{:S(2)}) async-start(), calls=%async_computation.5 | async-start | bytes 4128768 | tf_op jit(solution)/shard_map/all_gather | solution.py:275
  9.2 51.9 %collective-permute-start.1 = (bf16[320,3584]{1,0:T(8,128)(2,1)}, bf16[320,3584]{1,0:T(8,128)(2,1)S(1)}, u32[]{:S(2)}, u32[]{:S(2)}) collective-permute-start(bf16[320,3584]{1,0:T(8,128)(2,1)} %bitcast.85), channel_id=1, source_target_pairs={{0,4},{4,0},{1,5},{5,1},{2,6},{6,2},{3,7},{7,3},{8,12},{12,8},{9,1... | collective-permute-start | bytes 6881288 | tf_op jit(solution)/shard_map/ppermute | solution.py:274
  10.7 69.5 %collective-permute-start = (bf16[320,3584]{1,0:T(8,128)(2,1)}, bf16[320,3584]{1,0:T(8,128)(2,1)}, u32[]{:S(2)}, u32[]{:S(2)}) collective-permute-start(bf16[320,3584]{1,0:T(8,128)(2,1)} %bitcast.86), channel_id=1, source_target_pairs={{0,16},{16,0},{1,17},{17,1},{2,18},{18,2},{3,19},{19,3},{4,20},{20... | collective-permute-start | bytes 6881288 | tf_op jit(solution)/shard_map/ppermute | solution.py:278
  61.1 19.2 %copy-start.2 = (bf16[320,3584]{1,0:T(8,128)(2,1)}, bf16[320,3584]{1,0:T(8,128)(2,1)S(1)}, u32[]{:S(2)}) copy-start(bf16[320,3584]{1,0:T(8,128)(2,1)S(1)} %collective-permute-done.1.refs_2_) | copy-start | bytes 6881284
  61.1 19.2 %collective-permute-start.2 = (bf16[320,3584]{1,0:T(8,128)(2,1)S(1)}, bf16[320,3584]{1,0:T(8,128)(2,1)}, u32[]{:S(2)}, u32[]{:S(2)}) collective-permute-start(bf16[320,3584]{1,0:T(8,128)(2,1)S(1)} %collective-permute-done.1.refs_2_), channel_id=1, source_target_pairs={{0,16},{16,0},{1,17},{17,1},{2,18},{18,2},{3,19},{19,3},{4,20},{20... | collective-permute-start | bytes 6881288 | tf_op jit(solution)/shard_map/ppermute | solution.py:278
  63.1 16.3 %all-to-all-start = ((f32[16,3,128]{2,1,0:T(4,128)}), f32[16,3,128]{2,1,0:T(4,128)S(1)}, u32[]{:S(2)}, u32[]{:S(2)}) async-start(f32[16,3,128]{2,1,0:T(4,128)} %broadcast_in_dim.8), calls=%async_computation | async-start | bytes 65536 | tf_op jit(solution)/shard_map/all_to_all | solution.py:23
  71.7 103.9 %reduce-scatter.2.cloned.1.call-start = ((), (), s32[]{:S(2)}) async-start(), calls=%async_computation.6 | async-start | bytes 4128768 | tf_op jit(solution)/shard_map/reduce_scatter | solution.py:308
  141.3 10.9 %slice-start = ((s8[4587520]{0:T(1024)(128)(4,1)}), s8[4194304]{0:T(1024)(128)(4,1)S(1)}, s32[]{:S(2)}) async-start(s8[4587520]{0:T(1024)(128)(4,1)} %bitcast.72), calls=%async_computation.7 | async-start | bytes 8388608
  141.3 10.9 %slice-start.1 = ((s8[4587520]{0:T(1024)(128)(4,1)}), s8[393216]{0:T(1024)(128)(4,1)S(1)}, s32[]{:S(2)}) async-start(s8[4587520]{0:T(1024)(128)(4,1)} %bitcast.72), calls=%async_computation.8 | async-start | bytes 786432
  141.3 9.5 %collective-permute-start.4 = (bf16[320,3584]{1,0:T(8,128)(2,1)}, bf16[320,3584]{1,0:T(8,128)(2,1)S(1)}, u32[]{:S(2)}, u32[]{:S(2)}) collective-permute-start(bf16[320,3584]{1,0:T(8,128)(2,1)} %get-tuple-element.13), channel_id=1, source_target_pairs={{0,16},{16,0},{1,17},{17,1},{2,18},{18,2},{3,19},{19,3},{4,20},{20... | collective-permute-start | bytes 6881288 | tf_op jit(solution)/shard_map/ppermute | solution.py:331
  150.3 37.2 %collective-permute-start.3 = (bf16[320,3584]{1,0:T(8,128)(2,1)}, bf16[320,3584]{1,0:T(8,128)(2,1)}, u32[]{:S(2)}, u32[]{:S(2)}) collective-permute-start(bf16[320,3584]{1,0:T(8,128)(2,1)} %get-tuple-element.11), channel_id=1, source_target_pairs={{0,16},{16,0},{1,17},{17,1},{2,18},{18,2},{3,19},{19,3},{4,20},{20... | collective-permute-start | bytes 6881288 | tf_op jit(solution)/shard_map/ppermute | solution.py:334
  150.8 1.4 copy-start.1
  154.5 52.9 %collective-permute-start.5 = (bf16[320,3584]{1,0:T(8,128)(2,1)S(1)}, bf16[320,3584]{1,0:T(8,128)(2,1)}, u32[]{:S(2)}, u32[]{:S(2)}) collective-permute-start(bf16[320,3584]{1,0:T(8,128)(2,1)S(1)} %add_convert_fusion.1), channel_id=1, source_target_pairs={{0,4},{4,0},{1,5},{5,1},{2,6},{6,2},{3,7},{7,3},{8,12},{12,8},{9,1... | collective-permute-start | bytes 6881288 | tf_op jit(solution)/shard_map/ppermute | solution.py:332
  180.2 33.7 %all-to-all-start.3 = ((bf16[16,64,224]{2,1,0:T(8,128)(2,1)}), bf16[16,64,224]{2,1,0:T(8,128)(2,1)}, u32[]{:S(2)}, u32[]{:S(2)}) async-start(bf16[16,64,224]{2,1,0:T(8,128)(2,1)} %bitcast.74), calls=%async_computation.4 | async-start | bytes 1048576 | tf_op jit(solution)/shard_map/all_to_all | solution.py:311
Sparse Core Ops, SparseCore 0:
  9.8 52.7 all-gather.1
  131.5 44.1 reduce-scatter.1

commit v8 on v7

v8 whole, which is shorter than its diff:
```python
import jax
import jax.numpy as jnp
from jax import lax
from jax.experimental import pallas as pl
from jax.experimental.pallas import tpu as pltpu
from jax.sharding import Mesh, PartitionSpec as P

F32 = jnp.float32
BF16 = jnp.bfloat16
Z, CORES, XH, XL, Y = 8, 2, 2, 2, 4
PLANE = XH * XL * Y
SWAP = [(0, 1), (1, 0)]
LANES = 128
STEPS = 7
PARAMS = pltpu.CompilerParams(vmem_limit_bytes=56 << 20)
SMEM = pl.BlockSpec(memory_space=pltpu.SMEM)
VMEM = pl.BlockSpec(memory_space=pltpu.VMEM)
ANY = pl.BlockSpec(memory_space=pl.ANY)


def broadcast_gather(part, axes, count):
    copies = jnp.broadcast_to(part[None], (count,) + part.shape)
    return lax.all_to_all(copies, axes, 0, 0, tiled=True)


def dot(left, right, contract):
    return lax.dot_general(left, right, (contract, ((), ())), preferred_element_type=F32)


def cost(flops, nbytes):
    return pl.CostEstimate(flops=flops, bytes_accessed=nbytes, transcendentals=0)


def matches_of(starts_ref, low, rows, columns_here, ids):
    number = low // columns_here
    row = lax.broadcasted_iota(jnp.int32, (rows, ids.shape[1]), 0) + (low - number * columns_here)
    return row + starts_ref[number] == ids


def logits_and_stats(starts, hidden, weights, columns_here):
    features = weights[0].shape[1]
    count = len(weights)
    sizes = [piece.shape[0] for piece in weights]
    offsets = [sum(sizes[:i]) for i in range(count)]
    columns, tokens = sum(sizes), hidden.shape[0]
    block = features // STEPS
    blocks = columns // columns_here

    def body(starts_ref, h_ref, *refs):
        w_refs = refs[:count]
        exps_ref, stats_ref, facts_ref, w, h, f, held, exps, sems, out = refs[count:]

        def loads(k):
            span = pl.ds(k * block, block)
            return [pltpu.make_async_copy(h_ref.at[:, span], h.at[k], sems.at[k, count])] + [
                pltpu.make_async_copy(
                    w_refs[i].at[:, span], w.at[k, pl.ds(offsets[i], sizes[i])], sems.at[k, i]
                )
                for i in range(count)
            ]

        copies = [loads(k) for k in range(STEPS)]
        facts_copy = pltpu.make_async_copy(
            h_ref.at[:, pl.ds(features, LANES)], f, sems.at[STEPS, 0]
        )
        for copy in copies[0] + copies[1] + [facts_copy]:
            copy.start()
        for k in range(STEPS):
            for copy in copies[k]:
                copy.wait()
            if k + 2 < STEPS:
                for copy in copies[k + 2]:
                    copy.start()
            part = dot(w[k], h[k], ((1,), (1,)))
            held[...] = part if k == 0 else held[...] + part
        facts_copy.wait()
        facts = f[...].astype(F32).T
        token_id = facts[0:1] * 16384.0 + facts[1:2] * 128.0 + facts[2:3]
        teacher = facts[4:5] + facts[5:6] + facts[6:7]
        ids = token_id.astype(jnp.int32)
        top = jnp.max(held[...], axis=0, keepdims=True)
        total, picked = jnp.zeros_like(top), jnp.zeros_like(top)
        sends = []
        for i in range(blocks):
            low = i * columns_here
            logits = held[low : low + columns_here]
            grown = jnp.exp(logits - top)
            total += jnp.sum(grown, axis=0, keepdims=True)
            exps[low : low + columns_here] = grown.astype(BF16)
            span = pl.ds(low, columns_here)
            sends.append(pltpu.make_async_copy(exps.at[span], exps_ref.at[span], out.at[i]))
            sends[-1].start()
            match = matches_of(starts_ref, low, columns_here, columns_here, ids)
            picked += jnp.sum(jnp.where(match, logits, 0.0), axis=0, keepdims=True)
        zero = jnp.zeros_like(top)
        stats_ref[...] = jnp.concatenate([top, total, picked, facts[3:4], teacher] + [zero] * 3)
        facts_ref[...] = jnp.concatenate([token_id, facts[3:4], teacher] + [zero] * 5)
        for send in sends:
            send.wait()

    return pl.pallas_call(
        body,
        in_specs=[SMEM, ANY] + [ANY] * count,
        out_specs=[ANY, VMEM, VMEM],
        out_shape=[
            jax.ShapeDtypeStruct((columns, tokens), BF16),
            jax.ShapeDtypeStruct((8, tokens), F32),
            jax.ShapeDtypeStruct((8, tokens), F32),
        ],
        scratch_shapes=[
            pltpu.VMEM((STEPS, columns, block), BF16),
            pltpu.VMEM((STEPS, tokens, block), BF16),
            pltpu.VMEM((tokens, LANES), BF16),
            pltpu.VMEM((columns, tokens), F32),
            pltpu.VMEM((columns, tokens), BF16),
            pltpu.SemaphoreType.DMA((STEPS + 1, count + 1)),
            pltpu.SemaphoreType.DMA((blocks,)),
        ],
        compiler_params=PARAMS,
        cost_estimate=cost(
            2 * columns * tokens * features, 2 * features * (columns + tokens) + 2 * columns * tokens
        ),
    )(starts, hidden, *weights)


def fill_changes(starts_ref, facts_ref, stats_ref, norm_ref, copies, exps, held, spans, columns_here, scale_ref):
    ids = facts_ref[0:1].astype(jnp.int32)
    shrink = jnp.exp(stats_ref[0:1] - norm_ref[...])
    at = 0
    for copy, (low, rows) in zip(copies, spans):
        copy.wait()
        match = matches_of(starts_ref, low, rows, columns_here, ids)
        change = jnp.where(match, 1.0, 0.0) - exps[at : at + rows].astype(F32) * shrink
        if scale_ref is not None:
            change = change * scale_ref[...]
        held[at : at + rows] = change.astype(BF16)
        at += rows


def partial_product(starts, facts, exps_t, stats, norm, weights, columns_here):
    columns, tokens = exps_t.shape
    features = weights[0].shape[1]
    count = len(weights)
    sizes = [piece.shape[0] for piece in weights]
    offsets = [sum(sizes[:i]) for i in range(count)]
    spans = [(low, columns_here) for low in range(0, columns, columns_here)]
    block = features // STEPS

    def body(starts_ref, facts_ref, exps_ref, stats_ref, norm_ref, *refs):
        w_refs = refs[:count]
        out_ref, exps, w, held, ready, e_sems, w_sems, sems = refs[count:]
        first = [
            pltpu.make_async_copy(
                exps_ref.at[pl.ds(low, rows)], exps.at[pl.ds(low, rows)], e_sems.at[i]
            )
            for i, (low, rows) in enumerate(spans)
        ]
        loads = [
            [
                pltpu.make_async_copy(
                    w_refs[i].at[:, pl.ds(k * block, block)],
                    w.at[k, pl.ds(offsets[i], sizes[i])],
                    w_sems.at[k, i],
                )
                for i in range(count)
            ]
            for k in range(STEPS)
        ]
        for copy in first + loads[0] + loads[1]:
            copy.start()
        fill_changes(
            starts_ref, facts_ref, stats_ref, norm_ref, first, exps, held, spans, columns_here, None
        )

        def send(k):
            return pltpu.make_async_copy(
                ready.at[k % 2], out_ref.at[:, pl.ds(k * block, block)], sems.at[k % 2]
            )

        for k in range(STEPS):
            for copy in loads[k]:
                copy.wait()
            if k + 2 < STEPS:
                for copy in loads[k + 2]:
                    copy.start()
            out = dot(held[...], w[k], ((0,), (0,)))
            if k >= 2:
                send(k - 2).wait()
            ready[k % 2] = out.astype(BF16)
            send(k).start()
        send(STEPS - 2).wait()
        send(STEPS - 1).wait()

    return pl.pallas_call(
        body,
        in_specs=[SMEM, VMEM, ANY, VMEM, VMEM] + [ANY] * count,
        out_specs=ANY,
        out_shape=jax.ShapeDtypeStruct((tokens, features), BF16),
        scratch_shapes=[
            pltpu.VMEM((columns, tokens), BF16),
            pltpu.VMEM((STEPS, columns, block), BF16),
            pltpu.VMEM((columns, tokens), BF16),
            pltpu.VMEM((2, tokens, block), BF16),
            pltpu.SemaphoreType.DMA((len(spans),)),
            pltpu.SemaphoreType.DMA((STEPS, count)),
            pltpu.SemaphoreType.DMA((2,)),
        ],
        compiler_params=PARAMS,
        cost_estimate=cost(
            2 * columns * tokens * features, 2 * features * (columns + tokens) + 2 * columns * tokens
        ),
    )(starts, facts, exps_t, stats, norm, *weights)


def head_parts(starts, facts, exps_t, stats, norm, scale, hidden, after, lows, rows, columns_here, features):
    tokens = hidden.shape[0]
    block = features // STEPS
    spans = [(low, rows) for low in lows]

    def body(starts_ref, facts_ref, exps_ref, stats_ref, norm_ref, scale_ref, h_ref, _, keep_ref, give_ref,
             exps, h, held, keep, give, e_sems, h_sems, sems):
        first = [
            pltpu.make_async_copy(
                exps_ref.at[pl.ds(low, rows)], exps.at[pl.ds(i * rows, rows)], e_sems.at[i]
            )
            for i, low in enumerate(lows)
        ]
        loads = [
            pltpu.make_async_copy(h_ref.at[:, pl.ds(k * block, block)], h.at[k], h_sems.at[k])
            for k in range(STEPS)
        ]
        for copy in first + loads:
            copy.start()
        fill_changes(
            starts_ref, facts_ref, stats_ref, norm_ref, first, exps, held, spans, columns_here, scale_ref
        )

        def sends(k):
            span = pl.ds(k * block, block)
            return (
                pltpu.make_async_copy(keep.at[k % 2], keep_ref.at[:, span], sems.at[k % 2, 0]),
                pltpu.make_async_copy(give.at[k % 2], give_ref.at[:, span], sems.at[k % 2, 1]),
            )

        for k in range(STEPS):
            loads[k].wait()
            out = dot(held[...], h[k], ((1,), (0,)))
            if k >= 2:
                for send in sends(k - 2):
                    send.wait()
            keep[k % 2] = out[:rows]
            give[k % 2] = out[rows:].astype(BF16)
            for send in sends(k):
                send.start()
        for k in (STEPS - 2, STEPS - 1):
            for send in sends(k):
                send.wait()

    return pl.pallas_call(
        body,
        in_specs=[SMEM, VMEM, ANY, VMEM, VMEM, VMEM, ANY, ANY],
        out_specs=[ANY, ANY],
        out_shape=[
            jax.ShapeDtypeStruct((rows, features), F32),
            jax.ShapeDtypeStruct((rows, features), BF16),
        ],
        scratch_shapes=[
            pltpu.VMEM((2 * rows, tokens), BF16),
            pltpu.VMEM((STEPS, tokens, block), BF16),
            pltpu.VMEM((2 * rows, tokens), BF16),
            pltpu.VMEM((2, rows, block), F32),
            pltpu.VMEM((2, rows, block), BF16),
            pltpu.SemaphoreType.DMA((2,)),
            pltpu.SemaphoreType.DMA((STEPS,)),
            pltpu.SemaphoreType.DMA((2, 2)),
        ],
        compiler_params=PARAMS,
        cost_estimate=cost(
            4 * rows * tokens * features, 2 * features * (5 * rows + tokens) + 4 * rows * tokens
        ),
    )(starts, facts, exps_t, stats, norm, scale, hidden, after)


def pack_facts(token_ids, response_mask, teacher_logprob):
    high = lax.reduce_precision(teacher_logprob, 8, 7)
    rest = teacher_logprob - high
    middle = lax.reduce_precision(rest, 8, 7)
    fields = [
        token_ids // 16384,
        token_ids // 128 % 128,
        token_ids % 128,
        response_mask,
        high,
        middle,
        rest - middle,
    ]
    fields = jnp.stack([field.astype(F32) for field in fields], axis=1).astype(BF16)
    return jnp.pad(fields, ((0, 0), (0, LANES - fields.shape[1])))


def pick_one(values, *places):
    for place in places:
        values = lax.dynamic_index_in_dim(values, place, 0, False)
    return values


def on_device(hidden, weight, token_ids, response_mask, teacher_logprob):
    own_rows, features = hidden.shape
    columns_here = weight.shape[1]
    core, z = lax.axis_index("core"), lax.axis_index("z")
    xh, side, y = lax.axis_index("xh"), lax.axis_index("xl"), lax.axis_index("y")
    rows = own_rows // 2
    here = Z * rows
    lines = here // LANES
    tokens = own_rows * Z * CORES

    own = weight.T
    cut_rows = columns_here // 2
    own_other = lax.ppermute(own, "core", SWAP)
    across = [lax.ppermute(part, "xl", SWAP) for part in (own[:cut_rows], own[cut_rows:])]
    facts = pack_facts(token_ids, response_mask, teacher_logprob)
    gathered = lax.all_gather(
        lax.dynamic_slice_in_dim(jnp.concatenate([hidden, facts], axis=1), side * rows, rows, 0),
        "z",
        axis=0,
        tiled=True,
    )
    weights = [own, own_other] + across + [lax.ppermute(part, "core", SWAP) for part in across]
    starts = jnp.stack(
        [
            (((z * CORES + c) * XH + xh) * XL + s) * Y * columns_here + y * columns_here
            for s in (side, 1 - side)
            for c in (core, 1 - core)
        ]
    ).astype(jnp.int32)

    exps, stats, facts = logits_and_stats(starts, gathered, weights, columns_here)
    shared = broadcast_gather(stats[:3].reshape(3 * lines, LANES), "z", Z)
    shared = shared.reshape(Z, 3, lines, LANES)
    top = jnp.max(shared[:, 0], axis=0)
    total = jnp.sum(shared[:, 1] * jnp.exp(shared[:, 0] - top[None]), axis=0)
    known = stats[3:5].reshape(2 * lines, LANES)
    shared = jnp.concatenate([top, total, jnp.sum(shared[:, 2], axis=0), known])
    shared = broadcast_gather(shared, ("xh", "xl", "y"), PLANE)
    shared = shared.reshape(XH, XL, Y, 5, lines, LANES)
    top = jnp.max(shared[:, :, :, 0], axis=(0, 2))
    shrink = jnp.exp(shared[:, :, :, 0] - top[None, :, None])
    total = jnp.sum(shared[:, :, :, 1] * shrink, axis=(0, 2))
    picked = jnp.sum(shared[:, :, :, 2], axis=(0, 2))
    norms = top + jnp.log(total)
    norm = pick_one(norms, side).reshape(1, here)

    partial = partial_product(starts, facts, exps, stats, norm, weights, columns_here)
    summed = lax.psum_scatter(partial, "z", scatter_dimension=0, tiled=True)
    cut = features // PLANE
    summed = summed.reshape(rows, PLANE, cut).transpose(1, 0, 2)
    summed = lax.all_to_all(summed, ("xh", "xl", "y"), 0, 0, tiled=True)
    summed = summed.reshape(XH, XL, Y, rows, cut).astype(F32)
    summed = jnp.sum(summed, axis=(0, 2)).reshape(own_rows, cut)

    mask, teacher = shared[0, :, 0, 3], shared[0, :, 0, 4]
    mask, ratio = (
        part.reshape(XL, Z, rows) for part in (mask, mask * (picked - norms - teacher))
    )
    steps = jnp.arange(rows, dtype=jnp.int32)
    later = (steps[None, :] >= steps[:, None]).astype(F32)
    within = jnp.sum(ratio[..., None, :] * later, axis=-1)
    parts = jnp.sum(ratio, axis=-1).reshape(XL * Z)
    other_parts = lax.ppermute(parts, "core", SWAP)
    number = jnp.arange(XL * Z, dtype=jnp.int32)
    order = number % Z * (CORES * XL) + number // Z
    after = order[None, :] + core * XL
    far_after = order[None, :] + (1 - core) * XL
    here_order = order[:, None] + core * XL
    beyond = parts[None, :] * (after > here_order) + other_parts[None, :] * (far_after > here_order)
    beyond = jnp.sum(beyond, axis=1).reshape(XL, Z, 1)
    scales = mask * (within + beyond) / float(tokens)

    own_scale = lax.dynamic_index_in_dim(scales, z, 1, False).reshape(own_rows)
    hidden_grad = summed * own_scale[:, None]

    scale = pick_one(scales, side).reshape(1, here)

    def parts_of(low, count, after):
        lows = (low, low + columns_here)
        keep, give = head_parts(
            starts, facts, exps, stats, norm, scale, gathered, after, lows, count, columns_here, features
        )
        return (keep + lax.ppermute(give, "core", SWAP).astype(F32)).astype(BF16)

    from_across, after = [], partial
    for low in (0, cut_rows):
        after = parts_of(2 * columns_here + low, cut_rows, after)
        from_across.append(lax.ppermute(after, "xl", SWAP))
    head_grad = parts_of(0, columns_here, after).astype(F32)
    head_grad += jnp.concatenate(from_across).astype(F32)
    return hidden_grad.astype(BF16), head_grad.astype(BF16).T


def solution(mesh):
    names = ("z", "core", "xh", "xl", "y")
    fine = Mesh(mesh.devices.reshape(Z, CORES, XH, XL, Y), names)
    by_token, by_column = ("z", "core"), P(None, names)
    return jax.shard_map(
        on_device,
        mesh=fine,
        in_specs=(P(by_token, None), by_column, P(by_token), P(by_token), P(by_token)),
        out_specs=(P(by_token, names[2:]), by_column),
        check_vma=False,
    )
```

time: 224 us -> 228 us (1.018)
  blocking collectives: 25.7 us -> 0 us
  waiting for transfers between devices: 98.3 us -> 113 us
  starting transfers between devices: 18.8 us -> 28.6 us
  other arithmetic: 12.3 us -> 16.8 us
    all_to_all x2 -> x0, blocking collectives: 25.7 us -> none  [broadcast_gather(): return lax.all_to_all(copies, axes, 0, 0, tiled=True)]
    ppermute x6 -> x11, waiting for transfers between devices: 70.2 us -> 91.2 us  [the longest x2 49.6 us: on_device(): lax.ppermute(part, 'xl', SWAP)]
    reduce_scatter x1, waiting for transfers between devices: 20.5 us -> 6.3 us  [on_device(): summed = lax.psum_scatter(partial, 'z', scatter_dimension=0, tiled=True)]
    all_to_all x1 -> x2, starting transfers between devices: 8.62 us -> 15.9 us  [broadcast_gather(): return lax.all_to_all(copies, axes, 0, 0, tiled=True)]
    all_to_all x1 -> x2, waiting for transfers between devices: 6.99 us -> 14.1 us  [broadcast_gather(): return lax.all_to_all(copies, axes, 0, 0, tiled=True)]
    convert_element_type x2, other arithmetic: 2.25 us -> 5.85 us  [parts_of(): return (keep + lax.ppermute(give, 'core', SWAP).astype(F32)).astype(BF16)]
    slice x2 -> x6, local copies, waits for them, and re-layouts: 0.72 us -> 3.36 us  [the longest x1 1.9 us: on_device(): own[cut_rows:]]
    unnamed x11 -> x7, local copies, waits for them, and re-layouts: 3.25 us -> 0.74 us
  transfers between devices with their start and end apart: 10 -> 16, of which waited for: 5 -> 12; matrix products, arithmetic and copies ran while one was open for 8% -> 9% of each run, Pallas kernels for 8% -> 9%
where the time goes in v8:
time: 228 us; the launch traced here: 227 us
  waiting for transfers between devices  113 us (50%)
  Pallas kernels  42.5 us (19%)
  starting transfers between devices  28.6 us (13%)
  other arithmetic  16.8 us (7%)
  between operations  14.2 us (6%)
  local copies, waits for them, and re-layouts  11.9 us (5%)
    ppermute x2, waiting for transfers between devices, on_device(): lax.ppermute(part, 'xl', SWAP)  49.6 us
    ppermute x2, waiting for transfers between devices, on_device(): from_across.append(lax.ppermute(after, 'xl', SWAP))  32.5 us
    pallas_call x3, Pallas kernels, head_parts(): pl.pallas_call(body, in_specs=[SMEM, VMEM, ANY, VMEM, VMEM, VMEM, ANY, AN...  21 us
    all_to_all x2, starting transfers between devices, broadcast_gather(): return lax.all_to_all(copies, axes, 0, 0, tiled=True)  15.9 us
    all_to_all x2, waiting for transfers between devices, broadcast_gather(): return lax.all_to_all(copies, axes, 0, 0, tiled=True)  14.1 us
    pallas_call x1, Pallas kernels, logits_and_stats(): pl.pallas_call(body, in_specs=[SMEM, ANY] + [ANY] * count, out_specs=[ANY...  10.8 us
    pallas_call x1, Pallas kernels, partial_product(): pl.pallas_call(body, in_specs=[SMEM, VMEM, ANY, VMEM, VMEM] + [ANY] * cou...  10.6 us
    all_to_all x1, starting transfers between devices, on_device(): summed = lax.all_to_all(summed, ('xh', 'xl', 'y'), 0, 0, tiled=True)  7.26 us
  transfers between devices with their start and end apart: 16, of which 12 were waited for; matrix products, arithmetic and copies ran while one was open for 9% of the time, Pallas kernels for 9%

profile of v8, /device:TPU:8, one launch (start us, length us, event | category | flops | bytes accessed | tf_op | source)
XLA Modules:
  0.0 226.7 jit_solution(8991010698838922469)
XLA Ops:
  7.2 0.7 fusion.17
  7.9 0.7 fusion.23
  8.7 1.9 fusion.2
  10.6 1.9 fusion.27
  12.6 1.6 collective-permute-start.2
  14.1 0.5 collective-permute-start.1
  14.7 26.1 %collective-permute-done.2.refs_3_ = bf16[160,3584]{1,0:T(8,128)(2,1)S(1)} collective-permute-done((bf16[160,3584]{1,0:T(8,128)(2,1)S(1)}, bf16[160,3584]{1,0:T(8,128)(2,1)S(1)}, u32[]{:S(2)}, u32[]{:S(2)}) %collective-permute-start.2) | collective-permute-done | bytes 1146912 | tf_op jit(solution)/shard_map/ppermute | solution.py:320
  40.8 23.5 %collective-permute-done.1.refs_2_ = bf16[160,3584]{1,0:T(8,128)(2,1)} collective-permute-done((bf16[160,3584]{1,0:T(8,128)(2,1)S(1)}, bf16[160,3584]{1,0:T(8,128)(2,1)}, u32[]{:S(2)}, u32[]{:S(2)}) %collective-permute-start.1) | collective-permute-done | bytes 1146912 | tf_op jit(solution)/shard_map/ppermute | solution.py:320
  64.3 0.6 pad_add_fusion.starts_ref
  64.9 2.5 %collective-permute-done.3.refs_4_ = bf16[160,3584]{1,0:T(8,128)(2,1)} collective-permute-done((bf16[160,3584]{1,0:T(8,128)(2,1)}, bf16[160,3584]{1,0:T(8,128)(2,1)}, u32[]{:S(2)}, u32[]{:S(2)}) %collective-permute-start.3) | collective-permute-done | bytes 1146912 | tf_op jit(solution)/shard_map/ppermute | solution.py:328
  67.5 10.8 %shard_map.68 = (bf16[1280,512]{1,0:T(8,128)(2,1)}, f32[8,512]{1,0:T(8,128)}, f32[8,512]{1,0:T(8,128)}) custom-call(s32[4]{0:T(128)} %pad_add_fusion.starts_ref, bf16[512,3712]{1,0:T(8,128)(2,1)} %all-gather.2.cloned.1.call-done.h_ref, bf16[320,3584]{1,0:T(8,128)(2,1)} %bitcast.68, bf16[320,3584]{1,0:T(8,128)(2,1)} %collective-permute-done.refs_1_, ...), custom_call_target="tpu_custom_call" | custom-call | flops 4697620480 | bytes 14155776 | tf_op jit(solution)/shard_map/pallas_call | solution.py:101
  78.3 0.7 slice.40
  79.1 0.6 broadcast_in_dim.7
  79.7 8.5 %all-to-all-start = ((f32[8,12,128]{2,1,0:T(8,128)}), f32[8,12,128]{2,1,0:T(8,128)S(1)}, u32[]{:S(2)}, u32[]{:S(2)}) async-start(f32[8,12,128]{2,1,0:T(8,128)} %broadcast_in_dim.7), calls=%async_computation | async-start | bytes 131072 | tf_op jit(solution)/shard_map/all_to_all | solution.py:23
  88.2 0.7 slice.44
  88.9 7.6 %all-to-all-done = f32[8,12,128]{2,1,0:T(8,128)S(1)} async-done(((f32[8,12,128]{2,1,0:T(8,128)}), f32[8,12,128]{2,1,0:T(8,128)S(1)}, u32[]{:S(2)}, u32[]{:S(2)}) %all-to-all-start) | async-done | bytes 49184 | tf_op jit(solution)/shard_map/all_to_all | solution.py:23
  96.6 0.7 broadcast_in_dim.8
  97.3 7.4 %all-to-all-start.1 = ((f32[16,20,128]{2,1,0:T(8,128)}), f32[16,20,128]{2,1,0:T(8,128)S(1)}, u32[]{:S(2)}, u32[]{:S(2)}) async-start(f32[16,20,128]{2,1,0:T(8,128)} %broadcast_in_dim.8), calls=%async_computation.1 | async-start | bytes 393216 | tf_op jit(solution)/shard_map/all_to_all | solution.py:23
  104.7 0.2 reduce-scatter.2.cloned.1.call-start
  105.0 6.4 %all-to-all-done.1 = f32[16,20,128]{2,1,0:T(8,128)S(1)} async-done(((f32[16,20,128]{2,1,0:T(8,128)}), f32[16,20,128]{2,1,0:T(8,128)S(1)}, u32[]{:S(2)}, u32[]{:S(2)}) %all-to-all-start.1) | async-done | bytes 163872 | tf_op jit(solution)/shard_map/all_to_all | solution.py:23
  111.5 0.6 dynamic-slice_bitcast_fusion.norm_ref
  112.1 10.6 %shard_map.69._ = bf16[512,3584]{1,0:T(8,128)(2,1)} custom-call(s32[4]{0:T(128)} %pad_add_fusion.starts_ref, f32[8,512]{1,0:T(8,128)} %get-tuple-element.11.facts_ref, bf16[1280,512]{1,0:T(8,128)(2,1)} %get-tuple-element.12.exps_ref, f32[8,512]{1,0:T(8,128)} %get-tuple-element.13.stats_ref, f32[1,512]{1,0:T(1,128)} %dynamic-slice_bitcast_fusion.norm_ref, ...), custom_call_target="tpu_custom_call" | custom-call | flops 4697620480 | bytes 14155776 | tf_op jit(solution)/shard_map/pallas_call | solution.py:194
  123.2 0.2 multiply_reduce_fusion
  123.4 0.9 collective-permute-done.5
  124.3 0.2 add_reduce_fusion
  124.7 0.6 reshape.158.scale_ref
  125.3 6.4 %shard_map.70 = (f32[160,3584]{1,0:T(8,128)}, bf16[160,3584]{1,0:T(8,128)(2,1)}) custom-call(s32[4]{0:T(128)} %pad_add_fusion.starts_ref, f32[8,512]{1,0:T(8,128)} %get-tuple-element.11.facts_ref, bf16[1280,512]{1,0:T(8,128)(2,1)} %get-tuple-element.12.exps_ref, f32[8,512]{1,0:T(8,128)} %get-tuple-element.13.stats_ref, ...), custom_call_target="tpu_custom_call" | custom-call | flops 1174405120 | bytes 9732096 | tf_op jit(solution)/shard_map/pallas_call | solution.py:259
  131.7 0.3 collective-permute-start.6
  132.0 2.8 %collective-permute-done.6 = bf16[160,3584]{1,0:T(8,128)(2,1)S(1)} collective-permute-done((bf16[160,3584]{1,0:T(8,128)(2,1)}, bf16[160,3584]{1,0:T(8,128)(2,1)S(1)}, u32[]{:S(2)}, u32[]{:S(2)}) %collective-permute-start.6) | collective-permute-done | bytes 1146912 | tf_op jit(solution)/shard_map/ppermute | solution.py:389
  134.8 2.9 %add_convert_fusion.3._ = bf16[160,3584]{1,0:T(8,128)(2,1)} fusion(f32[160,3584]{1,0:T(8,128)} %get-tuple-element.14, bf16[160,3584]{1,0:T(8,128)(2,1)S(1)} %collective-permute-done.6), kind=kLoop, calls=%fused_computation.4 | loop fusion | flops 1720320 | bytes 4587520 | tf_op jit(solution)/shard_map/convert_element_type | solution.py:389
  137.7 6.6 %shard_map.71 = (f32[160,3584]{1,0:T(8,128)}, bf16[160,3584]{1,0:T(8,128)(2,1)}) custom-call(s32[4]{0:T(128)} %pad_add_fusion.starts_ref, f32[8,512]{1,0:T(8,128)} %get-tuple-element.11.facts_ref, bf16[1280,512]{1,0:T(8,128)(2,1)} %get-tuple-element.12.exps_ref, f32[8,512]{1,0:T(8,128)} %get-tuple-element.13.stats_ref, ...), custom_call_target="tpu_custom_call" | custom-call | flops 1174405120 | bytes 9732096 | tf_op jit(solution)/shard_map/pallas_call | solution.py:259
  144.3 0.5 collective-permute-start.7
  144.8 2.8 %collective-permute-done.7 = bf16[160,3584]{1,0:T(8,128)(2,1)S(1)} collective-permute-done((bf16[160,3584]{1,0:T(8,128)(2,1)}, bf16[160,3584]{1,0:T(8,128)(2,1)S(1)}, u32[]{:S(2)}, u32[]{:S(2)}) %collective-permute-start.7) | collective-permute-done | bytes 1146912 | tf_op jit(solution)/shard_map/ppermute | solution.py:389
  147.6 2.9 %add_convert_fusion.2._ = bf16[160,3584]{1,0:T(8,128)(2,1)} fusion(f32[160,3584]{1,0:T(8,128)} %get-tuple-element.16, bf16[160,3584]{1,0:T(8,128)(2,1)S(1)} %collective-permute-done.7), kind=kLoop, calls=%fused_computation.3 | loop fusion | flops 1720320 | bytes 4587520 | tf_op jit(solution)/shard_map/convert_element_type | solution.py:389
  150.5 8.0 %shard_map.72 = (f32[320,3584]{1,0:T(8,128)}, bf16[320,3584]{1,0:T(8,128)(2,1)}) custom-call(s32[4]{0:T(128)} %pad_add_fusion.starts_ref, f32[8,512]{1,0:T(8,128)} %get-tuple-element.11.facts_ref, bf16[1280,512]{1,0:T(8,128)(2,1)} %get-tuple-element.12.exps_ref, f32[8,512]{1,0:T(8,128)} %get-tuple-element.13.stats_ref, ...), custom_call_target="tpu_custom_call" | custom-call | flops 2348810240 | bytes 15794176 | tf_op jit(solution)/shard_map/pallas_call | solution.py:259
  158.6 0.3 collective-permute-start.8
  158.8 0.3 collective-permute-start.9
  159.1 1.7 collective-permute-start.10
  161.0 6.3 %reduce-scatter.2.cloned.1.call-done = bf16[64,3584]{1,0:T(8,128)(2,1)} async-done(((bf16[512,3584]{1,0:T(8,128)(2,1)}), bf16[64,3584]{1,0:T(8,128)(2,1)}) %reduce-scatter.2.cloned.1.call-update) | async-done | bytes 458768 | tf_op jit(solution)/shard_map/reduce_scatter | solution.py:354
  167.3 2.6 %reshape.156 = bf16[64,16,224]{2,1,0:T(8,128)(2,1)} reshape(bf16[64,3584]{1,0:T(8,128)(2,1)} %reduce-scatter.2.cloned.1.call-done) | data formatting | bytes 917504 | tf_op jit(solution)/shard_map/reshape | solution.py:356
  169.8 2.0 copy.51
  171.8 7.3 %all-to-all-start.2 = ((bf16[16,64,224]{2,1,0:T(8,128)(2,1)}), bf16[16,64,224]{2,1,0:T(8,128)(2,1)}, u32[]{:S(2)}, u32[]{:S(2)}) async-start(bf16[16,64,224]{2,1,0:T(8,128)(2,1)} %bitcast.71), calls=%async_computation.3 | async-start | bytes 1048576 | tf_op jit(solution)/shard_map/all_to_all | solution.py:357
  179.1 7.9 %collective-permute-done.9 = bf16[160,3584]{1,0:T(8,128)(2,1)} collective-permute-done((bf16[160,3584]{1,0:T(8,128)(2,1)S(1)}, bf16[160,3584]{1,0:T(8,128)(2,1)}, u32[]{:S(2)}, u32[]{:S(2)}) %collective-permute-start.9) | collective-permute-done | bytes 1146912 | tf_op jit(solution)/shard_map/ppermute | solution.py:394
  187.0 24.6 %collective-permute-done.10 = bf16[160,3584]{1,0:T(8,128)(2,1)} collective-permute-done((bf16[160,3584]{1,0:T(8,128)(2,1)}, bf16[160,3584]{1,0:T(8,128)(2,1)}, u32[]{:S(2)}, u32[]{:S(2)}) %collective-permute-start.10) | collective-permute-done | bytes 1146912 | tf_op jit(solution)/shard_map/ppermute | solution.py:394
  211.6 5.2 %fusion = bf16[3584,320]{0,1:T(8,128)(2,1)} fusion(f32[320,3584]{1,0:T(8,128)} %get-tuple-element.18, bf16[320,3584]{1,0:T(8,128)(2,1)S(1)} %collective-permute-done.8, bf16[160,3584]{1,0:T(8,128)(2,1)} %collective-permute-done.10, bf16[160,3584]{1,0:T(8,128)(2,1)} %collective-permute-done.9), kind=kLoop, calls=%fused_computation.2 | loop fusion | flops 11468800 | bytes 11468800 | tf_op jit(solution)/shard_map/transpose | solution.py:397
  216.8 1.0 all-to-all-done.2
  217.9 1.1 convert_reduce_fusion
  219.1 0.7 copy.48
  (46 shorter events, 1.3 us)
Async XLA Ops:
  7.2 60.3 %all-gather.2.cloned.1.call-start = ((), (), s32[]{:S(2)}) async-start(), calls=%async_computation.4 | async-start | bytes 4276224 | tf_op jit(solution)/shard_map/all_gather | solution.py:322
  10.6 4.0 %copy-start.1 = (bf16[3584,320]{0,1:T(8,128)(2,1)S(1)}, bf16[3584,320]{0,1:T(8,128)(2,1)}, u32[]{:S(2)}) copy-start(bf16[3584,320]{0,1:T(8,128)(2,1)} %param.6) | copy-start | bytes 6881284
  12.6 28.2 %collective-permute-start.2 = (bf16[160,3584]{1,0:T(8,128)(2,1)S(1)}, bf16[160,3584]{1,0:T(8,128)(2,1)S(1)}, u32[]{:S(2)}, u32[]{:S(2)}) collective-permute-start(bf16[160,3584]{1,0:T(8,128)(2,1)S(1)} %get-tuple-element.34), channel_id=1, source_target_pairs={{0,4},{4,0},{1,5},{5,1},{2,6},{6,2},{3,7},{7,3},{8,12},{12,8},{9,1... | collective-permute-start | bytes 3440648 | tf_op jit(solution)/shard_map/ppermute | solution.py:320
  14.1 50.2 %collective-permute-start.1 = (bf16[160,3584]{1,0:T(8,128)(2,1)S(1)}, bf16[160,3584]{1,0:T(8,128)(2,1)}, u32[]{:S(2)}, u32[]{:S(2)}) collective-permute-start(bf16[160,3584]{1,0:T(8,128)(2,1)S(1)} %get-tuple-element.35), channel_id=1, source_target_pairs={{0,4},{4,0},{1,5},{5,1},{2,6},{6,2},{3,7},{7,3},{8,12},{12,8},{9,1... | collective-permute-start | bytes 3440648 | tf_op jit(solution)/shard_map/ppermute | solution.py:320
  14.7 52.8 %collective-permute-start = (bf16[320,3584]{1,0:T(8,128)(2,1)S(1)}, bf16[320,3584]{1,0:T(8,128)(2,1)}, u32[]{:S(2)}, u32[]{:S(2)}) collective-permute-start(bf16[320,3584]{1,0:T(8,128)(2,1)S(1)} %bitcast.70), channel_id=1, source_target_pairs={{0,16},{16,0},{1,17},{17,1},{2,18},{18,2},{3,19},{19,3},{4,20},{20... | collective-permute-start | bytes 6881288 | tf_op jit(solution)/shard_map/ppermute | solution.py:319
  40.8 26.7 %copy-start.2 = (bf16[160,3584]{1,0:T(8,128)(2,1)}, bf16[160,3584]{1,0:T(8,128)(2,1)S(1)}, u32[]{:S(2)}) copy-start(bf16[160,3584]{1,0:T(8,128)(2,1)S(1)} %collective-permute-done.2.refs_3_) | copy-start | bytes 3440644
  40.8 24.1 %collective-permute-start.4 = (bf16[160,3584]{1,0:T(8,128)(2,1)S(1)}, bf16[160,3584]{1,0:T(8,128)(2,1)}, u32[]{:S(2)}, u32[]{:S(2)}) collective-permute-start(bf16[160,3584]{1,0:T(8,128)(2,1)S(1)} %collective-permute-done.2.refs_3_), channel_id=1, source_target_pairs={{0,16},{16,0},{1,17},{17,1},{2,18},{18,2},{3,19},{19,3},{4,20},{20... | collective-permute-start | bytes 3440648 | tf_op jit(solution)/shard_map/ppermute | solution.py:328
  64.3 3.1 %collective-permute-start.3 = (bf16[160,3584]{1,0:T(8,128)(2,1)}, bf16[160,3584]{1,0:T(8,128)(2,1)}, u32[]{:S(2)}, u32[]{:S(2)}) collective-permute-start(bf16[160,3584]{1,0:T(8,128)(2,1)} %collective-permute-done.1.refs_2_), channel_id=1, source_target_pairs={{0,16},{16,0},{1,17},{17,1},{2,18},{18,2},{3,19},{19,3},{4,20},{20... | collective-permute-start | bytes 3440648 | tf_op jit(solution)/shard_map/ppermute | solution.py:328
  79.7 16.8 %all-to-all-start = ((f32[8,12,128]{2,1,0:T(8,128)}), f32[8,12,128]{2,1,0:T(8,128)S(1)}, u32[]{:S(2)}, u32[]{:S(2)}) async-start(f32[8,12,128]{2,1,0:T(8,128)} %broadcast_in_dim.7), calls=%async_computation | async-start | bytes 131072 | tf_op jit(solution)/shard_map/all_to_all | solution.py:23
  97.3 14.1 %all-to-all-start.1 = ((f32[16,20,128]{2,1,0:T(8,128)}), f32[16,20,128]{2,1,0:T(8,128)S(1)}, u32[]{:S(2)}, u32[]{:S(2)}) async-start(f32[16,20,128]{2,1,0:T(8,128)} %broadcast_in_dim.8), calls=%async_computation.1 | async-start | bytes 393216 | tf_op jit(solution)/shard_map/all_to_all | solution.py:23
  104.7 62.6 %reduce-scatter.2.cloned.1.call-start = ((), (), s32[]{:S(2)}) async-start(), calls=%async_computation.5 | async-start | bytes 4128768 | tf_op jit(solution)/shard_map/reduce_scatter | solution.py:354
  123.2 1.1 collective-permute-start.5
  131.7 3.1 %collective-permute-start.6 = (bf16[160,3584]{1,0:T(8,128)(2,1)}, bf16[160,3584]{1,0:T(8,128)(2,1)S(1)}, u32[]{:S(2)}, u32[]{:S(2)}) collective-permute-start(bf16[160,3584]{1,0:T(8,128)(2,1)} %get-tuple-element.15), channel_id=1, source_target_pairs={{0,16},{16,0},{1,17},{17,1},{2,18},{18,2},{3,19},{19,3},{4,20},{20... | collective-permute-start | bytes 3440648 | tf_op jit(solution)/shard_map/ppermute | solution.py:389
  144.3 3.3 %collective-permute-start.7 = (bf16[160,3584]{1,0:T(8,128)(2,1)}, bf16[160,3584]{1,0:T(8,128)(2,1)S(1)}, u32[]{:S(2)}, u32[]{:S(2)}) collective-permute-start(bf16[160,3584]{1,0:T(8,128)(2,1)} %get-tuple-element.17), channel_id=1, source_target_pairs={{0,16},{16,0},{1,17},{17,1},{2,18},{18,2},{3,19},{19,3},{4,20},{20... | collective-permute-start | bytes 3440648 | tf_op jit(solution)/shard_map/ppermute | solution.py:389
  150.5 8.3 %copy-start = (bf16[160,3584]{1,0:T(8,128)(2,1)S(1)}, bf16[160,3584]{1,0:T(8,128)(2,1)}, u32[]{:S(2)}) copy-start(bf16[160,3584]{1,0:T(8,128)(2,1)} %add_convert_fusion.3._) | copy-start | bytes 3440644
  158.6 53.1 %collective-permute-start.8 = (bf16[320,3584]{1,0:T(8,128)(2,1)}, bf16[320,3584]{1,0:T(8,128)(2,1)S(1)}, u32[]{:S(2)}, u32[]{:S(2)}) collective-permute-start(bf16[320,3584]{1,0:T(8,128)(2,1)} %get-tuple-element.19), channel_id=1, source_target_pairs={{0,16},{16,0},{1,17},{17,1},{2,18},{18,2},{3,19},{19,3},{4,20},{20... | collective-permute-start | bytes 6881288 | tf_op jit(solution)/shard_map/ppermute | solution.py:389
  158.8 28.2 %collective-permute-start.9 = (bf16[160,3584]{1,0:T(8,128)(2,1)S(1)}, bf16[160,3584]{1,0:T(8,128)(2,1)}, u32[]{:S(2)}, u32[]{:S(2)}) collective-permute-start(bf16[160,3584]{1,0:T(8,128)(2,1)S(1)} %copy-done), channel_id=1, source_target_pairs={{0,4},{4,0},{1,5},{5,1},{2,6},{6,2},{3,7},{7,3},{8,12},{12,8},{9,1... | collective-permute-start | bytes 3440648 | tf_op jit(solution)/shard_map/ppermute | solution.py:394
  159.1 52.5 %collective-permute-start.10 = (bf16[160,3584]{1,0:T(8,128)(2,1)}, bf16[160,3584]{1,0:T(8,128)(2,1)}, u32[]{:S(2)}, u32[]{:S(2)}) collective-permute-start(bf16[160,3584]{1,0:T(8,128)(2,1)} %add_convert_fusion.2._), channel_id=1, source_target_pairs={{0,4},{4,0},{1,5},{5,1},{2,6},{6,2},{3,7},{7,3},{8,12},{12,8},{9,1... | collective-permute-start | bytes 3440648 | tf_op jit(solution)/shard_map/ppermute | solution.py:394
  171.8 46.0 %all-to-all-start.2 = ((bf16[16,64,224]{2,1,0:T(8,128)(2,1)}), bf16[16,64,224]{2,1,0:T(8,128)(2,1)}, u32[]{:S(2)}, u32[]{:S(2)}) async-start(bf16[16,64,224]{2,1,0:T(8,128)(2,1)} %bitcast.71), calls=%async_computation.3 | async-start | bytes 1048576 | tf_op jit(solution)/shard_map/all_to_all | solution.py:357
Sparse Core Ops, SparseCore 0:
  10.8 54.0 all-gather.1
  122.9 44.3 reduce-scatter.1

commit v9 on v8

v9 whole, which is shorter than its diff:
```python
import jax
import jax.numpy as jnp
from jax import lax
from jax.experimental import pallas as pl
from jax.experimental.pallas import tpu as pltpu
from jax.sharding import Mesh, PartitionSpec as P

F32 = jnp.float32
BF16 = jnp.bfloat16
Z, CORES, XH, XL, Y = 8, 2, 2, 2, 4
PLANE = XH * XL * Y
SWAP = [(0, 1), (1, 0)]
LANES = 128
STEPS = 7
PARAMS = pltpu.CompilerParams(vmem_limit_bytes=56 << 20)
SMEM = pl.BlockSpec(memory_space=pltpu.SMEM)
VMEM = pl.BlockSpec(memory_space=pltpu.VMEM)
ANY = pl.BlockSpec(memory_space=pl.ANY)


def broadcast_gather(part, axes, count):
    copies = jnp.broadcast_to(part[None], (count,) + part.shape)
    return lax.all_to_all(copies, axes, 0, 0, tiled=True)


def dot(left, right, contract):
    return lax.dot_general(left, right, (contract, ((), ())), preferred_element_type=F32)


def cost(flops, nbytes):
    return pl.CostEstimate(flops=flops, bytes_accessed=nbytes, transcendentals=0)


def matches_of(starts_ref, low, rows, columns_here, ids):
    number = low // columns_here
    row = lax.broadcasted_iota(jnp.int32, (rows, ids.shape[1]), 0) + (low - number * columns_here)
    return row + starts_ref[number] == ids


def logits_and_stats(starts, hidden, weights, columns_here):
    features = weights[0].shape[1]
    count = len(weights)
    sizes = [piece.shape[0] for piece in weights]
    offsets = [sum(sizes[:i]) for i in range(count)]
    columns, tokens = sum(sizes), hidden.shape[0]
    block = features // STEPS
    blocks = columns // columns_here

    def body(starts_ref, h_ref, *refs):
        w_refs = refs[:count]
        *exps_refs, stats_ref, w, h, f, held, exps, sems, out = refs[count:]

        def loads(k):
            span = pl.ds(k * block, block)
            return [pltpu.make_async_copy(h_ref.at[:, span], h.at[k], sems.at[k, count])] + [
                pltpu.make_async_copy(
                    w_refs[i].at[:, span], w.at[k, pl.ds(offsets[i], sizes[i])], sems.at[k, i]
                )
                for i in range(count)
            ]

        copies = [loads(k) for k in range(STEPS)]
        facts_copy = pltpu.make_async_copy(
            h_ref.at[:, pl.ds(features, LANES)], f, sems.at[STEPS, 0]
        )
        for copy in copies[0] + copies[1] + [facts_copy]:
            copy.start()
        for k in range(STEPS):
            for copy in copies[k]:
                copy.wait()
            if k + 2 < STEPS:
                for copy in copies[k + 2]:
                    copy.start()
            part = dot(w[k], h[k], ((1,), (1,)))
            held[...] = part if k == 0 else held[...] + part
        facts_copy.wait()
        facts = f[...].astype(F32).T
        token_id = facts[0:1] * 16384.0 + facts[1:2] * 128.0 + facts[2:3]
        teacher = facts[4:5] + facts[5:6] + facts[6:7]
        ids = token_id.astype(jnp.int32)
        top = jnp.max(held[...], axis=0, keepdims=True)
        total, picked = jnp.zeros_like(top), jnp.zeros_like(top)
        sends = []
        for i in range(blocks):
            low = i * columns_here
            logits = held[low : low + columns_here]
            grown = jnp.exp(logits - top)
            total += jnp.sum(grown, axis=0, keepdims=True)
            exps[low : low + columns_here] = grown.astype(BF16)
            into = exps_refs[2 * i // blocks].at[pl.ds(low % (columns // 2), columns_here)]
            sends.append(
                pltpu.make_async_copy(exps.at[pl.ds(low, columns_here)], into, out.at[i])
            )
            sends[-1].start()
            match = matches_of(starts_ref, low, columns_here, columns_here, ids)
            picked += jnp.sum(jnp.where(match, logits, 0.0), axis=0, keepdims=True)
        zero = jnp.zeros_like(top)
        stats_ref[...] = jnp.concatenate(
            [top, total, picked, facts[3:4], teacher, token_id, zero, zero]
        )
        for send in sends:
            send.wait()

    return pl.pallas_call(
        body,
        in_specs=[SMEM, ANY] + [ANY] * count,
        out_specs=[ANY, ANY, VMEM],
        out_shape=[jax.ShapeDtypeStruct((columns // 2, tokens), BF16)] * 2
        + [jax.ShapeDtypeStruct((8, tokens), F32)],
        scratch_shapes=[
            pltpu.VMEM((STEPS, columns, block), BF16),
            pltpu.VMEM((STEPS, tokens, block), BF16),
            pltpu.VMEM((tokens, LANES), BF16),
            pltpu.VMEM((columns, tokens), F32),
            pltpu.VMEM((columns, tokens), BF16),
            pltpu.SemaphoreType.DMA((STEPS + 1, count + 1)),
            pltpu.SemaphoreType.DMA((blocks,)),
        ],
        compiler_params=PARAMS,
        cost_estimate=cost(
            2 * columns * tokens * features, 2 * features * (columns + tokens) + 2 * columns * tokens
        ),
    )(starts, hidden, *weights)


def change_of(starts_ref, rows_ref, exps, low, columns_here, scaled):
    ids = rows_ref[0:1].astype(jnp.int32)
    match = matches_of(starts_ref, low, exps.shape[0], columns_here, ids)
    change = jnp.where(match, 1.0, 0.0) - exps.astype(F32) * rows_ref[1:2]
    return (change * rows_ref[2:3] if scaled else change).astype(BF16)


def partial_product(starts, token_rows, exps_t, weights, columns_here):
    half, tokens = exps_t[0].shape
    columns = 2 * half
    features = weights[0].shape[1]
    count = len(weights)
    sizes = [piece.shape[0] for piece in weights]
    offsets = [sum(sizes[:i]) for i in range(count)]
    block = features // STEPS

    def body(starts_ref, rows_ref, first_ref, last_ref, *refs):
        w_refs = refs[:count]
        out_ref, exps, w, held, ready, e_sems, w_sems, sems = refs[count:]
        first = [
            pltpu.make_async_copy(ref, exps.at[pl.ds(i * half, half)], e_sems.at[i])
            for i, ref in enumerate((first_ref, last_ref))
        ]
        loads = [
            [
                pltpu.make_async_copy(
                    w_refs[i].at[:, pl.ds(k * block, block)],
                    w.at[k, pl.ds(offsets[i], sizes[i])],
                    w_sems.at[k, i],
                )
                for i in range(count)
            ]
            for k in range(STEPS)
        ]
        for copy in first + loads[0] + loads[1]:
            copy.start()
        for low in range(0, columns, columns_here):
            if low % half == 0:
                first[low // half].wait()
            held[low : low + columns_here] = change_of(
                starts_ref, rows_ref, exps[low : low + columns_here], low, columns_here, False
            )

        def send(k):
            return pltpu.make_async_copy(
                ready.at[k % 2], out_ref.at[:, pl.ds(k * block, block)], sems.at[k % 2]
            )

        for k in range(STEPS):
            for copy in loads[k]:
                copy.wait()
            if k + 2 < STEPS:
                for copy in loads[k + 2]:
                    copy.start()
            out = dot(held[...], w[k], ((0,), (0,)))
            if k >= 2:
                send(k - 2).wait()
            ready[k % 2] = out.astype(BF16)
            send(k).start()
        send(STEPS - 2).wait()
        send(STEPS - 1).wait()

    return pl.pallas_call(
        body,
        in_specs=[SMEM, VMEM, ANY, ANY] + [ANY] * count,
        out_specs=ANY,
        out_shape=jax.ShapeDtypeStruct((tokens, features), BF16),
        scratch_shapes=[
            pltpu.VMEM((columns, tokens), BF16),
            pltpu.VMEM((STEPS, columns, block), BF16),
            pltpu.VMEM((columns, tokens), BF16),
            pltpu.VMEM((2, tokens, block), BF16),
            pltpu.SemaphoreType.DMA((2,)),
            pltpu.SemaphoreType.DMA((STEPS, count)),
            pltpu.SemaphoreType.DMA((2,)),
        ],
        compiler_params=PARAMS,
        cost_estimate=cost(
            2 * columns * tokens * features, 2 * features * (columns + tokens) + 2 * columns * tokens
        ),
    )(starts, token_rows, *exps_t, *weights)


def head_block(starts, sides, low, columns_here, features, after):
    tokens = sides[0][2].shape[0]
    block = features // STEPS
    count = len(sides)

    def body(starts_ref, *refs):
        rows_refs, exps_refs, h_refs = refs[0 : 3 * count : 3], refs[1 : 3 * count : 3], refs[2 : 3 * count : 3]
        out_ref, exps, h, held, ready, e_sems, h_sems, sems = refs[3 * count + 1 :]
        first = [
            pltpu.make_async_copy(ref.at[pl.ds(low, columns_here)], exps.at[i], e_sems.at[i])
            for i, ref in enumerate(exps_refs)
        ]
        loads = [
            [
                pltpu.make_async_copy(
                    ref.at[:, pl.ds(k * block, block)], h.at[k, i], h_sems.at[k, i]
                )
                for i, ref in enumerate(h_refs)
            ]
            for k in range(STEPS)
        ]
        for copy in first + loads[0] + loads[1]:
            copy.start()
        for i in range(count):
            first[i].wait()
            held[i] = change_of(starts_ref, rows_refs[i], exps[i], low, columns_here, True)

        def send(k):
            return pltpu.make_async_copy(
                ready.at[k % 2], out_ref.at[:, pl.ds(k * block, block)], sems.at[k % 2]
            )

        for k in range(STEPS):
            if k + 2 < STEPS:
                for copy in loads[k + 2]:
                    copy.start()
            out = None
            for i in range(count):
                loads[k][i].wait()
                part = dot(held[i], h[k, i], ((1,), (0,)))
                out = part if out is None else out + part
            if k >= 2:
                send(k - 2).wait()
            ready[k % 2] = out.astype(BF16)
            send(k).start()
        send(STEPS - 2).wait()
        send(STEPS - 1).wait()

    return pl.pallas_call(
        body,
        in_specs=[SMEM] + [VMEM, ANY, ANY] * count + [ANY],
        out_specs=ANY,
        out_shape=jax.ShapeDtypeStruct((columns_here, features), BF16),
        scratch_shapes=[
            pltpu.VMEM((count, columns_here, tokens), BF16),
            pltpu.VMEM((STEPS, count, tokens, block), BF16),
            pltpu.VMEM((count, columns_here, tokens), BF16),
            pltpu.VMEM((2, columns_here, block), BF16),
            pltpu.SemaphoreType.DMA((count,)),
            pltpu.SemaphoreType.DMA((STEPS, count)),
            pltpu.SemaphoreType.DMA((2,)),
        ],
        compiler_params=PARAMS,
        cost_estimate=cost(
            2 * count * columns_here * tokens * features, 2 * features * (columns_here + count * tokens)
        ),
    )(starts, *(operand for side in sides for operand in side), after)


def cut_features(values, width):
    rows, features = values.shape
    count = features // width

    def body(in_ref, out_ref):
        values = in_ref[...]
        for i in range(count):
            out_ref[i] = values[:, i * width : (i + 1) * width]

    return pl.pallas_call(
        body,
        in_specs=[VMEM],
        out_specs=VMEM,
        out_shape=jax.ShapeDtypeStruct((count, rows, width), values.dtype),
        compiler_params=PARAMS,
        cost_estimate=cost(0, 4 * rows * features),
    )(values)


def pack_facts(token_ids, response_mask, teacher_logprob):
    high = lax.reduce_precision(teacher_logprob, 8, 7)
    rest = teacher_logprob - high
    middle = lax.reduce_precision(rest, 8, 7)
    fields = [
        token_ids // 16384,
        token_ids // 128 % 128,
        token_ids % 128,
        response_mask,
        high,
        middle,
        rest - middle,
    ]
    fields = jnp.stack([field.astype(F32) for field in fields], axis=1).astype(BF16)
    return jnp.pad(fields, ((0, 0), (0, LANES - fields.shape[1])))


def pick_one(values, *places):
    for place in places:
        values = lax.dynamic_index_in_dim(values, place, 0, False)
    return values


def on_device(hidden, weight, token_ids, response_mask, teacher_logprob):
    own_rows, features = hidden.shape
    columns_here = weight.shape[1]
    core, z = lax.axis_index("core"), lax.axis_index("z")
    xh, side, y = lax.axis_index("xh"), lax.axis_index("xl"), lax.axis_index("y")
    rows = own_rows // 2
    here = Z * rows
    lines = here // LANES
    tokens = own_rows * Z * CORES

    own = weight.T
    across = lax.ppermute(own, "xl", SWAP)
    own_other = lax.ppermute(own, "core", SWAP)
    facts = pack_facts(token_ids, response_mask, teacher_logprob)
    gathered = lax.all_gather(
        lax.dynamic_slice_in_dim(jnp.concatenate([hidden, facts], axis=1), side * rows, rows, 0),
        "z",
        axis=0,
        tiled=True,
    )
    weights = [own, across, own_other, lax.ppermute(across, "core", SWAP)]
    starts = jnp.stack(
        [
            (((z * CORES + c) * XH + xh) * XL + s) * Y * columns_here + y * columns_here
            for c in (core, 1 - core)
            for s in (side, 1 - side)
        ]
    ).astype(jnp.int32)

    mine, theirs, stats = logits_and_stats(starts, gathered, weights, columns_here)
    far_gathered = lax.ppermute(gathered, "core", SWAP)
    far_exps = lax.ppermute(theirs, "core", SWAP)
    shared = broadcast_gather(stats[:5].reshape(5 * lines, LANES), "z", Z)
    shared = shared.reshape(Z, 5, lines, LANES)
    top = jnp.max(shared[:, 0], axis=0)
    total = jnp.sum(shared[:, 1] * jnp.exp(shared[:, 0] - top[None]), axis=0)
    known = shared[0, 3:].reshape(2 * lines, LANES)
    shared = jnp.concatenate([top, total, jnp.sum(shared[:, 2], axis=0), known])
    shared = broadcast_gather(shared, ("xh", "xl", "y"), PLANE)
    shared = shared.reshape(XH, XL, Y, 5, lines, LANES)
    top = jnp.max(shared[:, :, :, 0], axis=(0, 2))
    shrink = jnp.exp(shared[:, :, :, 0] - top[None, :, None])
    total = jnp.sum(shared[:, :, :, 1] * shrink, axis=(0, 2))
    picked = jnp.sum(shared[:, :, :, 2], axis=(0, 2))
    norms = top + jnp.log(total)
    factor = jnp.exp(stats[0] - pick_one(norms, side).reshape(here))
    token_rows = jnp.stack([stats[5], factor])

    partial = partial_product(starts, token_rows, (mine, theirs), weights, columns_here)
    summed = lax.psum_scatter(partial, "z", scatter_dimension=0, tiled=True)
    cut = features // PLANE
    shares = cut_features(summed, cut)
    summed = lax.all_to_all(shares, ("xh", "xl", "y"), 0, 0, tiled=True)
    summed = summed.reshape(XH, XL, Y, rows, cut).astype(F32)
    summed = jnp.sum(summed, axis=(0, 2)).reshape(own_rows, cut)

    mask, teacher = shared[0, :, 0, 3], shared[0, :, 0, 4]
    ratio = mask * (picked - norms - teacher)
    known = jnp.concatenate([part.reshape(XL, here) for part in (mask, ratio)] + [token_rows])
    known = jnp.stack([known, lax.ppermute(known, "core", SWAP)])
    mask, ratio = (
        part.reshape(CORES, XL, Z, rows) for part in (known[:, :XL], known[:, XL : 2 * XL])
    )
    steps = jnp.arange(rows, dtype=jnp.int32)
    later = (steps[None, :] >= steps[:, None]).astype(F32)
    within = jnp.sum(ratio[..., None, :] * later, axis=-1)
    parts = jnp.sum(ratio, axis=-1).reshape(-1)
    number = jnp.arange(XL * Z, dtype=jnp.int32)
    order = number % Z * (CORES * XL) + number // Z
    order = jnp.concatenate([order + core * XL, order + (1 - core) * XL])
    beyond = jnp.sum(parts[None, :] * (order[None, :] > order[:, None]), axis=1)
    scales = mask * (within + beyond.reshape(CORES, XL, Z, 1)) / float(tokens)

    own_scale = lax.dynamic_index_in_dim(scales[0], z, 1, False).reshape(own_rows)
    hidden_grad = summed * own_scale[:, None]

    scale = lax.dynamic_index_in_dim(scales, side, 1, False).reshape(CORES, 1, here)
    rows_of = jnp.concatenate([known[:, 2 * XL :], scale], axis=1)
    sides = [(rows_of[0], mine, gathered), (rows_of[1], far_exps, far_gathered)]
    given = head_block(starts, sides, columns_here, columns_here, features, partial)
    from_across = lax.ppermute(given, "xl", SWAP)
    kept = head_block(starts, sides, 0, columns_here, features, shares)
    head_grad = kept.astype(F32) + from_across.astype(F32)
    return hidden_grad.astype(BF16), head_grad.astype(BF16).T


def solution(mesh):
    names = ("z", "core", "xh", "xl", "y")
    fine = Mesh(mesh.devices.reshape(Z, CORES, XH, XL, Y), names)
    by_token, by_column = ("z", "core"), P(None, names)
    return jax.shard_map(
        on_device,
        mesh=fine,
        in_specs=(P(by_token, None), by_column, P(by_token), P(by_token), P(by_token)),
        out_specs=(P(by_token, names[2:]), by_column),
        check_vma=False,
    )
```

time: 228 us -> 207 us (0.908)
  blocking collectives: 0 us -> 17.1 us
  starting transfers between devices: 28.6 us -> 17.5 us
  waiting for transfers between devices: 113 us -> 104 us
  local copies, waits for them, and re-layouts: 11.9 us -> 4.68 us
  other arithmetic: 16.8 us -> 10.1 us
  Pallas kernels: 42.5 us -> 38.3 us
    ppermute x10 -> x6, waiting for transfers between devices: 91.2 us -> 67.5 us  [the longest x1 50.3 us: on_device(): across = lax.ppermute(own, 'xl', SWAP)]
    reduce_scatter x1, waiting for transfers between devices: 6.3 us -> 27.5 us  [on_device(): summed = lax.psum_scatter(partial, 'z', scatter_dimension=0, tiled=True)]
    all_to_all x0 -> x1, blocking collectives: none -> 17.1 us  [broadcast_gather(): return lax.all_to_all(copies, axes, 0, 0, tiled=True)]
    all_to_all x2 -> x1, starting transfers between devices: 15.9 us -> 7.4 us  [broadcast_gather(): return lax.all_to_all(copies, axes, 0, 0, tiled=True)]
    all_to_all x2 -> x1, waiting for transfers between devices: 14.1 us -> 6.44 us  [broadcast_gather(): return lax.all_to_all(copies, axes, 0, 0, tiled=True)]
    convert_element_type x2 -> x0, other arithmetic: 5.85 us -> none  [parts_of(): return (keep + lax.ppermute(give, 'core', SWAP).astype(F32)).astype(BF16)]
    reshape x5 -> x2, local copies, waits for them, and re-layouts: 5.77 us -> 0.16 us  [the longest x1 0.08 us: on_device(): lax.dynamic_index_in_dim(scales, side, 1, False).reshape(CORES, 1, here)]
    pallas_call x4, Pallas kernels: 31.6 us -> 27.6 us  [the longest x2 15 us: head_block(): pl.pallas_call(body, in_specs=[SMEM] + [VMEM, ANY, ANY] * count + [ANY],...]
  transfers between devices with their start and end apart: 16 -> 11, of which waited for: 12 -> 7; matrix products, arithmetic and copies ran while one was open for 9% -> 3% of each run, Pallas kernels for 9% -> 8%
where the time goes in v9:
time: 207 us; the launch traced here: 206 us
  waiting for transfers between devices  104 us (50%)
  Pallas kernels  38.3 us (19%)
  starting transfers between devices  17.5 us (8%)
  blocking collectives  17.1 us (8%)
  between operations  14.2 us (7%)
  other arithmetic  10.1 us (5%)
  local copies, waits for them, and re-layouts  4.68 us (2%)
    ppermute x1, waiting for transfers between devices, on_device(): across = lax.ppermute(own, 'xl', SWAP)  50.3 us
    reduce_scatter x1, waiting for transfers between devices, on_device(): summed = lax.psum_scatter(partial, 'z', scatter_dimension=0, tiled=True)  27.5 us
    all_to_all x1, blocking collectives, broadcast_gather(): return lax.all_to_all(copies, axes, 0, 0, tiled=True)  17.1 us
    pallas_call x2, Pallas kernels, head_block(): pl.pallas_call(body, in_specs=[SMEM] + [VMEM, ANY, ANY] * count + [ANY],...  15 us
    pallas_call x1, Pallas kernels, logits_and_stats(): pl.pallas_call(body, in_specs=[SMEM, ANY] + [ANY] * count, out_specs=[ANY...  10.7 us
    pallas_call x1, Pallas kernels, partial_product(): pl.pallas_call(body, in_specs=[SMEM, VMEM, ANY, ANY] + [ANY] * count, out...  10.4 us
    ppermute x1, waiting for transfers between devices, on_device(): from_across = lax.ppermute(given, 'xl', SWAP)  8.08 us
    all_to_all x1, starting transfers between devices, broadcast_gather(): return lax.all_to_all(copies, axes, 0, 0, tiled=True)  7.4 us
  transfers between devices with their start and end apart: 11, of which 7 were waited for; matrix products, arithmetic and copies ran while one was open for 3% of the time, Pallas kernels for 8%

profile of v9, /device:TPU:8, one launch (start us, length us, event | category | flops | bytes accessed | tf_op | source)
XLA Modules:
  0.0 205.9 jit_solution(15356897411048025494)
XLA Ops:
  7.2 0.0 all-gather.2.cloned.1.call-start
  7.2 0.7 fusion.20
  7.9 0.7 fusion.26
  8.6 0.1 copy.39
  8.7 1.8 fusion.2
  10.6 1.6 collective-permute-start
  12.2 50.3 %collective-permute-done.refs_1_ = bf16[320,3584]{1,0:T(8,128)(2,1)S(1)} collective-permute-done((bf16[320,3584]{1,0:T(8,128)(2,1)}, bf16[320,3584]{1,0:T(8,128)(2,1)S(1)}, u32[]{:S(2)}, u32[]{:S(2)}) %collective-permute-start) | collective-permute-done | bytes 2293792 | tf_op jit(solution)/shard_map/ppermute | solution.py:331
  62.5 0.8 pad_add_fusion.starts_ref
  63.3 3.8 %collective-permute-done.2.refs_3_ = bf16[320,3584]{1,0:T(8,128)(2,1)} collective-permute-done((bf16[320,3584]{1,0:T(8,128)(2,1)S(1)}, bf16[320,3584]{1,0:T(8,128)(2,1)}, u32[]{:S(2)}, u32[]{:S(2)}) %collective-permute-start.2) | collective-permute-done | bytes 2293792 | tf_op jit(solution)/shard_map/ppermute | solution.py:340
  67.1 10.7 %shard_map.68 = (bf16[640,512]{1,0:T(8,128)(2,1)}, bf16[640,512]{1,0:T(8,128)(2,1)}, f32[8,512]{1,0:T(8,128)}) custom-call(s32[4]{0:T(128)} %pad_add_fusion.starts_ref, bf16[512,3712]{1,0:T(8,128)(2,1)} %all-gather.2.cloned.1.call-done.h_ref.refs_2_, bf16[320,3584]{1,0:T(8,128)(2,1)} %bitcast.90, bf16[320,3584]{1,0:T(8,128)(2,1)} %copy-done.1, ...), custom_call_target="tpu_custom_call" | custom-call | flops 4697620480 | bytes 14155776 | tf_op jit(solution)/shard_map/pallas_call | solution.py:104
  77.8 0.7 broadcast_in_dim.6
  78.5 17.1 %all_to_all.15 = f32[8,20,128]{2,1,0:T(8,128)S(1)} all-to-all(f32[8,20,128]{2,1,0:T(8,128)S(1)} %broadcast_in_dim.7), channel_id=1, replica_groups=mesh['z'=8,'core'=2,'xh'=2,'xl'=2,'y'=4] {'z'}, dimensions={0} | all-to-all | bytes 163840 | tf_op jit(solution)/shard_map/all_to_all | solution.py:23
  95.7 0.7 broadcast_in_dim.8
  96.4 7.4 %all-to-all-start.1 = ((f32[16,20,128]{2,1,0:T(8,128)}), f32[16,20,128]{2,1,0:T(8,128)S(1)}, u32[]{:S(2)}, u32[]{:S(2)}) async-start(f32[16,20,128]{2,1,0:T(8,128)} %broadcast_in_dim.8), calls=%async_computation.1 | async-start | bytes 393216 | tf_op jit(solution)/shard_map/all_to_all | solution.py:23
  103.8 0.2 reduce-scatter.2.cloned.1.call-start
  104.0 6.4 %all-to-all-done.1 = f32[16,20,128]{2,1,0:T(8,128)S(1)} async-done(((f32[16,20,128]{2,1,0:T(8,128)}), f32[16,20,128]{2,1,0:T(8,128)S(1)}, u32[]{:S(2)}, u32[]{:S(2)}) %all-to-all-start.1) | async-done | bytes 163872 | tf_op jit(solution)/shard_map/all_to_all | solution.py:23
  110.6 0.8 fusion.30
  111.4 0.6 pad_maximum_fusion.5.rows_ref
  112.0 10.4 %shard_map.69.refs_6_ = bf16[512,3584]{1,0:T(8,128)(2,1)} custom-call(s32[4]{0:T(128)} %pad_add_fusion.starts_ref, f32[2,512]{1,0:T(2,128)} %pad_maximum_fusion.5.rows_ref, bf16[640,512]{1,0:T(8,128)(2,1)} %get-tuple-element.6.first_ref.refs_1_, bf16[640,512]{1,0:T(8,128)(2,1)} %get-tuple-element.7.last_ref, bf16[320,3584]{1,0:T(8,128)(2,1)} %bitcast.91, ...), custom_call_target="tpu_custom_call" | custom-call | flops 4697620480 | bytes 14155776 | tf_op jit(solution)/shard_map/pallas_call | solution.py:188
  122.5 0.1 collective-permute-start.5
  122.6 0.6 collective-permute-start.3
  123.2 0.1 pad_add_fusion.1
  123.3 0.3 copy-done.2
  123.5 5.3 %collective-permute-done.3 = f32[6,512]{1,0:T(8,128)S(1)} collective-permute-done((f32[6,512]{1,0:T(8,128)S(1)}, f32[6,512]{1,0:T(8,128)S(1)}, u32[]{:S(2)}, u32[]{:S(2)}) %collective-permute-start.3) | collective-permute-done | bytes 12320 | tf_op jit(solution)/shard_map/ppermute | solution.py:379
  128.8 0.1 reshape.69
  128.9 0.1 mul.120
  129.0 0.1 reduce_sum.78
  129.1 0.1 mul.127
  129.2 0.2 select_reduce_fusion
  129.3 0.1 add.136
  129.4 0.4 multiply_reduce_fusion
  129.8 0.1 multiply_multiply_fusion
  129.9 0.1 reshape.70
  130.0 0.6 slice_bitcast_fusion.2
  130.6 0.9 copy-done
  131.5 7.5 %shard_map.72 = bf16[320,3584]{1,0:T(8,128)(2,1)} custom-call(s32[4]{0:T(128)} %pad_add_fusion.starts_ref, f32[3,512]{1,0:T(4,128)} %get-tuple-element.25.refs_0_, bf16[640,512]{1,0:T(8,128)(2,1)} %get-tuple-element.6.first_ref.refs_1_, bf16[512,3712]{1,0:T(8,128)(2,1)} %all-gather.2.cloned.1.call-done.h_ref.refs_2_, f32[3,512]{1,0:T(4,128)} %get-tuple-element.24.refs_3_, ...), custom_call_target="tpu_custom_call" | custom-call | flops 2348810240 | bytes 9633792 | tf_op jit(solution)/shard_map/pallas_call | solution.py:257
  139.0 0.4 collective-permute-start.6
  139.4 0.1 mul.131
  139.5 27.5 %reduce-scatter.2.cloned.1.call-done.in_ref = bf16[64,3584]{1,0:T(8,128)(2,1)} async-done(((bf16[512,3584]{1,0:T(8,128)(2,1)}), bf16[64,3584]{1,0:T(8,128)(2,1)}) %reduce-scatter.2.cloned.1.call-update) | async-done | bytes 458768 | tf_op jit(solution)/shard_map/reduce_scatter | solution.py:369
  167.0 2.1 %shard_map.70.refs_6_ = bf16[16,64,224]{2,1,0:T(8,128)(2,1)} custom-call(bf16[64,3584]{1,0:T(8,128)(2,1)} %reduce-scatter.2.cloned.1.call-done.in_ref), custom_call_target="tpu_custom_call" | custom-call | bytes 917504 | tf_op jit(solution)/shard_map/pallas_call | solution.py:287
  169.1 7.3 %all-to-all-start.2 = ((bf16[16,64,224]{2,1,0:T(8,128)(2,1)}), bf16[16,64,224]{2,1,0:T(8,128)(2,1)S(1)}, u32[]{:S(2)}, u32[]{:S(2)}) async-start(bf16[16,64,224]{2,1,0:T(8,128)(2,1)} %shard_map.70.refs_6_), calls=%async_computation.3 | async-start | bytes 1048576 | tf_op jit(solution)/shard_map/all_to_all | solution.py:372
  176.4 7.5 %shard_map.71 = bf16[320,3584]{1,0:T(8,128)(2,1)} custom-call(s32[4]{0:T(128)} %pad_add_fusion.starts_ref, f32[3,512]{1,0:T(4,128)} %get-tuple-element.25.refs_0_, bf16[640,512]{1,0:T(8,128)(2,1)} %get-tuple-element.6.first_ref.refs_1_, bf16[512,3712]{1,0:T(8,128)(2,1)} %all-gather.2.cloned.1.call-done.h_ref.refs_2_, f32[3,512]{1,0:T(4,128)} %get-tuple-element.24.refs_3_, ...), custom_call_target="tpu_custom_call" | custom-call | flops 2348810240 | bytes 9633792 | tf_op jit(solution)/shard_map/pallas_call | solution.py:257
  183.9 8.1 %collective-permute-done.6 = bf16[320,3584]{1,0:T(8,128)(2,1)S(1)} collective-permute-done((bf16[320,3584]{1,0:T(8,128)(2,1)}, bf16[320,3584]{1,0:T(8,128)(2,1)S(1)}, u32[]{:S(2)}, u32[]{:S(2)}) %collective-permute-start.6) | collective-permute-done | bytes 2293792 | tf_op jit(solution)/shard_map/ppermute | solution.py:400
  192.0 3.6 %fusion = bf16[3584,320]{0,1:T(8,128)(2,1)} fusion(bf16[320,3584]{1,0:T(8,128)(2,1)S(1)} %collective-permute-done.6, bf16[320,3584]{1,0:T(8,128)(2,1)} %shard_map.71), kind=kLoop, calls=%fused_computation.1 | loop fusion | flops 4587520 | bytes 6881280 | tf_op jit(solution)/shard_map/transpose | solution.py:403
  195.5 2.7 %all-to-all-done.2 = bf16[16,64,224]{2,1,0:T(8,128)(2,1)S(1)} async-done(((bf16[16,64,224]{2,1,0:T(8,128)(2,1)}), bf16[16,64,224]{2,1,0:T(8,128)(2,1)S(1)}, u32[]{:S(2)}, u32[]{:S(2)}) %all-to-all-start.2) | async-done | bytes 458784 | tf_op jit(solution)/shard_map/all_to_all | solution.py:372
  198.2 0.1 convert_reduce_fusion
  198.3 0.1 fusion.3
  198.4 0.7 copy.44
  (33 shorter events, 0.4 us)
Async XLA Ops:
  7.2 59.9 %all-gather.2.cloned.1.call-start = ((), (), s32[]{:S(2)}) async-start(), calls=%async_computation.4 | async-start | bytes 4276224 | tf_op jit(solution)/shard_map/all_gather | solution.py:334
  10.6 51.9 %collective-permute-start = (bf16[320,3584]{1,0:T(8,128)(2,1)}, bf16[320,3584]{1,0:T(8,128)(2,1)S(1)}, u32[]{:S(2)}, u32[]{:S(2)}) collective-permute-start(bf16[320,3584]{1,0:T(8,128)(2,1)} %bitcast.88), channel_id=1, source_target_pairs={{0,4},{4,0},{1,5},{5,1},{2,6},{6,2},{3,7},{7,3},{8,12},{12,8},{9,1... | collective-permute-start | bytes 6881288 | tf_op jit(solution)/shard_map/ppermute | solution.py:331
  12.2 51.1 %collective-permute-start.1 = (bf16[320,3584]{1,0:T(8,128)(2,1)}, bf16[320,3584]{1,0:T(8,128)(2,1)}, u32[]{:S(2)}, u32[]{:S(2)}) collective-permute-start(bf16[320,3584]{1,0:T(8,128)(2,1)} %bitcast.89), channel_id=1, source_target_pairs={{0,16},{16,0},{1,17},{17,1},{2,18},{18,2},{3,19},{19,3},{4,20},{20... | collective-permute-start | bytes 6881288 | tf_op jit(solution)/shard_map/ppermute | solution.py:332
  62.5 4.6 %copy-start.1 = (bf16[320,3584]{1,0:T(8,128)(2,1)}, bf16[320,3584]{1,0:T(8,128)(2,1)S(1)}, u32[]{:S(2)}) copy-start(bf16[320,3584]{1,0:T(8,128)(2,1)S(1)} %collective-permute-done.refs_1_) | copy-start | bytes 6881284
  62.5 4.6 %collective-permute-start.2 = (bf16[320,3584]{1,0:T(8,128)(2,1)S(1)}, bf16[320,3584]{1,0:T(8,128)(2,1)}, u32[]{:S(2)}, u32[]{:S(2)}) collective-permute-start(bf16[320,3584]{1,0:T(8,128)(2,1)S(1)} %collective-permute-done.refs_1_), channel_id=1, source_target_pairs={{0,16},{16,0},{1,17},{17,1},{2,18},{18,2},{3,19},{19,3},{4,20},{20... | collective-permute-start | bytes 6881288 | tf_op jit(solution)/shard_map/ppermute | solution.py:340
  96.4 14.1 %all-to-all-start.1 = ((f32[16,20,128]{2,1,0:T(8,128)}), f32[16,20,128]{2,1,0:T(8,128)S(1)}, u32[]{:S(2)}, u32[]{:S(2)}) async-start(f32[16,20,128]{2,1,0:T(8,128)} %broadcast_in_dim.8), calls=%async_computation.1 | async-start | bytes 393216 | tf_op jit(solution)/shard_map/all_to_all | solution.py:23
  103.8 63.2 %reduce-scatter.2.cloned.1.call-start = ((), (), s32[]{:S(2)}) async-start(), calls=%async_computation.5 | async-start | bytes 4128768 | tf_op jit(solution)/shard_map/reduce_scatter | solution.py:369
  122.4 1.1 copy-start.2
  122.5 8.1 %collective-permute-start.5 = (bf16[512,3712]{1,0:T(8,128)(2,1)}, bf16[512,3712]{1,0:T(8,128)(2,1)}, u32[]{:S(2)}, u32[]{:S(2)}) collective-permute-start(bf16[512,3712]{1,0:T(8,128)(2,1)} %all-gather.2.cloned.1.call-done.h_ref.refs_2_), channel_id=1, source_target_pairs={{0,16},{16,0},{1,17},{17,1},{2,18},{18,2},{3,19},{19,3},{4,20},{20... | collective-permute-start | bytes 11403272 | tf_op jit(solution)/shard_map/ppermute | solution.py:350
  122.6 6.2 %collective-permute-start.3 = (f32[6,512]{1,0:T(8,128)S(1)}, f32[6,512]{1,0:T(8,128)S(1)}, u32[]{:S(2)}, u32[]{:S(2)}) collective-permute-start(f32[6,512]{1,0:T(8,128)S(1)} %get-tuple-element.29), channel_id=1, source_target_pairs={{0,16},{16,0},{1,17},{17,1},{2,18},{18,2},{3,19},{19,3},{4,20},{20... | collective-permute-start | bytes 36872 | tf_op jit(solution)/shard_map/ppermute | solution.py:379
  123.5 7.1 %collective-permute-start.4 = (bf16[640,512]{1,0:T(8,128)(2,1)S(1)}, bf16[640,512]{1,0:T(8,128)(2,1)S(1)}, u32[]{:S(2)}, u32[]{:S(2)}) collective-permute-start(bf16[640,512]{1,0:T(8,128)(2,1)S(1)} %copy-done.2), channel_id=1, source_target_pairs={{0,16},{16,0},{1,17},{17,1},{2,18},{18,2},{3,19},{19,3},{4,20},{20... | collective-permute-start | bytes 1966088 | tf_op jit(solution)/shard_map/ppermute | solution.py:351
  130.6 0.9 copy-start
  139.0 53.0 %collective-permute-start.6 = (bf16[320,3584]{1,0:T(8,128)(2,1)}, bf16[320,3584]{1,0:T(8,128)(2,1)S(1)}, u32[]{:S(2)}, u32[]{:S(2)}) collective-permute-start(bf16[320,3584]{1,0:T(8,128)(2,1)} %shard_map.72), channel_id=1, source_target_pairs={{0,4},{4,0},{1,5},{5,1},{2,6},{6,2},{3,7},{7,3},{8,12},{12,8},{9,1... | collective-permute-start | bytes 6881288 | tf_op jit(solution)/shard_map/ppermute | solution.py:400
  169.1 29.1 %all-to-all-start.2 = ((bf16[16,64,224]{2,1,0:T(8,128)(2,1)}), bf16[16,64,224]{2,1,0:T(8,128)(2,1)S(1)}, u32[]{:S(2)}, u32[]{:S(2)}) async-start(bf16[16,64,224]{2,1,0:T(8,128)(2,1)} %shard_map.70.refs_6_), calls=%async_computation.3 | async-start | bytes 1048576 | tf_op jit(solution)/shard_map/all_to_all | solution.py:372
Sparse Core Ops, SparseCore 0:
  10.7 54.0 all-gather.1
  122.6 44.3 reduce-scatter.1

commit v10 on v9

--- a/solution.py
+++ b/solution.py
@@ -123,6 +123,30 @@
     )(starts, hidden, *weights)
 
 
+def merge_stats(parts, own, after):
+    lines = own.shape[0] // 8
+
+    def body(parts_ref, own_ref, _, out_ref):
+        tops = parts_ref[:, :lines]
+        top = jnp.max(tops, axis=0)
+        out_ref[:lines] = top
+        out_ref[lines : 2 * lines] = jnp.sum(
+            parts_ref[:, lines : 2 * lines] * jnp.exp(tops - top[None]), axis=0
+        )
+        out_ref[2 * lines : 3 * lines] = jnp.sum(parts_ref[:, 2 * lines :], axis=0)
+        out_ref[3 * lines : 6 * lines] = own_ref[3 * lines : 6 * lines]
+        out_ref[6 * lines :] = own_ref[:lines]
+
+    return pl.pallas_call(
+        body,
+        in_specs=[VMEM, VMEM, ANY],
+        out_specs=VMEM,
+        out_shape=jax.ShapeDtypeStruct((7 * lines, LANES), F32),
+        compiler_params=PARAMS,
+        cost_estimate=cost(0, 4 * parts.size),
+    )(parts, own, after)
+
+
 def change_of(starts_ref, rows_ref, exps, low, columns_here, scaled):
     ids = rows_ref[0:1].astype(jnp.int32)
     match = matches_of(starts_ref, low, exps.shape[0], columns_here, ids)
@@ -349,23 +373,25 @@
     mine, theirs, stats = logits_and_stats(starts, gathered, weights, columns_here)
     far_gathered = lax.ppermute(gathered, "core", SWAP)
     far_exps = lax.ppermute(theirs, "core", SWAP)
-    shared = broadcast_gather(stats[:5].reshape(5 * lines, LANES), "z", Z)
-    shared = shared.reshape(Z, 5, lines, LANES)
-    top = jnp.max(shared[:, 0], axis=0)
-    total = jnp.sum(shared[:, 1] * jnp.exp(shared[:, 0] - top[None]), axis=0)
-    known = shared[0, 3:].reshape(2 * lines, LANES)
-    shared = jnp.concatenate([top, total, jnp.sum(shared[:, 2], axis=0), known])
-    shared = broadcast_gather(shared, ("xh", "xl", "y"), PLANE)
-    shared = shared.reshape(XH, XL, Y, 5, lines, LANES)
-    top = jnp.max(shared[:, :, :, 0], axis=(0, 2))
-    shrink = jnp.exp(shared[:, :, :, 0] - top[None, :, None])
-    total = jnp.sum(shared[:, :, :, 1] * shrink, axis=(0, 2))
-    picked = jnp.sum(shared[:, :, :, 2], axis=(0, 2))
+    stats = stats.reshape(8 * lines, LANES)
+    shared = broadcast_gather(stats[: 3 * lines], "z", Z)
+    shared = merge_stats(shared, stats, far_gathered)
+    shared = broadcast_gather(shared, ("core", "xh", "xl", "y"), CORES * PLANE)
+    shared = shared.reshape(CORES, XH, XL, Y, 7, lines, LANES)
+    top = jnp.max(shared[:, :, :, :, 0], axis=(1, 3))
+    shrink = jnp.exp(shared[:, :, :, :, 0] - top[:, None, :, None])
+    total = jnp.sum(shared[:, :, :, :, 1] * shrink, axis=(1, 3))
+    picked = jnp.sum(shared[:, :, :, :, 2], axis=(1, 3))
     norms = top + jnp.log(total)
-    factor = jnp.exp(stats[0] - pick_one(norms, side).reshape(here))
-    token_rows = jnp.stack([stats[5], factor])
-
-    partial = partial_product(starts, token_rows, (mine, theirs), weights, columns_here)
+    at_place = lax.dynamic_slice(
+        shared, (0, xh, side, y, 5, 0, 0), (CORES, 1, 1, 1, 2, lines, LANES)
+    ).reshape(CORES, 2, here)
+    own_norms = lax.dynamic_index_in_dim(norms, side, 1, False).reshape(CORES, here)
+    token_rows = jnp.stack([at_place[:, 0], jnp.exp(at_place[:, 1] - own_norms)], axis=1)
+
+    partial = partial_product(
+        starts, pick_one(token_rows, core), (mine, theirs), weights, columns_here
+    )
     summed = lax.psum_scatter(partial, "z", scatter_dimension=0, tiled=True)
     cut = features // PLANE
     shares = cut_features(summed, cut)
@@ -373,29 +399,28 @@
     summed = summed.reshape(XH, XL, Y, rows, cut).astype(F32)
     summed = jnp.sum(summed, axis=(0, 2)).reshape(own_rows, cut)
 
-    mask, teacher = shared[0, :, 0, 3], shared[0, :, 0, 4]
-    ratio = mask * (picked - norms - teacher)
-    known = jnp.concatenate([part.reshape(XL, here) for part in (mask, ratio)] + [token_rows])
-    known = jnp.stack([known, lax.ppermute(known, "core", SWAP)])
+    mask, teacher = shared[:, 0, :, 0, 3], shared[:, 0, :, 0, 4]
     mask, ratio = (
-        part.reshape(CORES, XL, Z, rows) for part in (known[:, :XL], known[:, XL : 2 * XL])
+        part.reshape(CORES, XL, Z, rows) for part in (mask, mask * (picked - norms - teacher))
     )
     steps = jnp.arange(rows, dtype=jnp.int32)
     later = (steps[None, :] >= steps[:, None]).astype(F32)
     within = jnp.sum(ratio[..., None, :] * later, axis=-1)
-    parts = jnp.sum(ratio, axis=-1).reshape(-1)
-    number = jnp.arange(XL * Z, dtype=jnp.int32)
-    order = number % Z * (CORES * XL) + number // Z
-    order = jnp.concatenate([order + core * XL, order + (1 - core) * XL])
-    beyond = jnp.sum(parts[None, :] * (order[None, :] > order[:, None]), axis=1)
-    scales = mask * (within + beyond.reshape(CORES, XL, Z, 1)) / float(tokens)
-
-    own_scale = lax.dynamic_index_in_dim(scales[0], z, 1, False).reshape(own_rows)
+    parts = jnp.sum(ratio, axis=-1).transpose(2, 0, 1).reshape(-1)
+    order = jnp.arange(parts.shape[0], dtype=jnp.int32)
+    after = (order[None, :] > order[:, None]).astype(F32)
+    beyond = jnp.sum(parts[None, :] * after, axis=1).reshape(Z, CORES, XL).transpose(1, 2, 0)
+    scales = mask * (within + beyond[..., None]) / float(tokens)
+
+    own_scale = lax.dynamic_index_in_dim(pick_one(scales, core), z, 1, False).reshape(own_rows)
     hidden_grad = summed * own_scale[:, None]
 
     scale = lax.dynamic_index_in_dim(scales, side, 1, False).reshape(CORES, 1, here)
-    rows_of = jnp.concatenate([known[:, 2 * XL :], scale], axis=1)
-    sides = [(rows_of[0], mine, gathered), (rows_of[1], far_exps, far_gathered)]
+    rows_of = jnp.concatenate([token_rows, scale], axis=1)
+    sides = [
+        (pick_one(rows_of, core), mine, gathered),
+        (pick_one(rows_of, 1 - core), far_exps, far_gathered),
+    ]
     given = head_block(starts, sides, columns_here, columns_here, features, partial)
     from_across = lax.ppermute(given, "xl", SWAP)
     kept = head_block(starts, sides, 0, columns_here, features, shares)

time: 207 us -> 216 us (1.043)
  blocking collectives: 17.1 us -> 0 us
  waiting for transfers between devices: 104 us -> 121 us
  local copies, waits for them, and re-layouts: 4.68 us -> 9.45 us
  starting transfers between devices: 17.5 us -> 21.6 us
    all_gather x1, waiting for transfers between devices: 0.01 us -> 52.6 us  [on_device(): lax.all_gather(lax.dynamic_slice_in_dim(jnp.concatenate([hidden, facts],...]
    ppermute x1, waiting for transfers between devices: 50.3 us -> 0.01 us  [on_device(): across = lax.ppermute(own, 'xl', SWAP)]
    all_to_all x1 -> x0, blocking collectives: 17.1 us -> none  [broadcast_gather(): return lax.all_to_all(copies, axes, 0, 0, tiled=True)]
    ppermute x1, waiting for transfers between devices: 0.01 us -> 12.2 us  [on_device(): own_other = lax.ppermute(own, 'core', SWAP)]
    all_to_all x1 -> x2, waiting for transfers between devices: 6.44 us -> 17.2 us  [broadcast_gather(): return lax.all_to_all(copies, axes, 0, 0, tiled=True)]
    ppermute x1 -> x0, waiting for transfers between devices: 5.28 us -> none  [on_device(): known = jnp.stack([known, lax.ppermute(known, 'core', SWAP)])]
    reduce_scatter x1, waiting for transfers between devices: 27.5 us -> 32.2 us  [on_device(): summed = lax.psum_scatter(partial, 'z', scatter_dimension=0, tiled=True)]
    ppermute x1, waiting for transfers between devices: 8.08 us -> 3.68 us  [on_device(): from_across = lax.ppermute(given, 'xl', SWAP)]
  transfers between devices with their start and end apart: 11 -> 11, of which waited for: 7 -> 7; matrix products, arithmetic and copies ran while one was open for 3% -> 4% of each run, Pallas kernels for 8% -> 13%
where the time goes in v10:
time: 216 us; the launch traced here: 215 us
  waiting for transfers between devices  121 us (56%)
  Pallas kernels  39.7 us (18%)
  starting transfers between devices  21.6 us (10%)
  between operations  14.2 us (7%)
  local copies, waits for them, and re-layouts  9.45 us (4%)
  other arithmetic  9.07 us (4%)
    all_gather x1, waiting for transfers between devices, on_device(): lax.all_gather(lax.dynamic_slice_in_dim(jnp.concatenate([hidden, facts],...  52.6 us
    reduce_scatter x1, waiting for transfers between devices, on_device(): summed = lax.psum_scatter(partial, 'z', scatter_dimension=0, tiled=True)  32.2 us
    all_to_all x2, waiting for transfers between devices, broadcast_gather(): return lax.all_to_all(copies, axes, 0, 0, tiled=True)  17.2 us
    pallas_call x2, Pallas kernels, head_block(): pl.pallas_call(body, in_specs=[SMEM] + [VMEM, ANY, ANY] * count + [ANY],...  15.1 us
    ppermute x1, waiting for transfers between devices, on_device(): own_other = lax.ppermute(own, 'core', SWAP)  12.2 us
    all_to_all x2, starting transfers between devices, broadcast_gather(): return lax.all_to_all(copies, axes, 0, 0, tiled=True)  11.7 us
    pallas_call x1, Pallas kernels, logits_and_stats(): pl.pallas_call(body, in_specs=[SMEM, ANY] + [ANY] * count, out_specs=[ANY...  10.6 us
    pallas_call x1, Pallas kernels, partial_product(): pl.pallas_call(body, in_specs=[SMEM, VMEM, ANY, ANY] + [ANY] * count, out...  10.4 us
  transfers between devices with their start and end apart: 11, of which 7 were waited for; matrix products, arithmetic and copies ran while one was open for 4% of the time, Pallas kernels for 13%

profile of v10, /device:TPU:8, one launch (start us, length us, event | category | flops | bytes accessed | tf_op | source)
XLA Modules:
  0.0 215.0 jit_solution(702269479690188744)
XLA Ops:
  7.2 0.7 fusion.15
  7.9 0.7 fusion.21
  8.6 0.1 copy.61
  8.7 1.8 fusion.2
  10.6 1.6 collective-permute-start
  12.2 52.6 %all-gather.2.cloned.1.call-done.h_ref.refs_2_ = bf16[512,3712]{1,0:T(8,128)(2,1)} async-done(((bf16[64,3712]{1,0:T(8,128)(2,1)}), bf16[512,3712]{1,0:T(8,128)(2,1)}) %all-gather.2.cloned.1.call-update) | async-done | bytes 3801104 | tf_op jit(solution)/shard_map/all_gather | solution.py:358
  64.8 0.5 collective-permute-start.1
  65.3 0.1 collective-permute-start.2
  65.4 0.7 pad_add_fusion.starts_ref
  66.1 12.2 %collective-permute-done.1.refs_2_ = bf16[320,3584]{1,0:T(8,128)(2,1)} collective-permute-done((bf16[320,3584]{1,0:T(8,128)(2,1)}, bf16[320,3584]{1,0:T(8,128)(2,1)}, u32[]{:S(2)}, u32[]{:S(2)}) %collective-permute-start.1) | collective-permute-done | bytes 2293792 | tf_op jit(solution)/shard_map/ppermute | solution.py:356
  78.3 10.6 %shard_map.68 = (bf16[640,512]{1,0:T(8,128)(2,1)}, bf16[640,512]{1,0:T(8,128)(2,1)}, f32[8,512]{1,0:T(8,128)}) custom-call(s32[4]{0:T(128)} %pad_add_fusion.starts_ref, bf16[512,3712]{1,0:T(8,128)(2,1)} %all-gather.2.cloned.1.call-done.h_ref.refs_2_, bf16[320,3584]{1,0:T(8,128)(2,1)} %bitcast.67, bf16[320,3584]{1,0:T(8,128)(2,1)} %copy-done.2, ...), custom_call_target="tpu_custom_call" | custom-call | flops 4697620480 | bytes 14155776 | tf_op jit(solution)/shard_map/pallas_call | solution.py:104
  88.9 0.7 slice.26
  89.6 0.6 broadcast_in_dim.7
  90.3 4.3 %all-to-all-start = ((f32[8,12,128]{2,1,0:T(8,128)}), f32[8,12,128]{2,1,0:T(8,128)S(1)}, u32[]{:S(2)}, u32[]{:S(2)}) async-start(f32[8,12,128]{2,1,0:T(8,128)} %broadcast_in_dim.7), calls=%async_computation | async-start | bytes 131072 | tf_op jit(solution)/shard_map/all_to_all | solution.py:23
  94.6 1.3 reshape.101.own_ref
  95.9 7.1 %all-to-all-done.parts_ref = f32[8,12,128]{2,1,0:T(8,128)S(1)} async-done(((f32[8,12,128]{2,1,0:T(8,128)}), f32[8,12,128]{2,1,0:T(8,128)S(1)}, u32[]{:S(2)}, u32[]{:S(2)}) %all-to-all-start) | async-done | bytes 49184 | tf_op jit(solution)/shard_map/all_to_all | solution.py:23
  103.0 0.6 copy-done.1
  103.6 1.5 shard_map.69
  105.1 1.6 broadcast_in_dim.8
  106.7 7.4 %all-to-all-start.1 = ((f32[32,28,128]{2,1,0:T(8,128)}), f32[32,28,128]{2,1,0:T(8,128)S(1)}, u32[]{:S(2)}, u32[]{:S(2)}) async-start(f32[32,28,128]{2,1,0:T(8,128)} %broadcast_in_dim.8), calls=%async_computation.1 | async-start | bytes 1048576 | tf_op jit(solution)/shard_map/all_to_all | solution.py:23
  114.1 0.2 reduce-scatter.2.cloned.1.call-start
  114.3 10.2 %all-to-all-done.1 = f32[32,28,128]{2,1,0:T(8,128)S(1)} async-done(((f32[32,28,128]{2,1,0:T(8,128)}), f32[32,28,128]{2,1,0:T(8,128)S(1)}, u32[]{:S(2)}, u32[]{:S(2)}) %all-to-all-start.1) | async-done | bytes 458784 | tf_op jit(solution)/shard_map/all_to_all | solution.py:23
  124.5 0.3 copy.62
  125.0 0.6 fusion.9.rows_ref
  125.6 10.4 %shard_map.70.refs_6_ = bf16[512,3584]{1,0:T(8,128)(2,1)} custom-call(s32[4]{0:T(128)} %pad_add_fusion.starts_ref, f32[2,512]{1,0:T(2,128)} %fusion.9.rows_ref, bf16[640,512]{1,0:T(8,128)(2,1)} %get-tuple-element.6.first_ref.refs_1_, bf16[640,512]{1,0:T(8,128)(2,1)} %get-tuple-element.7.last_ref, bf16[320,3584]{1,0:T(8,128)(2,1)} %bitcast.68, ...), custom_call_target="tpu_custom_call" | custom-call | flops 4697620480 | bytes 14155776 | tf_op jit(solution)/shard_map/pallas_call | solution.py:212
  136.1 1.0 copy-done.3
  137.5 0.1 fusion.23
  137.6 0.1 copy.68
  137.7 0.1 mul.114
  137.8 0.1 select_reduce_fusion
  137.9 0.1 reshape.106
  138.0 0.1 copy.69
  138.1 0.4 multiply_reduce_fusion
  138.6 0.6 dynamic-slice_bitcast_fusion
  139.3 0.8 copy-done
  140.1 7.6 %shard_map.73 = bf16[320,3584]{1,0:T(8,128)(2,1)} custom-call(s32[4]{0:T(128)} %pad_add_fusion.starts_ref, f32[3,512]{1,0:T(4,128)} %get-tuple-element.27.refs_0_, bf16[640,512]{1,0:T(8,128)(2,1)} %get-tuple-element.6.first_ref.refs_1_, bf16[512,3712]{1,0:T(8,128)(2,1)} %all-gather.2.cloned.1.call-done.h_ref.refs_2_, f32[3,512]{1,0:T(4,128)} %get-tuple-element.26.refs_3_, ...), custom_call_target="tpu_custom_call" | custom-call | flops 2348810240 | bytes 9633792 | tf_op jit(solution)/shard_map/pallas_call | solution.py:281
  147.7 0.2 collective-permute-start.5
  147.9 0.1 mul.118
  148.0 32.2 %reduce-scatter.2.cloned.1.call-done.in_ref = bf16[64,3584]{1,0:T(8,128)(2,1)} async-done(((bf16[512,3584]{1,0:T(8,128)(2,1)}), bf16[64,3584]{1,0:T(8,128)(2,1)}) %reduce-scatter.2.cloned.1.call-update) | async-done | bytes 458768 | tf_op jit(solution)/shard_map/reduce_scatter | solution.py:395
  180.2 2.1 shard_map.71.refs_6_
  182.2 7.3 %all-to-all-start.2 = ((bf16[16,64,224]{2,1,0:T(8,128)(2,1)}), bf16[16,64,224]{2,1,0:T(8,128)(2,1)S(1)}, u32[]{:S(2)}, u32[]{:S(2)}) async-start(bf16[16,64,224]{2,1,0:T(8,128)(2,1)} %shard_map.71.refs_6_), calls=%async_computation.3 | async-start | bytes 1048576 | tf_op jit(solution)/shard_map/all_to_all | solution.py:398
  189.5 7.5 %shard_map.72 = bf16[320,3584]{1,0:T(8,128)(2,1)} custom-call(s32[4]{0:T(128)} %pad_add_fusion.starts_ref, f32[3,512]{1,0:T(4,128)} %get-tuple-element.27.refs_0_, bf16[640,512]{1,0:T(8,128)(2,1)} %get-tuple-element.6.first_ref.refs_1_, bf16[512,3712]{1,0:T(8,128)(2,1)} %all-gather.2.cloned.1.call-done.h_ref.refs_2_, f32[3,512]{1,0:T(4,128)} %get-tuple-element.26.refs_3_, ...), custom_call_target="tpu_custom_call" | custom-call | flops 2348810240 | bytes 9633792 | tf_op jit(solution)/shard_map/pallas_call | solution.py:281
  197.0 3.7 %collective-permute-done.5 = bf16[320,3584]{1,0:T(8,128)(2,1)S(1)} collective-permute-done((bf16[320,3584]{1,0:T(8,128)(2,1)}, bf16[320,3584]{1,0:T(8,128)(2,1)S(1)}, u32[]{:S(2)}, u32[]{:S(2)}) %collective-permute-start.5) | collective-permute-done | bytes 2293792 | tf_op jit(solution)/shard_map/ppermute | solution.py:425
  200.7 3.6 %fusion = bf16[3584,320]{0,1:T(8,128)(2,1)} fusion(bf16[320,3584]{1,0:T(8,128)(2,1)S(1)} %collective-permute-done.5, bf16[320,3584]{1,0:T(8,128)(2,1)} %shard_map.72), kind=kLoop, calls=%fused_computation.1 | loop fusion | flops 4587520 | bytes 6881280 | tf_op jit(solution)/shard_map/transpose | solution.py:428
  204.3 3.0 %all-to-all-done.2 = bf16[16,64,224]{2,1,0:T(8,128)(2,1)S(1)} async-done(((bf16[16,64,224]{2,1,0:T(8,128)(2,1)}), bf16[16,64,224]{2,1,0:T(8,128)(2,1)S(1)}, u32[]{:S(2)}, u32[]{:S(2)}) %all-to-all-start.2) | async-done | bytes 458784 | tf_op jit(solution)/shard_map/all_to_all | solution.py:398
  207.2 0.1 convert_reduce_fusion
  207.3 0.1 fusion.3
  207.4 0.7 copy.70
  (38 shorter events, 0.9 us)
Async XLA Ops:
  7.2 57.6 %all-gather.2.cloned.1.call-start = ((), (), s32[]{:S(2)}) async-start(), calls=%async_computation.4 | async-start | bytes 4276224 | tf_op jit(solution)/shard_map/all_gather | solution.py:358
  10.6 54.7 %collective-permute-start = (bf16[320,3584]{1,0:T(8,128)(2,1)}, bf16[320,3584]{1,0:T(8,128)(2,1)S(1)}, u32[]{:S(2)}, u32[]{:S(2)}) collective-permute-start(bf16[320,3584]{1,0:T(8,128)(2,1)} %bitcast.65), channel_id=1, source_target_pairs={{0,4},{4,0},{1,5},{5,1},{2,6},{6,2},{3,7},{7,3},{8,12},{12,8},{9,1... | collective-permute-start | bytes 6881288 | tf_op jit(solution)/shard_map/ppermute | solution.py:355
  64.8 38.2 %collective-permute-start.3 = (bf16[512,3712]{1,0:T(8,128)(2,1)}, bf16[512,3712]{1,0:T(8,128)(2,1)}, u32[]{:S(2)}, u32[]{:S(2)}) collective-permute-start(bf16[512,3712]{1,0:T(8,128)(2,1)} %all-gather.2.cloned.1.call-done.h_ref.refs_2_), channel_id=1, source_target_pairs={{0,16},{16,0},{1,17},{17,1},{2,18},{18,2},{3,19},{19,3},{4,20},{20... | collective-permute-start | bytes 11403272 | tf_op jit(solution)/shard_map/ppermute | solution.py:374
  64.8 13.5 %collective-permute-start.1 = (bf16[320,3584]{1,0:T(8,128)(2,1)}, bf16[320,3584]{1,0:T(8,128)(2,1)}, u32[]{:S(2)}, u32[]{:S(2)}) collective-permute-start(bf16[320,3584]{1,0:T(8,128)(2,1)} %bitcast.66), channel_id=1, source_target_pairs={{0,16},{16,0},{1,17},{17,1},{2,18},{18,2},{3,19},{19,3},{4,20},{20... | collective-permute-start | bytes 6881288 | tf_op jit(solution)/shard_map/ppermute | solution.py:356
  65.3 13.0 %copy-start.2 = (bf16[320,3584]{1,0:T(8,128)(2,1)}, bf16[320,3584]{1,0:T(8,128)(2,1)S(1)}, u32[]{:S(2)}) copy-start(bf16[320,3584]{1,0:T(8,128)(2,1)S(1)} %collective-permute-done.refs_1_) | copy-start | bytes 6881284
  65.3 13.0 %collective-permute-start.2 = (bf16[320,3584]{1,0:T(8,128)(2,1)S(1)}, bf16[320,3584]{1,0:T(8,128)(2,1)}, u32[]{:S(2)}, u32[]{:S(2)}) collective-permute-start(bf16[320,3584]{1,0:T(8,128)(2,1)S(1)} %collective-permute-done.refs_1_), channel_id=1, source_target_pairs={{0,16},{16,0},{1,17},{17,1},{2,18},{18,2},{3,19},{19,3},{4,20},{20... | collective-permute-start | bytes 6881288 | tf_op jit(solution)/shard_map/ppermute | solution.py:364
  90.3 12.7 %all-to-all-start = ((f32[8,12,128]{2,1,0:T(8,128)}), f32[8,12,128]{2,1,0:T(8,128)S(1)}, u32[]{:S(2)}, u32[]{:S(2)}) async-start(f32[8,12,128]{2,1,0:T(8,128)} %broadcast_in_dim.7), calls=%async_computation | async-start | bytes 131072 | tf_op jit(solution)/shard_map/all_to_all | solution.py:23
  103.0 0.6 copy-start.1
  106.7 17.8 %all-to-all-start.1 = ((f32[32,28,128]{2,1,0:T(8,128)}), f32[32,28,128]{2,1,0:T(8,128)S(1)}, u32[]{:S(2)}, u32[]{:S(2)}) async-start(f32[32,28,128]{2,1,0:T(8,128)} %broadcast_in_dim.8), calls=%async_computation.1 | async-start | bytes 1048576 | tf_op jit(solution)/shard_map/all_to_all | solution.py:23
  114.1 66.1 %reduce-scatter.2.cloned.1.call-start = ((), (), s32[]{:S(2)}) async-start(), calls=%async_computation.5 | async-start | bytes 4128768 | tf_op jit(solution)/shard_map/reduce_scatter | solution.py:395
  136.1 1.1 copy-start.3
  137.2 2.1 collective-permute-start.4
  139.3 0.8 copy-start
  147.7 53.0 %collective-permute-start.5 = (bf16[320,3584]{1,0:T(8,128)(2,1)}, bf16[320,3584]{1,0:T(8,128)(2,1)S(1)}, u32[]{:S(2)}, u32[]{:S(2)}) collective-permute-start(bf16[320,3584]{1,0:T(8,128)(2,1)} %shard_map.73), channel_id=1, source_target_pairs={{0,4},{4,0},{1,5},{5,1},{2,6},{6,2},{3,7},{7,3},{8,12},{12,8},{9,1... | collective-permute-start | bytes 6881288 | tf_op jit(solution)/shard_map/ppermute | solution.py:425
  182.2 25.0 %all-to-all-start.2 = ((bf16[16,64,224]{2,1,0:T(8,128)(2,1)}), bf16[16,64,224]{2,1,0:T(8,128)(2,1)S(1)}, u32[]{:S(2)}, u32[]{:S(2)}) async-start(bf16[16,64,224]{2,1,0:T(8,128)(2,1)} %shard_map.71.refs_6_), calls=%async_computation.3 | async-start | bytes 1048576 | tf_op jit(solution)/shard_map/all_to_all | solution.py:398
Sparse Core Ops, SparseCore 0:
  10.7 54.0 all-gather.1
  136.2 43.9 reduce-scatter.1

commit v11 on v9

--- a/solution.py
+++ b/solution.py
@@ -48,7 +48,7 @@
 
     def body(starts_ref, h_ref, *refs):
         w_refs = refs[:count]
-        *exps_refs, stats_ref, w, h, f, held, exps, sems, out = refs[count:]
+        *exps_refs, stats_ref, _, w, h, f, held, exps, sems, out = refs[count:]
 
         def loads(k):
             span = pl.ds(k * block, block)
@@ -104,9 +104,13 @@
     return pl.pallas_call(
         body,
         in_specs=[SMEM, ANY] + [ANY] * count,
-        out_specs=[ANY, ANY, VMEM],
+        out_specs=[ANY, ANY, VMEM, ANY],
         out_shape=[jax.ShapeDtypeStruct((columns // 2, tokens), BF16)] * 2
-        + [jax.ShapeDtypeStruct((8, tokens), F32)],
+        + [
+            jax.ShapeDtypeStruct((8, tokens), F32),
+            jax.ShapeDtypeStruct(hidden.shape, hidden.dtype),
+        ],
+        input_output_aliases={1: 3},
         scratch_shapes=[
             pltpu.VMEM((STEPS, columns, block), BF16),
             pltpu.VMEM((STEPS, tokens, block), BF16),
@@ -121,6 +125,29 @@
             2 * columns * tokens * features, 2 * features * (columns + tokens) + 2 * columns * tokens
         ),
     )(starts, hidden, *weights)
+
+
+def merge_stats(parts, own, after):
+    lines = own.shape[0] // 8
+
+    def body(parts_ref, own_ref, _, out_ref):
+        tops = parts_ref[:, :lines]
+        top = jnp.max(tops, axis=0)
+        out_ref[:lines] = top
+        out_ref[lines : 2 * lines] = jnp.sum(
+            parts_ref[:, lines : 2 * lines] * jnp.exp(tops - top[None]), axis=0
+        )
+        out_ref[2 * lines : 3 * lines] = jnp.sum(parts_ref[:, 2 * lines :], axis=0)
+        out_ref[3 * lines :] = own_ref[3 * lines : 5 * lines]
+
+    return pl.pallas_call(
+        body,
+        in_specs=[VMEM, VMEM, ANY],
+        out_specs=VMEM,
+        out_shape=jax.ShapeDtypeStruct((5 * lines, LANES), F32),
+        compiler_params=PARAMS,
+        cost_estimate=cost(0, 4 * parts.size),
+    )(parts, own, after)
 
 
 def change_of(starts_ref, rows_ref, exps, low, columns_here, scaled):
@@ -346,15 +373,11 @@
         ]
     ).astype(jnp.int32)
 
-    mine, theirs, stats = logits_and_stats(starts, gathered, weights, columns_here)
+    mine, theirs, stats, gathered = logits_and_stats(starts, gathered, weights, columns_here)
     far_gathered = lax.ppermute(gathered, "core", SWAP)
     far_exps = lax.ppermute(theirs, "core", SWAP)
-    shared = broadcast_gather(stats[:5].reshape(5 * lines, LANES), "z", Z)
-    shared = shared.reshape(Z, 5, lines, LANES)
-    top = jnp.max(shared[:, 0], axis=0)
-    total = jnp.sum(shared[:, 1] * jnp.exp(shared[:, 0] - top[None]), axis=0)
-    known = shared[0, 3:].reshape(2 * lines, LANES)
-    shared = jnp.concatenate([top, total, jnp.sum(shared[:, 2], axis=0), known])
+    lined = stats.reshape(8 * lines, LANES)
+    shared = merge_stats(broadcast_gather(lined[: 3 * lines], "z", Z), lined, far_gathered)
     shared = broadcast_gather(shared, ("xh", "xl", "y"), PLANE)
     shared = shared.reshape(XH, XL, Y, 5, lines, LANES)
     top = jnp.max(shared[:, :, :, 0], axis=(0, 2))

time: 207 us -> 205 us (level)
  blocking collectives: 17.1 us -> 0 us
  starting transfers between devices: 17.5 us -> 25.4 us
  local copies, waits for them, and re-layouts: 4.68 us -> 8.4 us
    all_to_all x1 -> x0, blocking collectives: 17.1 us -> none  [broadcast_gather(): return lax.all_to_all(copies, axes, 0, 0, tiled=True)]
    all_to_all x1 -> x2, starting transfers between devices: 7.4 us -> 15.9 us  [broadcast_gather(): return lax.all_to_all(copies, axes, 0, 0, tiled=True)]
    all_to_all x1 -> x2, waiting for transfers between devices: 6.44 us -> 13.5 us  [broadcast_gather(): return lax.all_to_all(copies, axes, 0, 0, tiled=True)]
    ppermute x1, waiting for transfers between devices: 5.28 us -> 0.27 us  [on_device(): known = jnp.stack([known, lax.ppermute(known, 'core', SWAP)])]
    reduce_scatter x1, waiting for transfers between devices: 27.5 us -> 32.5 us  [on_device(): summed = lax.psum_scatter(partial, 'z', scatter_dimension=0, tiled=True)]
    ppermute x1, waiting for transfers between devices: 8.08 us -> 3.38 us  [on_device(): from_across = lax.ppermute(given, 'xl', SWAP)]
  transfers between devices with their start and end apart: 11 -> 12, of which waited for: 7 -> 9; matrix products, arithmetic and copies ran while one was open for 3% -> 4% of each run, Pallas kernels for 8% -> 9%
where the time goes in v11:
time: 205 us; the launch traced here: 204 us
  waiting for transfers between devices  106 us (52%)
  Pallas kernels  39.9 us (19%)
  starting transfers between devices  25.4 us (12%)
  between operations  14.2 us (7%)
  other arithmetic  9.93 us (5%)
  local copies, waits for them, and re-layouts  8.4 us (4%)
    ppermute x1, waiting for transfers between devices, on_device(): across = lax.ppermute(own, 'xl', SWAP)  50.3 us
    reduce_scatter x1, waiting for transfers between devices, on_device(): summed = lax.psum_scatter(partial, 'z', scatter_dimension=0, tiled=True)  32.5 us
    all_to_all x2, starting transfers between devices, broadcast_gather(): return lax.all_to_all(copies, axes, 0, 0, tiled=True)  15.9 us
    pallas_call x2, Pallas kernels, head_block(): pl.pallas_call(body, in_specs=[SMEM] + [VMEM, ANY, ANY] * count + [ANY],...  15.3 us
    all_to_all x2, waiting for transfers between devices, broadcast_gather(): return lax.all_to_all(copies, axes, 0, 0, tiled=True)  13.5 us
    pallas_call x1, Pallas kernels, logits_and_stats(): pl.pallas_call(body, in_specs=[SMEM, ANY] + [ANY] * count, out_specs=[ANY...  10.6 us
    pallas_call x1, Pallas kernels, partial_product(): pl.pallas_call(body, in_specs=[SMEM, VMEM, ANY, ANY] + [ANY] * count, out...  10.4 us
    all_to_all x1, starting transfers between devices, on_device(): summed = lax.all_to_all(shares, ('xh', 'xl', 'y'), 0, 0, tiled=True)  7.26 us
  transfers between devices with their start and end apart: 12, of which 9 were waited for; matrix products, arithmetic and copies ran while one was open for 4% of the time, Pallas kernels for 9%

profile of v11, /device:TPU:8, one launch (start us, length us, event | category | flops | bytes accessed | tf_op | source)
XLA Modules:
  0.0 204.1 jit_solution(954109684076724521)
XLA Ops:
  7.2 0.7 fusion.17
  7.9 0.7 fusion.23
  8.6 0.1 copy.38
  8.7 1.8 fusion.2
  10.6 1.6 collective-permute-start
  12.2 50.3 %collective-permute-done.refs_1_ = bf16[320,3584]{1,0:T(8,128)(2,1)S(1)} collective-permute-done((bf16[320,3584]{1,0:T(8,128)(2,1)}, bf16[320,3584]{1,0:T(8,128)(2,1)S(1)}, u32[]{:S(2)}, u32[]{:S(2)}) %collective-permute-start) | collective-permute-done | bytes 2293792 | tf_op jit(solution)/shard_map/ppermute | solution.py:358
  62.5 0.7 pad_add_fusion.starts_ref
  63.2 3.9 %collective-permute-done.2.refs_3_ = bf16[320,3584]{1,0:T(8,128)(2,1)} collective-permute-done((bf16[320,3584]{1,0:T(8,128)(2,1)S(1)}, bf16[320,3584]{1,0:T(8,128)(2,1)}, u32[]{:S(2)}, u32[]{:S(2)}) %collective-permute-start.2) | collective-permute-done | bytes 2293792 | tf_op jit(solution)/shard_map/ppermute | solution.py:367
  67.1 10.6 %shard_map.68 = (bf16[640,512]{1,0:T(8,128)(2,1)}, bf16[640,512]{1,0:T(8,128)(2,1)}, f32[8,512]{1,0:T(8,128)}, bf16[512,3712]{1,0:T(8,128)(2,1)}) custom-call(s32[4]{0:T(128)} %pad_add_fusion.starts_ref, bf16[512,3712]{1,0:T(8,128)(2,1)} %all-gather.2.cloned.1.call-done.h_ref, bf16[320,3584]{1,0:T(8,128)(2,1)} %bitcast.70, ...), custom_call_target="tpu_custom_call", output_to_operand_aliasing={{3}: (1, {})} | custom-call | flops 4697620480 | bytes 14155776 | tf_op jit(solution)/shard_map/pallas_call | solution.py:104
  77.7 0.2 collective-permute-start.3
  77.9 0.7 slice.46
  78.7 0.6 broadcast_in_dim.7
  79.3 8.5 %all-to-all-start = ((f32[8,12,128]{2,1,0:T(8,128)}), f32[8,12,128]{2,1,0:T(8,128)S(1)}, u32[]{:S(2)}, u32[]{:S(2)}) async-start(f32[8,12,128]{2,1,0:T(8,128)} %broadcast_in_dim.7), calls=%async_computation | async-start | bytes 131072 | tf_op jit(solution)/shard_map/all_to_all | solution.py:23
  87.8 1.3 reshape.66.own_ref
  89.1 7.1 %all-to-all-done.parts_ref = f32[8,12,128]{2,1,0:T(8,128)S(1)} async-done(((f32[8,12,128]{2,1,0:T(8,128)}), f32[8,12,128]{2,1,0:T(8,128)S(1)}, u32[]{:S(2)}, u32[]{:S(2)}) %all-to-all-start) | async-done | bytes 49184 | tf_op jit(solution)/shard_map/all_to_all | solution.py:23
  96.1 0.6 copy-done.1
  96.8 1.5 shard_map.69
  98.2 1.4 broadcast_in_dim.8
  99.6 7.4 %all-to-all-start.1 = ((f32[16,20,128]{2,1,0:T(8,128)}), f32[16,20,128]{2,1,0:T(8,128)S(1)}, u32[]{:S(2)}, u32[]{:S(2)}) async-start(f32[16,20,128]{2,1,0:T(8,128)} %broadcast_in_dim.8), calls=%async_computation.1 | async-start | bytes 393216 | tf_op jit(solution)/shard_map/all_to_all | solution.py:23
  107.0 0.2 reduce-scatter.2.cloned.1.call-start
  107.2 6.4 %all-to-all-done.1 = f32[16,20,128]{2,1,0:T(8,128)S(1)} async-done(((f32[16,20,128]{2,1,0:T(8,128)}), f32[16,20,128]{2,1,0:T(8,128)S(1)}, u32[]{:S(2)}, u32[]{:S(2)}) %all-to-all-start.1) | async-done | bytes 163872 | tf_op jit(solution)/shard_map/all_to_all | solution.py:23
  113.8 0.8 fusion.27
  114.6 0.6 pad_maximum_fusion.4.rows_ref
  115.2 10.4 %shard_map.70.refs_6_ = bf16[512,3584]{1,0:T(8,128)(2,1)} custom-call(s32[4]{0:T(128)} %pad_add_fusion.starts_ref, f32[2,512]{1,0:T(2,128)} %pad_maximum_fusion.4.rows_ref, bf16[640,512]{1,0:T(8,128)(2,1)} %get-tuple-element.8.first_ref.refs_1_, bf16[640,512]{1,0:T(8,128)(2,1)} %get-tuple-element.9.last_ref, bf16[320,3584]{1,0:T(8,128)(2,1)} %bitcast.71, ...), custom_call_target="tpu_custom_call" | custom-call | flops 4697620480 | bytes 14155776 | tf_op jit(solution)/shard_map/pallas_call | solution.py:215
  125.8 0.1 collective-permute-start.4
  125.9 0.8 copy-done.3
  126.8 0.3 collective-permute-done.4
  127.2 0.1 reduce_sum.58
  127.3 0.1 mul.123
  127.4 0.2 select_reduce_fusion
  127.6 0.1 add.136
  127.6 0.4 multiply_reduce_fusion
  128.1 0.1 reshape.71
  128.2 0.6 slice_bitcast_fusion.1
  128.9 0.8 copy-done
  129.7 7.8 %shard_map.73 = bf16[320,3584]{1,0:T(8,128)(2,1)} custom-call(s32[4]{0:T(128)} %pad_add_fusion.starts_ref, f32[3,512]{1,0:T(4,128)} %get-tuple-element.25.refs_0_, bf16[640,512]{1,0:T(8,128)(2,1)} %get-tuple-element.8.first_ref.refs_1_, bf16[512,3712]{1,0:T(8,128)(2,1)} %get-tuple-element.7.refs_2_, f32[3,512]{1,0:T(4,128)} %get-tuple-element.24.refs_3_, ...), custom_call_target="tpu_custom_call" | custom-call | flops 2348810240 | bytes 9633792 | tf_op jit(solution)/shard_map/pallas_call | solution.py:284
  137.5 0.1 collective-permute-start.6
  137.6 0.1 mul.127
  137.7 32.5 %reduce-scatter.2.cloned.1.call-done.in_ref = bf16[64,3584]{1,0:T(8,128)(2,1)} async-done(((bf16[512,3584]{1,0:T(8,128)(2,1)}), bf16[64,3584]{1,0:T(8,128)(2,1)}) %reduce-scatter.2.cloned.1.call-update) | async-done | bytes 458768 | tf_op jit(solution)/shard_map/reduce_scatter | solution.py:392
  170.2 2.0 %shard_map.71.refs_6_ = bf16[16,64,224]{2,1,0:T(8,128)(2,1)} custom-call(bf16[64,3584]{1,0:T(8,128)(2,1)} %reduce-scatter.2.cloned.1.call-done.in_ref), custom_call_target="tpu_custom_call" | custom-call | bytes 917504 | tf_op jit(solution)/shard_map/pallas_call | solution.py:314
  172.3 7.3 %all-to-all-start.2 = ((bf16[16,64,224]{2,1,0:T(8,128)(2,1)}), bf16[16,64,224]{2,1,0:T(8,128)(2,1)S(1)}, u32[]{:S(2)}, u32[]{:S(2)}) async-start(bf16[16,64,224]{2,1,0:T(8,128)(2,1)} %shard_map.71.refs_6_), calls=%async_computation.3 | async-start | bytes 1048576 | tf_op jit(solution)/shard_map/all_to_all | solution.py:395
  179.5 7.5 %shard_map.72 = bf16[320,3584]{1,0:T(8,128)(2,1)} custom-call(s32[4]{0:T(128)} %pad_add_fusion.starts_ref, f32[3,512]{1,0:T(4,128)} %get-tuple-element.25.refs_0_, bf16[640,512]{1,0:T(8,128)(2,1)} %get-tuple-element.8.first_ref.refs_1_, bf16[512,3712]{1,0:T(8,128)(2,1)} %get-tuple-element.7.refs_2_, f32[3,512]{1,0:T(4,128)} %get-tuple-element.24.refs_3_, ...), custom_call_target="tpu_custom_call" | custom-call | flops 2348810240 | bytes 9633792 | tf_op jit(solution)/shard_map/pallas_call | solution.py:284
  187.1 3.4 %collective-permute-done.6 = bf16[320,3584]{1,0:T(8,128)(2,1)S(1)} collective-permute-done((bf16[320,3584]{1,0:T(8,128)(2,1)}, bf16[320,3584]{1,0:T(8,128)(2,1)S(1)}, u32[]{:S(2)}, u32[]{:S(2)}) %collective-permute-start.6) | collective-permute-done | bytes 2293792 | tf_op jit(solution)/shard_map/ppermute | solution.py:423
  190.4 3.6 %fusion = bf16[3584,320]{0,1:T(8,128)(2,1)} fusion(bf16[320,3584]{1,0:T(8,128)(2,1)S(1)} %collective-permute-done.6, bf16[320,3584]{1,0:T(8,128)(2,1)} %shard_map.72), kind=kLoop, calls=%fused_computation.1 | loop fusion | flops 4587520 | bytes 6881280 | tf_op jit(solution)/shard_map/transpose | solution.py:426
  194.0 2.4 %all-to-all-done.2 = bf16[16,64,224]{2,1,0:T(8,128)(2,1)S(1)} async-done(((bf16[16,64,224]{2,1,0:T(8,128)(2,1)}), bf16[16,64,224]{2,1,0:T(8,128)(2,1)S(1)}, u32[]{:S(2)}, u32[]{:S(2)}) %all-to-all-start.2) | async-done | bytes 458784 | tf_op jit(solution)/shard_map/all_to_all | solution.py:395
  196.4 0.1 convert_reduce_fusion
  196.5 0.1 fusion.3
  196.5 0.7 copy.42
  (34 shorter events, 0.7 us)
Async XLA Ops:
  7.2 59.9 %all-gather.2.cloned.1.call-start = ((), (), s32[]{:S(2)}) async-start(), calls=%async_computation.4 | async-start | bytes 4276224 | tf_op jit(solution)/shard_map/all_gather | solution.py:361
  10.6 51.9 %collective-permute-start = (bf16[320,3584]{1,0:T(8,128)(2,1)}, bf16[320,3584]{1,0:T(8,128)(2,1)S(1)}, u32[]{:S(2)}, u32[]{:S(2)}) collective-permute-start(bf16[320,3584]{1,0:T(8,128)(2,1)} %bitcast.68), channel_id=1, source_target_pairs={{0,4},{4,0},{1,5},{5,1},{2,6},{6,2},{3,7},{7,3},{8,12},{12,8},{9,1... | collective-permute-start | bytes 6881288 | tf_op jit(solution)/shard_map/ppermute | solution.py:358
  12.2 51.0 %collective-permute-start.1 = (bf16[320,3584]{1,0:T(8,128)(2,1)}, bf16[320,3584]{1,0:T(8,128)(2,1)}, u32[]{:S(2)}, u32[]{:S(2)}) collective-permute-start(bf16[320,3584]{1,0:T(8,128)(2,1)} %bitcast.69), channel_id=1, source_target_pairs={{0,16},{16,0},{1,17},{17,1},{2,18},{18,2},{3,19},{19,3},{4,20},{20... | collective-permute-start | bytes 6881288 | tf_op jit(solution)/shard_map/ppermute | solution.py:359
  62.5 4.6 %copy-start.2 = (bf16[320,3584]{1,0:T(8,128)(2,1)}, bf16[320,3584]{1,0:T(8,128)(2,1)S(1)}, u32[]{:S(2)}) copy-start(bf16[320,3584]{1,0:T(8,128)(2,1)S(1)} %collective-permute-done.refs_1_) | copy-start | bytes 6881284
  62.5 4.6 %collective-permute-start.2 = (bf16[320,3584]{1,0:T(8,128)(2,1)S(1)}, bf16[320,3584]{1,0:T(8,128)(2,1)}, u32[]{:S(2)}, u32[]{:S(2)}) collective-permute-start(bf16[320,3584]{1,0:T(8,128)(2,1)S(1)} %collective-permute-done.refs_1_), channel_id=1, source_target_pairs={{0,16},{16,0},{1,17},{17,1},{2,18},{18,2},{3,19},{19,3},{4,20},{20... | collective-permute-start | bytes 6881288 | tf_op jit(solution)/shard_map/ppermute | solution.py:367
  77.7 18.4 %collective-permute-start.3 = (bf16[512,3712]{1,0:T(8,128)(2,1)}, bf16[512,3712]{1,0:T(8,128)(2,1)}, u32[]{:S(2)}, u32[]{:S(2)}) collective-permute-start(bf16[512,3712]{1,0:T(8,128)(2,1)} %get-tuple-element.7.refs_2_), channel_id=1, source_target_pairs={{0,16},{16,0},{1,17},{17,1},{2,18},{18,2},{3,19},{19,3},{4,20},{20... | collective-permute-start | bytes 11403272 | tf_op jit(solution)/shard_map/ppermute | solution.py:377
  79.3 16.9 %all-to-all-start = ((f32[8,12,128]{2,1,0:T(8,128)}), f32[8,12,128]{2,1,0:T(8,128)S(1)}, u32[]{:S(2)}, u32[]{:S(2)}) async-start(f32[8,12,128]{2,1,0:T(8,128)} %broadcast_in_dim.7), calls=%async_computation | async-start | bytes 131072 | tf_op jit(solution)/shard_map/all_to_all | solution.py:23
  96.1 0.6 copy-start.1
  99.6 14.1 %all-to-all-start.1 = ((f32[16,20,128]{2,1,0:T(8,128)}), f32[16,20,128]{2,1,0:T(8,128)S(1)}, u32[]{:S(2)}, u32[]{:S(2)}) async-start(f32[16,20,128]{2,1,0:T(8,128)} %broadcast_in_dim.8), calls=%async_computation.1 | async-start | bytes 393216 | tf_op jit(solution)/shard_map/all_to_all | solution.py:23
  107.0 63.2 %reduce-scatter.2.cloned.1.call-start = ((), (), s32[]{:S(2)}) async-start(), calls=%async_computation.5 | async-start | bytes 4128768 | tf_op jit(solution)/shard_map/reduce_scatter | solution.py:392
  125.7 1.1 copy-start.3
  125.8 1.3 collective-permute-start.4
  126.8 2.1 %collective-permute-start.5 = (bf16[640,512]{1,0:T(8,128)(2,1)S(1)}, bf16[640,512]{1,0:T(8,128)(2,1)S(1)}, u32[]{:S(2)}, u32[]{:S(2)}) collective-permute-start(bf16[640,512]{1,0:T(8,128)(2,1)S(1)} %copy-done.3), channel_id=1, source_target_pairs={{0,16},{16,0},{1,17},{17,1},{2,18},{18,2},{3,19},{19,3},{4,20},{20... | collective-permute-start | bytes 1966088 | tf_op jit(solution)/shard_map/ppermute | solution.py:378
  128.9 0.8 copy-start
  137.5 53.0 %collective-permute-start.6 = (bf16[320,3584]{1,0:T(8,128)(2,1)}, bf16[320,3584]{1,0:T(8,128)(2,1)S(1)}, u32[]{:S(2)}, u32[]{:S(2)}) collective-permute-start(bf16[320,3584]{1,0:T(8,128)(2,1)} %shard_map.73), channel_id=1, source_target_pairs={{0,4},{4,0},{1,5},{5,1},{2,6},{6,2},{3,7},{7,3},{8,12},{12,8},{9,1... | collective-permute-start | bytes 6881288 | tf_op jit(solution)/shard_map/ppermute | solution.py:423
  172.3 24.1 %all-to-all-start.2 = ((bf16[16,64,224]{2,1,0:T(8,128)(2,1)}), bf16[16,64,224]{2,1,0:T(8,128)(2,1)S(1)}, u32[]{:S(2)}, u32[]{:S(2)}) async-start(bf16[16,64,224]{2,1,0:T(8,128)(2,1)} %shard_map.71.refs_6_), calls=%async_computation.3 | async-start | bytes 1048576 | tf_op jit(solution)/shard_map/all_to_all | solution.py:395
Sparse Core Ops, SparseCore 0:
  10.7 54.0 all-gather.1
  125.8 44.3 reduce-scatter.1

commit v12 on v11

--- a/solution.py
+++ b/solution.py
@@ -131,20 +131,25 @@
     lines = own.shape[0] // 8
 
     def body(parts_ref, own_ref, _, out_ref):
+        def field(number):
+            return own_ref[number * lines : (number + 1) * lines]
+
         tops = parts_ref[:, :lines]
         top = jnp.max(tops, axis=0)
-        out_ref[:lines] = top
-        out_ref[lines : 2 * lines] = jnp.sum(
-            parts_ref[:, lines : 2 * lines] * jnp.exp(tops - top[None]), axis=0
-        )
-        out_ref[2 * lines : 3 * lines] = jnp.sum(parts_ref[:, 2 * lines :], axis=0)
-        out_ref[3 * lines :] = own_ref[3 * lines : 5 * lines]
+        sums = parts_ref[:, lines : 2 * lines] * jnp.exp(tops - top[None])
+        norm = top + jnp.log(jnp.sum(sums, axis=0))
+        picked = jnp.sum(parts_ref[:, 2 * lines :], axis=0)
+        mask = field(3)
+        out_ref[:lines] = field(5)
+        out_ref[lines : 2 * lines] = jnp.exp(field(0) - norm)
+        out_ref[2 * lines : 3 * lines] = mask
+        out_ref[3 * lines :] = mask * (picked - norm - field(4))
 
     return pl.pallas_call(
         body,
         in_specs=[VMEM, VMEM, ANY],
         out_specs=VMEM,
-        out_shape=jax.ShapeDtypeStruct((5 * lines, LANES), F32),
+        out_shape=jax.ShapeDtypeStruct((4 * lines, LANES), F32),
         compiler_params=PARAMS,
         cost_estimate=cost(0, 4 * parts.size),
     )(parts, own, after)
@@ -377,18 +382,10 @@
     far_gathered = lax.ppermute(gathered, "core", SWAP)
     far_exps = lax.ppermute(theirs, "core", SWAP)
     lined = stats.reshape(8 * lines, LANES)
-    shared = merge_stats(broadcast_gather(lined[: 3 * lines], "z", Z), lined, far_gathered)
-    shared = broadcast_gather(shared, ("xh", "xl", "y"), PLANE)
-    shared = shared.reshape(XH, XL, Y, 5, lines, LANES)
-    top = jnp.max(shared[:, :, :, 0], axis=(0, 2))
-    shrink = jnp.exp(shared[:, :, :, 0] - top[None, :, None])
-    total = jnp.sum(shared[:, :, :, 1] * shrink, axis=(0, 2))
-    picked = jnp.sum(shared[:, :, :, 2], axis=(0, 2))
-    norms = top + jnp.log(total)
-    factor = jnp.exp(stats[0] - pick_one(norms, side).reshape(here))
-    token_rows = jnp.stack([stats[5], factor])
-
-    partial = partial_product(starts, token_rows, (mine, theirs), weights, columns_here)
+    shared = broadcast_gather(lined[: 3 * lines], ("z", "xh", "y"), Z * XH * Y)
+    known = merge_stats(shared, lined, far_gathered).reshape(4, here)
+
+    partial = partial_product(starts, known, (mine, theirs), weights, columns_here)
     summed = lax.psum_scatter(partial, "z", scatter_dimension=0, tiled=True)
     cut = features // PLANE
     shares = cut_features(summed, cut)
@@ -396,28 +393,27 @@
     summed = summed.reshape(XH, XL, Y, rows, cut).astype(F32)
     summed = jnp.sum(summed, axis=(0, 2)).reshape(own_rows, cut)
 
-    mask, teacher = shared[0, :, 0, 3], shared[0, :, 0, 4]
-    ratio = mask * (picked - norms - teacher)
-    known = jnp.concatenate([part.reshape(XL, here) for part in (mask, ratio)] + [token_rows])
     known = jnp.stack([known, lax.ppermute(known, "core", SWAP)])
     mask, ratio = (
-        part.reshape(CORES, XL, Z, rows) for part in (known[:, :XL], known[:, XL : 2 * XL])
+        part.reshape(CORES, XL, Z, rows)
+        for part in jnp.stack([known[:, 2:], lax.ppermute(known[:, 2:], "xl", SWAP)], axis=1).transpose(2, 0, 1, 3)
     )
     steps = jnp.arange(rows, dtype=jnp.int32)
     later = (steps[None, :] >= steps[:, None]).astype(F32)
     within = jnp.sum(ratio[..., None, :] * later, axis=-1)
     parts = jnp.sum(ratio, axis=-1).reshape(-1)
-    number = jnp.arange(XL * Z, dtype=jnp.int32)
-    order = number % Z * (CORES * XL) + number // Z
-    order = jnp.concatenate([order + core * XL, order + (1 - core) * XL])
+    order = jnp.arange(Z, dtype=jnp.int32) * (CORES * XL)
+    order = jnp.concatenate(
+        [order + (c * XL + s) for c in (core, 1 - core) for s in (side, 1 - side)]
+    )
     beyond = jnp.sum(parts[None, :] * (order[None, :] > order[:, None]), axis=1)
     scales = mask * (within + beyond.reshape(CORES, XL, Z, 1)) / float(tokens)
 
-    own_scale = lax.dynamic_index_in_dim(scales[0], z, 1, False).reshape(own_rows)
+    own_scale = lax.dynamic_index_in_dim(scales[0], z, 1, False)
+    own_scale = jnp.where(side == 0, own_scale, own_scale[::-1]).reshape(own_rows)
     hidden_grad = summed * own_scale[:, None]
 
-    scale = lax.dynamic_index_in_dim(scales, side, 1, False).reshape(CORES, 1, here)
-    rows_of = jnp.concatenate([known[:, 2 * XL :], scale], axis=1)
+    rows_of = jnp.concatenate([known[:, :2], scales[:, 0].reshape(CORES, 1, here)], axis=1)
     sides = [(rows_of[0], mine, gathered), (rows_of[1], far_exps, far_gathered)]
     given = head_block(starts, sides, columns_here, columns_here, features, partial)
     from_across = lax.ppermute(given, "xl", SWAP)

time: 205 us -> 210 us (1.024)
  waiting for transfers between devices: 106 us -> 111 us
    all_to_all x2 -> x1, waiting for transfers between devices: 13.5 us -> 16.7 us  [broadcast_gather(): return lax.all_to_all(copies, axes, 0, 0, tiled=True)]
    ppermute x0 -> x1, waiting for transfers between devices: none -> 3.05 us  [on_device(): lax.ppermute(known[:, 2:], 'xl', SWAP)]
    reduce_scatter x1, waiting for transfers between devices: 32.5 us -> 29.7 us  [on_device(): summed = lax.psum_scatter(partial, 'z', scatter_dimension=0, tiled=True)]
    ppermute x1, waiting for transfers between devices: 3.38 us -> 5.77 us  [on_device(): from_across = lax.ppermute(given, 'xl', SWAP)]
    all_to_all x2 -> x1, starting transfers between devices: 15.9 us -> 14.6 us  [broadcast_gather(): return lax.all_to_all(copies, axes, 0, 0, tiled=True)]
  transfers between devices with their start and end apart: 12 -> 12, of which waited for: 9 -> 8; matrix products, arithmetic and copies ran while one was open for 4% -> 4% of each run, Pallas kernels for 9% -> 8%
where the time goes in v12:
time: 210 us; the launch traced here: 208 us
  waiting for transfers between devices  111 us (53%)
  Pallas kernels  39.9 us (19%)
  starting transfers between devices  25.4 us (12%)
  between operations  14.2 us (7%)
  local copies, waits for them, and re-layouts  8.85 us (4%)
  other arithmetic  8.49 us (4%)
    ppermute x1, waiting for transfers between devices, on_device(): across = lax.ppermute(own, 'xl', SWAP)  50.3 us
    reduce_scatter x1, waiting for transfers between devices, on_device(): summed = lax.psum_scatter(partial, 'z', scatter_dimension=0, tiled=True)  29.7 us
    all_to_all x1, waiting for transfers between devices, broadcast_gather(): return lax.all_to_all(copies, axes, 0, 0, tiled=True)  16.7 us
    pallas_call x2, Pallas kernels, head_block(): pl.pallas_call(body, in_specs=[SMEM] + [VMEM, ANY, ANY] * count + [ANY],...  15 us
    all_to_all x1, starting transfers between devices, broadcast_gather(): return lax.all_to_all(copies, axes, 0, 0, tiled=True)  14.6 us
    pallas_call x1, Pallas kernels, logits_and_stats(): pl.pallas_call(body, in_specs=[SMEM, ANY] + [ANY] * count, out_specs=[ANY...  10.6 us
    pallas_call x1, Pallas kernels, partial_product(): pl.pallas_call(body, in_specs=[SMEM, VMEM, ANY, ANY] + [ANY] * count, out...  10.5 us
    all_to_all x1, starting transfers between devices, on_device(): summed = lax.all_to_all(shares, ('xh', 'xl', 'y'), 0, 0, tiled=True)  7.26 us
  transfers between devices with their start and end apart: 12, of which 8 were waited for; matrix products, arithmetic and copies ran while one was open for 4% of the time, Pallas kernels for 8%

profile of v12, /device:TPU:8, one launch (start us, length us, event | category | flops | bytes accessed | tf_op | source)
XLA Modules:
  0.0 208.4 jit_solution(2703687292104349946)
XLA Ops:
  7.2 0.7 fusion.11
  7.9 0.7 fusion.17
  8.6 0.1 copy.35
  8.7 1.8 fusion.2
  10.6 1.6 collective-permute-start
  12.2 50.3 %collective-permute-done.refs_1_ = bf16[320,3584]{1,0:T(8,128)(2,1)S(1)} collective-permute-done((bf16[320,3584]{1,0:T(8,128)(2,1)}, bf16[320,3584]{1,0:T(8,128)(2,1)S(1)}, u32[]{:S(2)}, u32[]{:S(2)}) %collective-permute-start) | collective-permute-done | bytes 2293792 | tf_op jit(solution)/shard_map/ppermute | solution.py:363
  62.5 0.7 pad_add_fusion.starts_ref
  63.2 3.8 %collective-permute-done.2.refs_3_ = bf16[320,3584]{1,0:T(8,128)(2,1)} collective-permute-done((bf16[320,3584]{1,0:T(8,128)(2,1)S(1)}, bf16[320,3584]{1,0:T(8,128)(2,1)}, u32[]{:S(2)}, u32[]{:S(2)}) %collective-permute-start.2) | collective-permute-done | bytes 2293792 | tf_op jit(solution)/shard_map/ppermute | solution.py:372
  67.0 10.6 %shard_map.68 = (bf16[640,512]{1,0:T(8,128)(2,1)}, bf16[640,512]{1,0:T(8,128)(2,1)}, f32[8,512]{1,0:T(8,128)}, bf16[512,3712]{1,0:T(8,128)(2,1)}) custom-call(s32[4]{0:T(128)} %pad_add_fusion.starts_ref, bf16[512,3712]{1,0:T(8,128)(2,1)} %all-gather.2.cloned.1.call-done.h_ref, bf16[320,3584]{1,0:T(8,128)(2,1)} %bitcast.53, ...), custom_call_target="tpu_custom_call", output_to_operand_aliasing={{3}: (1, {})} | custom-call | flops 4697620480 | bytes 14155776 | tf_op jit(solution)/shard_map/pallas_call | solution.py:104
  77.7 0.2 collective-permute-start.3
  77.9 0.7 slice.23
  78.6 0.8 broadcast_in_dim.5
  79.5 14.6 %all-to-all-start = ((f32[64,12,128]{2,1,0:T(8,128)}), f32[64,12,128]{2,1,0:T(8,128)S(1)}, u32[]{:S(2)}, u32[]{:S(2)}) async-start(f32[64,12,128]{2,1,0:T(8,128)} %broadcast_in_dim.5), calls=%async_computation | async-start | bytes 1048576 | tf_op jit(solution)/shard_map/all_to_all | solution.py:23
  94.0 0.2 reduce-scatter.2.cloned.1.call-start
  94.3 1.3 reshape.41.own_ref
  95.6 16.7 %all-to-all-done.parts_ref = f32[64,12,128]{2,1,0:T(8,128)S(1)} async-done(((f32[64,12,128]{2,1,0:T(8,128)}), f32[64,12,128]{2,1,0:T(8,128)S(1)}, u32[]{:S(2)}, u32[]{:S(2)}) %all-to-all-start) | async-done | bytes 393248 | tf_op jit(solution)/shard_map/all_to_all | solution.py:23
  112.3 0.8 copy-done.1
  113.1 1.8 shard_map.69
  114.8 1.3 reshape.42.rows_ref
  116.1 10.5 %shard_map.70.refs_6_ = bf16[512,3584]{1,0:T(8,128)(2,1)} custom-call(s32[4]{0:T(128)} %pad_add_fusion.starts_ref, f32[4,512]{1,0:T(4,128)} %reshape.42.rows_ref, bf16[640,512]{1,0:T(8,128)(2,1)} %get-tuple-element.8.first_ref.refs_1_, bf16[640,512]{1,0:T(8,128)(2,1)} %get-tuple-element.9.last_ref, bf16[320,3584]{1,0:T(8,128)(2,1)} %bitcast.54, ...), custom_call_target="tpu_custom_call" | custom-call | flops 4697620480 | bytes 14155776 | tf_op jit(solution)/shard_map/pallas_call | solution.py:220
  126.7 0.6 copy-done.3
  127.4 0.3 copy-done.5
  127.7 0.2 collective-permute-start.6
  127.9 0.5 collective-permute-done.4
  128.5 0.7 collective-permute-start.5
  129.2 3.1 %collective-permute-done.5 = f32[2,2,512]{2,1,0:T(2,128)S(1)} collective-permute-done((f32[2,2,512]{2,1,0:T(2,128)S(1)}, f32[2,2,512]{2,1,0:T(2,128)S(1)}, u32[]{:S(2)}, u32[]{:S(2)}) %collective-permute-start.5) | collective-permute-done | bytes 8224 | tf_op jit(solution)/shard_map/ppermute | solution.py:399
  132.3 0.1 reshape_unstack.4
  132.5 0.1 reduce_sum.38
  132.6 0.1 mul.120
  132.6 0.2 select_reduce_fusion
  132.8 0.1 add.139
  132.9 0.4 multiply_reduce_fusion
  133.3 0.1 reshape_squeeze.3
  133.4 0.6 slice_bitcast_fusion
  134.1 0.8 copy-done
  134.9 7.5 %shard_map.73 = bf16[320,3584]{1,0:T(8,128)(2,1)} custom-call(s32[4]{0:T(128)} %pad_add_fusion.starts_ref, f32[3,512]{1,0:T(4,128)} %get-tuple-element.19.refs_0_, bf16[640,512]{1,0:T(8,128)(2,1)} %get-tuple-element.8.first_ref.refs_1_, bf16[512,3712]{1,0:T(8,128)(2,1)} %get-tuple-element.7.refs_2_, f32[3,512]{1,0:T(4,128)} %get-tuple-element.18.refs_3_, ...), custom_call_target="tpu_custom_call" | custom-call | flops 2348810240 | bytes 9633792 | tf_op jit(solution)/shard_map/pallas_call | solution.py:289
  142.4 0.7 collective-permute-start.7
  143.1 0.1 mul.124
  143.2 29.7 %reduce-scatter.2.cloned.1.call-done.in_ref = bf16[64,3584]{1,0:T(8,128)(2,1)} async-done(((bf16[512,3584]{1,0:T(8,128)(2,1)}), bf16[64,3584]{1,0:T(8,128)(2,1)}) %reduce-scatter.2.cloned.1.call-update) | async-done | bytes 458768 | tf_op jit(solution)/shard_map/reduce_scatter | solution.py:389
  172.9 2.1 shard_map.71.refs_6_
  174.9 7.3 %all-to-all-start.1 = ((bf16[16,64,224]{2,1,0:T(8,128)(2,1)}), bf16[16,64,224]{2,1,0:T(8,128)(2,1)S(1)}, u32[]{:S(2)}, u32[]{:S(2)}) async-start(bf16[16,64,224]{2,1,0:T(8,128)(2,1)} %shard_map.71.refs_6_), calls=%async_computation.2 | async-start | bytes 1048576 | tf_op jit(solution)/shard_map/all_to_all | solution.py:392
  182.2 7.5 %shard_map.72 = bf16[320,3584]{1,0:T(8,128)(2,1)} custom-call(s32[4]{0:T(128)} %pad_add_fusion.starts_ref, f32[3,512]{1,0:T(4,128)} %get-tuple-element.19.refs_0_, bf16[640,512]{1,0:T(8,128)(2,1)} %get-tuple-element.8.first_ref.refs_1_, bf16[512,3712]{1,0:T(8,128)(2,1)} %get-tuple-element.7.refs_2_, f32[3,512]{1,0:T(4,128)} %get-tuple-element.18.refs_3_, ...), custom_call_target="tpu_custom_call" | custom-call | flops 2348810240 | bytes 9633792 | tf_op jit(solution)/shard_map/pallas_call | solution.py:289
  189.7 5.8 %collective-permute-done.7 = bf16[320,3584]{1,0:T(8,128)(2,1)S(1)} collective-permute-done((bf16[320,3584]{1,0:T(8,128)(2,1)}, bf16[320,3584]{1,0:T(8,128)(2,1)S(1)}, u32[]{:S(2)}, u32[]{:S(2)}) %collective-permute-start.7) | collective-permute-done | bytes 2293792 | tf_op jit(solution)/shard_map/ppermute | solution.py:419
  195.5 3.6 %fusion = bf16[3584,320]{0,1:T(8,128)(2,1)} fusion(bf16[320,3584]{1,0:T(8,128)(2,1)S(1)} %collective-permute-done.7, bf16[320,3584]{1,0:T(8,128)(2,1)} %shard_map.72), kind=kLoop, calls=%fused_computation.1 | loop fusion | flops 4587520 | bytes 6881280 | tf_op jit(solution)/shard_map/transpose | solution.py:422
  199.0 1.6 all-to-all-done.1
  200.6 0.1 convert_reduce_fusion
  200.7 0.1 fusion.3
  200.8 0.7 copy.39
  (38 shorter events, 0.6 us)
Async XLA Ops:
  7.2 59.9 %all-gather.2.cloned.1.call-start = ((), (), s32[]{:S(2)}) async-start(), calls=%async_computation.3 | async-start | bytes 4276224 | tf_op jit(solution)/shard_map/all_gather | solution.py:366
  10.6 51.9 %collective-permute-start = (bf16[320,3584]{1,0:T(8,128)(2,1)}, bf16[320,3584]{1,0:T(8,128)(2,1)S(1)}, u32[]{:S(2)}, u32[]{:S(2)}) collective-permute-start(bf16[320,3584]{1,0:T(8,128)(2,1)} %bitcast.51), channel_id=1, source_target_pairs={{0,4},{4,0},{1,5},{5,1},{2,6},{6,2},{3,7},{7,3},{8,12},{12,8},{9,1... | collective-permute-start | bytes 6881288 | tf_op jit(solution)/shard_map/ppermute | solution.py:363
  12.2 51.0 %collective-permute-start.1 = (bf16[320,3584]{1,0:T(8,128)(2,1)}, bf16[320,3584]{1,0:T(8,128)(2,1)}, u32[]{:S(2)}, u32[]{:S(2)}) collective-permute-start(bf16[320,3584]{1,0:T(8,128)(2,1)} %bitcast.52), channel_id=1, source_target_pairs={{0,16},{16,0},{1,17},{17,1},{2,18},{18,2},{3,19},{19,3},{4,20},{20... | collective-permute-start | bytes 6881288 | tf_op jit(solution)/shard_map/ppermute | solution.py:364
  62.5 4.6 %copy-start.4 = (bf16[320,3584]{1,0:T(8,128)(2,1)}, bf16[320,3584]{1,0:T(8,128)(2,1)S(1)}, u32[]{:S(2)}) copy-start(bf16[320,3584]{1,0:T(8,128)(2,1)S(1)} %collective-permute-done.refs_1_) | copy-start | bytes 6881284
  62.5 4.6 %collective-permute-start.2 = (bf16[320,3584]{1,0:T(8,128)(2,1)S(1)}, bf16[320,3584]{1,0:T(8,128)(2,1)}, u32[]{:S(2)}, u32[]{:S(2)}) collective-permute-start(bf16[320,3584]{1,0:T(8,128)(2,1)S(1)} %collective-permute-done.refs_1_), channel_id=1, source_target_pairs={{0,16},{16,0},{1,17},{17,1},{2,18},{18,2},{3,19},{19,3},{4,20},{20... | collective-permute-start | bytes 6881288 | tf_op jit(solution)/shard_map/ppermute | solution.py:372
  77.7 34.6 %collective-permute-start.3 = (bf16[512,3712]{1,0:T(8,128)(2,1)}, bf16[512,3712]{1,0:T(8,128)(2,1)}, u32[]{:S(2)}, u32[]{:S(2)}) collective-permute-start(bf16[512,3712]{1,0:T(8,128)(2,1)} %get-tuple-element.7.refs_2_), channel_id=1, source_target_pairs={{0,16},{16,0},{1,17},{17,1},{2,18},{18,2},{3,19},{19,3},{4,20},{20... | collective-permute-start | bytes 11403272 | tf_op jit(solution)/shard_map/ppermute | solution.py:382
  79.5 32.8 %all-to-all-start = ((f32[64,12,128]{2,1,0:T(8,128)}), f32[64,12,128]{2,1,0:T(8,128)S(1)}, u32[]{:S(2)}, u32[]{:S(2)}) async-start(f32[64,12,128]{2,1,0:T(8,128)} %broadcast_in_dim.5), calls=%async_computation | async-start | bytes 1048576 | tf_op jit(solution)/shard_map/all_to_all | solution.py:23
  94.0 78.8 %reduce-scatter.2.cloned.1.call-start = ((), (), s32[]{:S(2)}) async-start(), calls=%async_computation.4 | async-start | bytes 4128768 | tf_op jit(solution)/shard_map/reduce_scatter | solution.py:389
  112.3 0.8 copy-start.1
  126.6 0.7 copy-start.3
  126.6 1.1 copy-start.5
  126.6 1.3 copy-start.2
  127.3 1.2 collective-permute-start.4
  127.7 6.3 %collective-permute-start.6 = (bf16[640,512]{1,0:T(8,128)(2,1)S(1)}, bf16[640,512]{1,0:T(8,128)(2,1)S(1)}, u32[]{:S(2)}, u32[]{:S(2)}) collective-permute-start(bf16[640,512]{1,0:T(8,128)(2,1)S(1)} %copy-done.5), channel_id=1, source_target_pairs={{0,16},{16,0},{1,17},{17,1},{2,18},{18,2},{3,19},{19,3},{4,20},{20... | collective-permute-start | bytes 1966088 | tf_op jit(solution)/shard_map/ppermute | solution.py:383
  128.5 3.7 %collective-permute-start.5 = (f32[2,2,512]{2,1,0:T(2,128)S(1)}, f32[2,2,512]{2,1,0:T(2,128)S(1)}, u32[]{:S(2)}, u32[]{:S(2)}) collective-permute-start(f32[2,2,512]{2,1,0:T(2,128)S(1)} %fusion.7), channel_id=1, source_target_pairs={{0,4},{4,0},{1,5},{5,1},{2,6},{6,2},{3,7},{7,3},{8,12},{12,8},{9,1... | collective-permute-start | bytes 24584 | tf_op jit(solution)/shard_map/ppermute | solution.py:399
  134.1 0.8 copy-start
  142.4 53.1 %collective-permute-start.7 = (bf16[320,3584]{1,0:T(8,128)(2,1)}, bf16[320,3584]{1,0:T(8,128)(2,1)S(1)}, u32[]{:S(2)}, u32[]{:S(2)}) collective-permute-start(bf16[320,3584]{1,0:T(8,128)(2,1)} %shard_map.73), channel_id=1, source_target_pairs={{0,4},{4,0},{1,5},{5,1},{2,6},{6,2},{3,7},{7,3},{8,12},{12,8},{9,1... | collective-permute-start | bytes 6881288 | tf_op jit(solution)/shard_map/ppermute | solution.py:419
  174.9 25.7 %all-to-all-start.1 = ((bf16[16,64,224]{2,1,0:T(8,128)(2,1)}), bf16[16,64,224]{2,1,0:T(8,128)(2,1)S(1)}, u32[]{:S(2)}, u32[]{:S(2)}) async-start(bf16[16,64,224]{2,1,0:T(8,128)(2,1)} %shard_map.71.refs_6_), calls=%async_computation.2 | async-start | bytes 1048576 | tf_op jit(solution)/shard_map/all_to_all | solution.py:392
Sparse Core Ops, SparseCore 0:
  10.7 54.0 all-gather.1
  126.8 46.0 reduce-scatter.1

commit v13 on v11

--- a/solution.py
+++ b/solution.py
@@ -130,7 +130,7 @@
 def merge_stats(parts, own, after):
     lines = own.shape[0] // 8
 
-    def body(parts_ref, own_ref, _, out_ref):
+    def body(parts_ref, own_ref, _, __, out_ref):
         tops = parts_ref[:, :lines]
         top = jnp.max(tops, axis=0)
         out_ref[:lines] = top
@@ -142,12 +142,12 @@
 
     return pl.pallas_call(
         body,
-        in_specs=[VMEM, VMEM, ANY],
+        in_specs=[VMEM, VMEM, ANY, ANY],
         out_specs=VMEM,
         out_shape=jax.ShapeDtypeStruct((5 * lines, LANES), F32),
         compiler_params=PARAMS,
         cost_estimate=cost(0, 4 * parts.size),
-    )(parts, own, after)
+    )(parts, own, *after)
 
 
 def change_of(starts_ref, rows_ref, exps, low, columns_here, scaled):
@@ -333,9 +333,55 @@
         high,
         middle,
         rest - middle,
+        jnp.zeros_like(high),
     ]
-    fields = jnp.stack([field.astype(F32) for field in fields], axis=1).astype(BF16)
-    return jnp.pad(fields, ((0, 0), (0, LANES - fields.shape[1])))
+    return jnp.stack([field.astype(F32) for field in fields])
+
+
+def half_shard(side, hidden, facts):
+    own_rows, features = hidden.shape
+    rows = own_rows // 2
+
+    def body(side_ref, hidden_ref, facts_ref, out_ref, sem):
+        first = pl.multiple_of(side_ref[0] * rows, rows)
+        copy = pltpu.make_async_copy(
+            hidden_ref.at[pl.ds(first, rows)], out_ref.at[:, pl.ds(0, features)], sem
+        )
+        copy.start()
+        facts = facts_ref[...]
+        facts = jnp.concatenate([facts, jnp.zeros((LANES - facts.shape[0], own_rows), F32)]).T
+        facts = jnp.where(side_ref[0] == 0, facts[:rows], facts[rows:])
+        out_ref[:, features:] = facts.astype(BF16)
+        copy.wait()
+
+    return pl.pallas_call(
+        body,
+        in_specs=[SMEM, ANY, VMEM],
+        out_specs=VMEM,
+        out_shape=jax.ShapeDtypeStruct((rows, features + LANES), BF16),
+        scratch_shapes=[pltpu.SemaphoreType.DMA],
+        compiler_params=PARAMS,
+        cost_estimate=cost(0, 4 * rows * features),
+    )(side, hidden, facts)
+
+
+def add_parts(kept, got, after):
+    rows, features = kept.shape
+    block = features // 4
+
+    def body(kept_ref, got_ref, _, out_ref):
+        out_ref[...] = (kept_ref[...].astype(F32) + got_ref[...].astype(F32)).astype(BF16)
+
+    spec = pl.BlockSpec((rows, block), lambda k: (0, k))
+    return pl.pallas_call(
+        body,
+        grid=(4,),
+        in_specs=[spec, spec, ANY],
+        out_specs=spec,
+        out_shape=jax.ShapeDtypeStruct((rows, features), BF16),
+        compiler_params=pltpu.CompilerParams(vmem_limit_bytes=16 << 20),
+        cost_estimate=cost(0, 6 * rows * features),
+    )(kept, got, after)
 
 
 def pick_one(values, *places):
@@ -359,10 +405,7 @@
     own_other = lax.ppermute(own, "core", SWAP)
     facts = pack_facts(token_ids, response_mask, teacher_logprob)
     gathered = lax.all_gather(
-        lax.dynamic_slice_in_dim(jnp.concatenate([hidden, facts], axis=1), side * rows, rows, 0),
-        "z",
-        axis=0,
-        tiled=True,
+        half_shard(side.astype(jnp.int32).reshape(1), hidden, facts), "z", axis=0, tiled=True
     )
     weights = [own, across, own_other, lax.ppermute(across, "core", SWAP)]
     starts = jnp.stack(
@@ -377,7 +420,7 @@
     far_gathered = lax.ppermute(gathered, "core", SWAP)
     far_exps = lax.ppermute(theirs, "core", SWAP)
     lined = stats.reshape(8 * lines, LANES)
-    shared = merge_stats(broadcast_gather(lined[: 3 * lines], "z", Z), lined, far_gathered)
+    shared = merge_stats(broadcast_gather(lined[: 3 * lines], "z", Z), lined, (far_gathered, far_exps))
     shared = broadcast_gather(shared, ("xh", "xl", "y"), PLANE)
     shared = shared.reshape(XH, XL, Y, 5, lines, LANES)
     top = jnp.max(shared[:, :, :, 0], axis=(0, 2))
@@ -414,7 +457,7 @@
     scales = mask * (within + beyond.reshape(CORES, XL, Z, 1)) / float(tokens)
 
     own_scale = lax.dynamic_index_in_dim(scales[0], z, 1, False).reshape(own_rows)
-    hidden_grad = summed * own_scale[:, None]
+    hidden_grad = (summed * own_scale[:, None]).astype(BF16)
 
     scale = lax.dynamic_index_in_dim(scales, side, 1, False).reshape(CORES, 1, here)
     rows_of = jnp.concatenate([known[:, 2 * XL :], scale], axis=1)
@@ -422,8 +465,8 @@
     given = head_block(starts, sides, columns_here, columns_here, features, partial)
     from_across = lax.ppermute(given, "xl", SWAP)
     kept = head_block(starts, sides, 0, columns_here, features, shares)
-    head_grad = kept.astype(F32) + from_across.astype(F32)
-    return hidden_grad.astype(BF16), head_grad.astype(BF16).T
+    head_grad = add_parts(kept, from_across, hidden_grad)
+    return hidden_grad, head_grad.T
 
 
 def solution(mesh):

time: 205 us -> 210 us (1.024)
  other arithmetic: 9.93 us -> 4.54 us
  waiting for transfers between devices: 106 us -> 111 us
  Pallas kernels: 39.9 us -> 44.5 us
    all_to_all x1, waiting for transfers between devices: 2.36 us -> 8.41 us  [on_device(): summed = lax.all_to_all(shares, ('xh', 'xl', 'y'), 0, 0, tiled=True)]
    pallas_call x1 -> x3, Pallas kernels: 1.46 us -> 6.33 us  [the longest x1 2.5 us: half_shard(): pl.pallas_call(body, in_specs=[SMEM, ANY, VMEM], out_specs=VMEM, out_shap...]
    transpose x1 -> x0, other arithmetic: 3.56 us -> none  [on_device(): return (hidden_grad.astype(BF16), head_grad.astype(BF16).T)]
    ppermute x1, waiting for transfers between devices: 3.38 us -> 0.01 us  [on_device(): from_across = lax.ppermute(given, 'xl', SWAP)]
  transfers between devices with their start and end apart: 12 -> 12, of which waited for: 9 -> 7; matrix products, arithmetic and copies ran while one was open for 4% -> 3% of each run, Pallas kernels for 9% -> 8%
where the time goes in v13:
time: 210 us; the launch traced here: 209 us
  waiting for transfers between devices  111 us (53%)
  Pallas kernels  44.5 us (21%)
  starting transfers between devices  26 us (12%)
  between operations  14.2 us (7%)
  local copies, waits for them, and re-layouts  9.1 us (4%)
  other arithmetic  4.54 us (2%)
    ppermute x1, waiting for transfers between devices, on_device(): across = lax.ppermute(own, 'xl', SWAP)  50.3 us
    reduce_scatter x1, waiting for transfers between devices, on_device(): summed = lax.psum_scatter(partial, 'z', scatter_dimension=0, tiled=True)  33.4 us
    all_to_all x2, starting transfers between devices, broadcast_gather(): return lax.all_to_all(copies, axes, 0, 0, tiled=True)  15.9 us
    pallas_call x2, Pallas kernels, head_block(): pl.pallas_call(body, in_specs=[SMEM] + [VMEM, ANY, ANY] * count + [ANY],...  15 us
    all_to_all x2, waiting for transfers between devices, broadcast_gather(): return lax.all_to_all(copies, axes, 0, 0, tiled=True)  13.5 us
    pallas_call x1, Pallas kernels, logits_and_stats(): pl.pallas_call(body, in_specs=[SMEM, ANY] + [ANY] * count, out_specs=[ANY...  10.6 us
    pallas_call x1, Pallas kernels, partial_product(): pl.pallas_call(body, in_specs=[SMEM, VMEM, ANY, ANY] + [ANY] * count, out...  10.4 us
    all_to_all x1, waiting for transfers between devices, on_device(): summed = lax.all_to_all(shares, ('xh', 'xl', 'y'), 0, 0, tiled=True)  8.41 us
  transfers between devices with their start and end apart: 12, of which 7 were waited for; matrix products, arithmetic and copies ran while one was open for 3% of the time, Pallas kernels for 8%

profile of v13, /device:TPU:8, one launch (start us, length us, event | category | flops | bytes accessed | tf_op | source)
XLA Modules:
  0.0 209.0 jit_solution(13648436091135844199)
XLA Ops:
  7.2 0.7 fusion.10
  7.9 0.7 fusion.14
  8.6 0.6 stack.64.facts_ref
  9.2 2.5 %shard_map.68 = bf16[64,3712]{1,0:T(8,128)(2,1)} custom-call(s32[1]{0:T(128)} %bitcast.4.side_ref, bf16[128,3584]{1,0:T(8,128)(2,1)} %hidden_ref.1, f32[8,128]{1,0:T(8,128)} %stack.64.facts_ref), custom_call_target="tpu_custom_call" | custom-call | bytes 917504 | tf_op jit(solution)/shard_map/pallas_call | solution.py:357
  11.7 1.6 collective-permute-start
  13.3 50.3 %collective-permute-done.refs_1_ = bf16[320,3584]{1,0:T(8,128)(2,1)S(1)} collective-permute-done((bf16[320,3584]{1,0:T(8,128)(2,1)}, bf16[320,3584]{1,0:T(8,128)(2,1)S(1)}, u32[]{:S(2)}, u32[]{:S(2)}) %collective-permute-start) | collective-permute-done | bytes 2293792 | tf_op jit(solution)/shard_map/ppermute | solution.py:404
  63.6 0.7 pad_add_fusion.starts_ref
  64.3 3.9 %collective-permute-done.2.refs_3_ = bf16[320,3584]{1,0:T(8,128)(2,1)} collective-permute-done((bf16[320,3584]{1,0:T(8,128)(2,1)S(1)}, bf16[320,3584]{1,0:T(8,128)(2,1)}, u32[]{:S(2)}, u32[]{:S(2)}) %collective-permute-start.2) | collective-permute-done | bytes 2293792 | tf_op jit(solution)/shard_map/ppermute | solution.py:410
  68.2 10.6 %shard_map.69 = (bf16[640,512]{1,0:T(8,128)(2,1)}, bf16[640,512]{1,0:T(8,128)(2,1)}, f32[8,512]{1,0:T(8,128)}, bf16[512,3712]{1,0:T(8,128)(2,1)}) custom-call(s32[4]{0:T(128)} %pad_add_fusion.starts_ref, bf16[512,3712]{1,0:T(8,128)(2,1)} %all-gather.2.cloned.1.call-done.h_ref, bf16[320,3584]{1,0:T(8,128)(2,1)} %bitcast.71, ...), custom_call_target="tpu_custom_call", output_to_operand_aliasing={{3}: (1, {})} | custom-call | flops 4697620480 | bytes 14155776 | tf_op jit(solution)/shard_map/pallas_call | solution.py:104
  78.8 0.2 collective-permute-start.3
  79.0 0.4 collective-permute-start.4
  79.4 0.7 slice.46
  80.1 0.6 broadcast_in_dim.7
  80.8 8.5 %all-to-all-start = ((f32[8,12,128]{2,1,0:T(8,128)}), f32[8,12,128]{2,1,0:T(8,128)S(1)}, u32[]{:S(2)}, u32[]{:S(2)}) async-start(f32[8,12,128]{2,1,0:T(8,128)} %broadcast_in_dim.7), calls=%async_computation | async-start | bytes 131072 | tf_op jit(solution)/shard_map/all_to_all | solution.py:23
  89.2 1.3 reshape.70.own_ref
  90.5 7.1 %all-to-all-done.parts_ref = f32[8,12,128]{2,1,0:T(8,128)S(1)} async-done(((f32[8,12,128]{2,1,0:T(8,128)}), f32[8,12,128]{2,1,0:T(8,128)S(1)}, u32[]{:S(2)}, u32[]{:S(2)}) %all-to-all-start) | async-done | bytes 49184 | tf_op jit(solution)/shard_map/all_to_all | solution.py:23
  97.6 0.6 copy-done.2
  98.2 0.3 copy-done.1
  98.5 1.5 shard_map.70
  99.9 1.4 broadcast_in_dim.8
  101.3 7.4 %all-to-all-start.1 = ((f32[16,20,128]{2,1,0:T(8,128)}), f32[16,20,128]{2,1,0:T(8,128)S(1)}, u32[]{:S(2)}, u32[]{:S(2)}) async-start(f32[16,20,128]{2,1,0:T(8,128)} %broadcast_in_dim.8), calls=%async_computation.1 | async-start | bytes 393216 | tf_op jit(solution)/shard_map/all_to_all | solution.py:23
  108.7 0.2 reduce-scatter.2.cloned.1.call-start
  108.9 6.4 %all-to-all-done.1 = f32[16,20,128]{2,1,0:T(8,128)S(1)} async-done(((f32[16,20,128]{2,1,0:T(8,128)}), f32[16,20,128]{2,1,0:T(8,128)S(1)}, u32[]{:S(2)}, u32[]{:S(2)}) %all-to-all-start.1) | async-done | bytes 163872 | tf_op jit(solution)/shard_map/all_to_all | solution.py:23
  115.5 0.8 fusion.18
  116.4 0.6 pad_maximum_fusion.4.rows_ref
  117.0 10.4 %shard_map.71.refs_6_ = bf16[512,3584]{1,0:T(8,128)(2,1)} custom-call(s32[4]{0:T(128)} %pad_add_fusion.starts_ref, f32[2,512]{1,0:T(2,128)} %pad_maximum_fusion.4.rows_ref, bf16[640,512]{1,0:T(8,128)(2,1)} %get-tuple-element.9.first_ref.refs_1_, bf16[640,512]{1,0:T(8,128)(2,1)} %get-tuple-element.8.last_ref, bf16[320,3584]{1,0:T(8,128)(2,1)} %bitcast.72, ...), custom_call_target="tpu_custom_call" | custom-call | flops 4697620480 | bytes 14155776 | tf_op jit(solution)/shard_map/pallas_call | solution.py:215
  127.5 0.1 collective-permute-start.5
  127.6 1.1 collective-permute-done.5
  128.8 0.1 reshape.74
  128.9 0.1 reduce_sum.58
  129.0 0.1 mul.119
  129.1 0.2 select_reduce_fusion
  129.3 0.1 add.127
  129.4 0.4 multiply_reduce_fusion
  129.9 0.6 slice_bitcast_fusion.1
  130.5 7.6 %shard_map.74 = bf16[320,3584]{1,0:T(8,128)(2,1)} custom-call(s32[4]{0:T(128)} %pad_add_fusion.starts_ref, f32[3,512]{1,0:T(4,128)} %get-tuple-element.27.refs_0_, bf16[640,512]{1,0:T(8,128)(2,1)} %get-tuple-element.9.first_ref.refs_1_, bf16[512,3712]{1,0:T(8,128)(2,1)} %get-tuple-element.7.refs_2_, f32[3,512]{1,0:T(4,128)} %get-tuple-element.26.refs_3_, ...), custom_call_target="tpu_custom_call" | custom-call | flops 2348810240 | bytes 9633792 | tf_op jit(solution)/shard_map/pallas_call | solution.py:284
  138.1 0.4 collective-permute-start.6
  138.5 33.4 %reduce-scatter.2.cloned.1.call-done.in_ref = bf16[64,3584]{1,0:T(8,128)(2,1)} async-done(((bf16[512,3584]{1,0:T(8,128)(2,1)}), bf16[64,3584]{1,0:T(8,128)(2,1)}) %reduce-scatter.2.cloned.1.call-update) | async-done | bytes 458768 | tf_op jit(solution)/shard_map/reduce_scatter | solution.py:435
  171.9 2.0 shard_map.72.refs_6_
  174.0 7.3 %all-to-all-start.2 = ((bf16[16,64,224]{2,1,0:T(8,128)(2,1)}), bf16[16,64,224]{2,1,0:T(8,128)(2,1)S(1)}, u32[]{:S(2)}, u32[]{:S(2)}) async-start(bf16[16,64,224]{2,1,0:T(8,128)(2,1)} %shard_map.72.refs_6_), calls=%async_computation.3 | async-start | bytes 1048576 | tf_op jit(solution)/shard_map/all_to_all | solution.py:438
  181.2 0.1 mul.123
  181.3 7.5 %shard_map.73.kept_ref = bf16[320,3584]{1,0:T(8,128)(2,1)} custom-call(s32[4]{0:T(128)} %pad_add_fusion.starts_ref, f32[3,512]{1,0:T(4,128)} %get-tuple-element.27.refs_0_, bf16[640,512]{1,0:T(8,128)(2,1)} %get-tuple-element.9.first_ref.refs_1_, bf16[512,3712]{1,0:T(8,128)(2,1)} %get-tuple-element.7.refs_2_, f32[3,512]{1,0:T(4,128)} %get-tuple-element.26.refs_3_, ...), custom_call_target="tpu_custom_call" | custom-call | flops 2348810240 | bytes 9633792 | tf_op jit(solution)/shard_map/pallas_call | solution.py:284
  188.8 8.4 %all-to-all-done.2 = bf16[16,64,224]{2,1,0:T(8,128)(2,1)S(1)} async-done(((bf16[16,64,224]{2,1,0:T(8,128)(2,1)}), bf16[16,64,224]{2,1,0:T(8,128)(2,1)S(1)}, u32[]{:S(2)}, u32[]{:S(2)}) %all-to-all-start.2) | async-done | bytes 458784 | tf_op jit(solution)/shard_map/all_to_all | solution.py:438
  197.2 0.1 convert_reduce_fusion
  197.3 0.1 fusion._
  197.4 0.7 copy.27
  198.1 1.6 copy-done
  199.8 2.4 %shard_map.75 = bf16[320,3584]{1,0:T(8,128)(2,1)} custom-call(bf16[320,3584]{1,0:T(8,128)(2,1)S(1)} %copy-done, bf16[320,3584]{1,0:T(8,128)(2,1)S(1)} %collective-permute-done.6.got_ref, bf16[128,224]{1,0:T(8,128)(2,1)S(1)} %fusion._), custom_call_target="tpu_custom_call" | custom-call | bytes 6881280 | tf_op jit(solution)/shard_map/pallas_call | solution.py:376
  (34 shorter events, 0.6 us)
Async XLA Ops:
  7.2 61.0 %all-gather.2.cloned.1.call-start = ((), (), s32[]{:S(2)}) async-start(), calls=%async_computation.4 | async-start | bytes 4276224 | tf_op jit(solution)/shard_map/all_gather | solution.py:407
  11.7 51.9 %collective-permute-start = (bf16[320,3584]{1,0:T(8,128)(2,1)}, bf16[320,3584]{1,0:T(8,128)(2,1)S(1)}, u32[]{:S(2)}, u32[]{:S(2)}) collective-permute-start(bf16[320,3584]{1,0:T(8,128)(2,1)} %bitcast.69), channel_id=1, source_target_pairs={{0,4},{4,0},{1,5},{5,1},{2,6},{6,2},{3,7},{7,3},{8,12},{12,8},{9,1... | collective-permute-start | bytes 6881288 | tf_op jit(solution)/shard_map/ppermute | solution.py:404
  13.3 51.0 %collective-permute-start.1 = (bf16[320,3584]{1,0:T(8,128)(2,1)}, bf16[320,3584]{1,0:T(8,128)(2,1)}, u32[]{:S(2)}, u32[]{:S(2)}) collective-permute-start(bf16[320,3584]{1,0:T(8,128)(2,1)} %bitcast.70), channel_id=1, source_target_pairs={{0,16},{16,0},{1,17},{17,1},{2,18},{18,2},{3,19},{19,3},{4,20},{20... | collective-permute-start | bytes 6881288 | tf_op jit(solution)/shard_map/ppermute | solution.py:405
  63.6 4.6 %copy-start.3 = (bf16[320,3584]{1,0:T(8,128)(2,1)}, bf16[320,3584]{1,0:T(8,128)(2,1)S(1)}, u32[]{:S(2)}) copy-start(bf16[320,3584]{1,0:T(8,128)(2,1)S(1)} %collective-permute-done.refs_1_) | copy-start | bytes 6881284
  63.6 4.6 %collective-permute-start.2 = (bf16[320,3584]{1,0:T(8,128)(2,1)S(1)}, bf16[320,3584]{1,0:T(8,128)(2,1)}, u32[]{:S(2)}, u32[]{:S(2)}) collective-permute-start(bf16[320,3584]{1,0:T(8,128)(2,1)S(1)} %collective-permute-done.refs_1_), channel_id=1, source_target_pairs={{0,16},{16,0},{1,17},{17,1},{2,18},{18,2},{3,19},{19,3},{4,20},{20... | collective-permute-start | bytes 6881288 | tf_op jit(solution)/shard_map/ppermute | solution.py:410
  78.8 18.8 %collective-permute-start.3 = (bf16[512,3712]{1,0:T(8,128)(2,1)}, bf16[512,3712]{1,0:T(8,128)(2,1)}, u32[]{:S(2)}, u32[]{:S(2)}) collective-permute-start(bf16[512,3712]{1,0:T(8,128)(2,1)} %get-tuple-element.7.refs_2_), channel_id=1, source_target_pairs={{0,16},{16,0},{1,17},{17,1},{2,18},{18,2},{3,19},{19,3},{4,20},{20... | collective-permute-start | bytes 11403272 | tf_op jit(solution)/shard_map/ppermute | solution.py:420
  79.0 18.6 %collective-permute-start.4 = (bf16[640,512]{1,0:T(8,128)(2,1)}, bf16[640,512]{1,0:T(8,128)(2,1)S(1)}, u32[]{:S(2)}, u32[]{:S(2)}) collective-permute-start(bf16[640,512]{1,0:T(8,128)(2,1)} %get-tuple-element.8.last_ref), channel_id=1, source_target_pairs={{0,16},{16,0},{1,17},{17,1},{2,18},{18,2},{3,19},{19,3},{4,20},{20... | collective-permute-start | bytes 1966088 | tf_op jit(solution)/shard_map/ppermute | solution.py:421
  80.8 16.8 %all-to-all-start = ((f32[8,12,128]{2,1,0:T(8,128)}), f32[8,12,128]{2,1,0:T(8,128)S(1)}, u32[]{:S(2)}, u32[]{:S(2)}) async-start(f32[8,12,128]{2,1,0:T(8,128)} %broadcast_in_dim.7), calls=%async_computation | async-start | bytes 131072 | tf_op jit(solution)/shard_map/all_to_all | solution.py:23
  97.6 0.6 copy-start.2
  97.6 0.9 copy-start.1
  101.3 14.1 %all-to-all-start.1 = ((f32[16,20,128]{2,1,0:T(8,128)}), f32[16,20,128]{2,1,0:T(8,128)S(1)}, u32[]{:S(2)}, u32[]{:S(2)}) async-start(f32[16,20,128]{2,1,0:T(8,128)} %broadcast_in_dim.8), calls=%async_computation.1 | async-start | bytes 393216 | tf_op jit(solution)/shard_map/all_to_all | solution.py:23
  108.7 63.2 %reduce-scatter.2.cloned.1.call-start = ((), (), s32[]{:S(2)}) async-start(), calls=%async_computation.5 | async-start | bytes 4128768 | tf_op jit(solution)/shard_map/reduce_scatter | solution.py:435
  127.5 1.3 collective-permute-start.5
  138.1 60.1 %collective-permute-start.6 = (bf16[320,3584]{1,0:T(8,128)(2,1)}, bf16[320,3584]{1,0:T(8,128)(2,1)S(1)}, u32[]{:S(2)}, u32[]{:S(2)}) collective-permute-start(bf16[320,3584]{1,0:T(8,128)(2,1)} %shard_map.74), channel_id=1, source_target_pairs={{0,4},{4,0},{1,5},{5,1},{2,6},{6,2},{3,7},{7,3},{8,12},{12,8},{9,1... | collective-permute-start | bytes 6881288 | tf_op jit(solution)/shard_map/ppermute | solution.py:466
  174.0 23.3 %all-to-all-start.2 = ((bf16[16,64,224]{2,1,0:T(8,128)(2,1)}), bf16[16,64,224]{2,1,0:T(8,128)(2,1)S(1)}, u32[]{:S(2)}, u32[]{:S(2)}) async-start(bf16[16,64,224]{2,1,0:T(8,128)(2,1)} %shard_map.72.refs_6_), calls=%async_computation.3 | async-start | bytes 1048576 | tf_op jit(solution)/shard_map/all_to_all | solution.py:438
  198.1 1.6 copy-start
Sparse Core Ops, SparseCore 0:
  11.8 54.0 all-gather.1
  127.5 44.3 reduce-scatter.1

commit v14 on v11

--- a/solution.py
+++ b/solution.py
@@ -18,11 +18,6 @@
 ANY = pl.BlockSpec(memory_space=pl.ANY)
 
 
-def broadcast_gather(part, axes, count):
-    copies = jnp.broadcast_to(part[None], (count,) + part.shape)
-    return lax.all_to_all(copies, axes, 0, 0, tiled=True)
-
-
 def dot(left, right, contract):
     return lax.dot_general(left, right, (contract, ((), ())), preferred_element_type=F32)
 
@@ -35,6 +30,10 @@
     number = low // columns_here
     row = lax.broadcasted_iota(jnp.int32, (rows, ids.shape[1]), 0) + (low - number * columns_here)
     return row + starts_ref[number] == ids
+
+
+def as_lines(row):
+    return [row[:, at : at + LANES] for at in range(0, row.shape[1], LANES)]
 
 
 def logits_and_stats(starts, hidden, weights, columns_here):
@@ -48,7 +47,7 @@
 
     def body(starts_ref, h_ref, *refs):
         w_refs = refs[:count]
-        *exps_refs, stats_ref, _, w, h, f, held, exps, sems, out = refs[count:]
+        *exps_refs, stats_ref, copies_ref, lines_ref, _, w, h, f, held, exps, sems, out = refs[count:]
 
         def loads(k):
             span = pl.ds(k * block, block)
@@ -98,19 +97,24 @@
         stats_ref[...] = jnp.concatenate(
             [top, total, picked, facts[3:4], teacher, token_id, zero, zero]
         )
+        lined = jnp.concatenate(as_lines(top) + as_lines(total) + as_lines(picked))
+        copies_ref[...] = jnp.broadcast_to(lined[None], copies_ref.shape)
+        lines_ref[...] = jnp.concatenate(as_lines(facts[3:4]) + as_lines(teacher))
         for send in sends:
             send.wait()
 
     return pl.pallas_call(
         body,
         in_specs=[SMEM, ANY] + [ANY] * count,
-        out_specs=[ANY, ANY, VMEM, ANY],
+        out_specs=[ANY, ANY, VMEM, VMEM, VMEM, ANY],
         out_shape=[jax.ShapeDtypeStruct((columns // 2, tokens), BF16)] * 2
         + [
             jax.ShapeDtypeStruct((8, tokens), F32),
+            jax.ShapeDtypeStruct((Z, 3 * tokens // LANES, LANES), F32),
+            jax.ShapeDtypeStruct((2 * tokens // LANES, LANES), F32),
             jax.ShapeDtypeStruct(hidden.shape, hidden.dtype),
         ],
-        input_output_aliases={1: 3},
+        input_output_aliases={1: 5},
         scratch_shapes=[
             pltpu.VMEM((STEPS, columns, block), BF16),
             pltpu.VMEM((STEPS, tokens, block), BF16),
@@ -128,26 +132,24 @@
 
 
 def merge_stats(parts, own, after):
-    lines = own.shape[0] // 8
-
-    def body(parts_ref, own_ref, _, out_ref):
+    lines = parts.shape[1] // 3
+
+    def body(parts_ref, own_ref, _, __, out_ref):
         tops = parts_ref[:, :lines]
         top = jnp.max(tops, axis=0)
-        out_ref[:lines] = top
-        out_ref[lines : 2 * lines] = jnp.sum(
-            parts_ref[:, lines : 2 * lines] * jnp.exp(tops - top[None]), axis=0
-        )
-        out_ref[2 * lines : 3 * lines] = jnp.sum(parts_ref[:, 2 * lines :], axis=0)
-        out_ref[3 * lines :] = own_ref[3 * lines : 5 * lines]
+        total = jnp.sum(parts_ref[:, lines : 2 * lines] * jnp.exp(tops - top[None]), axis=0)
+        picked = jnp.sum(parts_ref[:, 2 * lines :], axis=0)
+        merged = jnp.concatenate([top, total, picked, own_ref[...]])
+        out_ref[...] = jnp.broadcast_to(merged[None], out_ref.shape)
 
     return pl.pallas_call(
         body,
-        in_specs=[VMEM, VMEM, ANY],
+        in_specs=[VMEM, VMEM, ANY, ANY],
         out_specs=VMEM,
-        out_shape=jax.ShapeDtypeStruct((5 * lines, LANES), F32),
+        out_shape=jax.ShapeDtypeStruct((PLANE, 5 * lines, LANES), F32),
         compiler_params=PARAMS,
         cost_estimate=cost(0, 4 * parts.size),
-    )(parts, own, after)
+    )(parts, own, *after)
 
 
 def change_of(starts_ref, rows_ref, exps, low, columns_here, scaled):
@@ -373,12 +375,12 @@
         ]
     ).astype(jnp.int32)
 
-    mine, theirs, stats, gathered = logits_and_stats(starts, gathered, weights, columns_here)
+    mine, theirs, stats, copies, lined, gathered = logits_and_stats(starts, gathered, weights, columns_here)
     far_gathered = lax.ppermute(gathered, "core", SWAP)
     far_exps = lax.ppermute(theirs, "core", SWAP)
-    lined = stats.reshape(8 * lines, LANES)
-    shared = merge_stats(broadcast_gather(lined[: 3 * lines], "z", Z), lined, far_gathered)
-    shared = broadcast_gather(shared, ("xh", "xl", "y"), PLANE)
+    shared = lax.all_to_all(copies, "z", 0, 0, tiled=True)
+    shared = merge_stats(shared, lined, (far_gathered, far_exps))
+    shared = lax.all_to_all(shared, ("xh", "xl", "y"), 0, 0, tiled=True)
     shared = shared.reshape(XH, XL, Y, 5, lines, LANES)
     top = jnp.max(shared[:, :, :, 0], axis=(0, 2))
     shrink = jnp.exp(shared[:, :, :, 0] - top[None, :, None])

time: 205 us -> 203 us (level)
  blocking collectives: 0 us -> 16.9 us
  starting transfers between devices: 25.4 us -> 17.6 us
  waiting for transfers between devices: 106 us -> 100 us
  local copies, waits for them, and re-layouts: 8.4 us -> 4.09 us
    all_to_all x0 -> x1, blocking collectives: none -> 16.9 us  [on_device(): shared = lax.all_to_all(copies, 'z', 0, 0, tiled=True)]
    all_to_all x2 -> x1, starting transfers between devices: 15.9 us -> 7.4 us  [on_device(): shared = lax.all_to_all(shared, ('xh', 'xl', 'y'), 0, 0, tiled=True)]
    all_to_all x2 -> x1, waiting for transfers between devices: 13.5 us -> 6.44 us  [on_device(): shared = lax.all_to_all(shared, ('xh', 'xl', 'y'), 0, 0, tiled=True)]
  transfers between devices with their start and end apart: 12 -> 11, of which waited for: 9 -> 7; matrix products, arithmetic and copies ran while one was open for 4% -> 3% of each run, Pallas kernels for 9% -> 8%
where the time goes in v14:
time: 203 us; the launch traced here: 202 us
  waiting for transfers between devices  100 us (49%)
  Pallas kernels  39.7 us (20%)
  starting transfers between devices  17.6 us (9%)
  blocking collectives  16.9 us (8%)
  between operations  14.2 us (7%)
  other arithmetic  9.91 us (5%)
  local copies, waits for them, and re-layouts  4.09 us (2%)
    ppermute x1, waiting for transfers between devices, on_device(): across = lax.ppermute(own, 'xl', SWAP)  50.3 us
    reduce_scatter x1, waiting for transfers between devices, on_device(): summed = lax.psum_scatter(partial, 'z', scatter_dimension=0, tiled=True)  33.4 us
    all_to_all x1, blocking collectives, on_device(): shared = lax.all_to_all(copies, 'z', 0, 0, tiled=True)  16.9 us
    pallas_call x2, Pallas kernels, head_block(): pl.pallas_call(body, in_specs=[SMEM] + [VMEM, ANY, ANY] * count + [ANY],...  15 us
    pallas_call x1, Pallas kernels, logits_and_stats(): pl.pallas_call(body, in_specs=[SMEM, ANY] + [ANY] * count, out_specs=[ANY...  10.7 us
    pallas_call x1, Pallas kernels, partial_product(): pl.pallas_call(body, in_specs=[SMEM, VMEM, ANY, ANY] + [ANY] * count, out...  10.4 us
    all_to_all x1, starting transfers between devices, on_device(): shared = lax.all_to_all(shared, ('xh', 'xl', 'y'), 0, 0, tiled=True)  7.4 us
    all_to_all x1, starting transfers between devices, on_device(): summed = lax.all_to_all(shares, ('xh', 'xl', 'y'), 0, 0, tiled=True)  7.26 us
  transfers between devices with their start and end apart: 11, of which 7 were waited for; matrix products, arithmetic and copies ran while one was open for 3% of the time, Pallas kernels for 8%

profile of v14, /device:TPU:8, one launch (start us, length us, event | category | flops | bytes accessed | tf_op | source)
XLA Modules:
  0.0 202.4 jit_solution(569741893729553658)
XLA Ops:
  7.2 0.0 all-gather.2.cloned.1.call-start
  7.2 0.7 fusion.17
  7.9 0.7 fusion.23
  8.6 0.1 copy.41
  8.7 1.8 fusion.2
  10.6 1.6 collective-permute-start
  12.2 50.3 %collective-permute-done.refs_1_ = bf16[320,3584]{1,0:T(8,128)(2,1)S(1)} collective-permute-done((bf16[320,3584]{1,0:T(8,128)(2,1)}, bf16[320,3584]{1,0:T(8,128)(2,1)S(1)}, u32[]{:S(2)}, u32[]{:S(2)}) %collective-permute-start) | collective-permute-done | bytes 2293792 | tf_op jit(solution)/shard_map/ppermute | solution.py:360
  62.5 0.7 pad_add_fusion.starts_ref
  63.2 3.9 %collective-permute-done.2.refs_3_ = bf16[320,3584]{1,0:T(8,128)(2,1)} collective-permute-done((bf16[320,3584]{1,0:T(8,128)(2,1)S(1)}, bf16[320,3584]{1,0:T(8,128)(2,1)}, u32[]{:S(2)}, u32[]{:S(2)}) %collective-permute-start.2) | collective-permute-done | bytes 2293792 | tf_op jit(solution)/shard_map/ppermute | solution.py:369
  67.1 10.7 %shard_map.68 = (bf16[640,512]{1,0:T(8,128)(2,1)}, bf16[640,512]{1,0:T(8,128)(2,1)}, f32[8,512]{1,0:T(8,128)}, f32[8,12,128]{2,1,0:T(8,128)}, f32[8,128]{1,0:T(8,128)}, /*index=5*/bf16[512,3712]{1,0:T(8,128)(2,1)}) custom-call(s32[4]{0:T(128)} %pad_add_fusion.starts_ref, ...), custom_call_target="tpu_custom_call", output_to_operand_aliasing={{5}: (1, {})} | custom-call | flops 4697620480 | bytes 14155776 | tf_op jit(solution)/shard_map/pallas_call | solution.py:106
  77.7 0.2 collective-permute-start.3
  77.9 0.4 collective-permute-start.4
  78.3 16.9 %all_to_all.15.parts_ref = f32[8,12,128]{2,1,0:T(8,128)} all-to-all(f32[8,12,128]{2,1,0:T(8,128)} %get-tuple-element.9), channel_id=1, replica_groups=mesh['z'=8,'core'=2,'xh'=2,'xl'=2,'y'=4] {'z'}, dimensions={0} | all-to-all | bytes 98304 | tf_op jit(solution)/shard_map/all_to_all | solution.py:381
  95.3 0.8 copy-done.1
  96.1 1.2 copy-done
  97.3 1.5 shard_map.69
  98.8 7.4 %all-to-all-start.1 = ((f32[16,20,128]{2,1,0:T(8,128)}), f32[16,20,128]{2,1,0:T(8,128)S(1)}, u32[]{:S(2)}, u32[]{:S(2)}) async-start(f32[16,20,128]{2,1,0:T(8,128)} %shard_map.69), calls=%async_computation.1 | async-start | bytes 393216 | tf_op jit(solution)/shard_map/all_to_all | solution.py:383
  106.2 0.2 reduce-scatter.2.cloned.1.call-start
  106.4 6.4 %all-to-all-done.1 = f32[16,20,128]{2,1,0:T(8,128)S(1)} async-done(((f32[16,20,128]{2,1,0:T(8,128)}), f32[16,20,128]{2,1,0:T(8,128)S(1)}, u32[]{:S(2)}, u32[]{:S(2)}) %all-to-all-start.1) | async-done | bytes 163872 | tf_op jit(solution)/shard_map/all_to_all | solution.py:383
  113.0 0.8 fusion.27
  113.9 0.6 pad_maximum_fusion.4.rows_ref
  114.5 10.4 %shard_map.70.refs_6_ = bf16[512,3584]{1,0:T(8,128)(2,1)} custom-call(s32[4]{0:T(128)} %pad_add_fusion.starts_ref, f32[2,512]{1,0:T(2,128)} %pad_maximum_fusion.4.rows_ref, bf16[640,512]{1,0:T(8,128)(2,1)} %get-tuple-element.13.first_ref.refs_1_, bf16[640,512]{1,0:T(8,128)(2,1)} %get-tuple-element.12.last_ref, bf16[320,3584]{1,0:T(8,128)(2,1)} %bitcast.71, ...), custom_call_target="tpu_custom_call" | custom-call | flops 4697620480 | bytes 14155776 | tf_op jit(solution)/shard_map/pallas_call | solution.py:217
  125.0 0.1 collective-permute-start.5
  125.1 0.1 pad_add_fusion.1
  125.2 1.1 collective-permute-done.5
  126.3 0.1 reshape.62
  126.4 0.1 mul.116
  126.4 0.1 reduce_sum.58
  126.5 0.1 mul.123
  126.6 0.2 select_reduce_fusion
  126.8 0.1 add.136
  126.9 0.4 multiply_reduce_fusion
  127.2 0.1 multiply_multiply_fusion
  127.3 0.1 reshape.63
  127.4 0.6 slice_bitcast_fusion.1
  128.0 7.5 %shard_map.73 = bf16[320,3584]{1,0:T(8,128)(2,1)} custom-call(s32[4]{0:T(128)} %pad_add_fusion.starts_ref, f32[3,512]{1,0:T(4,128)} %get-tuple-element.29.refs_0_, bf16[640,512]{1,0:T(8,128)(2,1)} %get-tuple-element.13.first_ref.refs_1_, bf16[512,3712]{1,0:T(8,128)(2,1)} %get-tuple-element.11.refs_2_, f32[3,512]{1,0:T(4,128)} %get-tuple-element.28.refs_3_, ...), custom_call_target="tpu_custom_call" | custom-call | flops 2348810240 | bytes 9633792 | tf_op jit(solution)/shard_map/pallas_call | solution.py:286
  135.5 0.4 collective-permute-start.6
  135.9 0.1 mul.127
  136.0 33.4 %reduce-scatter.2.cloned.1.call-done.in_ref = bf16[64,3584]{1,0:T(8,128)(2,1)} async-done(((bf16[512,3584]{1,0:T(8,128)(2,1)}), bf16[64,3584]{1,0:T(8,128)(2,1)}) %reduce-scatter.2.cloned.1.call-update) | async-done | bytes 458768 | tf_op jit(solution)/shard_map/reduce_scatter | solution.py:394
  169.4 2.1 %shard_map.71.refs_6_ = bf16[16,64,224]{2,1,0:T(8,128)(2,1)} custom-call(bf16[64,3584]{1,0:T(8,128)(2,1)} %reduce-scatter.2.cloned.1.call-done.in_ref), custom_call_target="tpu_custom_call" | custom-call | bytes 917504 | tf_op jit(solution)/shard_map/pallas_call | solution.py:316
  171.5 7.3 %all-to-all-start.2 = ((bf16[16,64,224]{2,1,0:T(8,128)(2,1)}), bf16[16,64,224]{2,1,0:T(8,128)(2,1)S(1)}, u32[]{:S(2)}, u32[]{:S(2)}) async-start(bf16[16,64,224]{2,1,0:T(8,128)(2,1)} %shard_map.71.refs_6_), calls=%async_computation.3 | async-start | bytes 1048576 | tf_op jit(solution)/shard_map/all_to_all | solution.py:397
  178.7 7.5 %shard_map.72 = bf16[320,3584]{1,0:T(8,128)(2,1)} custom-call(s32[4]{0:T(128)} %pad_add_fusion.starts_ref, f32[3,512]{1,0:T(4,128)} %get-tuple-element.29.refs_0_, bf16[640,512]{1,0:T(8,128)(2,1)} %get-tuple-element.13.first_ref.refs_1_, bf16[512,3712]{1,0:T(8,128)(2,1)} %get-tuple-element.11.refs_2_, f32[3,512]{1,0:T(4,128)} %get-tuple-element.28.refs_3_, ...), custom_call_target="tpu_custom_call" | custom-call | flops 2348810240 | bytes 9633792 | tf_op jit(solution)/shard_map/pallas_call | solution.py:286
  186.3 2.2 %collective-permute-done.6 = bf16[320,3584]{1,0:T(8,128)(2,1)S(1)} collective-permute-done((bf16[320,3584]{1,0:T(8,128)(2,1)}, bf16[320,3584]{1,0:T(8,128)(2,1)S(1)}, u32[]{:S(2)}, u32[]{:S(2)}) %collective-permute-start.6) | collective-permute-done | bytes 2293792 | tf_op jit(solution)/shard_map/ppermute | solution.py:425
  188.5 3.6 %fusion = bf16[3584,320]{0,1:T(8,128)(2,1)} fusion(bf16[320,3584]{1,0:T(8,128)(2,1)S(1)} %collective-permute-done.6, bf16[320,3584]{1,0:T(8,128)(2,1)} %shard_map.72), kind=kLoop, calls=%fused_computation.1 | loop fusion | flops 4587520 | bytes 6881280 | tf_op jit(solution)/shard_map/transpose | solution.py:428
  192.1 2.6 %all-to-all-done.2 = bf16[16,64,224]{2,1,0:T(8,128)(2,1)S(1)} async-done(((bf16[16,64,224]{2,1,0:T(8,128)(2,1)}), bf16[16,64,224]{2,1,0:T(8,128)(2,1)S(1)}, u32[]{:S(2)}, u32[]{:S(2)}) %all-to-all-start.2) | async-done | bytes 458784 | tf_op jit(solution)/shard_map/all_to_all | solution.py:397
  194.7 0.1 convert_reduce_fusion
  194.8 0.1 fusion.3
  194.9 0.7 copy.45
  (26 shorter events, 0.3 us)
Async XLA Ops:
  7.2 59.9 %all-gather.2.cloned.1.call-start = ((), (), s32[]{:S(2)}) async-start(), calls=%async_computation.4 | async-start | bytes 4276224 | tf_op jit(solution)/shard_map/all_gather | solution.py:363
  10.6 51.9 %collective-permute-start = (bf16[320,3584]{1,0:T(8,128)(2,1)}, bf16[320,3584]{1,0:T(8,128)(2,1)S(1)}, u32[]{:S(2)}, u32[]{:S(2)}) collective-permute-start(bf16[320,3584]{1,0:T(8,128)(2,1)} %bitcast.68), channel_id=1, source_target_pairs={{0,4},{4,0},{1,5},{5,1},{2,6},{6,2},{3,7},{7,3},{8,12},{12,8},{9,1... | collective-permute-start | bytes 6881288 | tf_op jit(solution)/shard_map/ppermute | solution.py:360
  12.2 51.0 %collective-permute-start.1 = (bf16[320,3584]{1,0:T(8,128)(2,1)}, bf16[320,3584]{1,0:T(8,128)(2,1)}, u32[]{:S(2)}, u32[]{:S(2)}) collective-permute-start(bf16[320,3584]{1,0:T(8,128)(2,1)} %bitcast.69), channel_id=1, source_target_pairs={{0,16},{16,0},{1,17},{17,1},{2,18},{18,2},{3,19},{19,3},{4,20},{20... | collective-permute-start | bytes 6881288 | tf_op jit(solution)/shard_map/ppermute | solution.py:361
  62.5 4.6 %copy-start.2 = (bf16[320,3584]{1,0:T(8,128)(2,1)}, bf16[320,3584]{1,0:T(8,128)(2,1)S(1)}, u32[]{:S(2)}) copy-start(bf16[320,3584]{1,0:T(8,128)(2,1)S(1)} %collective-permute-done.refs_1_) | copy-start | bytes 6881284
  62.5 4.6 %collective-permute-start.2 = (bf16[320,3584]{1,0:T(8,128)(2,1)S(1)}, bf16[320,3584]{1,0:T(8,128)(2,1)}, u32[]{:S(2)}, u32[]{:S(2)}) collective-permute-start(bf16[320,3584]{1,0:T(8,128)(2,1)S(1)} %collective-permute-done.refs_1_), channel_id=1, source_target_pairs={{0,16},{16,0},{1,17},{17,1},{2,18},{18,2},{3,19},{19,3},{4,20},{20... | collective-permute-start | bytes 6881288 | tf_op jit(solution)/shard_map/ppermute | solution.py:369
  77.7 17.5 %collective-permute-start.3 = (bf16[512,3712]{1,0:T(8,128)(2,1)}, bf16[512,3712]{1,0:T(8,128)(2,1)S(1)}, u32[]{:S(2)}, u32[]{:S(2)}) collective-permute-start(bf16[512,3712]{1,0:T(8,128)(2,1)} %get-tuple-element.11.refs_2_), channel_id=1, source_target_pairs={{0,16},{16,0},{1,17},{17,1},{2,18},{18,2},{3,19},{19,3},{4,20},{20... | collective-permute-start | bytes 11403272 | tf_op jit(solution)/shard_map/ppermute | solution.py:379
  77.9 17.3 %collective-permute-start.4 = (bf16[640,512]{1,0:T(8,128)(2,1)}, bf16[640,512]{1,0:T(8,128)(2,1)S(1)}, u32[]{:S(2)}, u32[]{:S(2)}) collective-permute-start(bf16[640,512]{1,0:T(8,128)(2,1)} %get-tuple-element.12.last_ref), channel_id=1, source_target_pairs={{0,16},{16,0},{1,17},{17,1},{2,18},{18,2},{3,19},{19,3},{4,20},{20... | collective-permute-start | bytes 1966088 | tf_op jit(solution)/shard_map/ppermute | solution.py:380
  95.3 0.9 copy-start.1
  95.3 2.0 copy-start
  98.8 14.1 %all-to-all-start.1 = ((f32[16,20,128]{2,1,0:T(8,128)}), f32[16,20,128]{2,1,0:T(8,128)S(1)}, u32[]{:S(2)}, u32[]{:S(2)}) async-start(f32[16,20,128]{2,1,0:T(8,128)} %shard_map.69), calls=%async_computation.1 | async-start | bytes 393216 | tf_op jit(solution)/shard_map/all_to_all | solution.py:383
  106.2 63.2 %reduce-scatter.2.cloned.1.call-start = ((), (), s32[]{:S(2)}) async-start(), calls=%async_computation.5 | async-start | bytes 4128768 | tf_op jit(solution)/shard_map/reduce_scatter | solution.py:394
  125.0 1.3 collective-permute-start.5
  135.5 53.0 %collective-permute-start.6 = (bf16[320,3584]{1,0:T(8,128)(2,1)}, bf16[320,3584]{1,0:T(8,128)(2,1)S(1)}, u32[]{:S(2)}, u32[]{:S(2)}) collective-permute-start(bf16[320,3584]{1,0:T(8,128)(2,1)} %shard_map.73), channel_id=1, source_target_pairs={{0,4},{4,0},{1,5},{5,1},{2,6},{6,2},{3,7},{7,3},{8,12},{12,8},{9,1... | collective-permute-start | bytes 6881288 | tf_op jit(solution)/shard_map/ppermute | solution.py:425
  171.5 23.2 %all-to-all-start.2 = ((bf16[16,64,224]{2,1,0:T(8,128)(2,1)}), bf16[16,64,224]{2,1,0:T(8,128)(2,1)S(1)}, u32[]{:S(2)}, u32[]{:S(2)}) async-start(bf16[16,64,224]{2,1,0:T(8,128)(2,1)} %shard_map.71.refs_6_), calls=%async_computation.3 | async-start | bytes 1048576 | tf_op jit(solution)/shard_map/all_to_all | solution.py:397
Sparse Core Ops, SparseCore 0:
  10.7 54.0 all-gather.1
  125.1 44.3 reduce-scatter.1

commit v15 on v14

--- a/solution.py
+++ b/solution.py
@@ -147,7 +147,7 @@
         in_specs=[VMEM, VMEM, ANY, ANY],
         out_specs=VMEM,
         out_shape=jax.ShapeDtypeStruct((PLANE, 5 * lines, LANES), F32),
-        compiler_params=PARAMS,
+        compiler_params=pltpu.CompilerParams(vmem_limit_bytes=8 << 20),
         cost_estimate=cost(0, 4 * parts.size),
     )(parts, own, *after)
 

time: 203 us -> 203 us (level)
  no operation moved by 1% of the time
where the time goes in v15:
time: 203 us; the launch traced here: 202 us
  waiting for transfers between devices  100 us (49%)
  Pallas kernels  38.8 us (19%)
  starting transfers between devices  17.6 us (9%)
  blocking collectives  16.8 us (8%)
  between operations  14.2 us (7%)
  other arithmetic  9.92 us (5%)
  local copies, waits for them, and re-layouts  4.65 us (2%)
    ppermute x1, waiting for transfers between devices, on_device(): across = lax.ppermute(own, 'xl', SWAP)  50.3 us
    reduce_scatter x1, waiting for transfers between devices, on_device(): summed = lax.psum_scatter(partial, 'z', scatter_dimension=0, tiled=True)  33.4 us
    all_to_all x1, blocking collectives, on_device(): shared = lax.all_to_all(copies, 'z', 0, 0, tiled=True)  16.8 us
    pallas_call x2, Pallas kernels, head_block(): pl.pallas_call(body, in_specs=[SMEM] + [VMEM, ANY, ANY] * count + [ANY],...  15 us
    pallas_call x1, Pallas kernels, logits_and_stats(): pl.pallas_call(body, in_specs=[SMEM, ANY] + [ANY] * count, out_specs=[ANY...  10.6 us
    pallas_call x1, Pallas kernels, partial_product(): pl.pallas_call(body, in_specs=[SMEM, VMEM, ANY, ANY] + [ANY] * count, out...  10.5 us
    all_to_all x1, starting transfers between devices, on_device(): shared = lax.all_to_all(shared, ('xh', 'xl', 'y'), 0, 0, tiled=True)  7.39 us
    all_to_all x1, starting transfers between devices, on_device(): summed = lax.all_to_all(shares, ('xh', 'xl', 'y'), 0, 0, tiled=True)  7.26 us
  transfers between devices with their start and end apart: 11, of which 7 were waited for; matrix products, arithmetic and copies ran while one was open for 3% of the time, Pallas kernels for 8%

profile of v15, /device:TPU:8, one launch (start us, length us, event | category | flops | bytes accessed | tf_op | source)
XLA Modules:
  0.0 202.1 jit_solution(6299535930314468875)
XLA Ops:
  7.2 0.0 all-gather.2.cloned.1.call-start
  7.2 0.7 fusion.17
  7.9 0.7 fusion.23
  8.6 0.1 copy.41
  8.7 1.8 fusion.2
  10.6 1.6 collective-permute-start
  12.2 50.3 %collective-permute-done.refs_1_ = bf16[320,3584]{1,0:T(8,128)(2,1)S(1)} collective-permute-done((bf16[320,3584]{1,0:T(8,128)(2,1)}, bf16[320,3584]{1,0:T(8,128)(2,1)S(1)}, u32[]{:S(2)}, u32[]{:S(2)}) %collective-permute-start) | collective-permute-done | bytes 2293792 | tf_op jit(solution)/shard_map/ppermute | solution.py:360
  62.5 0.7 pad_add_fusion.starts_ref
  63.2 3.9 %collective-permute-done.2.refs_3_ = bf16[320,3584]{1,0:T(8,128)(2,1)} collective-permute-done((bf16[320,3584]{1,0:T(8,128)(2,1)S(1)}, bf16[320,3584]{1,0:T(8,128)(2,1)}, u32[]{:S(2)}, u32[]{:S(2)}) %collective-permute-start.2) | collective-permute-done | bytes 2293792 | tf_op jit(solution)/shard_map/ppermute | solution.py:369
  67.1 10.6 %shard_map.68 = (bf16[640,512]{1,0:T(8,128)(2,1)}, bf16[640,512]{1,0:T(8,128)(2,1)}, f32[8,512]{1,0:T(8,128)}, f32[8,12,128]{2,1,0:T(8,128)}, f32[8,128]{1,0:T(8,128)}, /*index=5*/bf16[512,3712]{1,0:T(8,128)(2,1)}) custom-call(s32[4]{0:T(128)} %pad_add_fusion.starts_ref, ...), custom_call_target="tpu_custom_call", output_to_operand_aliasing={{5}: (1, {})} | custom-call | flops 4697620480 | bytes 14155776 | tf_op jit(solution)/shard_map/pallas_call | solution.py:106
  77.7 0.2 collective-permute-start.3
  77.9 0.4 collective-permute-start.4
  78.3 16.8 %all_to_all.15.parts_ref = f32[8,12,128]{2,1,0:T(8,128)S(1)} all-to-all(f32[8,12,128]{2,1,0:T(8,128)} %get-tuple-element.9), channel_id=1, replica_groups=mesh['z'=8,'core'=2,'xh'=2,'xl'=2,'y'=4] {'z'}, dimensions={0} | all-to-all | bytes 98304 | tf_op jit(solution)/shard_map/all_to_all | solution.py:381
  95.2 0.7 copy-done.2
  95.8 0.7 shard_map.69
  96.5 1.9 copy-done
  98.4 7.4 %all-to-all-start.1 = ((f32[16,20,128]{2,1,0:T(8,128)}), f32[16,20,128]{2,1,0:T(8,128)S(1)}, u32[]{:S(2)}, u32[]{:S(2)}) async-start(f32[16,20,128]{2,1,0:T(8,128)} %shard_map.69), calls=%async_computation.1 | async-start | bytes 393216 | tf_op jit(solution)/shard_map/all_to_all | solution.py:383
  105.8 0.2 reduce-scatter.2.cloned.1.call-start
  106.0 6.4 %all-to-all-done.1 = f32[16,20,128]{2,1,0:T(8,128)S(1)} async-done(((f32[16,20,128]{2,1,0:T(8,128)}), f32[16,20,128]{2,1,0:T(8,128)S(1)}, u32[]{:S(2)}, u32[]{:S(2)}) %all-to-all-start.1) | async-done | bytes 163872 | tf_op jit(solution)/shard_map/all_to_all | solution.py:383
  112.6 0.8 fusion.27
  113.4 0.6 pad_maximum_fusion.4.rows_ref
  114.0 10.5 %shard_map.70.refs_6_ = bf16[512,3584]{1,0:T(8,128)(2,1)} custom-call(s32[4]{0:T(128)} %pad_add_fusion.starts_ref, f32[2,512]{1,0:T(2,128)} %pad_maximum_fusion.4.rows_ref, bf16[640,512]{1,0:T(8,128)(2,1)} %get-tuple-element.13.first_ref.refs_1_, bf16[640,512]{1,0:T(8,128)(2,1)} %get-tuple-element.12.last_ref, bf16[320,3584]{1,0:T(8,128)(2,1)} %bitcast.71, ...), custom_call_target="tpu_custom_call" | custom-call | flops 4697620480 | bytes 14155776 | tf_op jit(solution)/shard_map/pallas_call | solution.py:217
  124.6 0.1 collective-permute-start.5
  124.7 0.1 pad_add_fusion.1
  124.8 1.1 collective-permute-done.5
  125.9 0.1 reshape.62
  126.0 0.1 mul.116
  126.1 0.1 reduce_sum.58
  126.2 0.1 mul.123
  126.2 0.2 select_reduce_fusion
  126.4 0.1 add.136
  126.5 0.4 multiply_reduce_fusion
  126.9 0.1 multiply_multiply_fusion
  126.9 0.1 reshape.63
  127.0 0.6 slice_bitcast_fusion.1
  127.7 7.5 %shard_map.73 = bf16[320,3584]{1,0:T(8,128)(2,1)} custom-call(s32[4]{0:T(128)} %pad_add_fusion.starts_ref, f32[3,512]{1,0:T(4,128)} %get-tuple-element.29.refs_0_, bf16[640,512]{1,0:T(8,128)(2,1)} %get-tuple-element.13.first_ref.refs_1_, bf16[512,3712]{1,0:T(8,128)(2,1)} %get-tuple-element.11.refs_2_, f32[3,512]{1,0:T(4,128)} %get-tuple-element.28.refs_3_, ...), custom_call_target="tpu_custom_call" | custom-call | flops 2348810240 | bytes 9633792 | tf_op jit(solution)/shard_map/pallas_call | solution.py:286
  135.1 0.4 collective-permute-start.6
  135.6 0.1 mul.127
  135.7 33.4 %reduce-scatter.2.cloned.1.call-done.in_ref = bf16[64,3584]{1,0:T(8,128)(2,1)} async-done(((bf16[512,3584]{1,0:T(8,128)(2,1)}), bf16[64,3584]{1,0:T(8,128)(2,1)}) %reduce-scatter.2.cloned.1.call-update) | async-done | bytes 458768 | tf_op jit(solution)/shard_map/reduce_scatter | solution.py:394
  169.1 2.1 %shard_map.71.refs_6_ = bf16[16,64,224]{2,1,0:T(8,128)(2,1)} custom-call(bf16[64,3584]{1,0:T(8,128)(2,1)} %reduce-scatter.2.cloned.1.call-done.in_ref), custom_call_target="tpu_custom_call" | custom-call | bytes 917504 | tf_op jit(solution)/shard_map/pallas_call | solution.py:316
  171.1 7.3 %all-to-all-start.2 = ((bf16[16,64,224]{2,1,0:T(8,128)(2,1)}), bf16[16,64,224]{2,1,0:T(8,128)(2,1)S(1)}, u32[]{:S(2)}, u32[]{:S(2)}) async-start(bf16[16,64,224]{2,1,0:T(8,128)(2,1)} %shard_map.71.refs_6_), calls=%async_computation.3 | async-start | bytes 1048576 | tf_op jit(solution)/shard_map/all_to_all | solution.py:397
  178.4 7.5 %shard_map.72 = bf16[320,3584]{1,0:T(8,128)(2,1)} custom-call(s32[4]{0:T(128)} %pad_add_fusion.starts_ref, f32[3,512]{1,0:T(4,128)} %get-tuple-element.29.refs_0_, bf16[640,512]{1,0:T(8,128)(2,1)} %get-tuple-element.13.first_ref.refs_1_, bf16[512,3712]{1,0:T(8,128)(2,1)} %get-tuple-element.11.refs_2_, f32[3,512]{1,0:T(4,128)} %get-tuple-element.28.refs_3_, ...), custom_call_target="tpu_custom_call" | custom-call | flops 2348810240 | bytes 9633792 | tf_op jit(solution)/shard_map/pallas_call | solution.py:286
  185.9 2.3 %collective-permute-done.6 = bf16[320,3584]{1,0:T(8,128)(2,1)S(1)} collective-permute-done((bf16[320,3584]{1,0:T(8,128)(2,1)}, bf16[320,3584]{1,0:T(8,128)(2,1)S(1)}, u32[]{:S(2)}, u32[]{:S(2)}) %collective-permute-start.6) | collective-permute-done | bytes 2293792 | tf_op jit(solution)/shard_map/ppermute | solution.py:425
  188.1 3.6 %fusion = bf16[3584,320]{0,1:T(8,128)(2,1)} fusion(bf16[320,3584]{1,0:T(8,128)(2,1)S(1)} %collective-permute-done.6, bf16[320,3584]{1,0:T(8,128)(2,1)} %shard_map.72), kind=kLoop, calls=%fused_computation.1 | loop fusion | flops 4587520 | bytes 6881280 | tf_op jit(solution)/shard_map/transpose | solution.py:428
  191.7 2.6 %all-to-all-done.2 = bf16[16,64,224]{2,1,0:T(8,128)(2,1)S(1)} async-done(((bf16[16,64,224]{2,1,0:T(8,128)(2,1)}), bf16[16,64,224]{2,1,0:T(8,128)(2,1)S(1)}, u32[]{:S(2)}, u32[]{:S(2)}) %all-to-all-start.2) | async-done | bytes 458784 | tf_op jit(solution)/shard_map/all_to_all | solution.py:397
  194.3 0.1 convert_reduce_fusion
  194.4 0.1 fusion.3
  194.5 0.7 copy.45
  (28 shorter events, 0.3 us)
Async XLA Ops:
  7.2 59.9 %all-gather.2.cloned.1.call-start = ((), (), s32[]{:S(2)}) async-start(), calls=%async_computation.4 | async-start | bytes 4276224 | tf_op jit(solution)/shard_map/all_gather | solution.py:363
  10.6 51.9 %collective-permute-start = (bf16[320,3584]{1,0:T(8,128)(2,1)}, bf16[320,3584]{1,0:T(8,128)(2,1)S(1)}, u32[]{:S(2)}, u32[]{:S(2)}) collective-permute-start(bf16[320,3584]{1,0:T(8,128)(2,1)} %bitcast.68), channel_id=1, source_target_pairs={{0,4},{4,0},{1,5},{5,1},{2,6},{6,2},{3,7},{7,3},{8,12},{12,8},{9,1... | collective-permute-start | bytes 6881288 | tf_op jit(solution)/shard_map/ppermute | solution.py:360
  12.2 51.0 %collective-permute-start.1 = (bf16[320,3584]{1,0:T(8,128)(2,1)}, bf16[320,3584]{1,0:T(8,128)(2,1)}, u32[]{:S(2)}, u32[]{:S(2)}) collective-permute-start(bf16[320,3584]{1,0:T(8,128)(2,1)} %bitcast.69), channel_id=1, source_target_pairs={{0,16},{16,0},{1,17},{17,1},{2,18},{18,2},{3,19},{19,3},{4,20},{20... | collective-permute-start | bytes 6881288 | tf_op jit(solution)/shard_map/ppermute | solution.py:361
  62.5 4.6 %copy-start.3 = (bf16[320,3584]{1,0:T(8,128)(2,1)}, bf16[320,3584]{1,0:T(8,128)(2,1)S(1)}, u32[]{:S(2)}) copy-start(bf16[320,3584]{1,0:T(8,128)(2,1)S(1)} %collective-permute-done.refs_1_) | copy-start | bytes 6881284
  62.5 4.6 %collective-permute-start.2 = (bf16[320,3584]{1,0:T(8,128)(2,1)S(1)}, bf16[320,3584]{1,0:T(8,128)(2,1)}, u32[]{:S(2)}, u32[]{:S(2)}) collective-permute-start(bf16[320,3584]{1,0:T(8,128)(2,1)S(1)} %collective-permute-done.refs_1_), channel_id=1, source_target_pairs={{0,16},{16,0},{1,17},{17,1},{2,18},{18,2},{3,19},{19,3},{4,20},{20... | collective-permute-start | bytes 6881288 | tf_op jit(solution)/shard_map/ppermute | solution.py:369
  77.7 17.4 %collective-permute-start.3 = (bf16[512,3712]{1,0:T(8,128)(2,1)}, bf16[512,3712]{1,0:T(8,128)(2,1)S(1)}, u32[]{:S(2)}, u32[]{:S(2)}) collective-permute-start(bf16[512,3712]{1,0:T(8,128)(2,1)} %get-tuple-element.11.refs_2_), channel_id=1, source_target_pairs={{0,16},{16,0},{1,17},{17,1},{2,18},{18,2},{3,19},{19,3},{4,20},{20... | collective-permute-start | bytes 11403272 | tf_op jit(solution)/shard_map/ppermute | solution.py:379
  77.9 17.2 %collective-permute-start.4 = (bf16[640,512]{1,0:T(8,128)(2,1)}, bf16[640,512]{1,0:T(8,128)(2,1)S(1)}, u32[]{:S(2)}, u32[]{:S(2)}) collective-permute-start(bf16[640,512]{1,0:T(8,128)(2,1)} %get-tuple-element.12.last_ref), channel_id=1, source_target_pairs={{0,16},{16,0},{1,17},{17,1},{2,18},{18,2},{3,19},{19,3},{4,20},{20... | collective-permute-start | bytes 1966088 | tf_op jit(solution)/shard_map/ppermute | solution.py:380
  95.1 1.4 copy-start.1
  95.1 0.7 copy-start.2
  96.5 1.9 copy-start
  98.4 14.1 %all-to-all-start.1 = ((f32[16,20,128]{2,1,0:T(8,128)}), f32[16,20,128]{2,1,0:T(8,128)S(1)}, u32[]{:S(2)}, u32[]{:S(2)}) async-start(f32[16,20,128]{2,1,0:T(8,128)} %shard_map.69), calls=%async_computation.1 | async-start | bytes 393216 | tf_op jit(solution)/shard_map/all_to_all | solution.py:383
  105.8 63.2 %reduce-scatter.2.cloned.1.call-start = ((), (), s32[]{:S(2)}) async-start(), calls=%async_computation.5 | async-start | bytes 4128768 | tf_op jit(solution)/shard_map/reduce_scatter | solution.py:394
  124.6 1.3 collective-permute-start.5
  135.1 53.0 %collective-permute-start.6 = (bf16[320,3584]{1,0:T(8,128)(2,1)}, bf16[320,3584]{1,0:T(8,128)(2,1)S(1)}, u32[]{:S(2)}, u32[]{:S(2)}) collective-permute-start(bf16[320,3584]{1,0:T(8,128)(2,1)} %shard_map.73), channel_id=1, source_target_pairs={{0,4},{4,0},{1,5},{5,1},{2,6},{6,2},{3,7},{7,3},{8,12},{12,8},{9,1... | collective-permute-start | bytes 6881288 | tf_op jit(solution)/shard_map/ppermute | solution.py:425
  171.1 23.2 %all-to-all-start.2 = ((bf16[16,64,224]{2,1,0:T(8,128)(2,1)}), bf16[16,64,224]{2,1,0:T(8,128)(2,1)S(1)}, u32[]{:S(2)}, u32[]{:S(2)}) async-start(bf16[16,64,224]{2,1,0:T(8,128)(2,1)} %shard_map.71.refs_6_), calls=%async_computation.3 | async-start | bytes 1048576 | tf_op jit(solution)/shard_map/all_to_all | solution.py:397
Sparse Core Ops, SparseCore 0:
  10.7 54.0 all-gather.1
  124.7 44.3 reduce-scatter.1

commit v16 on v15

--- a/solution.py
+++ b/solution.py
@@ -12,6 +12,7 @@
 SWAP = [(0, 1), (1, 0)]
 LANES = 128
 STEPS = 7
+AHEAD = 3
 PARAMS = pltpu.CompilerParams(vmem_limit_bytes=56 << 20)
 SMEM = pl.BlockSpec(memory_space=pltpu.SMEM)
 VMEM = pl.BlockSpec(memory_space=pltpu.VMEM)
@@ -62,13 +63,13 @@
         facts_copy = pltpu.make_async_copy(
             h_ref.at[:, pl.ds(features, LANES)], f, sems.at[STEPS, 0]
         )
-        for copy in copies[0] + copies[1] + [facts_copy]:
+        for copy in sum(copies[:AHEAD], []) + [facts_copy]:
             copy.start()
         for k in range(STEPS):
             for copy in copies[k]:
                 copy.wait()
-            if k + 2 < STEPS:
-                for copy in copies[k + 2]:
+            if k + AHEAD < STEPS:
+                for copy in copies[k + AHEAD]:
                     copy.start()
             part = dot(w[k], h[k], ((1,), (1,)))
             held[...] = part if k == 0 else held[...] + part
@@ -186,7 +187,7 @@
             ]
             for k in range(STEPS)
         ]
-        for copy in first + loads[0] + loads[1]:
+        for copy in first + sum(loads[:AHEAD], []):
             copy.start()
         for low in range(0, columns, columns_here):
             if low % half == 0:
@@ -203,8 +204,8 @@
         for k in range(STEPS):
             for copy in loads[k]:
                 copy.wait()
-            if k + 2 < STEPS:
-                for copy in loads[k + 2]:
+            if k + AHEAD < STEPS:
+                for copy in loads[k + AHEAD]:
                     copy.start()
             out = dot(held[...], w[k], ((0,), (0,)))
             if k >= 2:
@@ -256,7 +257,7 @@
             ]
             for k in range(STEPS)
         ]
-        for copy in first + loads[0] + loads[1]:
+        for copy in first + sum(loads[:AHEAD], []):
             copy.start()
         for i in range(count):
             first[i].wait()
@@ -268,8 +269,8 @@
             )
 
         for k in range(STEPS):
-            if k + 2 < STEPS:
-                for copy in loads[k + 2]:
+            if k + AHEAD < STEPS:
+                for copy in loads[k + AHEAD]:
                     copy.start()
             out = None
             for i in range(count):

time: 203 us -> 203 us (level)
  transfers between devices with their start and end apart: 11 -> 11, of which waited for: 7 -> 7; matrix products, arithmetic and copies ran while one was open for 3% -> 3% of each run, Pallas kernels for 8% -> 9%
where the time goes in v16:
time: 203 us; the launch traced here: 202 us
  waiting for transfers between devices  99.8 us (49%)
  Pallas kernels  39.6 us (20%)
  starting transfers between devices  17.4 us (9%)
  blocking collectives  16.8 us (8%)
  between operations  14.2 us (7%)
  other arithmetic  9.92 us (5%)
  local copies, waits for them, and re-layouts  4.65 us (2%)
    ppermute x1, waiting for transfers between devices, on_device(): across = lax.ppermute(own, 'xl', SWAP)  50.3 us
    reduce_scatter x1, waiting for transfers between devices, on_device(): summed = lax.psum_scatter(partial, 'z', scatter_dimension=0, tiled=True)  33.3 us
    all_to_all x1, blocking collectives, on_device(): shared = lax.all_to_all(copies, 'z', 0, 0, tiled=True)  16.8 us
    pallas_call x2, Pallas kernels, head_block(): pl.pallas_call(body, in_specs=[SMEM] + [VMEM, ANY, ANY] * count + [ANY],...  15.3 us
    pallas_call x1, Pallas kernels, partial_product(): pl.pallas_call(body, in_specs=[SMEM, VMEM, ANY, ANY] + [ANY] * count, out...  10.9 us
    pallas_call x1, Pallas kernels, logits_and_stats(): pl.pallas_call(body, in_specs=[SMEM, ANY] + [ANY] * count, out_specs=[ANY...  10.6 us
    all_to_all x1, starting transfers between devices, on_device(): shared = lax.all_to_all(shared, ('xh', 'xl', 'y'), 0, 0, tiled=True)  7.39 us
    all_to_all x1, starting transfers between devices, on_device(): summed = lax.all_to_all(shares, ('xh', 'xl', 'y'), 0, 0, tiled=True)  7.26 us
  transfers between devices with their start and end apart: 11, of which 7 were waited for; matrix products, arithmetic and copies ran while one was open for 3% of the time, Pallas kernels for 9%

profile of v16, /device:TPU:8, one launch (start us, length us, event | category | flops | bytes accessed | tf_op | source)
XLA Modules:
  0.0 202.4 jit_solution(2567485190542403264)
XLA Ops:
  7.2 0.0 all-gather.2.cloned.1.call-start
  7.2 0.7 fusion.17
  7.9 0.7 fusion.23
  8.6 0.1 copy.41
  8.7 1.8 fusion.2
  10.6 1.6 collective-permute-start
  12.2 50.3 %collective-permute-done.refs_1_ = bf16[320,3584]{1,0:T(8,128)(2,1)S(1)} collective-permute-done((bf16[320,3584]{1,0:T(8,128)(2,1)}, bf16[320,3584]{1,0:T(8,128)(2,1)S(1)}, u32[]{:S(2)}, u32[]{:S(2)}) %collective-permute-start) | collective-permute-done | bytes 2293792 | tf_op jit(solution)/shard_map/ppermute | solution.py:361
  62.5 0.7 pad_add_fusion.starts_ref
  63.2 3.9 %collective-permute-done.2.refs_3_ = bf16[320,3584]{1,0:T(8,128)(2,1)} collective-permute-done((bf16[320,3584]{1,0:T(8,128)(2,1)S(1)}, bf16[320,3584]{1,0:T(8,128)(2,1)}, u32[]{:S(2)}, u32[]{:S(2)}) %collective-permute-start.2) | collective-permute-done | bytes 2293792 | tf_op jit(solution)/shard_map/ppermute | solution.py:370
  67.1 10.6 %shard_map.68 = (bf16[640,512]{1,0:T(8,128)(2,1)}, bf16[640,512]{1,0:T(8,128)(2,1)}, f32[8,512]{1,0:T(8,128)}, f32[8,12,128]{2,1,0:T(8,128)}, f32[8,128]{1,0:T(8,128)}, /*index=5*/bf16[512,3712]{1,0:T(8,128)(2,1)}) custom-call(s32[4]{0:T(128)} %pad_add_fusion.starts_ref, ...), custom_call_target="tpu_custom_call", output_to_operand_aliasing={{5}: (1, {})} | custom-call | flops 4697620480 | bytes 14155776 | tf_op jit(solution)/shard_map/pallas_call | solution.py:107
  77.7 0.2 collective-permute-start.3
  77.9 0.4 collective-permute-start.4
  78.3 16.8 %all_to_all.15.parts_ref = f32[8,12,128]{2,1,0:T(8,128)S(1)} all-to-all(f32[8,12,128]{2,1,0:T(8,128)} %get-tuple-element.9), channel_id=1, replica_groups=mesh['z'=8,'core'=2,'xh'=2,'xl'=2,'y'=4] {'z'}, dimensions={0} | all-to-all | bytes 98304 | tf_op jit(solution)/shard_map/all_to_all | solution.py:382
  95.2 0.7 copy-done.2
  95.8 0.7 shard_map.69
  96.5 1.9 copy-done
  98.4 7.4 %all-to-all-start.1 = ((f32[16,20,128]{2,1,0:T(8,128)}), f32[16,20,128]{2,1,0:T(8,128)S(1)}, u32[]{:S(2)}, u32[]{:S(2)}) async-start(f32[16,20,128]{2,1,0:T(8,128)} %shard_map.69), calls=%async_computation.1 | async-start | bytes 393216 | tf_op jit(solution)/shard_map/all_to_all | solution.py:384
  105.8 0.2 reduce-scatter.2.cloned.1.call-start
  106.0 6.4 %all-to-all-done.1 = f32[16,20,128]{2,1,0:T(8,128)S(1)} async-done(((f32[16,20,128]{2,1,0:T(8,128)}), f32[16,20,128]{2,1,0:T(8,128)S(1)}, u32[]{:S(2)}, u32[]{:S(2)}) %all-to-all-start.1) | async-done | bytes 163872 | tf_op jit(solution)/shard_map/all_to_all | solution.py:384
  112.6 0.8 fusion.27
  113.4 0.6 pad_maximum_fusion.4.rows_ref
  114.0 10.9 %shard_map.70.refs_6_ = bf16[512,3584]{1,0:T(8,128)(2,1)} custom-call(s32[4]{0:T(128)} %pad_add_fusion.starts_ref, f32[2,512]{1,0:T(2,128)} %pad_maximum_fusion.4.rows_ref, bf16[640,512]{1,0:T(8,128)(2,1)} %get-tuple-element.13.first_ref.refs_1_, bf16[640,512]{1,0:T(8,128)(2,1)} %get-tuple-element.12.last_ref, bf16[320,3584]{1,0:T(8,128)(2,1)} %bitcast.71, ...), custom_call_target="tpu_custom_call" | custom-call | flops 4697620480 | bytes 14155776 | tf_op jit(solution)/shard_map/pallas_call | solution.py:218
  125.0 0.1 collective-permute-start.5
  125.1 0.1 pad_add_fusion.1
  125.2 1.1 collective-permute-done.5
  126.3 0.1 reshape.62
  126.4 0.1 mul.116
  126.5 0.1 reduce_sum.58
  126.6 0.1 mul.123
  126.6 0.2 select_reduce_fusion
  126.8 0.1 add.136
  126.9 0.4 multiply_reduce_fusion
  127.3 0.1 multiply_multiply_fusion
  127.3 0.1 reshape.63
  127.4 0.6 slice_bitcast_fusion.1
  128.1 7.7 %shard_map.73 = bf16[320,3584]{1,0:T(8,128)(2,1)} custom-call(s32[4]{0:T(128)} %pad_add_fusion.starts_ref, f32[3,512]{1,0:T(4,128)} %get-tuple-element.29.refs_0_, bf16[640,512]{1,0:T(8,128)(2,1)} %get-tuple-element.13.first_ref.refs_1_, bf16[512,3712]{1,0:T(8,128)(2,1)} %get-tuple-element.11.refs_2_, f32[3,512]{1,0:T(4,128)} %get-tuple-element.28.refs_3_, ...), custom_call_target="tpu_custom_call" | custom-call | flops 2348810240 | bytes 9633792 | tf_op jit(solution)/shard_map/pallas_call | solution.py:287
  135.8 0.3 collective-permute-start.6
  136.1 0.1 mul.127
  136.2 33.3 %reduce-scatter.2.cloned.1.call-done.in_ref = bf16[64,3584]{1,0:T(8,128)(2,1)} async-done(((bf16[512,3584]{1,0:T(8,128)(2,1)}), bf16[64,3584]{1,0:T(8,128)(2,1)}) %reduce-scatter.2.cloned.1.call-update) | async-done | bytes 458768 | tf_op jit(solution)/shard_map/reduce_scatter | solution.py:395
  169.5 2.1 %shard_map.71.refs_6_ = bf16[16,64,224]{2,1,0:T(8,128)(2,1)} custom-call(bf16[64,3584]{1,0:T(8,128)(2,1)} %reduce-scatter.2.cloned.1.call-done.in_ref), custom_call_target="tpu_custom_call" | custom-call | bytes 917504 | tf_op jit(solution)/shard_map/pallas_call | solution.py:317
  171.5 7.3 %all-to-all-start.2 = ((bf16[16,64,224]{2,1,0:T(8,128)(2,1)}), bf16[16,64,224]{2,1,0:T(8,128)(2,1)S(1)}, u32[]{:S(2)}, u32[]{:S(2)}) async-start(bf16[16,64,224]{2,1,0:T(8,128)(2,1)} %shard_map.71.refs_6_), calls=%async_computation.3 | async-start | bytes 1048576 | tf_op jit(solution)/shard_map/all_to_all | solution.py:398
  178.8 7.6 %shard_map.72 = bf16[320,3584]{1,0:T(8,128)(2,1)} custom-call(s32[4]{0:T(128)} %pad_add_fusion.starts_ref, f32[3,512]{1,0:T(4,128)} %get-tuple-element.29.refs_0_, bf16[640,512]{1,0:T(8,128)(2,1)} %get-tuple-element.13.first_ref.refs_1_, bf16[512,3712]{1,0:T(8,128)(2,1)} %get-tuple-element.11.refs_2_, f32[3,512]{1,0:T(4,128)} %get-tuple-element.28.refs_3_, ...), custom_call_target="tpu_custom_call" | custom-call | flops 2348810240 | bytes 9633792 | tf_op jit(solution)/shard_map/pallas_call | solution.py:287
  186.4 2.4 %collective-permute-done.6 = bf16[320,3584]{1,0:T(8,128)(2,1)S(1)} collective-permute-done((bf16[320,3584]{1,0:T(8,128)(2,1)}, bf16[320,3584]{1,0:T(8,128)(2,1)S(1)}, u32[]{:S(2)}, u32[]{:S(2)}) %collective-permute-start.6) | collective-permute-done | bytes 2293792 | tf_op jit(solution)/shard_map/ppermute | solution.py:426
  188.8 3.6 %fusion = bf16[3584,320]{0,1:T(8,128)(2,1)} fusion(bf16[320,3584]{1,0:T(8,128)(2,1)S(1)} %collective-permute-done.6, bf16[320,3584]{1,0:T(8,128)(2,1)} %shard_map.72), kind=kLoop, calls=%fused_computation.1 | loop fusion | flops 4587520 | bytes 6881280 | tf_op jit(solution)/shard_map/transpose | solution.py:429
  192.3 2.4 %all-to-all-done.2 = bf16[16,64,224]{2,1,0:T(8,128)(2,1)S(1)} async-done(((bf16[16,64,224]{2,1,0:T(8,128)(2,1)}), bf16[16,64,224]{2,1,0:T(8,128)(2,1)S(1)}, u32[]{:S(2)}, u32[]{:S(2)}) %all-to-all-start.2) | async-done | bytes 458784 | tf_op jit(solution)/shard_map/all_to_all | solution.py:398
  194.7 0.1 convert_reduce_fusion
  194.8 0.1 fusion.3
  194.9 0.7 copy.45
  (28 shorter events, 0.3 us)
Async XLA Ops:
  7.2 59.9 %all-gather.2.cloned.1.call-start = ((), (), s32[]{:S(2)}) async-start(), calls=%async_computation.4 | async-start | bytes 4276224 | tf_op jit(solution)/shard_map/all_gather | solution.py:364
  10.6 51.9 %collective-permute-start = (bf16[320,3584]{1,0:T(8,128)(2,1)}, bf16[320,3584]{1,0:T(8,128)(2,1)S(1)}, u32[]{:S(2)}, u32[]{:S(2)}) collective-permute-start(bf16[320,3584]{1,0:T(8,128)(2,1)} %bitcast.68), channel_id=1, source_target_pairs={{0,4},{4,0},{1,5},{5,1},{2,6},{6,2},{3,7},{7,3},{8,12},{12,8},{9,1... | collective-permute-start | bytes 6881288 | tf_op jit(solution)/shard_map/ppermute | solution.py:361
  12.2 51.0 %collective-permute-start.1 = (bf16[320,3584]{1,0:T(8,128)(2,1)}, bf16[320,3584]{1,0:T(8,128)(2,1)}, u32[]{:S(2)}, u32[]{:S(2)}) collective-permute-start(bf16[320,3584]{1,0:T(8,128)(2,1)} %bitcast.69), channel_id=1, source_target_pairs={{0,16},{16,0},{1,17},{17,1},{2,18},{18,2},{3,19},{19,3},{4,20},{20... | collective-permute-start | bytes 6881288 | tf_op jit(solution)/shard_map/ppermute | solution.py:362
  62.5 4.6 %copy-start.3 = (bf16[320,3584]{1,0:T(8,128)(2,1)}, bf16[320,3584]{1,0:T(8,128)(2,1)S(1)}, u32[]{:S(2)}) copy-start(bf16[320,3584]{1,0:T(8,128)(2,1)S(1)} %collective-permute-done.refs_1_) | copy-start | bytes 6881284
  62.5 4.6 %collective-permute-start.2 = (bf16[320,3584]{1,0:T(8,128)(2,1)S(1)}, bf16[320,3584]{1,0:T(8,128)(2,1)}, u32[]{:S(2)}, u32[]{:S(2)}) collective-permute-start(bf16[320,3584]{1,0:T(8,128)(2,1)S(1)} %collective-permute-done.refs_1_), channel_id=1, source_target_pairs={{0,16},{16,0},{1,17},{17,1},{2,18},{18,2},{3,19},{19,3},{4,20},{20... | collective-permute-start | bytes 6881288 | tf_op jit(solution)/shard_map/ppermute | solution.py:370
  77.7 17.4 %collective-permute-start.3 = (bf16[512,3712]{1,0:T(8,128)(2,1)}, bf16[512,3712]{1,0:T(8,128)(2,1)S(1)}, u32[]{:S(2)}, u32[]{:S(2)}) collective-permute-start(bf16[512,3712]{1,0:T(8,128)(2,1)} %get-tuple-element.11.refs_2_), channel_id=1, source_target_pairs={{0,16},{16,0},{1,17},{17,1},{2,18},{18,2},{3,19},{19,3},{4,20},{20... | collective-permute-start | bytes 11403272 | tf_op jit(solution)/shard_map/ppermute | solution.py:380
  77.9 17.2 %collective-permute-start.4 = (bf16[640,512]{1,0:T(8,128)(2,1)}, bf16[640,512]{1,0:T(8,128)(2,1)S(1)}, u32[]{:S(2)}, u32[]{:S(2)}) collective-permute-start(bf16[640,512]{1,0:T(8,128)(2,1)} %get-tuple-element.12.last_ref), channel_id=1, source_target_pairs={{0,16},{16,0},{1,17},{17,1},{2,18},{18,2},{3,19},{19,3},{4,20},{20... | collective-permute-start | bytes 1966088 | tf_op jit(solution)/shard_map/ppermute | solution.py:381
  95.1 1.4 copy-start.1
  95.1 0.7 copy-start.2
  96.5 1.9 copy-start
  98.4 14.1 %all-to-all-start.1 = ((f32[16,20,128]{2,1,0:T(8,128)}), f32[16,20,128]{2,1,0:T(8,128)S(1)}, u32[]{:S(2)}, u32[]{:S(2)}) async-start(f32[16,20,128]{2,1,0:T(8,128)} %shard_map.69), calls=%async_computation.1 | async-start | bytes 393216 | tf_op jit(solution)/shard_map/all_to_all | solution.py:384
  105.8 63.6 %reduce-scatter.2.cloned.1.call-start = ((), (), s32[]{:S(2)}) async-start(), calls=%async_computation.5 | async-start | bytes 4128768 | tf_op jit(solution)/shard_map/reduce_scatter | solution.py:395
  125.0 1.3 collective-permute-start.5
  135.8 53.0 %collective-permute-start.6 = (bf16[320,3584]{1,0:T(8,128)(2,1)}, bf16[320,3584]{1,0:T(8,128)(2,1)S(1)}, u32[]{:S(2)}, u32[]{:S(2)}) collective-permute-start(bf16[320,3584]{1,0:T(8,128)(2,1)} %shard_map.73), channel_id=1, source_target_pairs={{0,4},{4,0},{1,5},{5,1},{2,6},{6,2},{3,7},{7,3},{8,12},{12,8},{9,1... | collective-permute-start | bytes 6881288 | tf_op jit(solution)/shard_map/ppermute | solution.py:426
  171.5 23.2 %all-to-all-start.2 = ((bf16[16,64,224]{2,1,0:T(8,128)(2,1)}), bf16[16,64,224]{2,1,0:T(8,128)(2,1)S(1)}, u32[]{:S(2)}, u32[]{:S(2)}) async-start(bf16[16,64,224]{2,1,0:T(8,128)(2,1)} %shard_map.71.refs_6_), calls=%async_computation.3 | async-start | bytes 1048576 | tf_op jit(solution)/shard_map/all_to_all | solution.py:398
Sparse Core Ops, SparseCore 0:
  10.7 54.0 all-gather.1
  125.1 44.3 reduce-scatter.1

commit v17 on v15

--- a/solution.py
+++ b/solution.py
@@ -139,14 +139,14 @@
         top = jnp.max(tops, axis=0)
         total = jnp.sum(parts_ref[:, lines : 2 * lines] * jnp.exp(tops - top[None]), axis=0)
         picked = jnp.sum(parts_ref[:, 2 * lines :], axis=0)
-        merged = jnp.concatenate([top, total, picked, own_ref[...]])
+        merged = jnp.concatenate([top, total, picked])
         out_ref[...] = jnp.broadcast_to(merged[None], out_ref.shape)
 
     return pl.pallas_call(
         body,
         in_specs=[VMEM, VMEM, ANY, ANY],
         out_specs=VMEM,
-        out_shape=jax.ShapeDtypeStruct((PLANE, 5 * lines, LANES), F32),
+        out_shape=jax.ShapeDtypeStruct((XH * Y, 3 * lines, LANES), F32),
         compiler_params=pltpu.CompilerParams(vmem_limit_bytes=8 << 20),
         cost_estimate=cost(0, 4 * parts.size),
     )(parts, own, *after)
@@ -380,17 +380,15 @@
     far_exps = lax.ppermute(theirs, "core", SWAP)
     shared = lax.all_to_all(copies, "z", 0, 0, tiled=True)
     shared = merge_stats(shared, lined, (far_gathered, far_exps))
-    shared = lax.all_to_all(shared, ("xh", "xl", "y"), 0, 0, tiled=True)
-    shared = shared.reshape(XH, XL, Y, 5, lines, LANES)
-    top = jnp.max(shared[:, :, :, 0], axis=(0, 2))
-    shrink = jnp.exp(shared[:, :, :, 0] - top[None, :, None])
-    total = jnp.sum(shared[:, :, :, 1] * shrink, axis=(0, 2))
-    picked = jnp.sum(shared[:, :, :, 2], axis=(0, 2))
-    norms = top + jnp.log(total)
-    factor = jnp.exp(stats[0] - pick_one(norms, side).reshape(here))
-    token_rows = jnp.stack([stats[5], factor])
-
-    partial = partial_product(starts, token_rows, (mine, theirs), weights, columns_here)
+    shared = lax.all_to_all(shared, ("xh", "y"), 0, 0, tiled=True)
+    shared = shared.reshape(XH * Y, 3, lines, LANES)
+    top = jnp.max(shared[:, 0], axis=0)
+    total = jnp.sum(shared[:, 1] * jnp.exp(shared[:, 0] - top[None]), axis=0)
+    norms = (top + jnp.log(total)).reshape(here)
+    ratio = stats[3] * (jnp.sum(shared[:, 2], axis=0).reshape(here) - norms - stats[4])
+    known = jnp.stack([stats[5], jnp.exp(stats[0] - norms), stats[3], ratio])
+
+    partial = partial_product(starts, known, (mine, theirs), weights, columns_here)
     summed = lax.psum_scatter(partial, "z", scatter_dimension=0, tiled=True)
     cut = features // PLANE
     shares = cut_features(summed, cut)
@@ -398,28 +396,29 @@
     summed = summed.reshape(XH, XL, Y, rows, cut).astype(F32)
     summed = jnp.sum(summed, axis=(0, 2)).reshape(own_rows, cut)
 
-    mask, teacher = shared[0, :, 0, 3], shared[0, :, 0, 4]
-    ratio = mask * (picked - norms - teacher)
-    known = jnp.concatenate([part.reshape(XL, here) for part in (mask, ratio)] + [token_rows])
-    known = jnp.stack([known, lax.ppermute(known, "core", SWAP)])
-    mask, ratio = (
-        part.reshape(CORES, XL, Z, rows) for part in (known[:, :XL], known[:, XL : 2 * XL])
+    far = lax.ppermute(known, "core", SWAP)
+    beside = lax.ppermute(known[2:], "xl", SWAP)
+    opposite = lax.ppermute(known[2:], ("core", "xl"), [(i, 3 - i) for i in range(4)])
+    mask, ratio = jnp.stack([known[2:], beside, far[2:], opposite], axis=1).reshape(
+        2, CORES, XL, Z, rows
     )
     steps = jnp.arange(rows, dtype=jnp.int32)
     later = (steps[None, :] >= steps[:, None]).astype(F32)
     within = jnp.sum(ratio[..., None, :] * later, axis=-1)
     parts = jnp.sum(ratio, axis=-1).reshape(-1)
-    number = jnp.arange(XL * Z, dtype=jnp.int32)
-    order = number % Z * (CORES * XL) + number // Z
-    order = jnp.concatenate([order + core * XL, order + (1 - core) * XL])
+    order = jnp.arange(Z, dtype=jnp.int32) * (CORES * XL)
+    order = jnp.concatenate(
+        [order + (c * XL + s) for c in (core, 1 - core) for s in (side, 1 - side)]
+    )
     beyond = jnp.sum(parts[None, :] * (order[None, :] > order[:, None]), axis=1)
     scales = mask * (within + beyond.reshape(CORES, XL, Z, 1)) / float(tokens)
 
-    own_scale = lax.dynamic_index_in_dim(scales[0], z, 1, False).reshape(own_rows)
+    own_scale = lax.dynamic_index_in_dim(scales[0], z, 1, False)
+    own_scale = jnp.where(side == 0, own_scale, own_scale[::-1]).reshape(own_rows)
     hidden_grad = summed * own_scale[:, None]
 
-    scale = lax.dynamic_index_in_dim(scales, side, 1, False).reshape(CORES, 1, here)
-    rows_of = jnp.concatenate([known[:, 2 * XL :], scale], axis=1)
+    scale = scales[:, 0].reshape(CORES, 1, here)
+    rows_of = jnp.concatenate([jnp.stack([known[:2], far[:2]]), scale], axis=1)
     sides = [(rows_of[0], mine, gathered), (rows_of[1], far_exps, far_gathered)]
     given = head_block(starts, sides, columns_here, columns_here, features, partial)
     from_across = lax.ppermute(given, "xl", SWAP)

time: 203 us -> 203 us (level)
  blocking collectives: 16.8 us -> 30.4 us
  waiting for transfers between devices: 100 us -> 92 us
  starting transfers between devices: 17.6 us -> 13.3 us
    all_to_all x0 -> x1, blocking collectives: none -> 13.6 us  [on_device(): shared = lax.all_to_all(shared, ('xh', 'y'), 0, 0, tiled=True)]
    all_to_all x1 -> x0, starting transfers between devices: 7.39 us -> none  [on_device(): shared = lax.all_to_all(shared, ('xh', 'xl', 'y'), 0, 0, tiled=True)]
    all_to_all x1 -> x0, waiting for transfers between devices: 6.44 us -> none  [on_device(): shared = lax.all_to_all(shared, ('xh', 'xl', 'y'), 0, 0, tiled=True)]
    reduce_scatter x1, waiting for transfers between devices: 33.4 us -> 27.4 us  [on_device(): summed = lax.psum_scatter(partial, 'z', scatter_dimension=0, tiled=True)]
    ppermute x1, waiting for transfers between devices: 2.26 us -> 7.19 us  [on_device(): from_across = lax.ppermute(given, 'xl', SWAP)]
    ppermute x1 -> x3, starting transfers between devices: 0.09 us -> 2.23 us  [the longest x1 1.43 us: on_device(): beside = lax.ppermute(known[2:], 'xl', SWAP)]
  transfers between devices with their start and end apart: 11 -> 12, of which waited for: 7 -> 7; matrix products, arithmetic and copies ran while one was open for 3% -> 3% of each run, Pallas kernels for 8% -> 8%
where the time goes in v17:
time: 203 us; the launch traced here: 202 us
  waiting for transfers between devices  92 us (45%)
  Pallas kernels  38.2 us (19%)
  blocking collectives  30.4 us (15%)
  between operations  14.2 us (7%)
  starting transfers between devices  13.3 us (7%)
  other arithmetic  9.11 us (4%)
  local copies, waits for them, and re-layouts  4.68 us (2%)
    ppermute x1, waiting for transfers between devices, on_device(): across = lax.ppermute(own, 'xl', SWAP)  50.3 us
    reduce_scatter x1, waiting for transfers between devices, on_device(): summed = lax.psum_scatter(partial, 'z', scatter_dimension=0, tiled=True)  27.4 us
    all_to_all x1, blocking collectives, on_device(): shared = lax.all_to_all(copies, 'z', 0, 0, tiled=True)  16.8 us
    pallas_call x2, Pallas kernels, head_block(): pl.pallas_call(body, in_specs=[SMEM] + [VMEM, ANY, ANY] * count + [ANY],...  15 us
    all_to_all x1, blocking collectives, on_device(): shared = lax.all_to_all(shared, ('xh', 'y'), 0, 0, tiled=True)  13.6 us
    pallas_call x1, Pallas kernels, logits_and_stats(): pl.pallas_call(body, in_specs=[SMEM, ANY] + [ANY] * count, out_specs=[ANY...  10.6 us
    pallas_call x1, Pallas kernels, partial_product(): pl.pallas_call(body, in_specs=[SMEM, VMEM, ANY, ANY] + [ANY] * count, out...  10.4 us
    all_to_all x1, starting transfers between devices, on_device(): summed = lax.all_to_all(shares, ('xh', 'xl', 'y'), 0, 0, tiled=True)  7.25 us
  transfers between devices with their start and end apart: 12, of which 7 were waited for; matrix products, arithmetic and copies ran while one was open for 3% of the time, Pallas kernels for 8%

profile of v17, /device:TPU:8, one launch (start us, length us, event | category | flops | bytes accessed | tf_op | source)
XLA Modules:
  0.0 201.8 jit_solution(14352237870693308687)
XLA Ops:
  7.2 0.7 fusion.11
  7.9 0.7 fusion.17
  8.6 0.1 copy.34
  8.7 1.8 fusion.2
  10.6 1.6 collective-permute-start
  12.2 50.3 %collective-permute-done.refs_1_ = bf16[320,3584]{1,0:T(8,128)(2,1)S(1)} collective-permute-done((bf16[320,3584]{1,0:T(8,128)(2,1)}, bf16[320,3584]{1,0:T(8,128)(2,1)S(1)}, u32[]{:S(2)}, u32[]{:S(2)}) %collective-permute-start) | collective-permute-done | bytes 2293792 | tf_op jit(solution)/shard_map/ppermute | solution.py:360
  62.5 0.7 pad_add_fusion.starts_ref
  63.2 3.9 %collective-permute-done.2.refs_3_ = bf16[320,3584]{1,0:T(8,128)(2,1)} collective-permute-done((bf16[320,3584]{1,0:T(8,128)(2,1)S(1)}, bf16[320,3584]{1,0:T(8,128)(2,1)}, u32[]{:S(2)}, u32[]{:S(2)}) %collective-permute-start.2) | collective-permute-done | bytes 2293792 | tf_op jit(solution)/shard_map/ppermute | solution.py:369
  67.1 10.6 %shard_map.68 = (bf16[640,512]{1,0:T(8,128)(2,1)}, bf16[640,512]{1,0:T(8,128)(2,1)}, f32[8,512]{1,0:T(8,128)}, f32[8,12,128]{2,1,0:T(8,128)}, f32[8,128]{1,0:T(8,128)}, /*index=5*/bf16[512,3712]{1,0:T(8,128)(2,1)}) custom-call(s32[4]{0:T(128)} %pad_add_fusion.starts_ref, ...), custom_call_target="tpu_custom_call", output_to_operand_aliasing={{5}: (1, {})} | custom-call | flops 4697620480 | bytes 14155776 | tf_op jit(solution)/shard_map/pallas_call | solution.py:106
  77.8 0.2 collective-permute-start.3
  78.0 0.4 collective-permute-start.4
  78.4 16.8 %all_to_all.15.parts_ref = f32[8,12,128]{2,1,0:T(8,128)S(1)} all-to-all(f32[8,12,128]{2,1,0:T(8,128)} %get-tuple-element.9), channel_id=1, replica_groups=mesh['z'=8,'core'=2,'xh'=2,'xl'=2,'y'=4] {'z'}, dimensions={0} | all-to-all | bytes 98304 | tf_op jit(solution)/shard_map/all_to_all | solution.py:381
  95.2 0.7 copy-done.2
  95.9 0.1 copy-done.1
  96.1 1.2 copy-done
  97.3 13.6 %all_to_all.16 = f32[8,12,128]{2,1,0:T(8,128)S(1)} all-to-all(f32[8,12,128]{2,1,0:T(8,128)S(1)} %shard_map.69), channel_id=1, replica_groups=mesh['z'=8,'core'=2,'xh'=2,'xl'=2,'y'=4] {'xh','y'}, dimensions={0} | all-to-all | bytes 98304 | tf_op jit(solution)/shard_map/all_to_all | solution.py:383
  110.9 0.6 pad_maximum_fusion.2.rows_ref
  111.6 10.4 %shard_map.70.refs_6_ = bf16[512,3584]{1,0:T(8,128)(2,1)} custom-call(s32[4]{0:T(128)} %pad_add_fusion.starts_ref, f32[4,512]{1,0:T(4,128)} %pad_maximum_fusion.2.rows_ref, bf16[640,512]{1,0:T(8,128)(2,1)} %get-tuple-element.13.first_ref.refs_1_, bf16[640,512]{1,0:T(8,128)(2,1)} %get-tuple-element.12.last_ref, bf16[320,3584]{1,0:T(8,128)(2,1)} %bitcast.71, ...), custom_call_target="tpu_custom_call" | custom-call | flops 4697620480 | bytes 14155776 | tf_op jit(solution)/shard_map/pallas_call | solution.py:217
  122.1 0.1 pad_add_fusion.1
  122.2 0.5 copy-done.3
  122.7 0.8 collective-permute-start.7
  123.5 1.4 collective-permute-start.5
  125.0 0.9 collective-permute-done.7
  125.9 1.3 collective-permute-done.5
  127.2 0.1 slice_reduce_fusion.2
  127.2 0.1 unstack.11
  127.3 0.1 mul.122
  127.4 0.1 reduce_sum.58
  127.5 0.1 mul.129
  127.5 0.2 select_reduce_fusion
  127.7 0.1 add.159
  127.8 0.4 multiply_reduce_fusion
  128.2 0.1 multiply_multiply_fusion
  128.2 0.1 reshape_squeeze.3
  128.3 0.6 slice_bitcast_fusion.1
  129.0 7.5 %shard_map.73 = bf16[320,3584]{1,0:T(8,128)(2,1)} custom-call(s32[4]{0:T(128)} %pad_add_fusion.starts_ref, f32[3,512]{1,0:T(4,128)} %get-tuple-element.27.refs_0_, bf16[640,512]{1,0:T(8,128)(2,1)} %get-tuple-element.13.first_ref.refs_1_, bf16[512,3712]{1,0:T(8,128)(2,1)} %get-tuple-element.11.refs_2_, f32[3,512]{1,0:T(4,128)} %get-tuple-element.26.refs_3_, ...), custom_call_target="tpu_custom_call" | custom-call | flops 2348810240 | bytes 9633792 | tf_op jit(solution)/shard_map/pallas_call | solution.py:286
  136.5 1.5 collective-permute-start.8
  138.0 0.1 mul.133
  138.1 27.4 %reduce-scatter.2.cloned.1.call-done.in_ref = bf16[64,3584]{1,0:T(8,128)(2,1)} async-done(((bf16[512,3584]{1,0:T(8,128)(2,1)}), bf16[64,3584]{1,0:T(8,128)(2,1)}) %reduce-scatter.2.cloned.1.call-update) | async-done | bytes 458768 | tf_op jit(solution)/shard_map/reduce_scatter | solution.py:392
  165.5 2.1 %shard_map.71.refs_6_ = bf16[16,64,224]{2,1,0:T(8,128)(2,1)} custom-call(bf16[64,3584]{1,0:T(8,128)(2,1)} %reduce-scatter.2.cloned.1.call-done.in_ref), custom_call_target="tpu_custom_call" | custom-call | bytes 917504 | tf_op jit(solution)/shard_map/pallas_call | solution.py:316
  167.6 7.3 %all-to-all-start.2 = ((bf16[16,64,224]{2,1,0:T(8,128)(2,1)}), bf16[16,64,224]{2,1,0:T(8,128)(2,1)S(1)}, u32[]{:S(2)}, u32[]{:S(2)}) async-start(bf16[16,64,224]{2,1,0:T(8,128)(2,1)} %shard_map.71.refs_6_), calls=%async_computation.3 | async-start | bytes 1048576 | tf_op jit(solution)/shard_map/all_to_all | solution.py:395
  174.8 7.5 %shard_map.72 = bf16[320,3584]{1,0:T(8,128)(2,1)} custom-call(s32[4]{0:T(128)} %pad_add_fusion.starts_ref, f32[3,512]{1,0:T(4,128)} %get-tuple-element.27.refs_0_, bf16[640,512]{1,0:T(8,128)(2,1)} %get-tuple-element.13.first_ref.refs_1_, bf16[512,3712]{1,0:T(8,128)(2,1)} %get-tuple-element.11.refs_2_, f32[3,512]{1,0:T(4,128)} %get-tuple-element.26.refs_3_, ...), custom_call_target="tpu_custom_call" | custom-call | flops 2348810240 | bytes 9633792 | tf_op jit(solution)/shard_map/pallas_call | solution.py:286
  182.3 7.2 %collective-permute-done.8 = bf16[320,3584]{1,0:T(8,128)(2,1)S(1)} collective-permute-done((bf16[320,3584]{1,0:T(8,128)(2,1)}, bf16[320,3584]{1,0:T(8,128)(2,1)S(1)}, u32[]{:S(2)}, u32[]{:S(2)}) %collective-permute-start.8) | collective-permute-done | bytes 2293792 | tf_op jit(solution)/shard_map/ppermute | solution.py:424
  189.5 3.6 %fusion = bf16[3584,320]{0,1:T(8,128)(2,1)} fusion(bf16[320,3584]{1,0:T(8,128)(2,1)S(1)} %collective-permute-done.8, bf16[320,3584]{1,0:T(8,128)(2,1)} %shard_map.72), kind=kLoop, calls=%fused_computation.1 | loop fusion | flops 4587520 | bytes 6881280 | tf_op jit(solution)/shard_map/transpose | solution.py:427
  193.1 1.0 all-to-all-done.2
  194.1 0.1 convert_reduce_fusion
  194.2 0.1 fusion.3
  194.3 0.7 copy.36
  (40 shorter events, 0.4 us)
Async XLA Ops:
  7.2 59.9 %all-gather.2.cloned.1.call-start = ((), (), s32[]{:S(2)}) async-start(), calls=%async_computation.4 | async-start | bytes 4276224 | tf_op jit(solution)/shard_map/all_gather | solution.py:363
  10.6 154.9 %reduce-scatter.2.cloned.1.call-start = ((), (), s32[]{:S(2)}) async-start(), calls=%async_computation.5 | async-start | bytes 4128768 | tf_op jit(solution)/shard_map/reduce_scatter | solution.py:392
  10.6 51.9 %collective-permute-start = (bf16[320,3584]{1,0:T(8,128)(2,1)}, bf16[320,3584]{1,0:T(8,128)(2,1)S(1)}, u32[]{:S(2)}, u32[]{:S(2)}) collective-permute-start(bf16[320,3584]{1,0:T(8,128)(2,1)} %bitcast.68), channel_id=1, source_target_pairs={{0,4},{4,0},{1,5},{5,1},{2,6},{6,2},{3,7},{7,3},{8,12},{12,8},{9,1... | collective-permute-start | bytes 6881288 | tf_op jit(solution)/shard_map/ppermute | solution.py:360
  12.2 51.0 %collective-permute-start.1 = (bf16[320,3584]{1,0:T(8,128)(2,1)}, bf16[320,3584]{1,0:T(8,128)(2,1)}, u32[]{:S(2)}, u32[]{:S(2)}) collective-permute-start(bf16[320,3584]{1,0:T(8,128)(2,1)} %bitcast.69), channel_id=1, source_target_pairs={{0,16},{16,0},{1,17},{17,1},{2,18},{18,2},{3,19},{19,3},{4,20},{20... | collective-permute-start | bytes 6881288 | tf_op jit(solution)/shard_map/ppermute | solution.py:361
  62.5 4.6 %copy-start.5 = (bf16[320,3584]{1,0:T(8,128)(2,1)}, bf16[320,3584]{1,0:T(8,128)(2,1)S(1)}, u32[]{:S(2)}) copy-start(bf16[320,3584]{1,0:T(8,128)(2,1)S(1)} %collective-permute-done.refs_1_) | copy-start | bytes 6881284
  62.5 4.6 %collective-permute-start.2 = (bf16[320,3584]{1,0:T(8,128)(2,1)S(1)}, bf16[320,3584]{1,0:T(8,128)(2,1)}, u32[]{:S(2)}, u32[]{:S(2)}) collective-permute-start(bf16[320,3584]{1,0:T(8,128)(2,1)S(1)} %collective-permute-done.refs_1_), channel_id=1, source_target_pairs={{0,16},{16,0},{1,17},{17,1},{2,18},{18,2},{3,19},{19,3},{4,20},{20... | collective-permute-start | bytes 6881288 | tf_op jit(solution)/shard_map/ppermute | solution.py:369
  77.8 17.4 %collective-permute-start.3 = (bf16[512,3712]{1,0:T(8,128)(2,1)}, bf16[512,3712]{1,0:T(8,128)(2,1)S(1)}, u32[]{:S(2)}, u32[]{:S(2)}) collective-permute-start(bf16[512,3712]{1,0:T(8,128)(2,1)} %get-tuple-element.11.refs_2_), channel_id=1, source_target_pairs={{0,16},{16,0},{1,17},{17,1},{2,18},{18,2},{3,19},{19,3},{4,20},{20... | collective-permute-start | bytes 11403272 | tf_op jit(solution)/shard_map/ppermute | solution.py:379
  78.0 17.2 %collective-permute-start.4 = (bf16[640,512]{1,0:T(8,128)(2,1)}, bf16[640,512]{1,0:T(8,128)(2,1)S(1)}, u32[]{:S(2)}, u32[]{:S(2)}) collective-permute-start(bf16[640,512]{1,0:T(8,128)(2,1)} %get-tuple-element.12.last_ref), channel_id=1, source_target_pairs={{0,16},{16,0},{1,17},{17,1},{2,18},{18,2},{3,19},{19,3},{4,20},{20... | collective-permute-start | bytes 1966088 | tf_op jit(solution)/shard_map/ppermute | solution.py:380
  95.2 0.9 copy-start.1
  95.2 2.1 %copy-start = (bf16[512,3712]{1,0:T(8,128)(2,1)}, bf16[512,3712]{1,0:T(8,128)(2,1)S(1)}, u32[]{:S(2)}) copy-start(bf16[512,3712]{1,0:T(8,128)(2,1)S(1)} %collective-permute-done.3._.refs_5_) | copy-start | bytes 11403268
  95.2 0.7 copy-start.2
  95.9 15.0 %copy-start.4 = (f32[8,512]{1,0:T(8,128)S(1)}, f32[8,512]{1,0:T(8,128)}, u32[]{:S(2)}) copy-start(f32[8,512]{1,0:T(8,128)} %get-tuple-element.8) | copy-start | bytes 49156
  122.0 0.7 copy-start.3
  122.7 2.3 %collective-permute-start.6 = (f32[4,512]{1,0:T(4,128)S(1)}, f32[4,512]{1,0:T(4,128)S(1)}, u32[]{:S(2)}, u32[]{:S(2)}) collective-permute-start(f32[4,512]{1,0:T(4,128)S(1)} %copy-done.3), channel_id=1, source_target_pairs={{0,16},{16,0},{1,17},{17,1},{2,18},{18,2},{3,19},{19,3},{4,20},{20... | collective-permute-start | bytes 24584 | tf_op jit(solution)/shard_map/ppermute | solution.py:399
  122.7 3.1 %collective-permute-start.7 = (f32[2,512]{1,0:T(2,128)S(1)}, f32[2,512]{1,0:T(2,128)S(1)}, u32[]{:S(2)}, u32[]{:S(2)}) collective-permute-start(f32[2,512]{1,0:T(2,128)S(1)} %get-tuple-element.35), channel_id=1, source_target_pairs={{0,20},{4,16},{16,4},{20,0},{1,21},{5,17},{17,5},{21,1},{2,22},{6,... | collective-permute-start | bytes 12296 | tf_op jit(solution)/shard_map/ppermute | solution.py:401
  123.5 3.6 %collective-permute-start.5 = (f32[2,512]{1,0:T(2,128)S(1)}, f32[2,512]{1,0:T(2,128)S(1)}, u32[]{:S(2)}, u32[]{:S(2)}) collective-permute-start(f32[2,512]{1,0:T(2,128)S(1)} %get-tuple-element.35), channel_id=1, source_target_pairs={{0,4},{4,0},{1,5},{5,1},{2,6},{6,2},{3,7},{7,3},{8,12},{12,8},{9,1... | collective-permute-start | bytes 12296 | tf_op jit(solution)/shard_map/ppermute | solution.py:400
  136.5 53.1 %collective-permute-start.8 = (bf16[320,3584]{1,0:T(8,128)(2,1)}, bf16[320,3584]{1,0:T(8,128)(2,1)S(1)}, u32[]{:S(2)}, u32[]{:S(2)}) collective-permute-start(bf16[320,3584]{1,0:T(8,128)(2,1)} %shard_map.73), channel_id=1, source_target_pairs={{0,4},{4,0},{1,5},{5,1},{2,6},{6,2},{3,7},{7,3},{8,12},{12,8},{9,1... | collective-permute-start | bytes 6881288 | tf_op jit(solution)/shard_map/ppermute | solution.py:424
  167.6 26.5 %all-to-all-start.2 = ((bf16[16,64,224]{2,1,0:T(8,128)(2,1)}), bf16[16,64,224]{2,1,0:T(8,128)(2,1)S(1)}, u32[]{:S(2)}, u32[]{:S(2)}) async-start(bf16[16,64,224]{2,1,0:T(8,128)(2,1)} %shard_map.71.refs_6_), calls=%async_computation.3 | async-start | bytes 1048576 | tf_op jit(solution)/shard_map/all_to_all | solution.py:395
Sparse Core Ops, SparseCore 0:
  10.7 54.0 all-gather.1
  122.2 43.2 reduce-scatter.1
